TPU v7x, 128 devices: a whole 4x4x4 slice. The times are simulated.
128 devices in a mesh: section: 2 (over y_lo), row: 4 (over y_hi, core), col: 16 (over x, z).
Axes of the slice: x: 4, y: 4 (y_hi: 2, y_lo: 2; y = y_hi * 2 + y_lo), z: 4, core: 2. Of those that a mesh axis runs over, the one named last changes fastest.
Arguments:
- inputs: bfloat16 [2, 16, 384, 1536], P(None, 'col', 'row'), may hold values from -6 to 6
- cotangent: bfloat16 [2, 16, 384, 1536], P(None, 'col', 'row'), may hold values from -6 to 6
- segment_ids: int32 [2, 16, 384], P(None, 'col'), may hold values from 0 to 1, as said below
- routes: int32 [2, 2, 16, 384, 4], P('section', None, 'col', 'row'), may hold values from 0 to 31, all different within a row; in each aligned block of 96 rows (0 to 95, 96 to 191, ..., all dimensions but the last counted through in order) at most 15 rows name the same one
- attn_gain: bfloat16 [2, 1536], P('section', ('row', 'col')), may hold values from 0.5 to 1.5
- w_query: bfloat16 [2, 1536, 1536], P('section', ('row', 'col')), may hold values from -0.15625 to 0.15625
- w_key: bfloat16 [2, 1536, 256], P('section', ('row', 'col')), may hold values from -0.15625 to 0.15625
- w_value: bfloat16 [2, 1536, 256], P('section', ('row', 'col')), may hold values from -0.15625 to 0.15625
- w_out: bfloat16 [2, 1536, 1536], P('section', ('row', 'col')), may hold values from -0.625 to 0.625
- ffn_gain: bfloat16 [2, 1536], P('section', ('row', 'col')), may hold values from 0.5 to 1.5
- w_router: bfloat16 [2, 1536, 32], P('section', ('row', 'col')), may hold values from -0.078125 to 0.078125
- w_gate: bfloat16 [2, 32, 768, 1536], P('section', 'col', 'row'), may hold values from -0.15625 to 0.15625
- w_up: bfloat16 [2, 32, 768, 1536], P('section', 'col', 'row'), may hold values from -0.15625 to 0.15625
- w_down: bfloat16 [2, 32, 768, 1536], P('section', 'col', 'row'), may hold values from -0.21875 to 0.21875
Outputs:
- layer_outputs: float32 [2, 2, 16, 384, 1536], P('section', None, 'col', 'row')
- input_grads: float32 [2, 2, 16, 384, 1536], P('section', None, 'col', 'row')
- attn_gain_grad: float32 [2, 1536], P('section', ('row', 'col'))
- query_grad: float32 [2, 1536, 1536], P('section', ('row', 'col'))
- key_grad: float32 [2, 1536, 256], P('section', ('row', 'col'))
- value_grad: float32 [2, 1536, 256], P('section', ('row', 'col'))
- out_grad: float32 [2, 1536, 1536], P('section', ('row', 'col'))
- ffn_gain_grad: float32 [2, 1536], P('section', ('row', 'col'))
- router_grad: float32 [2, 1536, 32], P('section', ('row', 'col'))
- gate_grad: float32 [2, 32, 768, 1536], P('section', 'col', 'row')
- up_grad: float32 [2, 32, 768, 1536], P('section', 'col', 'row')
- down_grad: float32 [2, 32, 768, 1536], P('section', 'col', 'row')
Inputs may be any that keep to these rules, and one draw needn't show every extreme that they name: `segment_ids`: segment ids never fall along a sequence; a sequence holds one document or two, and each document has 144 positions or more; in each micro-batch one sequence is a single document from its first position to its last. In the rows of one device (aligned blocks of 96 tokens of one sequence) no expert is named by more than 15 routes, a bound that some block reaches.
All inputs are finite; a program needn't handle non-finite values.
Results may differ from a plain program's by a relative error of at most 0.025.
Values may be sent and summed in bfloat16 or wider, within the bound.
No kernel may reach another device: no remote copies, remote signals or barrier semaphores. Data moves between devices by JAX's collectives and lax.ppermute only.
A program may use at most 448 MiB of HBM per device.

v0:
```python
import math

import jax
import jax.numpy as jnp
from jax import lax
from jax.sharding import PartitionSpec as P

HEADS = 12
KV_HEADS = 2
HEAD_DIM = 128
CAP = 15


EPSILON = 1e-06


def in_one_piece(arrays, axis, dim, along):
    widths = [a.shape[along] for a in arrays]
    both = jnp.concatenate(arrays, axis=along)
    whole = lax.all_gather(both, axis, axis=dim, tiled=True)
    return tuple(jnp.split(whole, [sum(widths[:k]) for k in range(1, len(widths))], axis=along))


def cut_along(value, dim, devices):
    before, after = (value.shape[:dim], value.shape[dim + 1 :])
    return jnp.moveaxis(value.reshape(*before, devices, -1, *after), dim, 0)


def summed_on_arrival(value, axis, dim):
    blocks = cut_along(value, dim, lax.axis_size(axis))
    arrived = lax.all_to_all(blocks, axis, split_axis=0, concat_axis=0, tiled=True)
    return arrived.astype(jnp.float32).sum(axis=0)


def in_one_piece_2(arrays, axis, dim, along):
    widths = [a.shape[along] for a in arrays]
    both = jnp.concatenate(arrays, axis=along)
    whole = summed_on_arrival(both, axis, dim)
    return tuple(jnp.split(whole, [sum(widths[:k]) for k in range(1, len(widths))], axis=along))


def sent_together(arrays, axis, dim, along):
    widths = [math.prod(a.shape[along:]) for a in arrays]
    both = jnp.concatenate(
        [a.reshape(*a.shape[:along], w) for a, w in zip(arrays, widths)], axis=along
    )
    whole = lax.psum_scatter(both, axis, scatter_dimension=dim, tiled=True)
    blocks = jnp.split(whole, [sum(widths[:k]) for k in range(1, len(widths))], axis=along)
    return tuple(
        (b.reshape(*whole.shape[:along], *a.shape[along:]) for a, b in zip(arrays, blocks))
    )


def gather_turned(arrays, axis, dims):
    turned = [jnp.moveaxis(a, dim, 0) for a, dim in zip(arrays, dims)]
    both = jnp.concatenate([t.reshape(len(t), -1) for t in turned], axis=1)
    whole, at, done = (lax.all_gather(both, axis, axis=0, tiled=True), 0, [])
    for t, dim in zip(turned, dims):
        slab = whole[:, at : at + t[0].size].reshape(-1, *t.shape[1:])
        done.append(jnp.moveaxis(slab, 0, dim))
        at += t[0].size
    return tuple(done)


def passed_along(value, axis, steps):
    count = lax.axis_size(axis)
    leading, last = (max(0, -steps), min(count, count - steps))
    return lax.ppermute(value, axis, [(source, source + steps) for source in range(leading, last)])


def norm_apply(stream, gain):
    return stream * lax.rsqrt(jnp.mean(stream * stream, -1, keepdims=True) + EPSILON) * gain


def rotate(vectors, positions):
    half = vectors.shape[-1] // 2
    freqs = 10000.0 ** (-2.0 * jnp.arange(half).astype(jnp.float32) / vectors.shape[-1])
    angles = positions.astype(jnp.float32)[:, None] * freqs[None, :]
    cosine = jnp.cos(angles)[:, None, :]
    sine = jnp.sin(angles)[:, None, :]
    first = vectors[..., :half]
    second = vectors[..., half:]
    return jnp.concatenate([first * cosine - second * sine, second * cosine + first * sine], -1)


def gelu_tanh(values):
    return (
        0.5
        * values
        * (1.0 + jnp.tanh(0.7978845608028654 * (values + 0.044715 * values * values * values)))
    )


def glu_piece(gate, lifted):
    return gelu_tanh(gate) * lifted


def route_gates(logits, chosen):
    probs = jax.nn.softmax(logits, -1)
    picked = jnp.sum(probs[:, None, :] * chosen, -1)
    return picked / jnp.sum(picked, -1, keepdims=True)


def contract_rows(left, right):
    return lax.dot_general(
        left, right, (((0,), (0,)), ((), ())), preferred_element_type=jnp.float32
    )


def contract_cols(left, right):
    return lax.dot_general(
        left, right, (((1,), (1,)), ((), ())), preferred_element_type=jnp.float32
    )


def attention_mask(positions, segments):
    key_positions = jnp.arange(segments.shape[0], dtype=jnp.int32)
    own_segment = jnp.take(segments, positions)
    return (key_positions[None, :] <= positions[:, None]) & (
        segments[None, :] == own_segment[:, None]
    )


def score_block(query, keys_all, mask):
    scores = jnp.einsum(
        "qhgd,khd->hgqk", query, keys_all, preferred_element_type=jnp.float32
    ) * HEAD_DIM ** (-0.5)
    return jnp.where(mask[None, None], scores, -1e30)


def assign_slots(chosen_routes, experts):
    tokens, top = chosen_routes.shape
    flat_routes = chosen_routes.reshape(tokens * top)
    hot_table = (flat_routes[:, None] == jnp.arange(experts, dtype=jnp.int32)[None, :]).astype(
        jnp.int32
    )
    before = jnp.cumsum(hot_table, 0) - hot_table
    slot_ids = flat_routes * CAP + jnp.sum(before * hot_table, -1)
    slot_hits = (jnp.arange(experts * CAP, dtype=jnp.int32)[:, None] == slot_ids[None, :]).reshape(
        experts * CAP, tokens, top
    )
    return (slot_ids, slot_hits)


def layer_forward(stream, segments, chosen_routes, dense, experts_local, positions):
    gain_attn, w_query, w_key, w_value, w_out, gain_ffn, w_router = dense
    w_gate, w_up, w_down = experts_local
    tokens, width = stream.shape
    experts = w_router.shape[1]
    group = HEADS // KV_HEADS
    normed = norm_apply(stream, gain_attn.astype(jnp.float32)).astype(jnp.bfloat16)
    query = rotate(
        jnp.dot(normed, w_query, preferred_element_type=jnp.float32).reshape(
            tokens, HEADS, HEAD_DIM
        ),
        positions,
    )
    query = query.astype(jnp.bfloat16).reshape(tokens, KV_HEADS, group, HEAD_DIM)
    key_local = rotate(
        jnp.dot(normed, w_key, preferred_element_type=jnp.float32).reshape(
            tokens, KV_HEADS, HEAD_DIM
        ),
        positions,
    )
    key_local = key_local.astype(jnp.bfloat16).reshape(tokens, KV_HEADS * HEAD_DIM)
    value_local = jnp.dot(normed, w_value, preferred_element_type=jnp.float32).astype(jnp.bfloat16)
    keys_all, values_all = in_one_piece((key_local, value_local), "row", 0, 1)
    seq_len = keys_all.shape[0]
    keys_all = keys_all.reshape(seq_len, KV_HEADS, HEAD_DIM)
    values_all = values_all.reshape(seq_len, KV_HEADS, HEAD_DIM)
    mask = attention_mask(positions, segments)
    scores = score_block(query, keys_all, mask)
    top_score = jnp.max(scores, -1, keepdims=True)
    expo = jnp.exp(scores - top_score)
    denom = jnp.sum(expo, -1, keepdims=True)
    weights = expo / denom
    log_total = top_score + jnp.log(denom)
    mixed = jnp.einsum(
        "hgqk,khd->qhgd",
        weights.astype(jnp.bfloat16),
        values_all,
        preferred_element_type=jnp.float32,
    )
    mixed = mixed.reshape(tokens, width).astype(jnp.bfloat16)
    middle = stream + jnp.dot(mixed, w_out, preferred_element_type=jnp.float32)
    normed_ffn = norm_apply(middle, gain_ffn.astype(jnp.float32)).astype(jnp.bfloat16)
    logits = jnp.dot(normed_ffn, w_router, preferred_element_type=jnp.float32)
    chosen = (
        chosen_routes[:, :, None] == jnp.arange(experts, dtype=jnp.int32)[None, None, :]
    ).astype(jnp.float32)
    gates = route_gates(logits, chosen)
    slot_ids, slot_hits = assign_slots(chosen_routes, experts)
    dispatch = jnp.any(slot_hits, -1).astype(jnp.bfloat16)
    per_owner = w_gate.shape[0]
    outgoing = jnp.dot(dispatch, normed_ffn, preferred_element_type=jnp.float32).astype(
        jnp.bfloat16
    )
    outgoing = outgoing.reshape(experts // per_owner, per_owner, CAP, width)
    arrived = lax.all_to_all(outgoing, "col", split_axis=0, concat_axis=0, tiled=True)
    gate = jnp.einsum("sjcd,jfd->sjcf", arrived, w_gate, preferred_element_type=jnp.float32)
    lifted = jnp.einsum("sjcd,jfd->sjcf", arrived, w_up, preferred_element_type=jnp.float32)
    hidden = glu_piece(gate, lifted).astype(jnp.bfloat16)
    produced = jnp.einsum(
        "sjcf,jfd->sjcd", hidden, w_down, preferred_element_type=jnp.float32
    ).astype(jnp.bfloat16)
    returned = lax.all_to_all(produced, "col", split_axis=0, concat_axis=0, tiled=True).reshape(
        experts * CAP, width
    )
    picked_rows = (
        jnp.take(returned, slot_ids, axis=0).astype(jnp.float32).reshape(tokens, -1, width)
    )
    result = middle + jnp.sum(gates[:, :, None] * picked_rows, 1)
    kept = (
        stream,
        middle,
        normed,
        query,
        keys_all,
        values_all,
        mask,
        log_total,
        mixed,
        normed_ffn,
        logits,
        chosen,
        gates,
        slot_hits,
        dispatch,
        arrived,
        gate,
        lifted,
        hidden,
        picked_rows,
    )
    return (result, kept)


def layer_backward(grad_out, kept, dense, experts_local, positions):
    (
        stream,
        middle,
        normed,
        query,
        keys_all,
        values_all,
        mask,
        log_total,
        mixed,
        normed_ffn,
        logits,
        chosen,
        gates,
        slot_hits,
        dispatch,
        arrived,
        gate,
        lifted,
        hidden,
        picked_rows,
    ) = kept
    gain_attn, w_query, w_key, w_value, w_out, gain_ffn, w_router = dense
    w_gate, w_up, w_down = experts_local
    tokens, width = stream.shape
    gate_grads = jnp.sum(grad_out[:, None, :] * picked_rows, -1)
    weighted = jnp.sum(slot_hits.astype(jnp.float32) * gates[None], -1)
    out_grads = jnp.dot(
        weighted, grad_out, precision=lax.Precision.HIGHEST, preferred_element_type=jnp.float32
    )
    out_grads = out_grads.astype(jnp.bfloat16).reshape(arrived.shape)
    arrived_grads = lax.all_to_all(out_grads, "col", split_axis=0, concat_axis=0, tiled=True)
    hidden_grads = jnp.einsum(
        "sjcd,jfd->sjcf", arrived_grads, w_down, preferred_element_type=jnp.float32
    )
    grad_down = jnp.einsum(
        "sjcf,sjcd->jfd", hidden, arrived_grads, preferred_element_type=jnp.float32
    )
    unused, glu_back = jax.vjp(glu_piece, gate, lifted)
    gate_back, lifted_back = glu_back(hidden_grads)
    gate_back = gate_back.astype(jnp.bfloat16)
    lifted_back = lifted_back.astype(jnp.bfloat16)
    grad_gate = jnp.einsum("sjcf,sjcd->jfd", gate_back, arrived, preferred_element_type=jnp.float32)
    grad_up = jnp.einsum("sjcf,sjcd->jfd", lifted_back, arrived, preferred_element_type=jnp.float32)
    sent_grads = jnp.einsum("sjcf,jfd->sjcd", gate_back, w_gate, preferred_element_type=jnp.float32)
    sent_grads = sent_grads + jnp.einsum(
        "sjcf,jfd->sjcd", lifted_back, w_up, preferred_element_type=jnp.float32
    )
    token_grads = (
        lax.all_to_all(
            sent_grads.astype(jnp.bfloat16), "col", split_axis=0, concat_axis=0, tiled=True
        )
        .astype(sent_grads.dtype)
        .reshape(dispatch.shape[0], width)
    )
    ffn_grads = lax.dot_general(
        dispatch.astype(jnp.float32),
        token_grads,
        (((0,), (0,)), ((), ())),
        precision=lax.Precision.HIGHEST,
        preferred_element_type=jnp.float32,
    )
    unused, route_back = jax.vjp(route_gates, logits, chosen)
    logit_grads = route_back(gate_grads)[0].astype(jnp.bfloat16)
    grad_router = contract_rows(normed_ffn, logit_grads)
    ffn_grads = ffn_grads + contract_cols(logit_grads, w_router)
    unused, norm_back = jax.vjp(norm_apply, middle, gain_ffn.astype(jnp.float32))
    middle_part, grad_gain_ffn = norm_back(ffn_grads)
    middle_grads = grad_out + middle_part
    branch_grads = middle_grads.astype(jnp.bfloat16)
    grad_out_proj = contract_rows(mixed, branch_grads)
    mixed_grads = contract_cols(branch_grads, w_out).astype(jnp.bfloat16).reshape(query.shape)
    weights = jnp.exp(score_block(query, keys_all, mask) - log_total)
    weight_grads = jnp.einsum(
        "qhgd,khd->hgqk", mixed_grads, values_all, preferred_element_type=jnp.float32
    )
    grad_values_all = jnp.einsum(
        "hgqk,qhgd->khd",
        weights.astype(jnp.bfloat16),
        mixed_grads,
        preferred_element_type=jnp.float32,
    )
    score_grads = (
        weights * (weight_grads - jnp.sum(weights * weight_grads, -1, keepdims=True))
    ).astype(jnp.bfloat16)
    scale = HEAD_DIM ** (-0.5)
    query_grads = (
        jnp.einsum("hgqk,khd->qhgd", score_grads, keys_all, preferred_element_type=jnp.float32)
        * scale
    )
    grad_keys_all = (
        jnp.einsum("hgqk,qhgd->khd", score_grads, query, preferred_element_type=jnp.float32) * scale
    )
    seq_len = keys_all.shape[0]
    key_grads, value_grads = in_one_piece_2(
        (
            grad_keys_all.reshape(seq_len, -1).astype(jnp.bfloat16),
            grad_values_all.reshape(seq_len, -1).astype(jnp.bfloat16),
        ),
        "row",
        0,
        1,
    )
    query_back = (
        rotate(query_grads.reshape(tokens, HEADS, HEAD_DIM), -positions)
        .reshape(tokens, width)
        .astype(jnp.bfloat16)
    )
    key_back = (
        rotate(key_grads.reshape(tokens, KV_HEADS, HEAD_DIM), -positions)
        .reshape(tokens, -1)
        .astype(jnp.bfloat16)
    )
    value_back = value_grads.astype(jnp.bfloat16)
    grad_query = contract_rows(normed, query_back)
    grad_key = contract_rows(normed, key_back)
    grad_value = contract_rows(normed, value_back)
    normed_grads = (
        contract_cols(query_back, w_query)
        + contract_cols(key_back, w_key)
        + contract_cols(value_back, w_value)
    )
    unused, norm_back_attn = jax.vjp(norm_apply, stream, gain_attn.astype(jnp.float32))
    stream_part, grad_gain_attn = norm_back_attn(normed_grads)
    dense_grads = (
        grad_gain_attn,
        grad_query,
        grad_key,
        grad_value,
        grad_out_proj,
        grad_gain_ffn,
        grad_router,
    )
    return (middle_grads + stream_part, dense_grads, (grad_gate, grad_up, grad_down))


def reduce_grads(dense_grads, expert_grads):
    dense_part = sent_together(
        (
            dense_grads[0],
            dense_grads[1],
            dense_grads[2],
            dense_grads[3],
            dense_grads[4],
            dense_grads[5],
            dense_grads[6],
        ),
        ("row", "col"),
        0,
        1,
    )
    expert_part = (
        lax.psum_scatter(
            expert_grads[0].astype(jnp.bfloat16), "row", scatter_dimension=1, tiled=True
        ).astype(jnp.float32),
        lax.psum_scatter(
            expert_grads[1].astype(jnp.bfloat16), "row", scatter_dimension=1, tiled=True
        ).astype(jnp.float32),
        lax.psum_scatter(
            expert_grads[2].astype(jnp.bfloat16), "row", scatter_dimension=1, tiled=True
        ).astype(jnp.float32),
    )
    return (dense_part, expert_part)


def on_device(
    inputs,
    cotangent,
    segment_ids,
    routes,
    attn_gain,
    w_query,
    w_key,
    w_value,
    w_out,
    ffn_gain,
    w_router,
    w_gate,
    w_up,
    w_down,
):
    section = lax.axis_index("section")
    row_index = lax.axis_index("row")
    micro = inputs.shape[0]
    tokens = inputs.shape[2]
    width = inputs.shape[3]
    dense = gather_turned(
        (attn_gain, w_query, w_key, w_value, w_out, ffn_gain, w_router),
        ("row", "col"),
        (1, 1, 1, 1, 1, 1, 1),
    )
    dense = tuple((piece[0] for piece in dense))
    experts_local = in_one_piece((w_gate, w_up, w_down), "row", 2, 0)
    experts_local = tuple((piece[0] for piece in experts_local))
    positions = row_index * tokens + jnp.arange(tokens, dtype=jnp.int32)
    route_table = routes[0, :, 0]
    segment_table = segment_ids[:, 0]
    carried = jnp.zeros((tokens, width), jnp.float32)
    kept_ticks = []
    out_ticks = []
    for tick in range(micro + 1):
        if tick < micro:
            first = inputs[tick, 0].astype(jnp.float32)
        else:
            first = jnp.zeros((tokens, width), jnp.float32)
        stream = jnp.where(section == 0, first, carried)
        offset = tick - section
        current = jnp.clip(offset, 0, micro - 1)
        chosen_routes = lax.dynamic_index_in_dim(route_table, current, 0, keepdims=False)
        segments = lax.dynamic_index_in_dim(segment_table, current, 0, keepdims=False)
        result, kept = layer_forward(
            stream, segments, chosen_routes, dense, experts_local, positions
        )
        kept_ticks.append(kept)
        out_ticks.append(result)
        if tick < micro:
            carried = passed_along(result, "section", 1)
    carried_grad = jnp.zeros((tokens, width), jnp.float32)
    grad_ticks = []
    for tick in range(micro + 1):
        if tick < micro:
            from_target = cotangent[micro - 1 - tick, 0].astype(jnp.float32)
        else:
            from_target = jnp.zeros((tokens, width), jnp.float32)
        grad_in = jnp.where(section == 1, from_target, carried_grad)
        stream_grad, step_dense, step_expert = layer_backward(
            grad_in, kept_ticks[micro - tick], dense, experts_local, positions
        )
        grad_ticks.append(stream_grad)
        if tick == 0:
            sums = (step_dense, step_expert)
        else:
            sums = jax.tree.map(jnp.add, sums, (step_dense, step_expert))
        if tick < micro:
            carried_grad = passed_along(stream_grad.astype(jnp.bfloat16), "section", -1).astype(
                stream_grad.dtype
            )
    dense_sum, expert_sum = sums
    dense_sum, expert_sum = reduce_grads(dense_sum, expert_sum)
    layer_outputs = jnp.stack(
        [jnp.where(section == 0, out_ticks[index], out_ticks[index + 1]) for index in range(micro)]
    )
    input_grads = jnp.stack(
        [
            jnp.where(section == 1, grad_ticks[micro - 1 - index], grad_ticks[micro - index])
            for index in range(micro)
        ]
    )
    return (
        layer_outputs[None, :, None],
        input_grads[None, :, None],
        dense_sum[0][None],
        dense_sum[1][None],
        dense_sum[2][None],
        dense_sum[3][None],
        dense_sum[4][None],
        dense_sum[5][None],
        dense_sum[6][None],
        expert_sum[0][None],
        expert_sum[1][None],
        expert_sum[2][None],
    )


def solution(mesh):
    placed = (
        P(None, "col", "row", None),
        P(None, "col", "row", None),
        P(None, "col", None),
        P("section", None, "col", "row", None),
        P("section", ("row", "col")),
        P("section", ("row", "col"), None),
        P("section", ("row", "col"), None),
        P("section", ("row", "col"), None),
        P("section", ("row", "col"), None),
        P("section", ("row", "col")),
        P("section", ("row", "col"), None),
        P("section", "col", "row", None),
        P("section", "col", "row", None),
        P("section", "col", "row", None),
    )
    return jax.shard_map(
        on_device,
        mesh=mesh,
        in_specs=placed,
        out_specs=(
            P("section", None, "col", "row", None),
            P("section", None, "col", "row", None),
            P("section", ("row", "col")),
            P("section", ("row", "col"), None),
            P("section", ("row", "col"), None),
            P("section", ("row", "col"), None),
            P("section", ("row", "col"), None),
            P("section", ("row", "col")),
            P("section", ("row", "col"), None),
            P("section", "col", "row", None),
            P("section", "col", "row", None),
            P("section", "col", "row", None),
        ),
        check_vma=False,
    )
```

profile of v0, /device:TPU:9, one launch (start us, length us, event | category | flops | bytes accessed | tf_op | source)
XLA Modules:
  0.0 1734.6 jit_solution(12565978149429064292)
XLA Ops:
  25.5 78.4 %all-gather.3.cloned.1.call-done = bf16[1536,3618]{1,0:T(8,128)(2,1)} async-done(((bf16[24,3618]{1,0:T(8,128)(2,1)}), bf16[1536,3618]{1,0:T(8,128)(2,1)}) %all-gather.3.cloned.1.call-update) | async-done | bytes 11114512 | tf_op jit(solution)/shard_map/all_gather | solution.py:57
  109.8 8.5 all_gather.16
  118.5 8.5 slice_bitcast_fusion.21
  127.0 6.6 copy.368
  156.7 41.8 %all-gather.5.cloned.1.call-done = bf16[3,2,768,1536]{3,2,1,0:T(8,128)(2,1)} async-done(((bf16[3,2,192,1536]{3,2,1,0:T(8,128)(2,1)}), bf16[3,2,768,1536]{3,2,1,0:T(8,128)(2,1)}) %all-gather.5.cloned.1.call-update) | async-done | bytes 14155792 | tf_op jit(solution)/shard_map/all_gather | solution.py:20
  212.0 6.6 all-to-all-start.1
  221.5 18.7 %all-to-all-done.1 = bf16[16,2,15,1536]{3,1,2,0:T(2,128)(2,1)S(1)} async-done(((bf16[16,2,15,1536]{3,1,2,0:T(2,128)(2,1)}), bf16[16,2,15,1536]{3,1,2,0:T(2,128)(2,1)S(1)}, u32[]{:S(2)}, u32[]{:S(2)}) %all-to-all-start.1) | async-done | bytes 1474592 | tf_op jit(solution)/shard_map/all_to_all | solution.py:206
  255.9 12.9 collective-permute-done
  273.6 10.9 all_gather.18
  309.3 20.0 %all-to-all-done.2 = bf16[16,2,15,1536]{3,1,2,0:T(2,128)(2,1)S(1)} async-done(((bf16[16,2,15,1536]{3,1,2,0:T(2,128)(2,1)}), bf16[16,2,15,1536]{3,1,2,0:T(2,128)(2,1)S(1)}, u32[]{:S(2)}, u32[]{:S(2)}) %all-to-all-start.2) | async-done | bytes 1474592 | tf_op jit(solution)/shard_map/all_to_all | solution.py:199
  356.4 13.3 all-to-all-done.3
  388.8 10.0 collective-permute-done.1
  404.2 12.3 all_gather.19
  452.8 11.9 all-to-all-done.4
  479.4 8.8 all-to-all-done.6
  488.2 7.4 fusion.72
  516.8 8.0 all-to-all-done.5
  572.3 8.3 all-to-all-start.8
  582.0 6.7 all-to-all-done.8
  621.0 16.3 all-to-all-done.9
  670.9 6.4 all-to-all-done.10
  693.1 9.0 all-to-all-start.11
  703.4 6.7 all-to-all-done.11
  746.4 13.4 all-to-all-done.12
  759.8 10.7 fusion
  774.5 6.8 fusion.113
  799.6 7.8 fusion.1
  845.1 9.9 fusion.2
  884.8 10.1 all-to-all-start.14
  896.9 10.1 convolution_add_fusion
  926.1 61.4 %concatenate.117 = f32[1536,3618]{0,1:T(8,128)} concatenate(f32[1536,1]{0,1:T(1,128)S(1)} %add.456, f32[1536,1536]{0,1:T(8,128)} %convolution_add_fusion.2, f32[1536,256]{0,1:T(8,128)S(1)} %convolution_add_fusion.9, f32[1536,256]{0,1:T(8,128)} %convolution_add_fusion.7, f32[1536,1536]{0,1:T(8,128)} %convolution_add_fusion, f32[1536,1]{0,1:T(1,128)S(1)} %add.467, ...), dimensions={1} | concatenate | bytes 44457984 | tf_op jit(solution)/shard_map/concatenate | solution.py:44
  1003.0 715.0 %all-reduce.3.cloned.1.call-done = f32[1536,3618]{0,1:T(8,128)} async-done(((f32[1536,3618]{0,1:T(8,128)}), f32[1536,3618]{0,1:T(8,128)}) %all-reduce.3.cloned.1.call-update) | async-done | bytes 22229008
  (928 shorter events, 532.0 us)
Async XLA Ops:
  7.2 96.8 %all-gather.3.cloned.1.call-start = ((), (), s32[]{:S(2)}) async-start(), calls=%async_computation.18 | async-start | bytes 11581440 | tf_op jit(solution)/shard_map/all_gather | solution.py:57
  10.5 187.9 %all-gather.5.cloned.1.call-start = ((), (), s32[]{:S(2)}) async-start(), calls=%async_computation.19 | async-start | bytes 17694720 | tf_op jit(solution)/shard_map/all_gather | solution.py:20
  15.3 205.6 %copy-start.145 = (s32[1,1,1,96,4]{3,4,2,1,0:T(4,128)}, s32[1,1,1,96,4]{3,4,2,1,0:T(4,128)S(1)}, u32[]{:S(2)}) copy-start(s32[1,1,1,96,4]{3,4,2,1,0:T(4,128)S(1)} %get-tuple-element.173) | copy-start | bytes 4612
  23.5 122.0 %copy-start.114 = (pred[480,96]{0,1:T(8,128)(4,1)}, pred[480,96]{0,1:T(8,128)(4,1)S(1)}, u32[]{:S(2)}) copy-start(pred[480,96]{0,1:T(8,128)(4,1)S(1)} %fusion.145) | copy-start | bytes 138244
  23.7 109.9 %copy-start.156 = (f32[96]{0:T(128)}, f32[96]{0:T(128)S(1)}, u32[]{:S(2)}) copy-start(f32[96]{0:T(128)S(1)} %fusion.266) | copy-start | bytes 1156
  107.4 575.4 %copy-start.101 = (f32[1536]{0:T(1024)}, f32[1536]{0:T(1024)S(1)}, u32[]{:S(2)}) copy-start(f32[1536]{0:T(1024)S(1)} %get-tuple-element.74) | copy-start | bytes 18436
  107.4 611.9 %copy-start.99 = (f32[1536]{0:T(1024)}, f32[1536]{0:T(1024)S(1)}, u32[]{:S(2)}) copy-start(f32[1536]{0:T(1024)S(1)} %get-tuple-element.75) | copy-start | bytes 18436
  145.4 108.8 %copy-start.10 = (f32[96,1536]{1,0:T(8,128)}, f32[96,1536]{1,0:T(8,128)S(1)}, u32[]{:S(2)}) copy-start(f32[96,1536]{1,0:T(8,128)S(1)} %get-tuple-element.187) | copy-start | bytes 1769476
  151.6 46.8 %all-to-all-start = ((bf16[16,2,15,1536]{3,1,2,0:T(2,128)(2,1)}), bf16[16,2,15,1536]{3,1,2,0:T(2,128)(2,1)S(1)}, u32[]{:S(2)}, u32[]{:S(2)}) async-start(bf16[16,2,15,1536]{3,1,2,0:T(2,128)(2,1)} %copy.377), calls=%async_computation | async-start | bytes 2949120 | tf_op jit(solution)/shard_map/all_to_all | solution.py:199
  212.0 28.2 %all-to-all-start.1 = ((bf16[16,2,15,1536]{3,1,2,0:T(2,128)(2,1)}), bf16[16,2,15,1536]{3,1,2,0:T(2,128)(2,1)S(1)}, u32[]{:S(2)}, u32[]{:S(2)}) async-start(bf16[16,2,15,1536]{3,1,2,0:T(2,128)(2,1)} %copy.380), calls=%async_computation.1 | async-start | bytes 2949120 | tf_op jit(solution)/shard_map/all_to_all | solution.py:206
  254.4 14.4 collective-permute-start
  296.7 88.4 %copy-start.12 = (f32[96,1536]{1,0:T(8,128)}, f32[96,1536]{1,0:T(8,128)S(1)}, u32[]{:S(2)}) copy-start(f32[96,1536]{1,0:T(8,128)S(1)} %get-tuple-element.195) | copy-start | bytes 1769476
  302.9 26.4 %all-to-all-start.2 = ((bf16[16,2,15,1536]{3,1,2,0:T(2,128)(2,1)}), bf16[16,2,15,1536]{3,1,2,0:T(2,128)(2,1)S(1)}, u32[]{:S(2)}, u32[]{:S(2)}) async-start(bf16[16,2,15,1536]{3,1,2,0:T(2,128)(2,1)} %copy.395), calls=%async_computation.2 | async-start | bytes 2949120 | tf_op jit(solution)/shard_map/all_to_all | solution.py:199
  345.7 24.0 %all-to-all-start.3 = ((bf16[16,2,15,1536]{3,1,2,0:T(2,128)(2,1)}), bf16[16,2,15,1536]{3,1,2,0:T(2,128)(2,1)}, u32[]{:S(2)}, u32[]{:S(2)}) async-start(bf16[16,2,15,1536]{3,1,2,0:T(2,128)(2,1)} %copy.398), calls=%async_computation.3 | async-start | bytes 2949120 | tf_op jit(solution)/shard_map/all_to_all | solution.py:206
  386.1 12.8 collective-permute-start.1
  438.0 26.6 %all-to-all-start.4 = ((bf16[16,2,15,1536]{3,1,2,0:T(2,128)(2,1)}), bf16[16,2,15,1536]{3,1,2,0:T(2,128)(2,1)}, u32[]{:S(2)}, u32[]{:S(2)}) async-start(bf16[16,2,15,1536]{3,1,2,0:T(2,128)(2,1)} %copy.413), calls=%async_computation.4 | async-start | bytes 2949120 | tf_op jit(solution)/shard_map/all_to_all | solution.py:199
  464.6 23.6 %all-to-all-start.6 = ((bf16[16,2,15,1536]{3,1,2,0:T(2,128)(2,1)}), bf16[16,2,15,1536]{3,1,2,0:T(2,128)(2,1)S(1)}, u32[]{:S(2)}, u32[]{:S(2)}) async-start(bf16[16,2,15,1536]{3,1,2,0:T(2,128)(2,1)} %copy.418), calls=%async_computation.6 | async-start | bytes 2949120 | tf_op jit(solution)/shard_map/all_to_all | solution.py:270
  502.2 22.6 %all-to-all-start.5 = ((bf16[16,2,15,1536]{3,1,2,0:T(2,128)(2,1)}), bf16[16,2,15,1536]{3,1,2,0:T(2,128)(2,1)S(1)}, u32[]{:S(2)}, u32[]{:S(2)}) async-start(bf16[16,2,15,1536]{3,1,2,0:T(2,128)(2,1)} %copy.416), calls=%async_computation.5 | async-start | bytes 2949120 | tf_op jit(solution)/shard_map/all_to_all | solution.py:206
  524.8 24.6 %all-to-all-start.7 = ((bf16[16,2,15,1536]{3,1,2,0:T(2,128)(2,1)}), bf16[16,2,15,1536]{3,1,2,0:T(2,128)(2,1)}, u32[]{:S(2)}, u32[]{:S(2)}) async-start(bf16[16,2,15,1536]{3,1,2,0:T(2,128)(2,1)} %copy.420), calls=%async_computation.7 | async-start | bytes 2949120 | tf_op jit(solution)/shard_map/all_to_all | solution.py:288
  572.3 16.4 all-to-all-start.8
  598.9 6.9 collective-permute-start.2
  613.8 23.5 %all-to-all-start.9 = ((bf16[16,2,15,1536]{3,1,2,0:T(2,128)(2,1)}), bf16[16,2,15,1536]{3,1,2,0:T(2,128)(2,1)S(1)}, u32[]{:S(2)}, u32[]{:S(2)}) async-start(bf16[16,2,15,1536]{3,1,2,0:T(2,128)(2,1)} %copy.432), calls=%async_computation.9 | async-start | bytes 2949120 | tf_op jit(solution)/shard_map/all_to_all | solution.py:270
  654.1 23.2 %all-to-all-start.10 = ((bf16[16,2,15,1536]{3,1,2,0:T(2,128)(2,1)}), bf16[16,2,15,1536]{3,1,2,0:T(2,128)(2,1)}, u32[]{:S(2)}, u32[]{:S(2)}) async-start(bf16[16,2,15,1536]{3,1,2,0:T(2,128)(2,1)} %copy.434), calls=%async_computation.10 | async-start | bytes 2949120 | tf_op jit(solution)/shard_map/all_to_all | solution.py:288
  693.1 17.0 all-to-all-start.11
  720.4 9.7 collective-permute-start.3
  736.4 23.4 %all-to-all-start.12 = ((bf16[16,2,15,1536]{3,1,2,0:T(2,128)(2,1)}), bf16[16,2,15,1536]{3,1,2,0:T(2,128)(2,1)S(1)}, u32[]{:S(2)}, u32[]{:S(2)}) async-start(bf16[16,2,15,1536]{3,1,2,0:T(2,128)(2,1)} %copy.446), calls=%async_computation.12 | async-start | bytes 2949120 | tf_op jit(solution)/shard_map/all_to_all | solution.py:270
  740.3 253.8 %reduce-scatter.9.cloned.1.call-start = ((), (), s32[]{:S(2)}) async-start(), calls=%async_computation.22 | async-start | bytes 5898240 | tf_op jit(solution)/shard_map/reduce_scatter | solution.py:397
  770.6 226.5 %reduce-scatter.7.cloned.1.call-start = ((), (), s32[]{:S(2)}) async-start(), calls=%async_computation.21 | async-start | bytes 5898240 | tf_op jit(solution)/shard_map/reduce_scatter | solution.py:394
  840.2 27.7 %all-to-all-start.13 = ((bf16[16,2,15,1536]{3,1,2,0:T(2,128)(2,1)}), bf16[16,2,15,1536]{3,1,2,0:T(2,128)(2,1)}, u32[]{:S(2)}, u32[]{:S(2)}) async-start(bf16[16,2,15,1536]{3,1,2,0:T(2,128)(2,1)} %copy.448), calls=%async_computation.13 | async-start | bytes 2949120 | tf_op jit(solution)/shard_map/all_to_all | solution.py:288
  844.9 155.1 %reduce-scatter.5.cloned.1.call-start = ((), (), s32[]{:S(2)}) async-start(), calls=%async_computation.20 | async-start | bytes 5898240 | tf_op jit(solution)/shard_map/reduce_scatter | solution.py:391
  884.8 27.7 %all-to-all-start.14 = ((bf16[4,96,512]{2,1,0:T(8,128)(2,1)}), bf16[4,96,512]{2,1,0:T(8,128)(2,1)}, u32[]{:S(2)}, u32[]{:S(2)}) async-start(bf16[4,96,512]{2,1,0:T(8,128)(2,1)} %pad_maximum_fusion.5), calls=%async_computation.14 | async-start | bytes 786432 | tf_op jit(solution)/shard_map/all_to_all | solution.py:31
  894.9 823.1 %all-reduce.3.cloned.1.call-start = ((), (), s32[]{:S(2)}) async-start(), calls=%async_computation.23 | async-start | bytes 44531712
  (242 other events, 1703.0 us)
Sparse Core Ops, SparseCore 0:
  11.7 92.2 all-gather.2
  105.7 92.7 all-gather.4
  770.7 54.5 reduce-scatter.8
  828.0 54.1 reduce-scatter.6
  884.7 54.1 reduce-scatter.4
  987.7 730.2 all-reduce.2
where the time goes:
time: 1770 us; the launch traced here: 1730 us
  waiting for transfers between devices  998 us (56%)
  matrix products  295 us (17%)
  local copies, waits for them, and re-layouts  219 us (12%)
  starting transfers between devices  93.7 us (5%)
  other arithmetic  78.2 us (4%)
  blocking collectives  31.8 us (2%)
  between operations  19.2 us (1%)
    unnamed x7, waiting for transfers between devices  715 us
    all_gather x1, waiting for transfers between devices, gather_turned(): whole, at, done = (lax.all_gather(both, axis, axis=0, tiled=True), 0, [])  78.4 us
    concatenate x1, local copies, waits for them, and re-layouts, sent_together(): jnp.concatenate([a.reshape(*a.shape[:along], w) for a, w in zip(arrays, w...  61.4 us
    dot_general x15, matrix products, contract_cols(): lax.dot_general(left, right, (((1,), (1,)), ((), ())), preferred_element_...  46.4 us
    all_gather x1, waiting for transfers between devices, in_one_piece(): whole = lax.all_gather(both, axis, axis=dim, tiled=True)  41.8 us
    dot_general x15, matrix products, contract_rows(): lax.dot_general(left, right, (((0,), (0,)), ((), ())), preferred_element_...  40.9 us
    all_to_all x3, waiting for transfers between devices, layer_forward(): lax.all_to_all(produced, 'col', split_axis=0, concat_axis=0, tiled=True)  39.9 us
    all_to_all x3, waiting for transfers between devices, layer_backward(): lax.all_to_all(out_grads, 'col', split_axis=0, concat_axis=0, tiled=True)  38.5 us
  transfers between devices with their start and end apart: 25, of which 19 were waited for; matrix products, arithmetic and copies ran while one was open for 20% of the time, Pallas kernels for 0%

commit v1 on v0

v1 whole, which is shorter than its diff:
```python
import jax
import jax.numpy as jnp
from jax import lax
from jax.sharding import PartitionSpec as P

HEAD_DIM = 128
ROOMS = 16
EPSILON = 1e-06
LANES = 128
BF = jnp.bfloat16
F32 = jnp.float32


def dot(left, right, contract=(1, 0)):
    return lax.dot_general(
        left, right, (((contract[0],), (contract[1],)), ((), ())), preferred_element_type=F32
    )


def swapped(value, step):
    rows = lax.axis_size("row")
    return lax.ppermute(value, "row", [(r, r ^ step) for r in range(rows)])


def norm_parts(stream):
    return lax.rsqrt(jnp.mean(stream * stream, -1, keepdims=True) + EPSILON)


def norm_back(grad, stream, gain):
    inverse = norm_parts(stream)
    unit = stream * inverse
    scaled = grad * gain
    back = inverse * (scaled - unit * jnp.mean(scaled * unit, -1, keepdims=True))
    return back, jnp.sum(grad * unit, 0, keepdims=True)


def turned(vectors, cosine, sine):
    done = []
    for at in range(0, vectors.shape[1], HEAD_DIM):
        one = vectors[:, at : at + HEAD_DIM]
        half = HEAD_DIM // 2
        other = jnp.concatenate([one[:, half:], one[:, :half]], -1)
        done.append(one * cosine + other * sine)
    return jnp.concatenate(done, -1) if len(done) > 1 else done[0]


def stacked_heads(value, first, count):
    return jnp.concatenate(
        [value[:, (first + j) * HEAD_DIM : (first + j + 1) * HEAD_DIM] for j in range(count)], 0
    )


def unstacked_heads(value, count):
    tokens = value.shape[0] // count
    return jnp.concatenate([value[j * tokens : (j + 1) * tokens] for j in range(count)], 1)


def project(stream, gain, w_qkv, cosine, sine, width):
    normed = (stream * norm_parts(stream) * gain).astype(BF)
    qkv = dot(normed, w_qkv)
    kv_width = (qkv.shape[1] - width) // 2
    turned_part = turned(qkv[:, : width + kv_width], cosine, sine)
    query = turned_part[:, :width].astype(BF)
    pair = jnp.concatenate([turned_part[:, width:], qkv[:, width + kv_width :]], -1).astype(BF)
    return normed, query, pair


def attend(stream, query, pairs, bias, w_out, gain, w_router, chosen, dispatch):
    kv_heads = pairs.shape[1] // (2 * HEAD_DIM)
    group = query.shape[1] // HEAD_DIM // kv_heads
    biases = jnp.concatenate([bias] * group, 0)
    mixed, kept = [], []
    for h in range(kv_heads):
        keys = pairs[:, h * HEAD_DIM : (h + 1) * HEAD_DIM]
        values = pairs[:, (kv_heads + h) * HEAD_DIM : (kv_heads + h + 1) * HEAD_DIM]
        queries = stacked_heads(query, h * group, group)
        scores = dot(queries, keys, (1, 1)) * HEAD_DIM ** (-0.5) + biases
        expo = jnp.exp(scores - jnp.max(scores, -1, keepdims=True))
        probs = (expo / jnp.sum(expo, -1, keepdims=True)).astype(BF)
        kept.append(probs)
        mixed.append(unstacked_heads(dot(probs, values).astype(BF), group))
    mixed = jnp.concatenate(mixed, 1)
    middle = stream + dot(mixed, w_out)
    normed_ffn = (middle * norm_parts(middle) * gain).astype(BF)
    logits = jnp.where(chosen > 0, dot(normed_ffn, w_router), -1e30)
    expo = jnp.where(chosen > 0, jnp.exp(logits - jnp.max(logits, -1, keepdims=True)), 0.0)
    gates = expo / jnp.sum(expo, -1, keepdims=True)
    outgoing = dot(dispatch, normed_ffn).astype(BF)
    return mixed, middle, normed_ffn, gates, outgoing, jnp.stack(kept)


def rows_of(arrived, j):
    columns, slots, width = arrived.shape
    return arrived[:, j * ROOMS : (j + 1) * ROOMS].reshape(columns * ROOMS, width)


def rows_back(parts, columns):
    return jnp.concatenate([p.reshape(columns, ROOMS, p.shape[1]) for p in parts], 1)


def expert_forward(arrived, w_gate, w_up, w_down):
    produced, kept = [], []
    for j in range(w_gate.shape[0]):
        rows = rows_of(arrived, j)
        gate = dot(rows, w_gate[j], (1, 1))
        lifted = dot(rows, w_up[j], (1, 1))
        square = gate * gate
        bend = jnp.tanh(0.7978845608028654 * gate * (1.0 + 0.044715 * square))
        slope = 0.5 * (1.0 + bend) + 0.5 * gate * (1.0 - bend * bend) * (
            0.7978845608028654 * (1.0 + 3 * 0.044715 * square)
        )
        active = 0.5 * gate * (1.0 + bend)
        hidden = (active * lifted).astype(BF)
        produced.append(dot(hidden, w_down[j]).astype(BF))
        kept.append((hidden, active.astype(BF), (slope * lifted).astype(BF)))
    return rows_back(produced, arrived.shape[0]), tuple(kept)


def gates_of_slots(gates, spread, places):
    return dot(gates.astype(BF), spread) * places.astype(F32)


def combine(returned, middle, gates, spread, places):
    weights = gates_of_slots(gates, spread, places).astype(BF)
    return middle + dot(weights, returned)


def split_grads(grad, returned, gates, spread, places, dispatch):
    low = grad.astype(BF)
    inner = dot(low, returned, (1, 1)) * places.astype(F32)
    gate_grads = dot(inner.astype(BF), spread, (1, 1))
    logit_grads = gates * (gate_grads - jnp.sum(gates * gate_grads, -1, keepdims=True))
    slots = dispatch.shape[0]
    own = lax.broadcasted_iota(jnp.int32, (slots, LANES), 0) // ROOMS
    here = own == lax.broadcasted_iota(jnp.int32, (slots, LANES), 1)
    scale = jnp.sum(
        jnp.where(here, dot(dispatch, gates.astype(BF)), 0.0), -1, keepdims=True
    )
    return logit_grads.astype(BF), (dot(dispatch, low) * scale).astype(BF)


def expert_backward(arrived_grads, kept, w_gate, w_up, w_down):
    sent, backs = [], []
    for j in range(w_gate.shape[0]):
        hidden, active, bent = kept[j]
        hidden_grads = dot(rows_of(arrived_grads, j), w_down[j], (1, 1))
        gate_back = (hidden_grads * bent.astype(F32)).astype(BF)
        lifted_back = (hidden_grads * active.astype(F32)).astype(BF)
        sent.append((dot(gate_back, w_gate[j]) + dot(lifted_back, w_up[j])).astype(BF))
        backs.append((gate_back, lifted_back))
    return rows_back(sent, arrived_grads.shape[0]), tuple(backs)


def attend_back(
    token_grads, places, logit_grads, w_router, middle, gain, grad, w_out, query, pairs, probs,
    cosine, sine,
):
    ffn_grads = dot(places, token_grads) + dot(logit_grads, w_router, (1, 1))
    part, gain_grad = norm_back(ffn_grads, middle, gain)
    middle_grads = grad + part
    branch = middle_grads.astype(BF)
    mixed_grads = dot(branch, w_out, (1, 1)).astype(BF)
    kv_heads = pairs.shape[1] // (2 * HEAD_DIM)
    group = query.shape[1] // HEAD_DIM // kv_heads
    scale = HEAD_DIM ** (-0.5)
    query_grads, key_grads, value_grads = [], [], []
    for h in range(kv_heads):
        keys = pairs[:, h * HEAD_DIM : (h + 1) * HEAD_DIM]
        values = pairs[:, (kv_heads + h) * HEAD_DIM : (kv_heads + h + 1) * HEAD_DIM]
        queries = stacked_heads(query, h * group, group)
        above = stacked_heads(mixed_grads, h * group, group)
        weights = probs[h]
        wide = weights.astype(F32)
        weight_grads = dot(above, values, (1, 1))
        value_grads.append(dot(weights, above, (0, 0)))
        score_grads = (
            wide * (weight_grads - jnp.sum(wide * weight_grads, -1, keepdims=True))
        ).astype(BF)
        query_grads.append(unstacked_heads(dot(score_grads, keys) * scale, group))
        key_grads.append(dot(score_grads, queries, (0, 0)) * scale)
    query_back = turned(jnp.concatenate(query_grads, 1), cosine, -sine).astype(BF)
    pair_grads = jnp.concatenate(key_grads + value_grads, 1).astype(BF)
    return middle_grads, branch, query_back, pair_grads, gain_grad


def project_back(pair_parts, query_back, w_qkv, stream, gain, middle_grads, cosine, sine):
    total = sum(part.astype(F32) for part in pair_parts)
    kv_width = total.shape[1] // 2
    key_back = turned(total[:, :kv_width], cosine, -sine)
    backs = jnp.concatenate(
        [query_back, key_back.astype(BF), total[:, kv_width:].astype(BF)], 1
    )
    part, gain_grad = norm_back(dot(backs, w_qkv, (1, 1)), stream, gain)
    return middle_grads + part, backs, gain_grad


def over_columns(value):
    return lax.all_to_all(value, "col", split_axis=0, concat_axis=0, tiled=True)


def on_device(
    inputs, cotangent, segment_ids, routes, attn_gain, w_query, w_key, w_value, w_out, ffn_gain,
    w_router, w_gate, w_up, w_down,
):
    section = lax.axis_index("section")
    row = lax.axis_index("row")
    rows = lax.axis_size("row")
    columns = lax.axis_size("col")
    micro, tokens, width = inputs.shape[0], inputs.shape[2], inputs.shape[3]
    experts = w_router.shape[2]
    kv_width = w_key.shape[2]
    slots = experts * ROOMS
    share = width // rows
    shard = width // (rows * columns)
    pieces = range(micro)
    steps = range(rows)

    small = jnp.concatenate(
        [w_router[0], attn_gain[0][:, None], ffn_gain[0][:, None],
         jnp.zeros((shard, LANES - experts - 2), BF)], 1
    )
    first = jnp.concatenate([w_query[0], w_key[0], w_value[0], small], 1)
    first = lax.all_gather(first, ("row", "col"), axis=0, tiled=True)
    w_qkv = first[:, : width + 2 * kv_width]
    small = first[:, width + 2 * kv_width :]
    w_o = lax.all_gather(w_out[0], ("row", "col"), axis=0, tiled=True)
    gain_a = small[:, experts].astype(F32)[None, :]
    gain_f = small[:, experts + 1].astype(F32)[None, :]
    lane = jnp.arange(LANES, dtype=jnp.int32)
    w_r = jnp.where(lane[None, :] < experts, small, jnp.zeros_like(small))

    order = (0, 2, 1, 3)

    def whole(own):
        two = swapped(own, 2)
        one = swapped(own, 1)
        three = swapped(two, 1)
        return jnp.concatenate([own, two, one, three], 1)

    w_g, w_u, w_d = whole(w_gate[0]), whole(w_up[0]), whole(w_down[0])

    half = HEAD_DIM // 2
    freqs = 10000.0 ** (-2.0 * jnp.arange(half).astype(F32) / HEAD_DIM)
    positions = row * tokens + jnp.arange(tokens, dtype=jnp.int32)
    angles = positions.astype(F32)[:, None] * freqs[None, :]
    cosine = jnp.concatenate([jnp.cos(angles)] * 2, 1)
    sine = jnp.concatenate([-jnp.sin(angles), jnp.sin(angles)], 1)
    key_positions = jnp.concatenate(
        [(row ^ step) * tokens + jnp.arange(tokens, dtype=jnp.int32) for step in steps]
    )
    spread = (lane[:, None] == jnp.arange(slots, dtype=jnp.int32)[None, :] // ROOMS).astype(BF)
    below = (
        jnp.arange(tokens)[:, None] > jnp.arange(tokens)[None, :]
    ).astype(BF)
    biases, chosens, places, dispatches = [], [], [], []
    for m in pieces:
        segments = segment_ids[m, 0]
        own_segments = lax.dynamic_slice_in_dim(segments, row * tokens, tokens)
        key_segments = jnp.concatenate(
            [lax.dynamic_slice_in_dim(segments, (row ^ s) * tokens, tokens) for s in steps]
        )
        counted = (key_positions[None, :] <= positions[:, None]) & (
            key_segments[None, :] == own_segments[:, None]
        )
        biases.append(jnp.where(counted, 0.0, -1e30).astype(F32))
        chosen = jnp.any(routes[0, m, 0][:, :, None] == lane[None, None, :], 1)
        chosens.append(chosen.astype(F32))
        rank = dot(below, chosen.astype(BF))
        rank = jnp.where(chosen, rank, -1.0)[:, :experts]
        place = (
            rank[:, :, None] == jnp.arange(ROOMS, dtype=F32)[None, None, :]
        ).reshape(tokens, slots)
        places.append(place.astype(BF))
        dispatches.append(place.T.astype(BF))

    def forward(streams):
        done = []
        projected = [project(x, gain_a, w_qkv, cosine, sine, width) for x in streams]
        pairs = [
            jnp.concatenate([pair] + [swapped(pair, s) for s in steps[1:]], 0)
            for normed, query, pair in projected
        ]
        attended = [
            attend(
                streams[m], projected[m][1], pairs[m], biases[m], w_o, gain_f, w_r, chosens[m],
                dispatches[m],
            )
            for m in pieces
        ]
        arrived = [
            over_columns(a[4].reshape(columns, slots // columns, width)) for a in attended
        ]
        applied = [expert_forward(x, w_g, w_u, w_d) for x in arrived]
        returned = [over_columns(a[0]).reshape(slots, width) for a in applied]
        results = [
            combine(returned[m], attended[m][1], attended[m][3], spread, places[m])
            for m in pieces
        ]
        kept = [
            dict(
                stream=streams[m], normed=projected[m][0], query=projected[m][1], pairs=pairs[m],
                mixed=attended[m][0], middle=attended[m][1], normed_ffn=attended[m][2],
                gates=attended[m][3], probs=attended[m][5], arrived=arrived[m],
                applied=applied[m][1], returned=returned[m],
            )
            for m in pieces
        ]
        return results, kept

    def backward(grads, kept):
        split = [
            split_grads(
                grads[m], kept[m]["returned"], kept[m]["gates"], spread, places[m], dispatches[m]
            )
            for m in pieces
        ]
        arrived = [
            over_columns(s[1].reshape(columns, slots // columns, width)) for s in split
        ]
        applied = [
            expert_backward(arrived[m], kept[m]["applied"], w_g, w_u, w_d) for m in pieces
        ]
        returned = [over_columns(a[0]).reshape(slots, width) for a in applied]
        attended = [
            attend_back(
                returned[m], places[m], split[m][0], w_r, kept[m]["middle"], gain_f, grads[m],
                w_o, kept[m]["query"], kept[m]["pairs"], kept[m]["probs"], cosine, sine,
            )
            for m in pieces
        ]
        parts = [
            [a[3][:tokens]]
            + [swapped(a[3][s * tokens : (s + 1) * tokens], s) for s in steps[1:]]
            for a in attended
        ]
        projected = [
            project_back(
                parts[m], attended[m][2], w_qkv, kept[m]["stream"], gain_a, attended[m][0],
                cosine, sine,
            )
            for m in pieces
        ]
        return split, arrived, applied, attended, projected

    entering = [inputs[m, 0].astype(F32) for m in pieces]
    results, unused = forward(entering)
    handed = [lax.ppermute(r.astype(BF), "section", [(0, 1)]) for r in results]
    streams = [
        jnp.where(section == 1, handed[m].astype(F32), entering[m]) for m in pieces
    ]
    outputs, kept = forward(streams)

    targets = [cotangent[m, 0].astype(F32) for m in pieces]
    projected = backward(targets, kept)[4]
    handed = [lax.ppermute(p[0].astype(BF), "section", [(1, 0)]) for p in projected]
    grads = [
        jnp.where(section == 0, handed[m].astype(F32), targets[m]) for m in pieces
    ]
    split, arrived, applied, attended, projected = backward(grads, kept)
    input_grads = [p[0] for p in projected]

    def both(make):
        return jnp.stack(
            [jnp.concatenate([make(m, j) for m in pieces], 0) for j in range(w_g.shape[0])]
        )

    def summed_rows(left, right):
        def part(lo, hi):
            return lax.dot_general(
                left[:, :, lo:hi], right, (((1,), (1,)), ((0,), (0,))), preferred_element_type=F32
            ).astype(BF)

        half, quarter = left.shape[2] // 2, left.shape[2] // 4
        came = swapped(part(half, 2 * half), 1)
        mine = part(0, half).astype(F32) + came.astype(F32)
        far = swapped(mine[:, quarter:].astype(BF), 2)
        return mine[:, :quarter] + far.astype(F32)

    x_rows = both(lambda m, j: rows_of(kept[m]["arrived"], j))
    y_rows = both(lambda m, j: rows_of(arrived[m], j))
    hidden = both(lambda m, j: kept[m]["applied"][j][0])
    gate_back = both(lambda m, j: applied[m][1][j][0])
    lifted_back = both(lambda m, j: applied[m][1][j][1])
    grad_down = summed_rows(hidden, y_rows)
    grad_gate = summed_rows(gate_back, x_rows)
    grad_up = summed_rows(lifted_back, x_rows)

    def slices(values):
        value = jnp.concatenate(values, 0)
        cuts = [lax.dynamic_slice_in_dim(value, (row ^ s) * share, share, 1) for s in steps]
        return jnp.concatenate([cuts[0]] + [swapped(cuts[s], s) for s in steps[1:]], 0)

    def everyone(values):
        value = jnp.concatenate(values, 0)
        return jnp.concatenate([value] + [swapped(value, s) for s in steps[1:]], 0)

    def summed_columns(value):
        blocks = value.astype(BF).reshape(columns, shard, value.shape[1])
        return over_columns(blocks).astype(F32).sum(0)

    x_normed = slices([kept[m]["normed"] for m in pieces])
    x_mixed = slices([kept[m]["mixed"] for m in pieces])
    x_ffn = slices([kept[m]["normed_ffn"] for m in pieces])
    y_branch = everyone(
        [jnp.concatenate([attended[m][1], split[m][0]], 1) for m in pieces]
    )
    y_qkv = everyone([projected[m][1] for m in pieces])
    grad_first = summed_columns(
        jnp.concatenate(
            [dot(x_mixed, y_branch[:, :width], (0, 0)), dot(x_ffn, y_branch[:, width:], (0, 0))], 1
        )
    )
    gains = jnp.concatenate(
        [sum(projected[m][2] for m in pieces), sum(attended[m][4] for m in pieces)], 0
    )
    gain_cuts = [lax.dynamic_slice_in_dim(gains, (row ^ s) * share, share, 1) for s in steps]
    gains = gain_cuts[0] + sum(swapped(gain_cuts[s], s) for s in steps[1:])
    gains = jnp.concatenate([gains, jnp.zeros((LANES - 2, share), F32)], 0).T
    grad_second = summed_columns(
        jnp.concatenate([dot(x_normed, y_qkv, (0, 0)), gains], 1)
    )
    qkv_width = width + 2 * kv_width

    return (
        jnp.stack(outputs)[None, :, None],
        jnp.stack(input_grads)[None, :, None],
        grad_second[:, qkv_width][None],
        grad_second[:, :width][None],
        grad_second[:, width : width + kv_width][None],
        grad_second[:, width + kv_width : qkv_width][None],
        grad_first[:, :width][None],
        grad_second[:, qkv_width + 1][None],
        grad_first[:, width : width + experts][None],
        grad_gate[None],
        grad_up[None],
        grad_down[None],
    )


def solution(mesh):
    dense = P("section", ("row", "col"), None)
    gain = P("section", ("row", "col"))
    expert = P("section", "col", "row", None)
    token = P(None, "col", "row", None)
    layered = P("section", None, "col", "row", None)
    return jax.shard_map(
        on_device,
        mesh=mesh,
        in_specs=(
            token, token, P(None, "col", None), layered, gain, dense, dense, dense, dense, gain,
            dense, expert, expert, expert,
        ),
        out_specs=(
            layered, layered, gain, dense, dense, dense, dense, gain, dense, expert, expert, expert,
        ),
        check_vma=False,
    )
```

time: 1770 us -> 1080 us (0.61); the launches traced: 1730 us -> 1070 us
  waiting for transfers between devices: 998 us -> 349 us
  local copies, waits for them, and re-layouts: 219 us -> 43.6 us
  blocking collectives: 31.8 us -> 121 us
  starting transfers between devices: 93.7 us -> 182 us
  matrix products: 295 us -> 227 us
  other arithmetic: 78.2 us -> 125 us
    unnamed x7 -> x2, waiting for transfers between devices: 715 us -> 0.03 us
    all_to_all x0 -> x5, blocking collectives: none -> 121 us  [over_columns(): return lax.all_to_all(value, 'col', split_axis=0, concat_axis=0, tiled=True)]
    ppermute x4 -> x61, starting transfers between devices: 8.28 us -> 120 us  [the longest x57 110 us: swapped(): return lax.ppermute(value, 'row', [(r, r ^ step) for r in range(rows)])]
    ppermute x4 -> x61, waiting for transfers between devices: 28.6 us -> 121 us  [the longest x57 104 us: swapped(): return lax.ppermute(value, 'row', [(r, r ^ step) for r in range(rows)])]
    dot_general x99 -> x149, matrix products: 295 us -> 227 us  [the longest x143 206 us: dot(): lax.dot_general(left, right, (((contract[0],), (contract[1],)), ((), ()))...]
    concatenate x2 -> x14, local copies, waits for them, and re-layouts: 63.2 us -> 3.39 us  [the longest x1 1.63 us: on_device(): first = jnp.concatenate([w_query[0], w_key[0], w_value[0], small], 1)]
    reshape x37 -> x0, local copies, waits for them, and re-layouts: 45.2 us -> none  [the longest x6 12.9 us: layer_forward(): outgoing = outgoing.reshape(experts // per_owner, per_owner, CAP, width)]
    all_to_all x15 -> x13, waiting for transfers between devices: 134 us -> 94.9 us  [over_columns(): return lax.all_to_all(value, 'col', split_axis=0, concat_axis=0, tiled=True)]
  transfers between devices with their start and end apart: 25 -> 76, of which waited for: 19 -> 34; matrix products, arithmetic and copies ran while one was open for 20% -> 24% of each run, Pallas kernels for 0% -> 0%
where the time goes in v1:
time: 1080 us; the launch traced here: 1070 us
  waiting for transfers between devices  349 us (32%)
  matrix products  227 us (21%)
  starting transfers between devices  182 us (17%)
  other arithmetic  125 us (12%)
  blocking collectives  121 us (11%)
  local copies, waits for them, and re-layouts  43.6 us (4%)
  between operations  20.6 us (2%)
    dot_general x143, matrix products, dot(): lax.dot_general(left, right, (((contract[0],), (contract[1],)), ((), ()))...  206 us
    all_to_all x5, blocking collectives, over_columns(): return lax.all_to_all(value, 'col', split_axis=0, concat_axis=0, tiled=True)  121 us
    ppermute x57, starting transfers between devices, swapped(): return lax.ppermute(value, 'row', [(r, r ^ step) for r in range(rows)])  110 us
    ppermute x57, waiting for transfers between devices, swapped(): return lax.ppermute(value, 'row', [(r, r ^ step) for r in range(rows)])  104 us
    all_to_all x13, waiting for transfers between devices, over_columns(): return lax.all_to_all(value, 'col', split_axis=0, concat_axis=0, tiled=True)  94.9 us
    all_gather x1, waiting for transfers between devices, on_device(): first = lax.all_gather(first, ('row', 'col'), axis=0, tiled=True)  74.9 us
    all_to_all x13, starting transfers between devices, over_columns(): return lax.all_to_all(value, 'col', split_axis=0, concat_axis=0, tiled=True)  61.9 us
    all_gather x1, waiting for transfers between devices, on_device(): w_o = lax.all_gather(w_out[0], ('row', 'col'), axis=0, tiled=True)  58.2 us
  transfers between devices with their start and end apart: 76, of which 34 were waited for; matrix products, arithmetic and copies ran while one was open for 24% of the time, Pallas kernels for 0%

profile of v1, /device:TPU:9, one launch (start us, length us, event | category | flops | bytes accessed | tf_op | source)
XLA Modules:
  0.0 1067.9 jit_solution(3036079097099182513)
XLA Ops:
  19.0 74.9 %all-gather.4.cloned.1.call-done = bf16[1536,2176]{1,0:T(8,128)(2,1)} async-done(((bf16[24,2176]{1,0:T(8,128)(2,1)}), bf16[1536,2176]{1,0:T(8,128)(2,1)}) %all-gather.4.cloned.1.call-update) | async-done | bytes 6684688 | tf_op jit(solution)/shard_map/all_gather | solution.py:223
  111.6 58.2 %all-gather.6.cloned.1.call-done = bf16[1,1536,1536]{2,1,0:T(8,128)(2,1)} async-done(((bf16[1,24,1536]{2,1,0:T(8,128)(2,1)}), bf16[1,1536,1536]{2,1,0:T(8,128)(2,1)}) %all-gather.6.cloned.1.call-update) | async-done | bytes 4718608 | tf_op jit(solution)/shard_map/all_gather | solution.py:226
  180.2 5.4 pad_maximum_fusion
  185.7 5.4 pad_maximum_fusion.1
  191.1 5.4 pad_maximum_fusion.2
  196.5 6.7 all-to-all-done
  227.6 18.4 %all-to-all-done.1 = bf16[16,32,1536]{2,1,0:T(8,128)(2,1)S(1)} async-done(((bf16[16,32,1536]{2,1,0:T(8,128)(2,1)}), bf16[16,32,1536]{2,1,0:T(8,128)(2,1)S(1)}, u32[]{:S(2)}, u32[]{:S(2)}) %all-to-all-start.1) | async-done | bytes 1572896 | tf_op jit(solution)/shard_map/all_to_all | solution.py:198
  249.8 6.2 collective-permute-done.12
  260.7 6.3 collective-permute-start.18
  277.2 24.8 %all_to_all.90 = bf16[16,32,1536]{2,1,0:T(8,128)(2,1)S(1)} all-to-all(bf16[16,32,1536]{2,1,0:T(8,128)(2,1)S(1)} %bitcast.554), channel_id=1, replica_groups=mesh['section'=2,'row'=4,'col'=16] {'col'}, dimensions={0} | all-to-all | bytes 3145728 | tf_op jit(solution)/shard_map/all_to_all | solution.py:198
  304.7 5.5 convolution_convert_fusion.14
  327.6 18.8 %all-to-all-done.5 = bf16[16,32,1536]{2,1,0:T(8,128)(2,1)} async-done(((bf16[16,32,1536]{2,1,0:T(8,128)(2,1)}), bf16[16,32,1536]{2,1,0:T(8,128)(2,1)}, u32[]{:S(2)}, u32[]{:S(2)}) %all-to-all-start.5) | async-done | bytes 1572896 | tf_op jit(solution)/shard_map/all_to_all | solution.py:198
  349.7 6.1 collective-permute-done.19
  362.0 6.5 collective-permute-start.15
  380.2 24.7 %all_to_all.91 = bf16[16,32,1536]{2,1,0:T(8,128)(2,1)S(1)} all-to-all(bf16[16,32,1536]{2,1,0:T(8,128)(2,1)S(1)} %bitcast.558), channel_id=1, replica_groups=mesh['section'=2,'row'=4,'col'=16] {'col'}, dimensions={0} | all-to-all | bytes 3145728 | tf_op jit(solution)/shard_map/all_to_all | solution.py:198
  424.5 15.0 %all-to-all-done.3 = bf16[16,32,1536]{2,1,0:T(8,128)(2,1)} async-done(((bf16[16,32,1536]{2,1,0:T(8,128)(2,1)}), bf16[16,32,1536]{2,1,0:T(8,128)(2,1)}, u32[]{:S(2)}, u32[]{:S(2)}) %all-to-all-start.3) | async-done | bytes 1572896 | tf_op jit(solution)/shard_map/all_to_all | solution.py:198
  443.8 23.4 %all_to_all.92 = bf16[16,32,1536]{2,1,0:T(8,128)(2,1)S(1)} all-to-all(bf16[16,32,1536]{2,1,0:T(8,128)(2,1)S(1)} %bitcast.555), channel_id=1, replica_groups=mesh['section'=2,'row'=4,'col'=16] {'col'}, dimensions={0} | all-to-all | bytes 3145728 | tf_op jit(solution)/shard_map/all_to_all | solution.py:198
  487.7 6.0 collective-permute-start.22
  512.8 5.6 collective-permute-start.23
  532.8 25.0 %all_to_all.93 = bf16[16,32,1536]{2,1,0:T(8,128)(2,1)S(1)} all-to-all(bf16[16,32,1536]{2,1,0:T(8,128)(2,1)S(1)} %bitcast.559), channel_id=1, replica_groups=mesh['section'=2,'row'=4,'col'=16] {'col'}, dimensions={0} | all-to-all | bytes 3145728 | tf_op jit(solution)/shard_map/all_to_all | solution.py:198
  574.2 17.2 %all-to-all-done.7 = bf16[16,32,1536]{2,1,0:T(8,128)(2,1)} async-done(((bf16[16,32,1536]{2,1,0:T(8,128)(2,1)}), bf16[16,32,1536]{2,1,0:T(8,128)(2,1)}, u32[]{:S(2)}, u32[]{:S(2)}) %all-to-all-start.7) | async-done | bytes 1572896 | tf_op jit(solution)/shard_map/all_to_all | solution.py:198
  597.2 23.5 %all_to_all.94 = bf16[16,32,1536]{2,1,0:T(8,128)(2,1)S(1)} all-to-all(bf16[16,32,1536]{2,1,0:T(8,128)(2,1)S(1)} %bitcast.556), channel_id=1, replica_groups=mesh['section'=2,'row'=4,'col'=16] {'col'}, dimensions={0} | all-to-all | bytes 3145728 | tf_op jit(solution)/shard_map/all_to_all | solution.py:198
  665.6 6.4 collective-permute-start.30
  739.2 6.4 all-to-all-done.14
  763.8 6.5 all-to-all-start.15
  780.3 9.9 all-to-all-done.15
  908.3 7.5 collective-permute-done.51
  962.3 17.2 %collective-permute-done.42 = bf16[192,2048]{1,0:T(8,128)(2,1)S(1)} collective-permute-done((bf16[192,2048]{1,0:T(8,128)(2,1)S(1)}, bf16[192,2048]{1,0:T(8,128)(2,1)S(1)}, u32[]{:S(2)}, u32[]{:S(2)}) %collective-permute-start.42) | collective-permute-done | bytes 786464 | tf_op jit(solution)/shard_map/ppermute | solution.py:22
  986.5 6.9 all-to-all-start.16
  996.1 8.6 collective-permute-done.60
  1008.5 21.6 %collective-permute-done.56 = bf16[2,192,1536]{2,1,0:T(8,128)(2,1)} collective-permute-done((bf16[2,192,1536]{2,1,0:T(8,128)(2,1)S(1)}, bf16[2,192,1536]{2,1,0:T(8,128)(2,1)}, u32[]{:S(2)}, u32[]{:S(2)}) %collective-permute-start.56) | collective-permute-done | bytes 1179680 | tf_op jit(solution)/shard_map/ppermute | solution.py:22
  1033.8 21.6 %collective-permute-done.58 = bf16[2,192,1536]{2,1,0:T(8,128)(2,1)} collective-permute-done((bf16[2,192,1536]{2,1,0:T(8,128)(2,1)}, bf16[2,192,1536]{2,1,0:T(8,128)(2,1)}, u32[]{:S(2)}, u32[]{:S(2)}) %collective-permute-start.58) | collective-permute-done | bytes 1179680 | tf_op jit(solution)/shard_map/ppermute | solution.py:22
  (1307 shorter events, 545.7 us)
Async XLA Ops:
  7.2 86.7 %all-gather.4.cloned.1.call-start = ((), (), s32[]{:S(2)}) async-start(), calls=%async_computation.18 | async-start | bytes 6789120 | tf_op jit(solution)/shard_map/all_gather | solution.py:223
  10.4 159.4 %all-gather.6.cloned.1.call-start = ((), (), s32[]{:S(2)}) async-start(), calls=%async_computation.19 | async-start | bytes 4792320 | tf_op jit(solution)/shard_map/all_gather | solution.py:226
  10.4 94.3 %collective-permute-start.3 = (bf16[2,192,1536]{2,1,0:T(8,128)(2,1)}, bf16[2,192,1536]{2,1,0:T(8,128)(2,1)}, u32[]{:S(2)}, u32[]{:S(2)}) collective-permute-start(bf16[2,192,1536]{2,1,0:T(8,128)(2,1)} %bitcast.17), channel_id=1, source_target_pairs={{0,32},{16,48},{32,0},{48,16},{1,33},{17,49},{33,1},{49,17},{2,34}... | collective-permute-start | bytes 3538952 | tf_op jit(solution)/shard_map/ppermute | solution.py:22
  12.5 92.3 %collective-permute-start.6 = (bf16[2,192,1536]{2,1,0:T(8,128)(2,1)}, bf16[2,192,1536]{2,1,0:T(8,128)(2,1)}, u32[]{:S(2)}, u32[]{:S(2)}) collective-permute-start(bf16[2,192,1536]{2,1,0:T(8,128)(2,1)} %bitcast.19), channel_id=1, source_target_pairs={{0,32},{16,48},{32,0},{48,16},{1,33},{17,49},{33,1},{49,17},{2,34}... | collective-permute-start | bytes 3538952 | tf_op jit(solution)/shard_map/ppermute | solution.py:22
  104.8 68.3 %collective-permute-start.4 = (bf16[2,192,1536]{2,1,0:T(8,128)(2,1)}, bf16[2,192,1536]{2,1,0:T(8,128)(2,1)}, u32[]{:S(2)}, u32[]{:S(2)}) collective-permute-start(bf16[2,192,1536]{2,1,0:T(8,128)(2,1)} %bitcast.17), channel_id=1, source_target_pairs={{0,16},{16,0},{32,48},{48,32},{1,17},{17,1},{33,49},{49,33},{2,18}... | collective-permute-start | bytes 3538952 | tf_op jit(solution)/shard_map/ppermute | solution.py:22
  104.9 80.8 %collective-permute-start.7 = (bf16[2,192,1536]{2,1,0:T(8,128)(2,1)}, bf16[2,192,1536]{2,1,0:T(8,128)(2,1)}, u32[]{:S(2)}, u32[]{:S(2)}) collective-permute-start(bf16[2,192,1536]{2,1,0:T(8,128)(2,1)} %bitcast.19), channel_id=1, source_target_pairs={{0,16},{16,0},{32,48},{48,32},{1,17},{17,1},{33,49},{49,33},{2,18}... | collective-permute-start | bytes 3538952 | tf_op jit(solution)/shard_map/ppermute | solution.py:22
  106.7 66.7 %collective-permute-start.9 = (bf16[2,192,1536]{2,1,0:T(8,128)(2,1)}, bf16[2,192,1536]{2,1,0:T(8,128)(2,1)}, u32[]{:S(2)}, u32[]{:S(2)}) collective-permute-start(bf16[2,192,1536]{2,1,0:T(8,128)(2,1)} %bitcast.21), channel_id=1, source_target_pairs={{0,32},{16,48},{32,0},{48,16},{1,33},{17,49},{33,1},{49,17},{2,34}... | collective-permute-start | bytes 3538952 | tf_op jit(solution)/shard_map/ppermute | solution.py:22
  108.4 71.8 %collective-permute-start.5 = (bf16[2,192,1536]{2,1,0:T(8,128)(2,1)}, bf16[2,192,1536]{2,1,0:T(8,128)(2,1)}, u32[]{:S(2)}, u32[]{:S(2)}) collective-permute-start(bf16[2,192,1536]{2,1,0:T(8,128)(2,1)} %collective-permute-done.3), channel_id=1, source_target_pairs={{0,16},{16,0},{32,48},{48,32},{1,17},{17,1},{33,49},{49,33},{2,18}... | collective-permute-start | bytes 3538952 | tf_op jit(solution)/shard_map/ppermute | solution.py:22
  109.2 76.5 %collective-permute-start.8 = (bf16[2,192,1536]{2,1,0:T(8,128)(2,1)}, bf16[2,192,1536]{2,1,0:T(8,128)(2,1)}, u32[]{:S(2)}, u32[]{:S(2)}) collective-permute-start(bf16[2,192,1536]{2,1,0:T(8,128)(2,1)} %collective-permute-done.6), channel_id=1, source_target_pairs={{0,16},{16,0},{32,48},{48,32},{1,17},{17,1},{33,49},{49,33},{2,18}... | collective-permute-start | bytes 3538952 | tf_op jit(solution)/shard_map/ppermute | solution.py:22
  175.7 27.4 %all-to-all-start = ((bf16[16,32,1536]{2,1,0:T(8,128)(2,1)}), bf16[16,32,1536]{2,1,0:T(8,128)(2,1)S(1)}, u32[]{:S(2)}, u32[]{:S(2)}) async-start(bf16[16,32,1536]{2,1,0:T(8,128)(2,1)} %bitcast.552), calls=%async_computation | async-start | bytes 3145728 | tf_op jit(solution)/shard_map/all_to_all | solution.py:198
  222.0 24.0 %all-to-all-start.1 = ((bf16[16,32,1536]{2,1,0:T(8,128)(2,1)}), bf16[16,32,1536]{2,1,0:T(8,128)(2,1)S(1)}, u32[]{:S(2)}, u32[]{:S(2)}) async-start(bf16[16,32,1536]{2,1,0:T(8,128)(2,1)} %pad_maximum_fusion.8), calls=%async_computation.1 | async-start | bytes 3145728 | tf_op jit(solution)/shard_map/all_to_all | solution.py:198
  321.4 25.0 %all-to-all-start.5 = ((bf16[16,32,1536]{2,1,0:T(8,128)(2,1)}), bf16[16,32,1536]{2,1,0:T(8,128)(2,1)}, u32[]{:S(2)}, u32[]{:S(2)}) async-start(bf16[16,32,1536]{2,1,0:T(8,128)(2,1)} %pad_maximum_fusion.10), calls=%async_computation.5 | async-start | bytes 3145728 | tf_op jit(solution)/shard_map/all_to_all | solution.py:198
  414.6 25.0 %all-to-all-start.3 = ((bf16[16,32,1536]{2,1,0:T(8,128)(2,1)}), bf16[16,32,1536]{2,1,0:T(8,128)(2,1)}, u32[]{:S(2)}, u32[]{:S(2)}) async-start(bf16[16,32,1536]{2,1,0:T(8,128)(2,1)} %pad_maximum_fusion.9), calls=%async_computation.3 | async-start | bytes 3145728 | tf_op jit(solution)/shard_map/all_to_all | solution.py:198
  566.7 24.7 %all-to-all-start.7 = ((bf16[16,32,1536]{2,1,0:T(8,128)(2,1)}), bf16[16,32,1536]{2,1,0:T(8,128)(2,1)}, u32[]{:S(2)}, u32[]{:S(2)}) async-start(bf16[16,32,1536]{2,1,0:T(8,128)(2,1)} %pad_maximum_fusion.11), calls=%async_computation.7 | async-start | bytes 3145728 | tf_op jit(solution)/shard_map/all_to_all | solution.py:198
  642.9 248.9 %collective-permute-start.46 = (bf16[192,384]{1,0:T(8,128)(2,1)}, bf16[192,384]{1,0:T(8,128)(2,1)}, u32[]{:S(2)}, u32[]{:S(2)}) collective-permute-start(bf16[192,384]{1,0:T(8,128)(2,1)} %get-tuple-element.349), channel_id=1, source_target_pairs={{0,16},{16,0},{32,48},{48,32},{1,17},{17,1},{33,49},{49,33},{2,18}... | collective-permute-start | bytes 442376 | tf_op jit(solution)/shard_map/ppermute | solution.py:22
  696.9 24.8 %all-to-all-start.10 = ((bf16[16,32,1536]{2,1,0:T(8,128)(2,1)}), bf16[16,32,1536]{2,1,0:T(8,128)(2,1)}, u32[]{:S(2)}, u32[]{:S(2)}) async-start(bf16[16,32,1536]{2,1,0:T(8,128)(2,1)} %bitcast.553), calls=%async_computation.10 | async-start | bytes 3145728 | tf_op jit(solution)/shard_map/all_to_all | solution.py:198
  721.8 23.8 %all-to-all-start.14 = ((bf16[16,32,1536]{2,1,0:T(8,128)(2,1)}), bf16[16,32,1536]{2,1,0:T(8,128)(2,1)}, u32[]{:S(2)}, u32[]{:S(2)}) async-start(bf16[16,32,1536]{2,1,0:T(8,128)(2,1)} %bitcast.551), calls=%async_computation.14 | async-start | bytes 3145728 | tf_op jit(solution)/shard_map/all_to_all | solution.py:198
  763.8 26.5 %all-to-all-start.15 = ((bf16[16,32,1536]{2,1,0:T(8,128)(2,1)}), bf16[16,32,1536]{2,1,0:T(8,128)(2,1)}, u32[]{:S(2)}, u32[]{:S(2)}) async-start(bf16[16,32,1536]{2,1,0:T(8,128)(2,1)} %pad_maximum_fusion.15), calls=%async_computation.15 | async-start | bytes 3145728 | tf_op jit(solution)/shard_map/all_to_all | solution.py:198
  790.2 25.3 %all-to-all-start.11 = ((bf16[16,32,1536]{2,1,0:T(8,128)(2,1)}), bf16[16,32,1536]{2,1,0:T(8,128)(2,1)}, u32[]{:S(2)}, u32[]{:S(2)}) async-start(bf16[16,32,1536]{2,1,0:T(8,128)(2,1)} %pad_maximum_fusion.13), calls=%async_computation.11 | async-start | bytes 3145728 | tf_op jit(solution)/shard_map/all_to_all | solution.py:198
  800.1 139.7 %collective-permute-start.59 = (bf16[2,384,1536]{2,1,0:T(8,128)(2,1)}, bf16[2,384,1536]{2,1,0:T(8,128)(2,1)}, u32[]{:S(2)}, u32[]{:S(2)}) collective-permute-start(bf16[2,384,1536]{2,1,0:T(8,128)(2,1)} %convolution_convert_fusion), channel_id=1, source_target_pairs={{0,16},{16,0},{32,48},{48,32},{1,17},{17,1},{33,49},{49,33},{2,18}... | collective-permute-start | bytes 7077896 | tf_op jit(solution)/shard_map/ppermute | solution.py:22
  860.2 42.8 %collective-permute-start.50 = (bf16[192,1664]{1,0:T(8,128)(2,1)S(1)}, bf16[192,1664]{1,0:T(8,128)(2,1)S(1)}, u32[]{:S(2)}, u32[]{:S(2)}) collective-permute-start(bf16[192,1664]{1,0:T(8,128)(2,1)S(1)} %maximum_maximum_fusion), channel_id=1, source_target_pairs={{0,32},{16,48},{32,0},{48,16},{1,33},{17,49},{33,1},{49,17},{2,34}... | collective-permute-start | bytes 1916936 | tf_op jit(solution)/shard_map/ppermute | solution.py:22
  863.2 39.0 %collective-permute-start.49 = (bf16[192,1664]{1,0:T(8,128)(2,1)S(1)}, bf16[192,1664]{1,0:T(8,128)(2,1)S(1)}, u32[]{:S(2)}, u32[]{:S(2)}) collective-permute-start(bf16[192,1664]{1,0:T(8,128)(2,1)S(1)} %maximum_maximum_fusion), channel_id=1, source_target_pairs={{0,16},{16,0},{32,48},{48,32},{1,17},{17,1},{33,49},{49,33},{2,18}... | collective-permute-start | bytes 1916936 | tf_op jit(solution)/shard_map/ppermute | solution.py:22
  897.7 48.1 %collective-permute-start.55 = (bf16[2,384,1536]{2,1,0:T(8,128)(2,1)}, bf16[2,384,1536]{2,1,0:T(8,128)(2,1)}, u32[]{:S(2)}, u32[]{:S(2)}) collective-permute-start(bf16[2,384,1536]{2,1,0:T(8,128)(2,1)} %convolution_convert_fusion.4), channel_id=1, source_target_pairs={{0,16},{16,0},{32,48},{48,32},{1,17},{17,1},{33,49},{49,33},{2,18}... | collective-permute-start | bytes 7077896 | tf_op jit(solution)/shard_map/ppermute | solution.py:22
  902.1 49.8 %collective-permute-start.57 = (bf16[2,384,1536]{2,1,0:T(8,128)(2,1)}, bf16[2,384,1536]{2,1,0:T(8,128)(2,1)}, u32[]{:S(2)}, u32[]{:S(2)}) collective-permute-start(bf16[2,384,1536]{2,1,0:T(8,128)(2,1)} %convolution_convert_fusion.2), channel_id=1, source_target_pairs={{0,16},{16,0},{32,48},{48,32},{1,17},{17,1},{33,49},{49,33},{2,18}... | collective-permute-start | bytes 7077896 | tf_op jit(solution)/shard_map/ppermute | solution.py:22
  927.1 54.5 %collective-permute-start.37 = (bf16[192,384]{1,0:T(8,128)(2,1)}, bf16[192,384]{1,0:T(8,128)(2,1)S(1)}, u32[]{:S(2)}, u32[]{:S(2)}) collective-permute-start(bf16[192,384]{1,0:T(8,128)(2,1)} %get-tuple-element.357), channel_id=1, source_target_pairs={{0,16},{16,0},{32,48},{48,32},{1,17},{17,1},{33,49},{49,33},{2,18}... | collective-permute-start | bytes 442376 | tf_op jit(solution)/shard_map/ppermute | solution.py:22
  930.9 51.8 %collective-permute-start.38 = (bf16[192,384]{1,0:T(8,128)(2,1)}, bf16[192,384]{1,0:T(8,128)(2,1)S(1)}, u32[]{:S(2)}, u32[]{:S(2)}) collective-permute-start(bf16[192,384]{1,0:T(8,128)(2,1)} %get-tuple-element.358), channel_id=1, source_target_pairs={{0,32},{16,48},{32,0},{48,16},{1,33},{17,49},{33,1},{49,17},{2,34}... | collective-permute-start | bytes 442376 | tf_op jit(solution)/shard_map/ppermute | solution.py:22
  936.0 49.4 %all-to-all-start.17 = ((bf16[16,24,1664]{2,1,0:T(8,128)(2,1)}), bf16[16,24,1664]{2,1,0:T(8,128)(2,1)S(1)}, u32[]{:S(2)}, u32[]{:S(2)}) async-start(bf16[16,24,1664]{2,1,0:T(8,128)(2,1)} %pad_maximum_fusion.16), calls=%async_computation.17 | async-start | bytes 2555904 | tf_op jit(solution)/shard_map/all_to_all | solution.py:198
  951.9 27.6 %collective-permute-start.42 = (bf16[192,2048]{1,0:T(8,128)(2,1)S(1)}, bf16[192,2048]{1,0:T(8,128)(2,1)S(1)}, u32[]{:S(2)}, u32[]{:S(2)}) collective-permute-start(bf16[192,2048]{1,0:T(8,128)(2,1)S(1)} %copy-done.114), channel_id=1, source_target_pairs={{0,48},{16,32},{32,16},{48,0},{1,49},{17,33},{33,17},{49,1},{2,50}... | collective-permute-start | bytes 2359304 | tf_op jit(solution)/shard_map/ppermute | solution.py:22
  960.3 44.4 %collective-permute-start.60 = (bf16[2,192,1536]{2,1,0:T(8,128)(2,1)}, bf16[2,192,1536]{2,1,0:T(8,128)(2,1)}, u32[]{:S(2)}, u32[]{:S(2)}) collective-permute-start(bf16[2,192,1536]{2,1,0:T(8,128)(2,1)} %slice.4540), channel_id=1, source_target_pairs={{0,32},{16,48},{32,0},{48,16},{1,33},{17,49},{33,1},{49,17},{2,34}... | collective-permute-start | bytes 3538952 | tf_op jit(solution)/shard_map/ppermute | solution.py:22
  979.5 50.6 %collective-permute-start.56 = (bf16[2,192,1536]{2,1,0:T(8,128)(2,1)S(1)}, bf16[2,192,1536]{2,1,0:T(8,128)(2,1)}, u32[]{:S(2)}, u32[]{:S(2)}) collective-permute-start(bf16[2,192,1536]{2,1,0:T(8,128)(2,1)S(1)} %slice.4542), channel_id=1, source_target_pairs={{0,32},{16,48},{32,0},{48,16},{1,33},{17,49},{33,1},{49,17},{2,34}... | collective-permute-start | bytes 3538952 | tf_op jit(solution)/shard_map/ppermute | solution.py:22
  981.6 73.7 %collective-permute-start.58 = (bf16[2,192,1536]{2,1,0:T(8,128)(2,1)}, bf16[2,192,1536]{2,1,0:T(8,128)(2,1)}, u32[]{:S(2)}, u32[]{:S(2)}) collective-permute-start(bf16[2,192,1536]{2,1,0:T(8,128)(2,1)} %slice.4541), channel_id=1, source_target_pairs={{0,32},{16,48},{32,0},{48,16},{1,33},{17,49},{33,1},{49,17},{2,34}... | collective-permute-start | bytes 3538952 | tf_op jit(solution)/shard_map/ppermute | solution.py:22
  986.5 71.9 %all-to-all-start.16 = ((bf16[16,24,2176]{2,1,0:T(8,128)(2,1)}), bf16[16,24,2176]{2,1,0:T(8,128)(2,1)S(1)}, u32[]{:S(2)}, u32[]{:S(2)}) async-start(bf16[16,24,2176]{2,1,0:T(8,128)(2,1)} %pad_maximum_fusion.7), calls=%async_computation.16 | async-start | bytes 3342336 | tf_op jit(solution)/shard_map/all_to_all | solution.py:198
  (355 other events, 4345.4 us)
Sparse Core Ops, SparseCore 0:
  11.7 82.1 all-gather.3
  97.0 72.6 all-gather.5

commit v2 on v1

v2 whole, which is shorter than its diff:
```python
import functools

import jax
import jax.numpy as jnp
from jax import lax
from jax.experimental import pallas as pl
from jax.experimental.pallas import tpu as pltpu
from jax.sharding import PartitionSpec as P

HEAD_DIM = 128
ROOMS = 16
EPSILON = 1e-06
LANES = 128
BF = jnp.bfloat16
F32 = jnp.float32
MIB = 1 << 20


def dot(left, right, contract=(1, 0)):
    return lax.dot_general(
        left, right, (((contract[0],), (contract[1],)), ((), ())), preferred_element_type=F32
    )


def like(shape, dtype):
    return jax.ShapeDtypeStruct(shape, dtype)


def call(body, outs, args, flops, far=(), scratch=(), vmem=48, scalars=(), waits=()):
    moved = sum(a.size * a.dtype.itemsize for a in (*args, *far, *outs))
    used = len(scalars) + len(args) + len(far)

    def run(*refs):
        body(*refs[:used], *refs[used + len(waits) :])

    return pl.pallas_call(
        run,
        out_shape=tuple(outs),
        in_specs=[pl.BlockSpec(memory_space=pltpu.SMEM)] * len(scalars)
        + [pl.BlockSpec(memory_space=pltpu.VMEM)] * len(args)
        + [pl.BlockSpec(memory_space=pl.ANY)] * (len(far) + len(waits)),
        out_specs=tuple(pl.BlockSpec(memory_space=pltpu.VMEM) for unused in outs),
        scratch_shapes=list(scratch),
        compiler_params=pltpu.CompilerParams(vmem_limit_bytes=vmem * MIB),
        cost_estimate=pl.CostEstimate(
            flops=int(flops), bytes_accessed=int(moved), transcendentals=0
        ),
        name=body.func.__name__ if isinstance(body, functools.partial) else body.__name__,
    )(*scalars, *args, *far, *waits)


def swapped(value, step):
    rows = lax.axis_size("row")
    return lax.ppermute(value, "row", [(r, r ^ step) for r in range(rows)])


def norm_parts(stream):
    return lax.rsqrt(jnp.mean(stream * stream, -1, keepdims=True) + EPSILON)


def norm_back(grad, stream, gain):
    inverse = norm_parts(stream)
    unit = stream * inverse
    scaled = grad * gain
    back = inverse * (scaled - unit * jnp.mean(scaled * unit, -1, keepdims=True))
    return back, jnp.sum(grad * unit, 0, keepdims=True)


def turned(vectors, cosine, sine):
    done = []
    for at in range(0, vectors.shape[1], HEAD_DIM):
        one = vectors[:, at : at + HEAD_DIM]
        done.append(one * cosine + pltpu.roll(one, HEAD_DIM // 2, 1) * sine)
    return jnp.concatenate(done, -1) if len(done) > 1 else done[0]


def stacked_heads(value, first, count):
    return jnp.concatenate(
        [value[:, (first + j) * HEAD_DIM : (first + j + 1) * HEAD_DIM] for j in range(count)], 0
    )


def unstacked_heads(value, count):
    tokens = value.shape[0] // count
    return jnp.concatenate([value[j * tokens : (j + 1) * tokens] for j in range(count)], 1)


def cuts_of(total, most=512):
    return [(at, min(most, total - at)) for at in range(0, total, most)]


def project(
    flag, came, entering, gain, cosine, sine, dense, stream, normed, query, pair, weights, sems
):
    width = stream.shape[1]
    cuts = cuts_of(weights.shape[1])
    copies = [
        pltpu.make_async_copy(
            dense.at[:, pl.ds(at, size)], weights.at[:, pl.ds(at, size)], sems.at[k]
        )
        for k, (at, size) in enumerate(cuts)
    ]
    for copy in copies:
        copy.start()
    x = jnp.where(flag[0] > 0, came[...].astype(F32), entering[...].astype(F32))
    stream[...] = x
    low = (x * norm_parts(x) * gain[...]).astype(BF)
    normed[...] = low
    keys = pair.shape[1] // 2
    for copy, (at, size) in zip(copies, cuts):
        copy.wait()
        part = dot(low, weights[:, at : at + size])
        for begin in range(at, at + size, HEAD_DIM):
            head = part[:, begin - at : begin - at + HEAD_DIM]
            if begin < width + keys:
                head = turned(head, cosine[...], sine[...])
            if begin < width:
                query[:, begin : begin + HEAD_DIM] = head.astype(BF)
            else:
                pair[:, begin - width : begin - width + HEAD_DIM] = head.astype(BF)


def attend(
    stream, query, pair0, pair1, pair2, pair3, bias, gain, chosen, dispatch, dense, mixed, middle,
    normed_ffn, gates, outgoing, probs, weights, router, sems,
):
    width = stream.shape[1]
    at = dense.shape[1] - width - LANES
    copies = [
        pltpu.make_async_copy(dense.at[:, pl.ds(at + LANES, width)], weights, sems.at[0]),
        pltpu.make_async_copy(dense.at[:, pl.ds(at, LANES)], router, sems.at[1]),
    ]
    for copy in copies:
        copy.start()
    pairs = jnp.concatenate([pair0[...], pair1[...], pair2[...], pair3[...]], 0)
    kv_heads = pairs.shape[1] // (2 * HEAD_DIM)
    group = width // HEAD_DIM // kv_heads
    biases = jnp.concatenate([bias[...]] * group, 0)
    tokens = stream.shape[0]
    for h in range(kv_heads):
        keys = pairs[:, h * HEAD_DIM : (h + 1) * HEAD_DIM]
        values = pairs[:, (kv_heads + h) * HEAD_DIM : (kv_heads + h + 1) * HEAD_DIM]
        queries = stacked_heads(query, h * group, group)
        scores = dot(queries, keys, (1, 1)) * HEAD_DIM ** (-0.5) + biases
        expo = jnp.exp(scores - jnp.max(scores, -1, keepdims=True))
        weight = (expo * (1.0 / jnp.sum(expo, -1, keepdims=True))).astype(BF)
        probs[h] = weight
        done = dot(weight, values).astype(BF)
        for j in range(group):
            begin = (h * group + j) * HEAD_DIM
            mixed[:, begin : begin + HEAD_DIM] = done[j * tokens : (j + 1) * tokens]
    copies[0].wait()
    x = stream[...] + dot(mixed[...], weights[...])
    middle[...] = x
    low = (x * norm_parts(x) * gain[...]).astype(BF)
    normed_ffn[...] = low
    copies[1].wait()
    taken = chosen[...] > 0
    logits = jnp.where(taken, dot(low, router[...]), -1e30)
    expo = jnp.where(taken, jnp.exp(logits - jnp.max(logits, -1, keepdims=True)), 0.0)
    gates[...] = expo / jnp.sum(expo, -1, keepdims=True)
    outgoing[...] = dot(dispatch[...], low).astype(BF).reshape(outgoing.shape)


def fetch(shards, weights, sems):
    copies = []
    for j in range(weights.shape[1]):
        line = []
        for k in range(weights.shape[0]):
            some = []
            for p in range(4):
                size = shards[k][p].shape[1]
                some.append(
                    pltpu.make_async_copy(
                        shards[k][p].at[j],
                        weights.at[k, j, pl.ds(p * size, size)],
                        sems.at[k, j, p],
                    )
                )
            line.append(some)
        copies.append(line)
    for line in copies:
        for some in line:
            for copy in some:
                copy.start()
    return copies


def done_with(copies):
    for copy in copies:
        copy.wait()


def rows_of(value, j):
    columns, unused, width = value.shape
    return value[:, j * ROOMS : (j + 1) * ROOMS, :].reshape(columns * ROOMS, width)


def expert_forward(keep, arrived, *refs):
    shards = [refs[4 * k : 4 * k + 4] for k in range(3)]
    outs, weights, sems = refs[12:-2], refs[-2], refs[-1]
    copies = fetch(shards, weights, sems)
    for j in range(weights.shape[1]):
        rows = rows_of(arrived, j)
        done_with(copies[j][0])
        gate = dot(rows, weights[0, j], (1, 1))
        done_with(copies[j][1])
        lifted = dot(rows, weights[1, j], (1, 1))
        square = gate * gate
        bend = jnp.tanh(0.7978845608028654 * gate * (1.0 + 0.044715 * square))
        active = 0.5 * gate * (1.0 + bend)
        hidden = (active * lifted).astype(BF)
        if keep:
            slope = 0.5 * (1.0 + bend) + 0.5 * gate * (1.0 - bend * bend) * (
                0.7978845608028654 * (1.0 + 3 * 0.044715 * square)
            )
            outs[1][j] = hidden
            outs[2][j] = active.astype(BF)
            outs[3][j] = (slope * lifted).astype(BF)
        done_with(copies[j][2])
        made = dot(hidden, weights[2, j]).astype(BF)
        outs[0][:, j * ROOMS : (j + 1) * ROOMS, :] = made.reshape(-1, ROOMS, made.shape[1])


def combine(returned, middle, gates, spread, places, result, low):
    weights = dot(gates[...].astype(BF), spread[...]) * places[...].astype(F32)
    rows = returned[...].reshape(-1, returned.shape[2])
    done = middle[...] + dot(weights.astype(BF), rows)
    result[...] = done
    low[...] = done.astype(BF)


def send_grads(flag, came, target, gates, dispatch, grad, outgoing):
    low = jnp.where(flag[0] > 0, came[...], target[...])
    grad[...] = low
    slots = dispatch.shape[0]
    own = lax.broadcasted_iota(jnp.int32, (slots, LANES), 0) // ROOMS
    here = own == lax.broadcasted_iota(jnp.int32, (slots, LANES), 1)
    scale = jnp.sum(
        jnp.where(here, dot(dispatch[...], gates[...].astype(BF)), 0.0), -1, keepdims=True
    )
    outgoing[...] = (dot(dispatch[...], low) * scale).astype(BF).reshape(outgoing.shape)


def expert_backward(arrived, active, bent, *refs):
    shards = [refs[4 * k : 4 * k + 4] for k in range(3)]
    sent, gate_back, lifted_back, weights, sems = refs[12:]
    copies = fetch(shards, weights, sems)
    for j in range(weights.shape[1]):
        done_with(copies[j][0])
        hidden_grads = dot(rows_of(arrived, j), weights[0, j], (1, 1))
        gate_part = (hidden_grads * bent[j].astype(F32)).astype(BF)
        lifted_part = (hidden_grads * active[j].astype(F32)).astype(BF)
        gate_back[j] = gate_part
        lifted_back[j] = lifted_part
        done_with(copies[j][1])
        done = dot(gate_part, weights[1, j])
        done_with(copies[j][2])
        done = (done + dot(lifted_part, weights[2, j])).astype(BF)
        sent[:, j * ROOMS : (j + 1) * ROOMS, :] = done.reshape(-1, ROOMS, done.shape[1])


def attend_back(
    keep, row, token_grads, returned, gates, spread, places, middle, gain, grad, query, pair0, pair1,
    pair2, pair3, probs, cosine, sine, dense, middle_grads, query_back, part0, part1, part2, part3,
    *rest,
):
    tokens, width = middle.shape
    kept, (branch, weights, router, sems) = rest[:-4], rest[-4:]
    at = dense.shape[1] - width - LANES
    copies = [
        pltpu.make_async_copy(dense.at[:, pl.ds(at, LANES)], router, sems.at[1]),
        pltpu.make_async_copy(dense.at[:, pl.ds(at + LANES, width)], weights, sems.at[0]),
    ]
    for copy in copies:
        copy.start()
    inner = dot(grad[...], returned[...].reshape(-1, width), (1, 1)) * places[...].astype(F32)
    gate_grads = dot(inner.astype(BF), spread[...], (1, 1))
    chances = gates[...]
    logit_grads = (
        chances * (gate_grads - jnp.sum(chances * gate_grads, -1, keepdims=True))
    ).astype(BF)
    ffn_grads = dot(places[...], token_grads[...].reshape(-1, width))
    copies[0].wait()
    ffn_grads = ffn_grads + dot(logit_grads, router[...], (1, 1))
    part, total = norm_back(ffn_grads, middle[...], gain[...])
    above = grad[...].astype(F32) + part
    middle_grads[...] = above
    low = above.astype(BF)
    if keep:
        kept[0][...] = logit_grads
        kept[1][...] = jnp.broadcast_to(total, kept[1].shape)
        branch[...] = low
        share = width // 4
        for s, out in enumerate(kept[2:]):
            out[...] = branch[:, pl.ds(pl.multiple_of((row[0] ^ s) * share, LANES), share)]
    copies[1].wait()
    mixed_grads = dot(low, weights[...], (1, 1)).astype(BF)
    pairs = jnp.concatenate([pair0[...], pair1[...], pair2[...], pair3[...]], 0)
    kv_heads = pairs.shape[1] // (2 * HEAD_DIM)
    group = width // HEAD_DIM // kv_heads
    scale = HEAD_DIM ** (-0.5)
    parts = (part0, part1, part2, part3)
    for h in range(kv_heads):
        keys = pairs[:, h * HEAD_DIM : (h + 1) * HEAD_DIM]
        values = pairs[:, (kv_heads + h) * HEAD_DIM : (kv_heads + h + 1) * HEAD_DIM]
        queries = stacked_heads(query, h * group, group)
        top = stacked_heads(mixed_grads, h * group, group)
        weight = probs[h]
        wide = weight.astype(F32)
        weight_grads = dot(top, values, (1, 1))
        value_grads = dot(weight, top, (0, 0)).astype(BF)
        inner = wide * weight_grads
        score_grads = (inner - wide * jnp.sum(inner, -1, keepdims=True)).astype(BF)
        query_grads = dot(score_grads, keys) * scale
        key_grads = (dot(score_grads, queries, (0, 0)) * scale).astype(BF)
        for j in range(group):
            begin = (h * group + j) * HEAD_DIM
            one = query_grads[j * tokens : (j + 1) * tokens]
            query_back[:, begin : begin + HEAD_DIM] = turned(one, cosine[...], -sine[...]).astype(BF)
        for p, part in enumerate(parts):
            part[:, h * HEAD_DIM : (h + 1) * HEAD_DIM] = key_grads[p * tokens : (p + 1) * tokens]
            begin = (kv_heads + h) * HEAD_DIM
            part[:, begin : begin + HEAD_DIM] = value_grads[p * tokens : (p + 1) * tokens]


def project_back(
    keep, row, part0, part1, part2, part3, query_back, stream, gain, middle_grads, cosine, sine,
    dense, grad, low, *rest,
):
    width = stream.shape[1]
    kept, (backs, weights, sems) = rest[:-3], rest[-3:]
    cuts = cuts_of(weights.shape[1])
    copies = [
        pltpu.make_async_copy(
            dense.at[:, pl.ds(at, size)], weights.at[:, pl.ds(at, size)], sems.at[k]
        )
        for k, (at, size) in enumerate(cuts)
    ]
    for copy in copies:
        copy.start()
    total = sum(part[...].astype(F32) for part in (part0, part1, part2, part3))
    keys = total.shape[1] // 2
    backs[:, :width] = query_back[...]
    backs[:, width : width + keys] = turned(total[:, :keys], cosine[...], -sine[...]).astype(BF)
    backs[:, width + keys :] = total[:, keys:].astype(BF)
    above = jnp.zeros(stream.shape, F32)
    for copy, (at, size) in zip(copies, cuts):
        copy.wait()
        above = above + dot(backs[:, at : at + size], weights[:, at : at + size], (1, 1))
    part, sums = norm_back(above, stream[...], gain[...])
    if keep:
        kept[0][...] = jnp.broadcast_to(sums, kept[0].shape)
        share = backs.shape[1] // 4
        for s, out in enumerate(kept[1:]):
            out[...] = backs[:, pl.ds(pl.multiple_of((row[0] ^ s) * share, LANES), share)]
    done = middle_grads[...] + part
    grad[...] = done
    low[...] = done.astype(BF)


def expert_weight_grads(half, left0, left1, right0, right1, first, second):
    size = first.shape[1]
    wide = 2 * size
    for j in range(first.shape[0]):
        total = dot(left0[j, :, half * wide : (half + 1) * wide], rows_of(right0, j), (0, 0))
        total = total + dot(
            left1[j, :, half * wide : (half + 1) * wide], rows_of(right1, j), (0, 0)
        )
        first[j] = total[:size].astype(BF)
        second[j] = total[size:].astype(BF)


def pack(*refs):
    for k, value in enumerate(refs[:-1]):
        refs[-1][k] = value[...]


def stacked(refs):
    return jnp.concatenate([r[...] for r in refs], 0)


def out_grads(*refs):
    lefts, rights, out = refs[:4], refs[4:12], refs[12]
    left = jnp.concatenate([one[k] for one in lefts for k in (2, 3)], 0)
    out[...] = dot(left, stacked(rights), (0, 0)).astype(BF)


def qkv_grads(*refs):
    lefts, rights, normed, logits, gains, out = (
        refs[:4], refs[4:12], refs[12:14], refs[14:16], refs[16:20], refs[20],
    )
    width, wide = out.shape
    left = jnp.concatenate([one[k] for one in lefts for k in (0, 1)], 0)
    out[:, : wide - LANES] = dot(left, stacked(rights), (0, 0)).astype(BF)
    first = gains[0][:1] + gains[1][:1]
    second = gains[2][:1] + gains[3][:1]
    line = lax.broadcasted_iota(jnp.int32, (LANES, width), 0)
    sums = jnp.where(
        line == LANES - 2, first, jnp.where(line == LANES - 1, second, jnp.zeros((1, 1), F32))
    )
    out[:, wide - LANES :] = (dot(stacked(normed), stacked(logits), (0, 0)) + sums.T).astype(BF)


def fold(row, first, second, out0, out1, out2, out3, total):
    share = first.shape[2]
    total[:, :share] = jnp.sum(first[...].astype(F32), 0)
    total[:, share:] = jnp.sum(second[...].astype(F32), 0)
    for s, out in enumerate((out0, out1, out2, out3)):
        size = out.shape[0]
        out[...] = total[pl.ds(pl.multiple_of((row[0] ^ s) * size, 8), size), :]


def finish(row, in0, in1, in2, in3, o_grad, q_grad, k_grad, v_grad, rest, total):
    share = o_grad.shape[1] // 4
    piece = total.shape[1] // 4
    ins = (in0, in1, in2, in3)
    for s, one in enumerate(ins):
        where = row[0] ^ s
        o_grad[:, pl.ds(pl.multiple_of(where * share, LANES), share)] = one[:, :share]
        total[:, pl.ds(pl.multiple_of(where * piece, LANES), piece)] = one[:, share : share + piece]
    rest[...] = sum(one[:, share + piece :] for one in ins)
    begin = 0
    for out in (q_grad, k_grad, v_grad):
        out[...] = total[:, begin : begin + out.shape[1]]
        begin += out.shape[1]


def over_columns(value):
    return lax.all_to_all(value, "col", split_axis=0, concat_axis=0, tiled=True)


def on_device(
    inputs, cotangent, segment_ids, routes, attn_gain, w_query, w_key, w_value, w_out, ffn_gain,
    w_router, w_gate, w_up, w_down,
):
    section = lax.axis_index("section")
    row = lax.axis_index("row")
    rows = lax.axis_size("row")
    columns = lax.axis_size("col")
    micro, tokens, width = inputs.shape[0], inputs.shape[2], inputs.shape[3]
    experts = w_router.shape[2]
    per_column = w_gate.shape[1]
    hidden_width = w_gate.shape[2] * rows
    kv_width = w_key.shape[2]
    qkv_width = width + 2 * kv_width
    slots = experts * ROOMS
    share = width // rows
    shard = width // (rows * columns)
    heads = width // HEAD_DIM
    kv_heads = kv_width // HEAD_DIM
    length = rows * tokens
    pieces = range(micro)
    steps = range(rows)
    here = row.astype(jnp.int32)[None]
    second = (section == 1).astype(jnp.int32)[None]
    block = (columns, slots // columns, width)

    dense = jnp.concatenate(
        [w_query[0], w_key[0], w_value[0], w_router[0], attn_gain[0][:, None], ffn_gain[0][:, None],
         jnp.zeros((shard, LANES - experts - 2), BF), w_out[0]], 1
    )
    dense = lax.all_gather(dense, ("row", "col"), axis=0, tiled=True)
    small = dense[:, qkv_width : qkv_width + LANES]
    gain_a = small[:, experts].astype(F32)[None, :]
    gain_f = small[:, experts + 1].astype(F32)[None, :]

    def shards_of(own):
        two = swapped(own, 2)
        return own, swapped(own, 1), two, swapped(two, 1)

    gate_shards, up_shards, down_shards = (
        shards_of(w_gate[0]), shards_of(w_up[0]), shards_of(w_down[0])
    )

    lane = jnp.arange(LANES, dtype=jnp.int32)
    half = HEAD_DIM // 2
    freqs = 10000.0 ** (-2.0 * jnp.arange(half).astype(F32) / HEAD_DIM)
    positions = row * tokens + jnp.arange(tokens, dtype=jnp.int32)
    angles = positions.astype(F32)[:, None] * freqs[None, :]
    cosine = jnp.concatenate([jnp.cos(angles)] * 2, 1)
    sine = jnp.concatenate([-jnp.sin(angles), jnp.sin(angles)], 1)
    key_positions = jnp.concatenate(
        [(row ^ step) * tokens + jnp.arange(tokens, dtype=jnp.int32) for step in steps]
    )
    spread = (lane[:, None] == jnp.arange(slots, dtype=jnp.int32)[None, :] // ROOMS).astype(BF)
    below = (jnp.arange(tokens)[:, None] > jnp.arange(tokens)[None, :]).astype(BF)
    biases, chosens, places, dispatches = [], [], [], []
    for m in pieces:
        segments = segment_ids[m, 0]
        own_segments = lax.dynamic_slice_in_dim(segments, row * tokens, tokens)
        key_segments = jnp.concatenate(
            [lax.dynamic_slice_in_dim(segments, (row ^ s) * tokens, tokens) for s in steps]
        )
        counted = (key_positions[None, :] <= positions[:, None]) & (
            key_segments[None, :] == own_segments[:, None]
        )
        biases.append(jnp.where(counted, 0.0, -1e30).astype(F32))
        chosen = jnp.any(routes[0, m, 0][:, :, None] == lane[None, None, :], 1)
        chosens.append(chosen.astype(F32))
        rank = dot(below, chosen.astype(BF))
        rank = jnp.where(chosen, rank, -1.0)[:, :experts]
        place = (
            rank[:, :, None] == jnp.arange(ROOMS, dtype=F32)[None, None, :]
        ).reshape(tokens, slots)
        places.append(place.astype(BF))
        dispatches.append(place.T.astype(BF))

    token_low, token_wide = like((tokens, width), BF), like((tokens, width), F32)
    pair_like = like((tokens, 2 * kv_width), BF)
    block_like = like(block, BF)
    sums_like = like((8, width), F32)
    kept_like = like((per_column, columns * ROOMS, hidden_width), BF)
    probs_like = like((kv_heads, heads // kv_heads * tokens, length), BF)
    qkv_scratch = [pltpu.VMEM((width, qkv_width), BF), pltpu.SemaphoreType.DMA((8,))]
    out_scratch = [
        pltpu.VMEM((width, width), BF), pltpu.VMEM((width, LANES), BF),
        pltpu.SemaphoreType.DMA((2,)),
    ]
    expert_scratch = [
        pltpu.VMEM((3, per_column, hidden_width, width), BF),
        pltpu.SemaphoreType.DMA((3, per_column, 4)),
    ]
    qkv_flops = 2 * tokens * width * qkv_width
    out_flops = 2 * tokens * width * width + 2 * slots * tokens * width
    score_flops = 2 * heads * tokens * length * HEAD_DIM
    expert_flops = 2 * slots * hidden_width * width

    def forward(came, entering, keep, waits=()):
        projected = [
            call(
                project, (token_wide, token_low, token_low, pair_like),
                (came[m], entering[m], gain_a, cosine, sine), qkv_flops, (dense,), qkv_scratch,
                scalars=(second,), waits=() if m else waits,
            )
            for m in pieces
        ]
        pairs = [[p[3]] + [swapped(p[3], s) for s in steps[1:]] for p in projected]
        attended = [
            call(
                attend,
                (token_low, token_wide, token_low, like((tokens, LANES), F32), block_like, probs_like),
                (projected[m][0], projected[m][2], *pairs[m], biases[m], gain_f, chosens[m],
                 dispatches[m]),
                out_flops + 2 * score_flops, (dense,), out_scratch,
            )
            for m in pieces
        ]
        arrived = [over_columns(a[4]) for a in attended]
        applied = [
            call(
                functools.partial(expert_forward, keep),
                (block_like,) + (kept_like,) * (3 if keep else 0), (arrived[m],), 3 * expert_flops,
                (*gate_shards, *up_shards, *down_shards), expert_scratch,
                waits=() if m else (attended[1][4],),
            )
            for m in pieces
        ]
        returned = [over_columns(a[0]) for a in applied]
        results = [
            call(
                combine, (token_wide, token_low),
                (returned[m], attended[m][1], attended[m][3], spread, places[m]),
                2 * slots * tokens * width, waits=() if m else (applied[1][0],),
            )
            for m in pieces
        ]
        return projected, pairs, attended, arrived, applied, returned, results

    def backward(came, targets, kept, lefts, keep, waits):
        projected, pairs, attended, entered, applied, returned, results = kept
        sent = [
            call(
                send_grads, (token_low, block_like),
                (came[m], targets[m], attended[m][3], dispatches[m]),
                2 * slots * tokens * width, scalars=(1 - second,),
            )
            for m in pieces
        ]
        arrived = [over_columns(s[1]) for s in sent]
        moved = [
            call(
                expert_backward, (block_like, kept_like, kept_like),
                (arrived[m], applied[m][2], applied[m][3]), 3 * expert_flops,
                (*down_shards, *gate_shards, *up_shards), expert_scratch,
                waits=() if m else (sent[1][1],),
            )
            for m in pieces
        ]
        back = [over_columns(a[0]) for a in moved]

        def halves(side):
            lefts = ([a[1] for a in applied], [a[1] for a in moved], [a[2] for a in moved])
            rights = (arrived, entered, entered)
            return [
                call(
                    functools.partial(expert_weight_grads, side),
                    (like((per_column, hidden_width // 4, width), BF),) * 2, (*left, *right),
                    expert_flops,
                )
                for left, right in zip(lefts, rights)
            ]

        far = halves(1)
        near = halves(0) if keep else []
        between = [p[0].astype(F32) + swapped(p[1], 1).astype(F32) for p in far]
        between = [b.astype(BF) for b in between]
        first_waits = [moved[1][0], *(p[0] for p in far), *(p[0] for p in near)]
        inner, parts, outer, branches = [], [], [], []
        for m in pieces:
            inner.append(
                call(
                    functools.partial(attend_back, keep),
                    (token_wide, token_low) + (pair_like,) * 4
                    + ((like((tokens, LANES), BF), sums_like)
                       + (like((tokens, share), BF),) * rows if keep else ()),
                    (back[m], returned[m], attended[m][3], spread, places[m], attended[m][1], gain_f,
                     sent[m][0], projected[m][2], *pairs[m], attended[m][5], cosine, sine),
                    out_flops + 4 * score_flops, (dense,),
                    [pltpu.VMEM((tokens, width), BF)] + out_scratch,
                    scalars=(here,),
                    waits=(*between, *waits[1]) if m else (*first_waits, *waits[0]),
                )
            )
        parts = [[a[2]] + [swapped(a[2 + s], s) for s in steps[1:]] for a in inner]
        if keep:
            branches = [[a[8]] + [swapped(a[8 + s], s) for s in steps[1:]] for a in inner]
            o_grads = call(
                out_grads, (like((width, share), BF),),
                (*lefts, *[b[s] for s in steps for b in branches]),
                2 * width * length * micro * share,
            )[0]
        outer = [
            call(
                functools.partial(project_back, keep),
                (token_wide, token_low)
                + ((sums_like,) + (like((tokens, qkv_width // rows), BF),) * rows if keep else ()),
                (*parts[m], inner[m][1], projected[m][0], gain_a, inner[m][0], cosine, sine),
                qkv_flops, (dense,), [pltpu.VMEM((tokens, qkv_width), BF)] + qkv_scratch,
                scalars=(here,), waits=(o_grads,) if m and keep else (),
            )
            for m in pieces
        ]
        if not keep:
            return outer, between
        backs = [[o[3]] + [swapped(o[3 + s], s) for s in steps[1:]] for o in outer]
        w_grads = call(
            qkv_grads, (like((width, qkv_width // rows + LANES), BF),),
            (*lefts, *[b[s] for s in steps for b in backs], *[a[2] for a in attended],
             *[a[6] for a in inner], *[o[2] for o in outer], *[a[7] for a in inner]),
            2 * width * length * micro * qkv_width // rows,
        )[0]
        return outer, between, near, o_grads, w_grads

    def by_columns(value):
        cut = value.reshape(rows, columns, shard, value.shape[1]).transpose(1, 0, 2, 3)
        return over_columns(cut.reshape(columns, rows * shard, value.shape[1]))

    def across(value, only):
        lines = [(only * rows + r, only * rows + (r ^ 2)) for r in range(rows)]
        return lax.ppermute(value, ("section", "row"), lines)

    entering = [inputs[m, 0] for m in pieces]
    moving = [g[k] for g in (gate_shards, up_shards, down_shards) for k in (1, 2)]
    results = forward(entering, entering, False, moving)[6]
    came = [lax.ppermute(r[1], "section", [(0, 1)]) for r in results]
    kept = forward(came, entering, True)
    projected, pairs, attended, arrived, applied, returned, results = kept
    left = call(
        pack, (like((2 * micro, tokens, width), BF),),
        [p[1] for p in projected] + [a[0] for a in attended], 0,
    )[0]
    two = swapped(left, 2)
    lefts = [left, swapped(left, 1), two, swapped(two, 1)]

    targets = [cotangent[m, 0] for m in pieces]
    outer, between = backward(targets, targets, kept, lefts, False, ((), lefts[1:]))
    came = [lax.ppermute(o[1], "section", [(1, 0)]) for o in outer]
    early = [across(b, 1) for b in between]
    done = [r[0] for r in results]
    outer, between, near, o_grads, w_grads = backward(
        came, targets, kept, lefts, True, ((*early, *done), ())
    )
    late = [across(b, 0) for b in between]
    expert_grads = [
        n[0].astype(F32) + swapped(n[1], 1).astype(F32) + e.astype(F32) + l.astype(F32)
        for n, e, l in zip(near, early, late)
    ]

    pieces_out = call(
        fold, (like((shard, share + qkv_width // rows + LANES), F32),) * rows,
        (by_columns(o_grads), by_columns(w_grads)), 0,
        scratch=[pltpu.VMEM((rows * shard, share + qkv_width // rows + LANES), F32)],
        scalars=(here,),
    )
    pieces_out = [pieces_out[0]] + [swapped(pieces_out[s], s) for s in steps[1:]]
    o_grad, q_grad, k_grad, v_grad, rest = call(
        finish,
        (like((shard, width), F32), like((shard, width), F32), like((shard, kv_width), F32),
         like((shard, kv_width), F32), like((shard, LANES), F32)),
        pieces_out, 0, scratch=[pltpu.VMEM((shard, qkv_width), F32)], scalars=(here,),
    )

    return (
        jnp.stack(done)[None, :, None],
        jnp.stack([o[0] for o in outer])[None, :, None],
        rest[:, LANES - 2][None],
        q_grad[None],
        k_grad[None],
        v_grad[None],
        o_grad[None],
        rest[:, LANES - 1][None],
        rest[:, :experts][None],
        expert_grads[1][None],
        expert_grads[2][None],
        expert_grads[0][None],
    )


def solution(mesh):
    dense = P("section", ("row", "col"), None)
    gain = P("section", ("row", "col"))
    expert = P("section", "col", "row", None)
    token = P(None, "col", "row", None)
    layered = P("section", None, "col", "row", None)
    return jax.shard_map(
        on_device,
        mesh=mesh,
        in_specs=(
            token, token, P(None, "col", None), layered, gain, dense, dense, dense, dense, gain,
            dense, expert, expert, expert,
        ),
        out_specs=(
            layered, layered, gain, dense, dense, dense, dense, gain, dense, expert, expert, expert,
        ),
        check_vma=False,
    )
```

time: 1080 us -> 914 us (0.85)
  Pallas kernels: 0 us -> 229 us
  matrix products: 227 us -> 1.12 us
  waiting for transfers between devices: 349 us -> 227 us
  other arithmetic: 125 us -> 43.2 us
  local copies, waits for them, and re-layouts: 43.6 us -> 101 us
  blocking collectives: 121 us -> 82.6 us
  starting transfers between devices: 182 us -> 201 us
    pallas_call x0 -> x46, Pallas kernels: none -> 229 us  [call(): pl.pallas_call(run, out_shape=tuple(outs), in_specs=[pl.BlockSpec(memory_...]
    dot_general x143 -> x2, matrix products: 206 us -> 1.12 us  [dot(): lax.dot_general(left, right, (((contract[0],), (contract[1],)), ((), ()))...]
    unnamed x721 -> x512, local copies, waits for them, and re-layouts: 20.7 us -> 81.6 us
    ppermute x57 -> x60, waiting for transfers between devices: 104 us -> 45.4 us  [swapped(): return lax.ppermute(value, 'row', [(r, r ^ step) for r in range(rows)])]
    all_gather x2 -> x1, waiting for transfers between devices: 133 us -> 81.8 us  [on_device(): dense = lax.all_gather(dense, ('row', 'col'), axis=0, tiled=True)]
    all_to_all x13 -> x15, waiting for transfers between devices: 94.9 us -> 45.4 us  [over_columns(): return lax.all_to_all(value, 'col', split_axis=0, concat_axis=0, tiled=True)]
    concatenate x37 -> x2, other arithmetic: 40.5 us -> 1.39 us  [the longest x1 0.7 us: on_device(): sine = jnp.concatenate([-jnp.sin(angles), jnp.sin(angles)], 1)]
    all_to_all x5 -> x3, blocking collectives: 121 us -> 82.6 us  [over_columns(): return lax.all_to_all(value, 'col', split_axis=0, concat_axis=0, tiled=True)]
  transfers between devices with their start and end apart: 76 -> 86, of which waited for: 34 -> 32; matrix products, arithmetic and copies ran while one was open for 24% -> 7% of each run, Pallas kernels for 0% -> 24%
where the time goes in v2:
time: 914 us; the launch traced here: 902 us
  Pallas kernels  229 us (25%)
  waiting for transfers between devices  227 us (25%)
  starting transfers between devices  201 us (22%)
  local copies, waits for them, and re-layouts  101 us (11%)
  blocking collectives  82.6 us (9%)
  other arithmetic  43.2 us (5%)
  between operations  16.8 us (2%)
    pallas_call x46, Pallas kernels, call(): pl.pallas_call(run, out_shape=tuple(outs), in_specs=[pl.BlockSpec(memory_...  229 us
    ppermute x60, starting transfers between devices, swapped(): return lax.ppermute(value, 'row', [(r, r ^ step) for r in range(rows)])  89.5 us
    all_to_all x15, starting transfers between devices, over_columns(): return lax.all_to_all(value, 'col', split_axis=0, concat_axis=0, tiled=True)  86.5 us
    all_to_all x3, blocking collectives, over_columns(): return lax.all_to_all(value, 'col', split_axis=0, concat_axis=0, tiled=True)  82.6 us
    all_gather x1, waiting for transfers between devices, on_device(): dense = lax.all_gather(dense, ('row', 'col'), axis=0, tiled=True)  81.8 us
    unnamed x512, local copies, waits for them, and re-layouts  81.6 us
    all_to_all x15, waiting for transfers between devices, over_columns(): return lax.all_to_all(value, 'col', split_axis=0, concat_axis=0, tiled=True)  45.4 us
    ppermute x60, waiting for transfers between devices, swapped(): return lax.ppermute(value, 'row', [(r, r ^ step) for r in range(rows)])  45.4 us
  transfers between devices with their start and end apart: 86, of which 32 were waited for; matrix products, arithmetic and copies ran while one was open for 7% of the time, Pallas kernels for 24%

profile of v2, /device:TPU:9, one launch (start us, length us, event | category | flops | bytes accessed | tf_op | source)
XLA Modules:
  0.0 901.7 jit_solution(3920436926144714396)
XLA Ops:
  34.0 6.3 collective-permute-done.1.refs_8_.refs_3_.refs_9_
  48.3 81.8 %all-gather.2.cloned.1.call-done.refs_6_.refs_10_.refs_17_.refs_11_ = bf16[1536,3712]{1,0:T(8,128)(2,1)} async-done(((bf16[24,3712]{1,0:T(8,128)(2,1)}), bf16[1536,3712]{1,0:T(8,128)(2,1)}) %all-gather.2.cloned.1.call-update) | async-done | bytes 11403280 | tf_op jit(solution)/shard_map/all_gather | solution.py:463
  149.5 6.6 attend.4
  186.9 7.1 all-to-all-start.2
  195.3 9.9 %expert_forward.4 = bf16[16,32,1536]{2,1,0:T(8,128)(2,1)} custom-call(bf16[16,32,1536]{2,1,0:T(8,128)(2,1)} %all-to-all-done.refs_0_, bf16[2,192,1536]{2,1,0:T(8,128)(2,1)S(1)} %bitcast.88, bf16[2,192,1536]{2,1,0:T(8,128)(2,1)S(1)} %collective-permute-done.refs_7_.refs_2_.refs_8_, bf16[2,192,1536]{2,1,0:T(8,128)(2,1)S(1)} %collective-permute-done.1.refs_8_.refs_3_.refs_9_, ...), custom_call_target="tpu_custom_call" | custom-call | flops 3623878656 | bytes 17301504 | tf_op jit(solution)/shard_map/expert_forward/pallas_call | solution.py:36
  205.2 12.6 %all-to-all-done.2.refs_0_ = bf16[16,32,1536]{2,1,0:T(8,128)(2,1)} async-done(((bf16[16,32,1536]{2,1,0:T(8,128)(2,1)}), bf16[16,32,1536]{2,1,0:T(8,128)(2,1)}, u32[]{:S(2)}, u32[]{:S(2)}) %all-to-all-start.2) | async-done | bytes 1572896 | tf_op jit(solution)/shard_map/all_to_all | solution.py:430
  223.4 9.9 %expert_forward.5.refs_5_ = bf16[16,32,1536]{2,1,0:T(8,128)(2,1)} custom-call(bf16[16,32,1536]{2,1,0:T(8,128)(2,1)} %all-to-all-done.2.refs_0_, bf16[2,192,1536]{2,1,0:T(8,128)(2,1)S(1)} %bitcast.89, bf16[2,192,1536]{2,1,0:T(8,128)(2,1)S(1)} %collective-permute-done.refs_7_.refs_2_.refs_8_, ...), custom_call_target="tpu_custom_call" | custom-call | flops 3623878656 | bytes 17301504 | tf_op jit(solution)/shard_map/expert_forward/pallas_call | solution.py:36
  233.4 9.5 %all-to-all-done.1.refs_0_ = bf16[16,32,1536]{2,1,0:T(8,128)(2,1)} async-done(((bf16[16,32,1536]{2,1,0:T(8,128)(2,1)}), bf16[16,32,1536]{2,1,0:T(8,128)(2,1)}, u32[]{:S(2)}, u32[]{:S(2)}) %all-to-all-start.1) | async-done | bytes 1572896 | tf_op jit(solution)/shard_map/all_to_all | solution.py:430
  252.8 6.4 collective-permute-done.15.refs_1_
  288.9 28.4 %all_to_all.90.refs_0_.refs_2_ = bf16[16,32,1536]{2,1,0:T(8,128)(2,1)} all-to-all(bf16[16,32,1536]{2,1,0:T(8,128)(2,1)} %copy-done.128), channel_id=1, replica_groups=mesh['section'=2,'row'=4,'col'=16] {'col'}, dimensions={0} | all-to-all | bytes 3145728 | tf_op jit(solution)/shard_map/all_to_all | solution.py:430
  326.8 7.2 collective-permute-done.19.refs_1_
  361.5 28.2 %all_to_all.91.refs_0_.refs_3_ = bf16[16,32,1536]{2,1,0:T(8,128)(2,1)} all-to-all(bf16[16,32,1536]{2,1,0:T(8,128)(2,1)} %copy-done.43), channel_id=1, replica_groups=mesh['section'=2,'row'=4,'col'=16] {'col'}, dimensions={0} | all-to-all | bytes 3145728 | tf_op jit(solution)/shard_map/all_to_all | solution.py:430
  394.7 10.4 %expert_forward.6 = (bf16[16,32,1536]{2,1,0:T(8,128)(2,1)}, bf16[2,256,768]{2,1,0:T(8,128)(2,1)S(1)}, bf16[2,256,768]{2,1,0:T(8,128)(2,1)S(1)}, bf16[2,256,768]{2,1,0:T(8,128)(2,1)S(1)}) custom-call(bf16[16,32,1536]{2,1,0:T(8,128)(2,1)} %copy-done, bf16[2,192,1536]{2,1,0:T(8,128)(2,1)S(1)} %bitcast.90, bf16[2,192,1536]{2,1,0:T(8,128)(2,1)S(1)} %copy-done.5, ...), custom_call_target="tpu_custom_call" | custom-call | flops 3623878656 | bytes 19660800 | tf_op jit(solution)/shard_map/expert_forward/pallas_call | solution.py:36
  406.0 10.1 %expert_backward.4 = (bf16[16,32,1536]{2,1,0:T(8,128)(2,1)}, bf16[2,256,768]{2,1,0:T(8,128)(2,1)S(1)}, bf16[2,256,768]{2,1,0:T(8,128)(2,1)S(1)}) custom-call(bf16[16,32,1536]{2,1,0:T(8,128)(2,1)} %all_to_all.90.refs_0_.refs_2_, bf16[2,256,768]{2,1,0:T(8,128)(2,1)S(1)} %get-tuple-element.184.refs_1_, bf16[2,256,768]{2,1,0:T(8,128)(2,1)S(1)} %get-tuple-element.185.refs_2_, ...), custom_call_target="tpu_custom_call" | custom-call | flops 3623878656 | bytes 20447232 | tf_op jit(solution)/shard_map/expert_backward/pallas_call | solution.py:36
  419.7 25.9 %all_to_all.92.refs_1_ = bf16[16,32,1536]{2,1,0:T(8,128)(2,1)} all-to-all(bf16[16,32,1536]{2,1,0:T(8,128)(2,1)} %get-tuple-element.187), channel_id=1, replica_groups=mesh['section'=2,'row'=4,'col'=16] {'col'}, dimensions={0} | all-to-all | bytes 3145728 | tf_op jit(solution)/shard_map/all_to_all | solution.py:430
  450.4 10.3 %expert_forward.7 = (bf16[16,32,1536]{2,1,0:T(8,128)(2,1)}, bf16[2,256,768]{2,1,0:T(8,128)(2,1)S(1)}, bf16[2,256,768]{2,1,0:T(8,128)(2,1)S(1)}, bf16[2,256,768]{2,1,0:T(8,128)(2,1)S(1)}) custom-call(bf16[16,32,1536]{2,1,0:T(8,128)(2,1)} %all-to-all-done.6.refs_0_.refs_3_, bf16[2,192,1536]{2,1,0:T(8,128)(2,1)S(1)} %bitcast.91, ...), custom_call_target="tpu_custom_call" | custom-call | flops 3623878656 | bytes 19660800 | tf_op jit(solution)/shard_map/expert_forward/pallas_call | solution.py:36
  461.6 10.1 %expert_backward.5 = (bf16[16,32,1536]{2,1,0:T(8,128)(2,1)}, bf16[2,256,768]{2,1,0:T(8,128)(2,1)S(1)}, bf16[2,256,768]{2,1,0:T(8,128)(2,1)S(1)}) custom-call(bf16[16,32,1536]{2,1,0:T(8,128)(2,1)} %all_to_all.91.refs_0_.refs_3_, bf16[2,256,768]{2,1,0:T(8,128)(2,1)S(1)} %get-tuple-element.190.refs_1_, bf16[2,256,768]{2,1,0:T(8,128)(2,1)S(1)} %get-tuple-element.191.refs_2_, ...), custom_call_target="tpu_custom_call" | custom-call | flops 3623878656 | bytes 20447232 | tf_op jit(solution)/shard_map/expert_backward/pallas_call | solution.py:36
  474.4 6.9 all-to-all-start.12
  510.4 6.6 collective-permute-start.28
  521.3 8.5 attend_back.4
  555.7 7.3 all-to-all-start.11
  569.0 8.1 attend_back.5
  605.4 7.2 all-to-all-start.14
  614.9 10.1 %expert_backward.6 = (bf16[16,32,1536]{2,1,0:T(8,128)(2,1)}, bf16[2,256,768]{2,1,0:T(8,128)(2,1)S(1)}, bf16[2,256,768]{2,1,0:T(8,128)(2,1)S(1)}) custom-call(bf16[16,32,1536]{2,1,0:T(8,128)(2,1)} %copy-done.16, bf16[2,256,768]{2,1,0:T(8,128)(2,1)S(1)} %copy-done.108, bf16[2,256,768]{2,1,0:T(8,128)(2,1)S(1)} %copy-done.110, ...), custom_call_target="tpu_custom_call" | custom-call | flops 3623878656 | bytes 20447232 | tf_op jit(solution)/shard_map/expert_backward/pallas_call | solution.py:36
  649.6 10.1 %expert_backward.7 = (bf16[16,32,1536]{2,1,0:T(8,128)(2,1)}, bf16[2,256,768]{2,1,0:T(8,128)(2,1)S(1)}, bf16[2,256,768]{2,1,0:T(8,128)(2,1)S(1)}) custom-call(bf16[16,32,1536]{2,1,0:T(8,128)(2,1)} %all-to-all-done.14.refs_0_.refs_3_, bf16[2,256,768]{2,1,0:T(8,128)(2,1)S(1)} %copy-done.104, bf16[2,256,768]{2,1,0:T(8,128)(2,1)S(1)} %copy-done.106, ...), custom_call_target="tpu_custom_call" | custom-call | flops 3623878656 | bytes 20447232 | tf_op jit(solution)/shard_map/expert_backward/pallas_call | solution.py:36
  700.6 7.0 all-to-all-start.15
  721.1 25.3 %collective-permute-done.38.refs_26_ = bf16[2,192,1536]{2,1,0:T(8,128)(2,1)} collective-permute-done((bf16[2,192,1536]{2,1,0:T(8,128)(2,1)}, bf16[2,192,1536]{2,1,0:T(8,128)(2,1)}, u32[]{:S(2)}, u32[]{:S(2)}) %collective-permute-start.38) | collective-permute-done | bytes 1179680 | tf_op jit(solution)/shard_map/ppermute | solution.py:661
  746.4 8.7 attend_back.6
  769.7 8.0 attend_back.7
  792.0 7.2 all-to-all-start.16
  845.8 6.9 all-to-all-start.17
  866.7 13.6 %all-to-all-done.17.refs_2_ = bf16[16,96,640]{2,1,0:T(8,128)(2,1)S(1)} async-done(((bf16[16,96,640]{2,1,0:T(8,128)(2,1)}), bf16[16,96,640]{2,1,0:T(8,128)(2,1)S(1)}, u32[]{:S(2)}, u32[]{:S(2)}) %all-to-all-start.17) | async-done | bytes 1966112 | tf_op jit(solution)/shard_map/all_to_all | solution.py:430
  (759 shorter events, 462.9 us)
Async XLA Ops:
  7.2 122.9 %all-gather.2.cloned.1.call-start = ((), (), s32[]{:S(2)}) async-start(), calls=%async_computation.18 | async-start | bytes 11581440 | tf_op jit(solution)/shard_map/all_gather | solution.py:463
  12.6 119.9 %collective-permute-start = (bf16[2,192,1536]{2,1,0:T(8,128)(2,1)}, bf16[2,192,1536]{2,1,0:T(8,128)(2,1)S(1)}, u32[]{:S(2)}, u32[]{:S(2)}) collective-permute-start(bf16[2,192,1536]{2,1,0:T(8,128)(2,1)} %bitcast.83), channel_id=1, source_target_pairs={{0,16},{16,0},{32,48},{48,32},{1,17},{17,1},{33,49},{49,33},{2,18}... | collective-permute-start | bytes 3538952 | tf_op jit(solution)/shard_map/ppermute | solution.py:54
  13.5 118.9 %collective-permute-start.3 = (bf16[2,192,1536]{2,1,0:T(8,128)(2,1)}, bf16[2,192,1536]{2,1,0:T(8,128)(2,1)}, u32[]{:S(2)}, u32[]{:S(2)}) collective-permute-start(bf16[2,192,1536]{2,1,0:T(8,128)(2,1)} %bitcast.92), channel_id=1, source_target_pairs={{0,32},{16,48},{32,0},{48,16},{1,33},{17,49},{33,1},{49,17},{2,34}... | collective-permute-start | bytes 3538952 | tf_op jit(solution)/shard_map/ppermute | solution.py:54
  14.5 118.0 %collective-permute-start.2 = (bf16[2,192,1536]{2,1,0:T(8,128)(2,1)}, bf16[2,192,1536]{2,1,0:T(8,128)(2,1)}, u32[]{:S(2)}, u32[]{:S(2)}) collective-permute-start(bf16[2,192,1536]{2,1,0:T(8,128)(2,1)} %bitcast.93), channel_id=1, source_target_pairs={{0,16},{16,0},{32,48},{48,32},{1,17},{17,1},{33,49},{49,33},{2,18}... | collective-permute-start | bytes 3538952 | tf_op jit(solution)/shard_map/ppermute | solution.py:54
  14.8 117.7 %collective-permute-start.5 = (bf16[2,192,1536]{2,1,0:T(8,128)(2,1)}, bf16[2,192,1536]{2,1,0:T(8,128)(2,1)}, u32[]{:S(2)}, u32[]{:S(2)}) collective-permute-start(bf16[2,192,1536]{2,1,0:T(8,128)(2,1)} %bitcast.102), channel_id=1, source_target_pairs={{0,32},{16,48},{32,0},{48,16},{1,33},{17,49},{33,1},{49,17},{2,34}... | collective-permute-start | bytes 3538952 | tf_op jit(solution)/shard_map/ppermute | solution.py:54
  40.4 92.1 %collective-permute-start.4 = (bf16[2,192,1536]{2,1,0:T(8,128)(2,1)S(1)}, bf16[2,192,1536]{2,1,0:T(8,128)(2,1)}, u32[]{:S(2)}, u32[]{:S(2)}) collective-permute-start(bf16[2,192,1536]{2,1,0:T(8,128)(2,1)S(1)} %bitcast.107), channel_id=1, source_target_pairs={{0,16},{16,0},{32,48},{48,32},{1,17},{17,1},{33,49},{49,33},{2,18}... | collective-permute-start | bytes 3538952 | tf_op jit(solution)/shard_map/ppermute | solution.py:54
  186.9 30.9 %all-to-all-start.2 = ((bf16[16,32,1536]{2,1,0:T(8,128)(2,1)}), bf16[16,32,1536]{2,1,0:T(8,128)(2,1)}, u32[]{:S(2)}, u32[]{:S(2)}) async-start(bf16[16,32,1536]{2,1,0:T(8,128)(2,1)} %copy-done.41), calls=%async_computation.2 | async-start | bytes 3145728 | tf_op jit(solution)/shard_map/all_to_all | solution.py:430
  242.8 46.1 %all-to-all-start.4 = ((bf16[16,32,1536]{2,1,0:T(8,128)(2,1)}), bf16[16,32,1536]{2,1,0:T(8,128)(2,1)}, u32[]{:S(2)}, u32[]{:S(2)}) async-start(bf16[16,32,1536]{2,1,0:T(8,128)(2,1)} %expert_forward.5.refs_5_), calls=%async_computation.4 | async-start | bytes 3145728 | tf_op jit(solution)/shard_map/all_to_all | solution.py:430
  317.3 44.2 %all-to-all-start.3 = ((bf16[16,32,1536]{2,1,0:T(8,128)(2,1)}), bf16[16,32,1536]{2,1,0:T(8,128)(2,1)S(1)}, u32[]{:S(2)}, u32[]{:S(2)}) async-start(bf16[16,32,1536]{2,1,0:T(8,128)(2,1)} %copy-done.126), calls=%async_computation.3 | async-start | bytes 3145728 | tf_op jit(solution)/shard_map/all_to_all | solution.py:430
  389.7 30.0 %all-to-all-start.6 = ((bf16[16,32,1536]{2,1,0:T(8,128)(2,1)}), bf16[16,32,1536]{2,1,0:T(8,128)(2,1)}, u32[]{:S(2)}, u32[]{:S(2)}) async-start(bf16[16,32,1536]{2,1,0:T(8,128)(2,1)} %copy-done.42), calls=%async_computation.6 | async-start | bytes 3145728 | tf_op jit(solution)/shard_map/all_to_all | solution.py:430
  483.4 48.0 %collective-permute-start.31 = (bf16[4,96,1536]{2,1,0:T(8,128)(2,1)}, bf16[4,96,1536]{2,1,0:T(8,128)(2,1)}, u32[]{:S(2)}, u32[]{:S(2)}) collective-permute-start(bf16[4,96,1536]{2,1,0:T(8,128)(2,1)} %pack.1.refs_0_), channel_id=1, source_target_pairs={{0,32},{16,48},{32,0},{48,16},{1,33},{17,49},{33,1},{49,17},{2,34}... | collective-permute-start | bytes 3538952 | tf_op jit(solution)/shard_map/ppermute | solution.py:54
  490.0 53.9 %collective-permute-start.29 = (bf16[2,192,1536]{2,1,0:T(8,128)(2,1)}, bf16[2,192,1536]{2,1,0:T(8,128)(2,1)}, u32[]{:S(2)}, u32[]{:S(2)}) collective-permute-start(bf16[2,192,1536]{2,1,0:T(8,128)(2,1)} %get-tuple-element.214), channel_id=1, source_target_pairs={{0,16},{16,0},{32,48},{48,32},{1,17},{17,1},{33,49},{49,33},{2,18}... | collective-permute-start | bytes 3538952 | tf_op jit(solution)/shard_map/ppermute | solution.py:54
  498.5 56.0 %all-to-all-start.7 = ((bf16[16,32,1536]{2,1,0:T(8,128)(2,1)}), bf16[16,32,1536]{2,1,0:T(8,128)(2,1)S(1)}, u32[]{:S(2)}, u32[]{:S(2)}) async-start(bf16[16,32,1536]{2,1,0:T(8,128)(2,1)} %get-tuple-element.178.refs_5_), calls=%async_computation.7 | async-start | bytes 3145728 | tf_op jit(solution)/shard_map/all_to_all | solution.py:430
  510.4 52.6 %collective-permute-start.28 = (bf16[2,192,1536]{2,1,0:T(8,128)(2,1)}, bf16[2,192,1536]{2,1,0:T(8,128)(2,1)}, u32[]{:S(2)}, u32[]{:S(2)}) collective-permute-start(bf16[2,192,1536]{2,1,0:T(8,128)(2,1)} %get-tuple-element.213), channel_id=1, source_target_pairs={{0,16},{16,0},{32,48},{48,32},{1,17},{17,1},{33,49},{49,33},{2,18}... | collective-permute-start | bytes 3538952 | tf_op jit(solution)/shard_map/ppermute | solution.py:54
  533.5 35.4 %collective-permute-start.30 = (bf16[4,96,1536]{2,1,0:T(8,128)(2,1)}, bf16[4,96,1536]{2,1,0:T(8,128)(2,1)}, u32[]{:S(2)}, u32[]{:S(2)}) collective-permute-start(bf16[4,96,1536]{2,1,0:T(8,128)(2,1)} %pack.1.refs_0_), channel_id=1, source_target_pairs={{0,16},{16,0},{32,48},{48,32},{1,17},{17,1},{33,49},{49,33},{2,18}... | collective-permute-start | bytes 3538952 | tf_op jit(solution)/shard_map/ppermute | solution.py:54
  535.4 33.5 %collective-permute-start.32 = (bf16[4,96,1536]{2,1,0:T(8,128)(2,1)}, bf16[4,96,1536]{2,1,0:T(8,128)(2,1)}, u32[]{:S(2)}, u32[]{:S(2)}) collective-permute-start(bf16[4,96,1536]{2,1,0:T(8,128)(2,1)} %collective-permute-done.31.refs_22_.refs_2_), channel_id=1, source_target_pairs={{0,16},{16,0},{32,48},{48,32},{1,17},{17,1},{33,49},{49,33},{2,18}... | collective-permute-start | bytes 3538952 | tf_op jit(solution)/shard_map/ppermute | solution.py:54
  555.7 48.5 %all-to-all-start.11 = ((bf16[16,32,1536]{2,1,0:T(8,128)(2,1)}), bf16[16,32,1536]{2,1,0:T(8,128)(2,1)S(1)}, u32[]{:S(2)}, u32[]{:S(2)}) async-start(bf16[16,32,1536]{2,1,0:T(8,128)(2,1)} %copy-done.125), calls=%async_computation.11 | async-start | bytes 3145728 | tf_op jit(solution)/shard_map/all_to_all | solution.py:430
  633.1 67.5 %all-to-all-start.13 = ((bf16[16,32,1536]{2,1,0:T(8,128)(2,1)}), bf16[16,32,1536]{2,1,0:T(8,128)(2,1)}, u32[]{:S(2)}, u32[]{:S(2)}) async-start(bf16[16,32,1536]{2,1,0:T(8,128)(2,1)} %get-tuple-element.227), calls=%async_computation.13 | async-start | bytes 3145728 | tf_op jit(solution)/shard_map/all_to_all | solution.py:430
  645.4 50.6 %collective-permute-start.43 = (bf16[2,192,1536]{2,1,0:T(8,128)(2,1)S(1)}, bf16[2,192,1536]{2,1,0:T(8,128)(2,1)S(1)}, u32[]{:S(2)}, u32[]{:S(2)}) collective-permute-start(bf16[2,192,1536]{2,1,0:T(8,128)(2,1)S(1)} %get-tuple-element.248), channel_id=1, source_target_pairs={{0,16},{16,0},{32,48},{48,32},{1,17},{17,1},{33,49},{49,33},{2,18}... | collective-permute-start | bytes 3538952 | tf_op jit(solution)/shard_map/ppermute | solution.py:54
  664.8 44.9 %collective-permute-start.45 = (bf16[2,192,1536]{2,1,0:T(8,128)(2,1)}, bf16[2,192,1536]{2,1,0:T(8,128)(2,1)}, u32[]{:S(2)}, u32[]{:S(2)}) collective-permute-start(bf16[2,192,1536]{2,1,0:T(8,128)(2,1)} %get-tuple-element.250), channel_id=1, source_target_pairs={{0,16},{16,0},{32,48},{48,32},{1,17},{17,1},{33,49},{49,33},{2,18}... | collective-permute-start | bytes 3538952 | tf_op jit(solution)/shard_map/ppermute | solution.py:54
  664.8 50.7 %collective-permute-start.37 = (bf16[2,192,1536]{2,1,0:T(8,128)(2,1)}, bf16[2,192,1536]{2,1,0:T(8,128)(2,1)}, u32[]{:S(2)}, u32[]{:S(2)}) collective-permute-start(bf16[2,192,1536]{2,1,0:T(8,128)(2,1)} %add_convert_fusion.5.refs_18_), channel_id=1, source_target_pairs={{64,96},{80,112},{96,64},{112,80},{65,97},{81,113},{97,65},{113,81... | collective-permute-start | bytes 3538952 | tf_op jit(solution)/shard_map/ppermute | solution.py:661
  668.2 52.9 %collective-permute-start.39 = (bf16[2,192,1536]{2,1,0:T(8,128)(2,1)}, bf16[2,192,1536]{2,1,0:T(8,128)(2,1)}, u32[]{:S(2)}, u32[]{:S(2)}) collective-permute-start(bf16[2,192,1536]{2,1,0:T(8,128)(2,1)} %add_convert_fusion.3.refs_20_), channel_id=1, source_target_pairs={{64,96},{80,112},{96,64},{112,80},{65,97},{81,113},{97,65},{113,81... | collective-permute-start | bytes 3538952 | tf_op jit(solution)/shard_map/ppermute | solution.py:661
  680.8 31.9 %collective-permute-start.44 = (bf16[2,192,1536]{2,1,0:T(8,128)(2,1)}, bf16[2,192,1536]{2,1,0:T(8,128)(2,1)}, u32[]{:S(2)}, u32[]{:S(2)}) collective-permute-start(bf16[2,192,1536]{2,1,0:T(8,128)(2,1)} %get-tuple-element.249), channel_id=1, source_target_pairs={{0,16},{16,0},{32,48},{48,32},{1,17},{17,1},{33,49},{49,33},{2,18}... | collective-permute-start | bytes 3538952 | tf_op jit(solution)/shard_map/ppermute | solution.py:54
  697.0 49.4 %collective-permute-start.38 = (bf16[2,192,1536]{2,1,0:T(8,128)(2,1)}, bf16[2,192,1536]{2,1,0:T(8,128)(2,1)}, u32[]{:S(2)}, u32[]{:S(2)}) collective-permute-start(bf16[2,192,1536]{2,1,0:T(8,128)(2,1)} %add_convert_fusion.4.refs_19_), channel_id=1, source_target_pairs={{64,96},{80,112},{96,64},{112,80},{65,97},{81,113},{97,65},{113,81... | collective-permute-start | bytes 3538952 | tf_op jit(solution)/shard_map/ppermute | solution.py:661
  700.6 64.2 %all-to-all-start.15 = ((bf16[16,32,1536]{2,1,0:T(8,128)(2,1)}), bf16[16,32,1536]{2,1,0:T(8,128)(2,1)}, u32[]{:S(2)}, u32[]{:S(2)}) async-start(bf16[16,32,1536]{2,1,0:T(8,128)(2,1)} %get-tuple-element.229.refs_18_), calls=%async_computation.15 | async-start | bytes 3145728 | tf_op jit(solution)/shard_map/all_to_all | solution.py:430
  792.0 53.8 %all-to-all-start.16 = ((bf16[16,96,384]{2,1,0:T(8,128)(2,1)}), bf16[16,96,384]{2,1,0:T(8,128)(2,1)}, u32[]{:S(2)}, u32[]{:S(2)}) async-start(bf16[16,96,384]{2,1,0:T(8,128)(2,1)} %bitcast.121), calls=%async_computation.16 | async-start | bytes 2359296 | tf_op jit(solution)/shard_map/all_to_all | solution.py:430
  799.2 57.7 %collective-permute-start.68 = (bf16[2,192,1536]{2,1,0:T(8,128)(2,1)}, bf16[2,192,1536]{2,1,0:T(8,128)(2,1)}, u32[]{:S(2)}, u32[]{:S(2)}) collective-permute-start(bf16[2,192,1536]{2,1,0:T(8,128)(2,1)} %copy-done.230), channel_id=1, source_target_pairs={{0,16},{16,0},{32,48},{48,32},{1,17},{17,1},{33,49},{49,33},{2,18}... | collective-permute-start | bytes 3538952 | tf_op jit(solution)/shard_map/ppermute | solution.py:54
  799.9 58.8 %collective-permute-start.69 = (bf16[2,192,1536]{2,1,0:T(8,128)(2,1)S(1)}, bf16[2,192,1536]{2,1,0:T(8,128)(2,1)}, u32[]{:S(2)}, u32[]{:S(2)}) collective-permute-start(bf16[2,192,1536]{2,1,0:T(8,128)(2,1)S(1)} %copy-done.65), channel_id=1, source_target_pairs={{0,32},{16,48},{32,0},{48,16},{1,33},{17,49},{33,1},{49,17},{2,34}... | collective-permute-start | bytes 3538952 | tf_op jit(solution)/shard_map/ppermute | solution.py:661
  832.3 30.4 %collective-permute-start.66 = (bf16[2,192,1536]{2,1,0:T(8,128)(2,1)}, bf16[2,192,1536]{2,1,0:T(8,128)(2,1)}, u32[]{:S(2)}, u32[]{:S(2)}) collective-permute-start(bf16[2,192,1536]{2,1,0:T(8,128)(2,1)} %get-tuple-element.292), channel_id=1, source_target_pairs={{0,16},{16,0},{32,48},{48,32},{1,17},{17,1},{33,49},{49,33},{2,18}... | collective-permute-start | bytes 3538952 | tf_op jit(solution)/shard_map/ppermute | solution.py:54
  845.8 34.5 %all-to-all-start.17 = ((bf16[16,96,640]{2,1,0:T(8,128)(2,1)}), bf16[16,96,640]{2,1,0:T(8,128)(2,1)S(1)}, u32[]{:S(2)}, u32[]{:S(2)}) async-start(bf16[16,96,640]{2,1,0:T(8,128)(2,1)} %bitcast.119), calls=%async_computation.17 | async-start | bytes 3932160 | tf_op jit(solution)/shard_map/all_to_all | solution.py:430
  855.1 32.6 %collective-permute-start.64 = (bf16[2,192,1536]{2,1,0:T(8,128)(2,1)}, bf16[2,192,1536]{2,1,0:T(8,128)(2,1)}, u32[]{:S(2)}, u32[]{:S(2)}) collective-permute-start(bf16[2,192,1536]{2,1,0:T(8,128)(2,1)} %get-tuple-element.291), channel_id=1, source_target_pairs={{0,16},{16,0},{32,48},{48,32},{1,17},{17,1},{33,49},{49,33},{2,18}... | collective-permute-start | bytes 3538952 | tf_op jit(solution)/shard_map/ppermute | solution.py:54
  856.9 30.9 %collective-permute-start.65 = (bf16[2,192,1536]{2,1,0:T(8,128)(2,1)}, bf16[2,192,1536]{2,1,0:T(8,128)(2,1)}, u32[]{:S(2)}, u32[]{:S(2)}) collective-permute-start(bf16[2,192,1536]{2,1,0:T(8,128)(2,1)} %add_convert_fusion.1.refs_19_), channel_id=1, source_target_pairs={{0,32},{16,48},{32,0},{48,16},{1,33},{17,49},{33,1},{49,17},{2,34}... | collective-permute-start | bytes 3538952 | tf_op jit(solution)/shard_map/ppermute | solution.py:661
  (309 other events, 3220.3 us)
Sparse Core Ops, SparseCore 0:
  11.7 118.3 all-gather.1

commit v3 on v2

--- a/solution.py
+++ b/solution.py
@@ -120,11 +120,22 @@
                 pair[:, begin - width : begin - width + HEAD_DIM] = head.astype(BF)
 
 
+def scaled_rows(dispatch, gates, low):
+    slots = dispatch.shape[0]
+    own = lax.broadcasted_iota(jnp.int32, (slots, LANES), 0) // ROOMS
+    here = own == lax.broadcasted_iota(jnp.int32, (slots, LANES), 1)
+    scale = jnp.sum(jnp.where(here, dot(dispatch, gates.astype(BF)), 0.0), -1, keepdims=True)
+    return (dot(dispatch, low) * scale).astype(BF)
+
+
 def attend(
-    stream, query, pair0, pair1, pair2, pair3, bias, gain, chosen, dispatch, dense, mixed, middle,
-    normed_ffn, gates, outgoing, probs, weights, router, sems,
+    stream, query, pair0, pair1, pair2, pair3, bias, gain, chosen, dispatch, *rest,
 ):
+    targets, rest = rest[:-10], rest[-10:]
+    dense, mixed, middle, normed_ffn, gates, outgoing, probs, weights, router, sems = rest
     width = stream.shape[1]
+    block = (outgoing.shape[0], -1, width)
+    per = dispatch.shape[0] // outgoing.shape[0]
     at = dense.shape[1] - width - LANES
     copies = [
         pltpu.make_async_copy(dense.at[:, pl.ds(at + LANES, width)], weights, sems.at[0]),
@@ -158,8 +169,11 @@
     taken = chosen[...] > 0
     logits = jnp.where(taken, dot(low, router[...]), -1e30)
     expo = jnp.where(taken, jnp.exp(logits - jnp.max(logits, -1, keepdims=True)), 0.0)
-    gates[...] = expo / jnp.sum(expo, -1, keepdims=True)
-    outgoing[...] = dot(dispatch[...], low).astype(BF).reshape(outgoing.shape)
+    share = expo / jnp.sum(expo, -1, keepdims=True)
+    gates[...] = share
+    outgoing[:, :per, :] = dot(dispatch[...], low).astype(BF).reshape(block)
+    if targets:
+        outgoing[:, per:, :] = scaled_rows(dispatch[...], share, targets[0][...]).reshape(block)
 
 
 def fetch(shards, weights, sems):
@@ -191,16 +205,19 @@
         copy.wait()
 
 
-def rows_of(value, j):
+def rows_of(value, j, begin=0):
     columns, unused, width = value.shape
-    return value[:, j * ROOMS : (j + 1) * ROOMS, :].reshape(columns * ROOMS, width)
-
-
-def expert_forward(keep, arrived, *refs):
+    at = begin + j * ROOMS
+    return value[:, at : at + ROOMS, :].reshape(columns * ROOMS, width)
+
+
+def expert_forward(both, arrived, *refs):
     shards = [refs[4 * k : 4 * k + 4] for k in range(3)]
     outs, weights, sems = refs[12:-2], refs[-2], refs[-1]
     copies = fetch(shards, weights, sems)
+    per = weights.shape[1] * ROOMS
     for j in range(weights.shape[1]):
+        at = j * ROOMS
         rows = rows_of(arrived, j)
         done_with(copies[j][0])
         gate = dot(rows, weights[0, j], (1, 1))
@@ -210,22 +227,36 @@
         bend = jnp.tanh(0.7978845608028654 * gate * (1.0 + 0.044715 * square))
         active = 0.5 * gate * (1.0 + bend)
         hidden = (active * lifted).astype(BF)
-        if keep:
+        done_with(copies[j][2])
+        made = dot(hidden, weights[2, j]).astype(BF)
+        outs[0][:, at : at + ROOMS, :] = made.reshape(-1, ROOMS, made.shape[1])
+        if both:
             slope = 0.5 * (1.0 + bend) + 0.5 * gate * (1.0 - bend * bend) * (
                 0.7978845608028654 * (1.0 + 3 * 0.044715 * square)
             )
+            bent = slope * lifted
             outs[1][j] = hidden
             outs[2][j] = active.astype(BF)
-            outs[3][j] = (slope * lifted).astype(BF)
-        done_with(copies[j][2])
-        made = dot(hidden, weights[2, j]).astype(BF)
-        outs[0][:, j * ROOMS : (j + 1) * ROOMS, :] = made.reshape(-1, ROOMS, made.shape[1])
+            outs[3][j] = bent.astype(BF)
+            hidden_grads = dot(rows_of(arrived, j, per), weights[2, j], (1, 1))
+            gate_part = (hidden_grads * bent).astype(BF)
+            lifted_part = (hidden_grads * active).astype(BF)
+            outs[4][j] = gate_part
+            outs[5][j] = lifted_part
+            back = dot(gate_part, weights[0, j]) + dot(lifted_part, weights[1, j])
+            outs[0][:, per + at : per + at + ROOMS, :] = back.astype(BF).reshape(
+                -1, ROOMS, back.shape[1]
+            )
+
+
+def first_rows(returned, places):
+    columns, unused, width = returned.shape
+    return returned[:, : places.shape[1] // columns, :].reshape(-1, width)
 
 
 def combine(returned, middle, gates, spread, places, result, low):
     weights = dot(gates[...].astype(BF), spread[...]) * places[...].astype(F32)
-    rows = returned[...].reshape(-1, returned.shape[2])
-    done = middle[...] + dot(weights.astype(BF), rows)
+    done = middle[...] + dot(weights.astype(BF), first_rows(returned, places))
     result[...] = done
     low[...] = done.astype(BF)
 
@@ -233,13 +264,7 @@
 def send_grads(flag, came, target, gates, dispatch, grad, outgoing):
     low = jnp.where(flag[0] > 0, came[...], target[...])
     grad[...] = low
-    slots = dispatch.shape[0]
-    own = lax.broadcasted_iota(jnp.int32, (slots, LANES), 0) // ROOMS
-    here = own == lax.broadcasted_iota(jnp.int32, (slots, LANES), 1)
-    scale = jnp.sum(
-        jnp.where(here, dot(dispatch[...], gates[...].astype(BF)), 0.0), -1, keepdims=True
-    )
-    outgoing[...] = (dot(dispatch[...], low) * scale).astype(BF).reshape(outgoing.shape)
+    outgoing[...] = scaled_rows(dispatch[...], gates[...], low).reshape(outgoing.shape)
 
 
 def expert_backward(arrived, active, bent, *refs):
@@ -274,13 +299,15 @@
     ]
     for copy in copies:
         copy.start()
-    inner = dot(grad[...], returned[...].reshape(-1, width), (1, 1)) * places[...].astype(F32)
+    inner = dot(grad[...], first_rows(returned, places), (1, 1)) * places[...].astype(F32)
     gate_grads = dot(inner.astype(BF), spread[...], (1, 1))
     chances = gates[...]
     logit_grads = (
         chances * (gate_grads - jnp.sum(chances * gate_grads, -1, keepdims=True))
     ).astype(BF)
-    ffn_grads = dot(places[...], token_grads[...].reshape(-1, width))
+    per = places.shape[1] // returned.shape[0]
+    came = token_grads[:, token_grads.shape[1] - per :, :].reshape(-1, width)
+    ffn_grads = dot(places[...], came)
     copies[0].wait()
     ffn_grads = ffn_grads + dot(logit_grads, router[...], (1, 1))
     part, total = norm_back(ffn_grads, middle[...], gain[...])
@@ -359,13 +386,13 @@
     low[...] = done.astype(BF)
 
 
-def expert_weight_grads(half, left0, left1, right0, right1, first, second):
+def expert_weight_grads(half, begin, left0, left1, right0, right1, first, second):
     size = first.shape[1]
     wide = 2 * size
     for j in range(first.shape[0]):
-        total = dot(left0[j, :, half * wide : (half + 1) * wide], rows_of(right0, j), (0, 0))
+        total = dot(left0[j, :, half * wide : (half + 1) * wide], rows_of(right0, j, begin), (0, 0))
         total = total + dot(
-            left1[j, :, half * wide : (half + 1) * wide], rows_of(right1, j), (0, 0)
+            left1[j, :, half * wide : (half + 1) * wide], rows_of(right1, j, begin), (0, 0)
         )
         first[j] = total[:size].astype(BF)
         second[j] = total[size:].astype(BF)
@@ -465,13 +492,20 @@
     gain_a = small[:, experts].astype(F32)[None, :]
     gain_f = small[:, experts + 1].astype(F32)[None, :]
 
-    def shards_of(own):
-        two = swapped(own, 2)
-        return own, swapped(own, 1), two, swapped(two, 1)
-
-    gate_shards, up_shards, down_shards = (
-        shards_of(w_gate[0]), shards_of(w_up[0]), shards_of(w_down[0])
-    )
+    def across(value, only):
+        lines = [(only * rows + r, only * rows + (r ^ 2)) for r in range(rows)]
+        return lax.ppermute(value, ("section", "row"), lines)
+
+    owns = (w_gate[0], w_up[0], w_down[0])
+    ones = [swapped(own, 1) for own in owns]
+    early_twos = [across(own, 0) for own in owns]
+    early_shards = [
+        (own, one, two, swapped(two, 1)) for own, one, two in zip(owns, ones, early_twos)
+    ]
+    twos = [two + across(own, 1) for own, two in zip(owns, early_twos)]
+    gate_shards, up_shards, down_shards = [
+        (own, one, two, swapped(two, 1)) for own, one, two in zip(owns, ones, twos)
+    ]
 
     lane = jnp.arange(LANES, dtype=jnp.int32)
     half = HEAD_DIM // 2
@@ -526,22 +560,28 @@
     score_flops = 2 * heads * tokens * length * HEAD_DIM
     expert_flops = 2 * slots * hidden_width * width
 
-    def forward(came, entering, keep, waits=()):
-        projected = [
-            call(
-                project, (token_wide, token_low, token_low, pair_like),
-                (came[m], entering[m], gain_a, cosine, sine), qkv_flops, (dense,), qkv_scratch,
-                scalars=(second,), waits=() if m else waits,
+    per = slots // columns
+    double_like = like((columns, 2 * per, width), BF)
+
+    def forward(came, entering, shards, targets, waits):
+        projected, pairs = [], []
+        for m in pieces:
+            projected.append(
+                call(
+                    project, (token_wide, token_low, token_low, pair_like),
+                    (came[m], entering[m], gain_a, cosine, sine), qkv_flops, (dense,), qkv_scratch,
+                    scalars=(second,), waits=(*waits[m], *(p[0] for p in projected)),
+                )
             )
-            for m in pieces
-        ]
-        pairs = [[p[3]] + [swapped(p[3], s) for s in steps[1:]] for p in projected]
+            pair = projected[m][3]
+            pairs.append([pair] + [swapped(pair, s) for s in steps[1:]])
         attended = [
             call(
                 attend,
-                (token_low, token_wide, token_low, like((tokens, LANES), F32), block_like, probs_like),
+                (token_low, token_wide, token_low, like((tokens, LANES), F32),
+                 double_like if targets else block_like, probs_like),
                 (projected[m][0], projected[m][2], *pairs[m], biases[m], gain_f, chosens[m],
-                 dispatches[m]),
+                 dispatches[m], *targets[m : m + 1]),
                 out_flops + 2 * score_flops, (dense,), out_scratch,
             )
             for m in pieces
@@ -549,9 +589,9 @@
         arrived = [over_columns(a[4]) for a in attended]
         applied = [
             call(
-                functools.partial(expert_forward, keep),
-                (block_like,) + (kept_like,) * (3 if keep else 0), (arrived[m],), 3 * expert_flops,
-                (*gate_shards, *up_shards, *down_shards), expert_scratch,
+                functools.partial(expert_forward, bool(targets)),
+                (double_like,) + (kept_like,) * 5 if targets else (block_like,), (arrived[m],),
+                (6 if targets else 3) * expert_flops, shards, expert_scratch,
                 waits=() if m else (attended[1][4],),
             )
             for m in pieces
@@ -567,104 +607,56 @@
         ]
         return projected, pairs, attended, arrived, applied, returned, results
 
-    def backward(came, targets, kept, lefts, keep, waits):
-        projected, pairs, attended, entered, applied, returned, results = kept
-        sent = [
+    def far_and_near(lefts, rights, begins, side):
+        return [
             call(
-                send_grads, (token_low, block_like),
-                (came[m], targets[m], attended[m][3], dispatches[m]),
-                2 * slots * tokens * width, scalars=(1 - second,),
+                functools.partial(expert_weight_grads, side, begin),
+                (like((per_column, hidden_width // 4, width), BF),) * 2, (*left, *right),
+                expert_flops,
             )
-            for m in pieces
+            for left, right, begin in zip(lefts, rights, begins)
         ]
-        arrived = [over_columns(s[1]) for s in sent]
-        moved = [
-            call(
-                expert_backward, (block_like, kept_like, kept_like),
-                (arrived[m], applied[m][2], applied[m][3]), 3 * expert_flops,
-                (*down_shards, *gate_shards, *up_shards), expert_scratch,
-                waits=() if m else (sent[1][1],),
-            )
-            for m in pieces
-        ]
-        back = [over_columns(a[0]) for a in moved]
-
-        def halves(side):
-            lefts = ([a[1] for a in applied], [a[1] for a in moved], [a[2] for a in moved])
-            rights = (arrived, entered, entered)
-            return [
-                call(
-                    functools.partial(expert_weight_grads, side),
-                    (like((per_column, hidden_width // 4, width), BF),) * 2, (*left, *right),
-                    expert_flops,
-                )
-                for left, right in zip(lefts, rights)
-            ]
-
-        far = halves(1)
-        near = halves(0) if keep else []
-        between = [p[0].astype(F32) + swapped(p[1], 1).astype(F32) for p in far]
-        between = [b.astype(BF) for b in between]
-        first_waits = [moved[1][0], *(p[0] for p in far), *(p[0] for p in near)]
-        inner, parts, outer, branches = [], [], [], []
-        for m in pieces:
-            inner.append(
-                call(
-                    functools.partial(attend_back, keep),
-                    (token_wide, token_low) + (pair_like,) * 4
-                    + ((like((tokens, LANES), BF), sums_like)
-                       + (like((tokens, share), BF),) * rows if keep else ()),
-                    (back[m], returned[m], attended[m][3], spread, places[m], attended[m][1], gain_f,
-                     sent[m][0], projected[m][2], *pairs[m], attended[m][5], cosine, sine),
-                    out_flops + 4 * score_flops, (dense,),
-                    [pltpu.VMEM((tokens, width), BF)] + out_scratch,
-                    scalars=(here,),
-                    waits=(*between, *waits[1]) if m else (*first_waits, *waits[0]),
-                )
-            )
-        parts = [[a[2]] + [swapped(a[2 + s], s) for s in steps[1:]] for a in inner]
-        if keep:
-            branches = [[a[8]] + [swapped(a[8 + s], s) for s in steps[1:]] for a in inner]
-            o_grads = call(
-                out_grads, (like((width, share), BF),),
-                (*lefts, *[b[s] for s in steps for b in branches]),
-                2 * width * length * micro * share,
-            )[0]
-        outer = [
-            call(
-                functools.partial(project_back, keep),
-                (token_wide, token_low)
-                + ((sums_like,) + (like((tokens, qkv_width // rows), BF),) * rows if keep else ()),
-                (*parts[m], inner[m][1], projected[m][0], gain_a, inner[m][0], cosine, sine),
-                qkv_flops, (dense,), [pltpu.VMEM((tokens, qkv_width), BF)] + qkv_scratch,
-                scalars=(here,), waits=(o_grads,) if m and keep else (),
-            )
-            for m in pieces
-        ]
-        if not keep:
-            return outer, between
-        backs = [[o[3]] + [swapped(o[3 + s], s) for s in steps[1:]] for o in outer]
-        w_grads = call(
-            qkv_grads, (like((width, qkv_width // rows + LANES), BF),),
-            (*lefts, *[b[s] for s in steps for b in backs], *[a[2] for a in attended],
-             *[a[6] for a in inner], *[o[2] for o in outer], *[a[7] for a in inner]),
-            2 * width * length * micro * qkv_width // rows,
-        )[0]
-        return outer, between, near, o_grads, w_grads
+
+    def merged(halves):
+        return [(h[0].astype(F32) + swapped(h[1], 1).astype(F32)).astype(BF) for h in halves]
+
+    def attention_back(keep, m, grad, token_grads, waits):
+        return call(
+            functools.partial(attend_back, keep),
+            (token_wide, token_low) + (pair_like,) * 4
+            + ((like((tokens, LANES), BF), sums_like) + (like((tokens, share), BF),) * rows
+               if keep else ()),
+            (token_grads, returned[m], attended[m][3], spread, places[m], attended[m][1], gain_f,
+             grad, projected[m][2], *pairs[m], attended[m][5], cosine, sine),
+            out_flops + 4 * score_flops, (dense,), [pltpu.VMEM((tokens, width), BF)] + out_scratch,
+            scalars=(here,), waits=waits,
+        )
+
+    def projection_back(keep, m, inner, waits):
+        parts = [inner[2]] + [swapped(inner[2 + s], s) for s in steps[1:]]
+        return call(
+            functools.partial(project_back, keep),
+            (token_wide, token_low)
+            + ((sums_like,) + (like((tokens, qkv_width // rows), BF),) * rows if keep else ()),
+            (*parts, inner[1], projected[m][0], gain_a, inner[0], cosine, sine),
+            qkv_flops, (dense,), [pltpu.VMEM((tokens, qkv_width), BF)] + qkv_scratch,
+            scalars=(here,), waits=waits,
+        )
 
     def by_columns(value):
         cut = value.reshape(rows, columns, shard, value.shape[1]).transpose(1, 0, 2, 3)
         return over_columns(cut.reshape(columns, rows * shard, value.shape[1]))
 
-    def across(value, only):
-        lines = [(only * rows + r, only * rows + (r ^ 2)) for r in range(rows)]
-        return lax.ppermute(value, ("section", "row"), lines)
-
     entering = [inputs[m, 0] for m in pieces]
-    moving = [g[k] for g in (gate_shards, up_shards, down_shards) for k in (1, 2)]
-    results = forward(entering, entering, False, moving)[6]
+    targets = [cotangent[m, 0] for m in pieces]
+    shards = [one for line in early_shards for one in line]
+    here_by_now = [one for line in early_shards for one in line[1:3]]
+    results = forward(entering, entering, shards, (), (here_by_now, ()))[6]
     came = [lax.ppermute(r[1], "section", [(0, 1)]) for r in results]
-    kept = forward(came, entering, True)
+
+    shards = (*gate_shards, *up_shards, *down_shards)
+    here_by_now = [line[3] for line in (gate_shards, up_shards, down_shards)]
+    kept = forward(came, entering, shards, targets, ((), here_by_now))
     projected, pairs, attended, arrived, applied, returned, results = kept
     left = call(
         pack, (like((2 * micro, tokens, width), BF),),
@@ -672,16 +664,70 @@
     )[0]
     two = swapped(left, 2)
     lefts = [left, swapped(left, 1), two, swapped(two, 1)]
-
-    targets = [cotangent[m, 0] for m in pieces]
-    outer, between = backward(targets, targets, kept, lefts, False, ((), lefts[1:]))
+    hidden = [a[1] for a in applied]
+
+    far = far_and_near(
+        (hidden, [a[4] for a in applied], [a[5] for a in applied]), (arrived,) * 3, (per, 0, 0), 1
+    )
+    between = merged(far)
+    inner, outer = [], []
+    for m in pieces:
+        waits = (*between, *lefts[1:], outer[0][0]) if m else (applied[1][0], *(f[0] for f in far))
+        inner.append(attention_back(False, m, targets[m], returned[m], waits))
+        outer.append(projection_back(False, m, inner[m], ()))
     came = [lax.ppermute(o[1], "section", [(1, 0)]) for o in outer]
     early = [across(b, 1) for b in between]
+
+    sent = [
+        call(
+            send_grads, (token_low, block_like),
+            (came[m], targets[m], attended[m][3], dispatches[m]),
+            2 * slots * tokens * width, scalars=(1 - second,),
+        )
+        for m in pieces
+    ]
+    arrived_grads = [over_columns(s[1]) for s in sent]
+    moved = [
+        call(
+            expert_backward, (block_like, kept_like, kept_like),
+            (arrived_grads[m], applied[m][2], applied[m][3]), 3 * expert_flops,
+            (*down_shards, *gate_shards, *up_shards), expert_scratch,
+            waits=() if m else (sent[1][1],),
+        )
+        for m in pieces
+    ]
+    back = [over_columns(a[0]) for a in moved]
+    operands = (
+        (hidden, [a[1] for a in moved], [a[2] for a in moved]), (arrived_grads, arrived, arrived),
+        (0, 0, 0),
+    )
+    far = far_and_near(*operands, 1)
+    between = merged(far)
+    late = [across(b, 0) for b in between]
+    near = far_and_near(*operands, 0)
     done = [r[0] for r in results]
-    outer, between, near, o_grads, w_grads = backward(
-        came, targets, kept, lefts, True, ((*early, *done), ())
-    )
-    late = [across(b, 0) for b in between]
+
+    inner = [attention_back(
+        True, 0, sent[0][0], back[0], (moved[1][0], *(p[0] for p in far), *early, *done)
+    )]
+    outer = [projection_back(True, 0, inner[0], ())]
+    inner.append(attention_back(
+        True, 1, sent[1][0], back[1], (*between, outer[0][0], *(p[0] for p in near))
+    ))
+    branches = [[a[8]] + [swapped(a[8 + s], s) for s in steps[1:]] for a in inner]
+    o_grads = call(
+        out_grads, (like((width, share), BF),),
+        (*lefts, *[b[s] for s in steps for b in branches]), 2 * width * length * micro * share,
+        waits=late,
+    )[0]
+    outer.append(projection_back(True, 1, inner[1], (o_grads,)))
+    backs = [[o[3]] + [swapped(o[3 + s], s) for s in steps[1:]] for o in outer]
+    w_grads = call(
+        qkv_grads, (like((width, qkv_width // rows + LANES), BF),),
+        (*lefts, *[b[s] for s in steps for b in backs], *[a[2] for a in attended],
+         *[a[6] for a in inner], *[o[2] for o in outer], *[a[7] for a in inner]),
+        2 * width * length * micro * qkv_width // rows,
+    )[0]
     expert_grads = [
         n[0].astype(F32) + swapped(n[1], 1).astype(F32) + e.astype(F32) + l.astype(F32)
         for n, e, l in zip(near, early, late)

time: 914 us -> 963 us (1.054)
  waiting for transfers between devices: 227 us -> 350 us
  blocking collectives: 82.6 us -> 0 us
  starting transfers between devices: 201 us -> 211 us
    all_to_all x3 -> x0, blocking collectives: 82.6 us -> none  [over_columns(): return lax.all_to_all(value, 'col', split_axis=0, concat_axis=0, tiled=True)]
    ppermute x6 -> x12, waiting for transfers between devices: 30.8 us -> 104 us  [across(): return lax.ppermute(value, ('section', 'row'), lines)]
    all_to_all x15 -> x14, waiting for transfers between devices: 45.4 us -> 77.4 us  [over_columns(): return lax.all_to_all(value, 'col', split_axis=0, concat_axis=0, tiled=True)]
    ppermute x2, waiting for transfers between devices: 13.6 us -> 34 us  [on_device(): came = [lax.ppermute(r[1], 'section', [(0, 1)]) for r in results]]
    ppermute x6 -> x12, starting transfers between devices: 15.8 us -> 30.3 us  [across(): return lax.ppermute(value, ('section', 'row'), lines)]
    ppermute x60, starting transfers between devices: 89.5 us -> 79.3 us  [swapped(): return lax.ppermute(value, 'row', [(r, r ^ step) for r in range(rows)])]
    pallas_call x46 -> x42, Pallas kernels: 229 us -> 236 us  [call(): pl.pallas_call(run, out_shape=tuple(outs), in_specs=[pl.BlockSpec(memory_...]
    all_to_all x15 -> x14, starting transfers between devices: 86.5 us -> 92.4 us  [over_columns(): return lax.all_to_all(value, 'col', split_axis=0, concat_axis=0, tiled=True)]
  transfers between devices with their start and end apart: 86 -> 91, of which waited for: 32 -> 39; matrix products, arithmetic and copies ran while one was open for 7% -> 6% of each run, Pallas kernels for 24% -> 22%
where the time goes in v3:
time: 963 us; the launch traced here: 952 us
  waiting for transfers between devices  350 us (36%)
  Pallas kernels  236 us (25%)
  starting transfers between devices  211 us (22%)
  local copies, waits for them, and re-layouts  95.9 us (10%)
  other arithmetic  41.1 us (4%)
  between operations  17.2 us (2%)
    pallas_call x42, Pallas kernels, call(): pl.pallas_call(run, out_shape=tuple(outs), in_specs=[pl.BlockSpec(memory_...  236 us
    ppermute x12, waiting for transfers between devices, across(): return lax.ppermute(value, ('section', 'row'), lines)  104 us
    all_to_all x14, starting transfers between devices, over_columns(): return lax.all_to_all(value, 'col', split_axis=0, concat_axis=0, tiled=True)  92.4 us
    all_gather x1, waiting for transfers between devices, on_device(): dense = lax.all_gather(dense, ('row', 'col'), axis=0, tiled=True)  82.6 us
    unnamed x518, local copies, waits for them, and re-layouts  80.1 us
    ppermute x60, starting transfers between devices, swapped(): return lax.ppermute(value, 'row', [(r, r ^ step) for r in range(rows)])  79.3 us
    all_to_all x14, waiting for transfers between devices, over_columns(): return lax.all_to_all(value, 'col', split_axis=0, concat_axis=0, tiled=True)  77.4 us
    ppermute x60, waiting for transfers between devices, swapped(): return lax.ppermute(value, 'row', [(r, r ^ step) for r in range(rows)])  41.5 us
  transfers between devices with their start and end apart: 91, of which 39 were waited for; matrix products, arithmetic and copies ran while one was open for 6% of the time, Pallas kernels for 22%

profile of v3, /device:TPU:9, one launch (start us, length us, event | category | flops | bytes accessed | tf_op | source)
XLA Modules:
  0.0 951.9 jit_solution(10814187777481614956)
XLA Ops:
  26.5 82.6 %all-gather.2.cloned.1.call-done.refs_6_.refs_10_.refs_11_.refs_17_ = bf16[1536,3712]{1,0:T(8,128)(2,1)} async-done(((bf16[24,3712]{1,0:T(8,128)(2,1)}), bf16[1536,3712]{1,0:T(8,128)(2,1)}) %all-gather.2.cloned.1.call-update) | async-done | bytes 11403280 | tf_op jit(solution)/shard_map/all_gather | solution.py:490
  166.2 6.8 all-to-all-start.2
  173.0 9.9 %expert_forward.4 = bf16[16,32,1536]{2,1,0:T(8,128)(2,1)} custom-call(bf16[16,32,1536]{2,1,0:T(8,128)(2,1)} %all-to-all-done.refs_0_, bf16[2,192,1536]{2,1,0:T(8,128)(2,1)S(1)} %bitcast.86, bf16[2,192,1536]{2,1,0:T(8,128)(2,1)S(1)} %collective-permute-done.refs_7_.refs_2_.refs_8_, bf16[2,192,1536]{2,1,0:T(8,128)(2,1)} %collective-permute-done.1.refs_8_.refs_3_, ...), custom_call_target="tpu_custom_call" | custom-call | flops 3623878656 | bytes 17301504 | tf_op jit(solution)/shard_map/expert_forward/pallas_call | solution.py:36
  182.9 10.6 %all-to-all-done.2.refs_0_ = bf16[16,32,1536]{2,1,0:T(8,128)(2,1)} async-done(((bf16[16,32,1536]{2,1,0:T(8,128)(2,1)}), bf16[16,32,1536]{2,1,0:T(8,128)(2,1)}, u32[]{:S(2)}, u32[]{:S(2)}) %all-to-all-start.2) | async-done | bytes 1572896 | tf_op jit(solution)/shard_map/all_to_all | solution.py:457
  198.4 9.9 %expert_forward.5.refs_5_ = bf16[16,32,1536]{2,1,0:T(8,128)(2,1)} custom-call(bf16[16,32,1536]{2,1,0:T(8,128)(2,1)} %all-to-all-done.2.refs_0_, bf16[2,192,1536]{2,1,0:T(8,128)(2,1)S(1)} %bitcast.87, bf16[2,192,1536]{2,1,0:T(8,128)(2,1)S(1)} %collective-permute-done.refs_7_.refs_2_.refs_8_, bf16[2,192,1536]{2,1,0:T(8,128)(2,1)} %collective-permute-done.1.refs_8_.refs_3_, ...), custom_call_target="tpu_custom_call" | custom-call | flops 3623878656 | bytes 17301504 | tf_op jit(solution)/shard_map/expert_forward/pallas_call | solution.py:36
  208.4 9.1 all-to-all-done.1.refs_0_
  230.2 25.1 %collective-permute-done.15.refs_1_ = bf16[96,1536]{1,0:T(8,128)(2,1)S(1)} collective-permute-done((bf16[96,1536]{1,0:T(8,128)(2,1)S(1)}, bf16[96,1536]{1,0:T(8,128)(2,1)S(1)}, u32[]{:S(2)}, u32[]{:S(2)}) %collective-permute-start.15) | collective-permute-done | bytes 294944 | tf_op jit(solution)/shard_map/ppermute | solution.py:655
  271.4 7.1 attend.6
  285.0 7.0 all-to-all-start.3
  302.3 20.4 %collective-permute-done.19 = bf16[2,192,1536]{2,1,0:T(8,128)(2,1)S(1)} collective-permute-done((bf16[2,192,1536]{2,1,0:T(8,128)(2,1)S(1)}, bf16[2,192,1536]{2,1,0:T(8,128)(2,1)S(1)}, u32[]{:S(2)}, u32[]{:S(2)}) %collective-permute-start.19) | collective-permute-done | bytes 1179680 | tf_op jit(solution)/shard_map/ppermute | solution.py:497
  326.1 21.7 %collective-permute-done.21 = bf16[2,192,1536]{2,1,0:T(8,128)(2,1)S(1)} collective-permute-done((bf16[2,192,1536]{2,1,0:T(8,128)(2,1)S(1)}, bf16[2,192,1536]{2,1,0:T(8,128)(2,1)S(1)}, u32[]{:S(2)}, u32[]{:S(2)}) %collective-permute-start.21) | collective-permute-done | bytes 1179680 | tf_op jit(solution)/shard_map/ppermute | solution.py:497
  351.5 21.7 %collective-permute-done.23 = bf16[2,192,1536]{2,1,0:T(8,128)(2,1)S(1)} collective-permute-done((bf16[2,192,1536]{2,1,0:T(8,128)(2,1)S(1)}, bf16[2,192,1536]{2,1,0:T(8,128)(2,1)S(1)}, u32[]{:S(2)}, u32[]{:S(2)}) %collective-permute-start.23) | collective-permute-done | bytes 1179680 | tf_op jit(solution)/shard_map/ppermute | solution.py:497
  380.3 8.9 collective-permute-done.25.refs_1_
  402.3 7.1 attend.7
  424.1 16.2 %expert_forward.6 = (bf16[16,64,1536]{2,1,0:T(8,128)(2,1)}, bf16[2,256,768]{2,1,0:T(8,128)(2,1)S(1)}, bf16[2,256,768]{2,1,0:T(8,128)(2,1)S(1)}, bf16[2,256,768]{...) custom-call(bf16[16,64,1536]{2,1,0:T(8,128)(2,1)} %all-to-all-done.3.refs_0_.refs_2_, ...), custom_call_target="tpu_custom_call" | custom-call | flops 7247757312 | bytes 24379392 | tf_op jit(solution)/shard_map/expert_forward/pallas_call | solution.py:36
  444.7 20.0 %all-to-all-done.6.refs_0_.refs_3_ = bf16[16,64,1536]{2,1,0:T(8,128)(2,1)} async-done(((bf16[16,64,1536]{2,1,0:T(8,128)(2,1)}), bf16[16,64,1536]{2,1,0:T(8,128)(2,1)}, u32[]{:S(2)}, u32[]{:S(2)}) %all-to-all-start.6) | async-done | bytes 3145760 | tf_op jit(solution)/shard_map/all_to_all | solution.py:457
  464.7 11.3 %all-to-all-start.5 = ((bf16[16,64,1536]{2,1,0:T(8,128)(2,1)}), bf16[16,64,1536]{2,1,0:T(8,128)(2,1)S(1)}, u32[]{:S(2)}, u32[]{:S(2)}) async-start(bf16[16,64,1536]{2,1,0:T(8,128)(2,1)} %get-tuple-element.170), calls=%async_computation.5 | async-start | bytes 6291456 | tf_op jit(solution)/shard_map/all_to_all | solution.py:457
  477.3 16.1 %expert_forward.7 = (bf16[16,64,1536]{2,1,0:T(8,128)(2,1)}, bf16[2,256,768]{2,1,0:T(8,128)(2,1)S(1)}, bf16[2,256,768]{2,1,0:T(8,128)(2,1)S(1)}, bf16[2,256,768]{...) custom-call(bf16[16,64,1536]{2,1,0:T(8,128)(2,1)} %all-to-all-done.6.refs_0_.refs_3_, ...), custom_call_target="tpu_custom_call" | custom-call | flops 7247757312 | bytes 24379392 | tf_op jit(solution)/shard_map/expert_forward/pallas_call | solution.py:36
  497.8 16.5 %all-to-all-done.5.refs_0_.refs_1_.refs_2_ = bf16[16,64,1536]{2,1,0:T(8,128)(2,1)S(1)} async-done(((bf16[16,64,1536]{2,1,0:T(8,128)(2,1)}), bf16[16,64,1536]{2,1,0:T(8,128)(2,1)S(1)}, u32[]{:S(2)}, u32[]{:S(2)}) %all-to-all-start.5) | async-done | bytes 3145760 | tf_op jit(solution)/shard_map/all_to_all | solution.py:457
  548.8 9.4 attend_back.4
  582.0 6.8 all-to-all-start.8
  594.9 9.0 attend_back.5
  632.5 7.4 all-to-all-start.10
  643.4 10.1 %expert_backward.2 = (bf16[16,32,1536]{2,1,0:T(8,128)(2,1)}, bf16[2,256,768]{2,1,0:T(8,128)(2,1)S(1)}, bf16[2,256,768]{2,1,0:T(8,128)(2,1)S(1)}) custom-call(bf16[16,32,1536]{2,1,0:T(8,128)(2,1)} %copy-done.6, bf16[2,256,768]{2,1,0:T(8,128)(2,1)S(1)} %copy-done.162, bf16[2,256,768]{2,1,0:T(8,128)(2,1)S(1)} %copy-done.164, ...), custom_call_target="tpu_custom_call" | custom-call | flops 3623878656 | bytes 20447232 | tf_op jit(solution)/shard_map/expert_backward/pallas_call | solution.py:36
  662.6 10.1 %expert_backward.3 = (bf16[16,32,1536]{2,1,0:T(8,128)(2,1)}, bf16[2,256,768]{2,1,0:T(8,128)(2,1)S(1)}, bf16[2,256,768]{2,1,0:T(8,128)(2,1)S(1)}) custom-call(bf16[16,32,1536]{2,1,0:T(8,128)(2,1)} %all-to-all-done.10.refs_0_.refs_3_, bf16[2,256,768]{2,1,0:T(8,128)(2,1)S(1)} %copy-done.158, bf16[2,256,768]{2,1,0:T(8,128)(2,1)S(1)} %copy-done.160, ...), custom_call_target="tpu_custom_call" | custom-call | flops 3623878656 | bytes 20447232 | tf_op jit(solution)/shard_map/expert_backward/pallas_call | solution.py:36
  745.1 12.1 %collective-permute-done.45.refs_24_ = bf16[2,192,1536]{2,1,0:T(8,128)(2,1)} collective-permute-done((bf16[2,192,1536]{2,1,0:T(8,128)(2,1)}, bf16[2,192,1536]{2,1,0:T(8,128)(2,1)}, u32[]{:S(2)}, u32[]{:S(2)}) %collective-permute-start.45) | collective-permute-done | bytes 1179680 | tf_op jit(solution)/shard_map/ppermute | solution.py:497
  757.3 25.3 %collective-permute-done.43.refs_22_ = bf16[2,192,1536]{2,1,0:T(8,128)(2,1)} collective-permute-done((bf16[2,192,1536]{2,1,0:T(8,128)(2,1)}, bf16[2,192,1536]{2,1,0:T(8,128)(2,1)}, u32[]{:S(2)}, u32[]{:S(2)}) %collective-permute-start.43) | collective-permute-done | bytes 1179680 | tf_op jit(solution)/shard_map/ppermute | solution.py:497
  782.6 9.2 attend_back.6
  825.4 8.6 attend_back.7
  854.2 7.1 all-to-all-start.12
  895.3 6.9 all-to-all-start.13
  914.3 15.7 %all-to-all-done.13.refs_2_ = bf16[16,96,640]{2,1,0:T(8,128)(2,1)S(1)} async-done(((bf16[16,96,640]{2,1,0:T(8,128)(2,1)}), bf16[16,96,640]{2,1,0:T(8,128)(2,1)S(1)}, u32[]{:S(2)}, u32[]{:S(2)}) %all-to-all-start.13) | async-done | bytes 1966112 | tf_op jit(solution)/shard_map/all_to_all | solution.py:457
  (771 shorter events, 469.0 us)
Async XLA Ops:
  7.2 102.0 %all-gather.2.cloned.1.call-start = ((), (), s32[]{:S(2)}) async-start(), calls=%async_computation.14 | async-start | bytes 11581440 | tf_op jit(solution)/shard_map/all_gather | solution.py:490
  12.2 99.2 %collective-permute-start = (bf16[2,192,1536]{2,1,0:T(8,128)(2,1)}, bf16[2,192,1536]{2,1,0:T(8,128)(2,1)S(1)}, u32[]{:S(2)}, u32[]{:S(2)}) collective-permute-start(bf16[2,192,1536]{2,1,0:T(8,128)(2,1)} %bitcast.83), channel_id=1, source_target_pairs={{0,16},{16,0},{32,48},{48,32},{1,17},{17,1},{33,49},{49,33},{2,18}... | collective-permute-start | bytes 3538952 | tf_op jit(solution)/shard_map/ppermute | solution.py:54
  12.9 98.6 %collective-permute-start.3 = (bf16[2,192,1536]{2,1,0:T(8,128)(2,1)}, bf16[2,192,1536]{2,1,0:T(8,128)(2,1)}, u32[]{:S(2)}, u32[]{:S(2)}) collective-permute-start(bf16[2,192,1536]{2,1,0:T(8,128)(2,1)} %bitcast.91), channel_id=1, source_target_pairs={{0,32},{16,48},{32,0},{48,16},{1,33},{17,49},{33,1},{49,17},{2,34}... | collective-permute-start | bytes 3538952 | tf_op jit(solution)/shard_map/ppermute | solution.py:497
  14.6 96.9 %collective-permute-start.2 = (bf16[2,192,1536]{2,1,0:T(8,128)(2,1)}, bf16[2,192,1536]{2,1,0:T(8,128)(2,1)S(1)}, u32[]{:S(2)}, u32[]{:S(2)}) collective-permute-start(bf16[2,192,1536]{2,1,0:T(8,128)(2,1)} %bitcast.92), channel_id=1, source_target_pairs={{0,16},{16,0},{32,48},{48,32},{1,17},{17,1},{33,49},{49,33},{2,18}... | collective-permute-start | bytes 3538952 | tf_op jit(solution)/shard_map/ppermute | solution.py:54
  14.6 96.9 %collective-permute-start.5 = (bf16[2,192,1536]{2,1,0:T(8,128)(2,1)}, bf16[2,192,1536]{2,1,0:T(8,128)(2,1)}, u32[]{:S(2)}, u32[]{:S(2)}) collective-permute-start(bf16[2,192,1536]{2,1,0:T(8,128)(2,1)} %bitcast.100), channel_id=1, source_target_pairs={{0,32},{16,48},{32,0},{48,16},{1,33},{17,49},{33,1},{49,17},{2,34}... | collective-permute-start | bytes 3538952 | tf_op jit(solution)/shard_map/ppermute | solution.py:497
  20.2 91.3 %collective-permute-start.4 = (bf16[2,192,1536]{2,1,0:T(8,128)(2,1)}, bf16[2,192,1536]{2,1,0:T(8,128)(2,1)S(1)}, u32[]{:S(2)}, u32[]{:S(2)}) collective-permute-start(bf16[2,192,1536]{2,1,0:T(8,128)(2,1)} %bitcast.101), channel_id=1, source_target_pairs={{0,16},{16,0},{32,48},{48,32},{1,17},{17,1},{33,49},{49,33},{2,18}... | collective-permute-start | bytes 3538952 | tf_op jit(solution)/shard_map/ppermute | solution.py:54
  217.4 67.6 %all-to-all-start.4 = ((bf16[16,32,1536]{2,1,0:T(8,128)(2,1)}), bf16[16,32,1536]{2,1,0:T(8,128)(2,1)}, u32[]{:S(2)}, u32[]{:S(2)}) async-start(bf16[16,32,1536]{2,1,0:T(8,128)(2,1)} %expert_forward.5.refs_5_), calls=%async_computation.4 | async-start | bytes 3145728 | tf_op jit(solution)/shard_map/all_to_all | solution.py:457
  285.0 132.5 %all-to-all-start.3 = ((bf16[16,64,1536]{2,1,0:T(8,128)(2,1)}), bf16[16,64,1536]{2,1,0:T(8,128)(2,1)}, u32[]{:S(2)}, u32[]{:S(2)}) async-start(bf16[16,64,1536]{2,1,0:T(8,128)(2,1)} %get-tuple-element.162), calls=%async_computation.3 | async-start | bytes 6291456 | tf_op jit(solution)/shard_map/all_to_all | solution.py:457
  292.0 30.7 %collective-permute-start.19 = (bf16[2,192,1536]{2,1,0:T(8,128)(2,1)S(1)}, bf16[2,192,1536]{2,1,0:T(8,128)(2,1)S(1)}, u32[]{:S(2)}, u32[]{:S(2)}) collective-permute-start(bf16[2,192,1536]{2,1,0:T(8,128)(2,1)S(1)} %bitcast.88), channel_id=1, source_target_pairs={{64,96},{80,112},{96,64},{112,80},{65,97},{81,113},{97,65},{113,81... | collective-permute-start | bytes 3538952 | tf_op jit(solution)/shard_map/ppermute | solution.py:497
  295.5 52.4 %collective-permute-start.21 = (bf16[2,192,1536]{2,1,0:T(8,128)(2,1)S(1)}, bf16[2,192,1536]{2,1,0:T(8,128)(2,1)S(1)}, u32[]{:S(2)}, u32[]{:S(2)}) collective-permute-start(bf16[2,192,1536]{2,1,0:T(8,128)(2,1)S(1)} %bitcast.99), channel_id=1, source_target_pairs={{64,96},{80,112},{96,64},{112,80},{65,97},{81,113},{97,65},{113,81... | collective-permute-start | bytes 3538952 | tf_op jit(solution)/shard_map/ppermute | solution.py:497
  298.8 74.4 %collective-permute-start.23 = (bf16[2,192,1536]{2,1,0:T(8,128)(2,1)S(1)}, bf16[2,192,1536]{2,1,0:T(8,128)(2,1)S(1)}, u32[]{:S(2)}, u32[]{:S(2)}) collective-permute-start(bf16[2,192,1536]{2,1,0:T(8,128)(2,1)S(1)} %bitcast.106), channel_id=1, source_target_pairs={{64,96},{80,112},{96,64},{112,80},{65,97},{81,113},{97,65},{113,81... | collective-permute-start | bytes 3538952 | tf_op jit(solution)/shard_map/ppermute | solution.py:497
  324.2 56.0 %collective-permute-start.20 = (bf16[2,192,1536]{2,1,0:T(8,128)(2,1)S(1)}, bf16[2,192,1536]{2,1,0:T(8,128)(2,1)S(1)}, u32[]{:S(2)}, u32[]{:S(2)}) collective-permute-start(bf16[2,192,1536]{2,1,0:T(8,128)(2,1)S(1)} %add.123.refs_3_.refs_9_), channel_id=1, source_target_pairs={{0,16},{16,0},{32,48},{48,32},{1,17},{17,1},{33,49},{49,33},{2,18}... | collective-permute-start | bytes 3538952 | tf_op jit(solution)/shard_map/ppermute | solution.py:54
  349.5 30.8 %collective-permute-start.22 = (bf16[2,192,1536]{2,1,0:T(8,128)(2,1)S(1)}, bf16[2,192,1536]{2,1,0:T(8,128)(2,1)S(1)}, u32[]{:S(2)}, u32[]{:S(2)}) collective-permute-start(bf16[2,192,1536]{2,1,0:T(8,128)(2,1)S(1)} %add.124.refs_7_.refs_13_), channel_id=1, source_target_pairs={{0,16},{16,0},{32,48},{48,32},{1,17},{17,1},{33,49},{49,33},{2,18}... | collective-permute-start | bytes 3538952 | tf_op jit(solution)/shard_map/ppermute | solution.py:54
  417.4 47.3 %all-to-all-start.6 = ((bf16[16,64,1536]{2,1,0:T(8,128)(2,1)}), bf16[16,64,1536]{2,1,0:T(8,128)(2,1)}, u32[]{:S(2)}, u32[]{:S(2)}) async-start(bf16[16,64,1536]{2,1,0:T(8,128)(2,1)} %get-tuple-element.169.refs_13_), calls=%async_computation.6 | async-start | bytes 6291456 | tf_op jit(solution)/shard_map/all_to_all | solution.py:457
  464.7 49.6 %all-to-all-start.5 = ((bf16[16,64,1536]{2,1,0:T(8,128)(2,1)}), bf16[16,64,1536]{2,1,0:T(8,128)(2,1)S(1)}, u32[]{:S(2)}, u32[]{:S(2)}) async-start(bf16[16,64,1536]{2,1,0:T(8,128)(2,1)} %get-tuple-element.170), calls=%async_computation.5 | async-start | bytes 6291456 | tf_op jit(solution)/shard_map/all_to_all | solution.py:457
  516.1 65.9 %all-to-all-start.7 = ((bf16[16,64,1536]{2,1,0:T(8,128)(2,1)}), bf16[16,64,1536]{2,1,0:T(8,128)(2,1)}, u32[]{:S(2)}, u32[]{:S(2)}) async-start(bf16[16,64,1536]{2,1,0:T(8,128)(2,1)} %get-tuple-element.173.refs_5_.refs_18_), calls=%async_computation.7 | async-start | bytes 6291456 | tf_op jit(solution)/shard_map/all_to_all | solution.py:457
  524.1 36.0 %collective-permute-start.37 = (bf16[4,96,1536]{2,1,0:T(8,128)(2,1)S(1)}, bf16[4,96,1536]{2,1,0:T(8,128)(2,1)}, u32[]{:S(2)}, u32[]{:S(2)}) collective-permute-start(bf16[4,96,1536]{2,1,0:T(8,128)(2,1)S(1)} %pack.1.refs_0_), channel_id=1, source_target_pairs={{0,32},{16,48},{32,0},{48,16},{1,33},{17,49},{33,1},{49,17},{2,34}... | collective-permute-start | bytes 3538952 | tf_op jit(solution)/shard_map/ppermute | solution.py:54
  531.2 40.3 %collective-permute-start.34 = (bf16[2,192,1536]{2,1,0:T(8,128)(2,1)S(1)}, bf16[2,192,1536]{2,1,0:T(8,128)(2,1)S(1)}, u32[]{:S(2)}, u32[]{:S(2)}) collective-permute-start(bf16[2,192,1536]{2,1,0:T(8,128)(2,1)S(1)} %get-tuple-element.200), channel_id=1, source_target_pairs={{0,16},{16,0},{32,48},{48,32},{1,17},{17,1},{33,49},{49,33},{2,18}... | collective-permute-start | bytes 3538952 | tf_op jit(solution)/shard_map/ppermute | solution.py:54
  542.9 46.0 %collective-permute-start.35 = (bf16[2,192,1536]{2,1,0:T(8,128)(2,1)}, bf16[2,192,1536]{2,1,0:T(8,128)(2,1)}, u32[]{:S(2)}, u32[]{:S(2)}) collective-permute-start(bf16[2,192,1536]{2,1,0:T(8,128)(2,1)} %get-tuple-element.201), channel_id=1, source_target_pairs={{0,16},{16,0},{32,48},{48,32},{1,17},{17,1},{33,49},{49,33},{2,18}... | collective-permute-start | bytes 3538952 | tf_op jit(solution)/shard_map/ppermute | solution.py:54
  562.0 32.8 %collective-permute-start.36 = (bf16[4,96,1536]{2,1,0:T(8,128)(2,1)S(1)}, bf16[4,96,1536]{2,1,0:T(8,128)(2,1)}, u32[]{:S(2)}, u32[]{:S(2)}) collective-permute-start(bf16[4,96,1536]{2,1,0:T(8,128)(2,1)S(1)} %pack.1.refs_0_), channel_id=1, source_target_pairs={{0,16},{16,0},{32,48},{48,32},{1,17},{17,1},{33,49},{49,33},{2,18}... | collective-permute-start | bytes 3538952 | tf_op jit(solution)/shard_map/ppermute | solution.py:54
  582.0 49.3 %all-to-all-start.8 = ((bf16[16,32,1536]{2,1,0:T(8,128)(2,1)}), bf16[16,32,1536]{2,1,0:T(8,128)(2,1)S(1)}, u32[]{:S(2)}, u32[]{:S(2)}) async-start(bf16[16,32,1536]{2,1,0:T(8,128)(2,1)} %copy-done.127), calls=%async_computation.8 | async-start | bytes 3145728 | tf_op jit(solution)/shard_map/all_to_all | solution.py:457
  700.7 31.3 %collective-permute-start.44 = (bf16[2,192,1536]{2,1,0:T(8,128)(2,1)}, bf16[2,192,1536]{2,1,0:T(8,128)(2,1)}, u32[]{:S(2)}, u32[]{:S(2)}) collective-permute-start(bf16[2,192,1536]{2,1,0:T(8,128)(2,1)} %add_convert_fusion.4.refs_19_), channel_id=1, source_target_pairs={{64,96},{80,112},{96,64},{112,80},{65,97},{81,113},{97,65},{113,81... | collective-permute-start | bytes 3538952 | tf_op jit(solution)/shard_map/ppermute | solution.py:497
  703.7 53.5 %collective-permute-start.45 = (bf16[2,192,1536]{2,1,0:T(8,128)(2,1)}, bf16[2,192,1536]{2,1,0:T(8,128)(2,1)}, u32[]{:S(2)}, u32[]{:S(2)}) collective-permute-start(bf16[2,192,1536]{2,1,0:T(8,128)(2,1)} %add_convert_fusion.3.refs_20_), channel_id=1, source_target_pairs={{64,96},{80,112},{96,64},{112,80},{65,97},{81,113},{97,65},{113,81... | collective-permute-start | bytes 3538952 | tf_op jit(solution)/shard_map/ppermute | solution.py:497
  707.5 75.0 %collective-permute-start.43 = (bf16[2,192,1536]{2,1,0:T(8,128)(2,1)}, bf16[2,192,1536]{2,1,0:T(8,128)(2,1)}, u32[]{:S(2)}, u32[]{:S(2)}) collective-permute-start(bf16[2,192,1536]{2,1,0:T(8,128)(2,1)} %add_convert_fusion.5.refs_18_), channel_id=1, source_target_pairs={{64,96},{80,112},{96,64},{112,80},{65,97},{81,113},{97,65},{113,81... | collective-permute-start | bytes 3538952 | tf_op jit(solution)/shard_map/ppermute | solution.py:497
  713.2 136.3 %collective-permute-start.62 = (bf16[2,192,1536]{2,1,0:T(8,128)(2,1)}, bf16[2,192,1536]{2,1,0:T(8,128)(2,1)}, u32[]{:S(2)}, u32[]{:S(2)}) collective-permute-start(bf16[2,192,1536]{2,1,0:T(8,128)(2,1)} %add_convert_fusion.1.refs_19_), channel_id=1, source_target_pairs={{0,32},{16,48},{32,0},{48,16},{1,33},{17,49},{33,1},{49,17},{2,34}... | collective-permute-start | bytes 3538952 | tf_op jit(solution)/shard_map/ppermute | solution.py:497
  718.1 99.9 %all-to-all-start.11 = ((bf16[16,32,1536]{2,1,0:T(8,128)(2,1)}), bf16[16,32,1536]{2,1,0:T(8,128)(2,1)}, u32[]{:S(2)}, u32[]{:S(2)}) async-start(bf16[16,32,1536]{2,1,0:T(8,128)(2,1)} %get-tuple-element.219.refs_18_), calls=%async_computation.11 | async-start | bytes 3145728 | tf_op jit(solution)/shard_map/all_to_all | solution.py:457
  724.5 125.0 %collective-permute-start.63 = (bf16[2,192,1536]{2,1,0:T(8,128)(2,1)}, bf16[2,192,1536]{2,1,0:T(8,128)(2,1)}, u32[]{:S(2)}, u32[]{:S(2)}) collective-permute-start(bf16[2,192,1536]{2,1,0:T(8,128)(2,1)} %add_convert_fusion.refs_20_), channel_id=1, source_target_pairs={{0,32},{16,48},{32,0},{48,16},{1,33},{17,49},{33,1},{49,17},{2,34}... | collective-permute-start | bytes 3538952 | tf_op jit(solution)/shard_map/ppermute | solution.py:497
  732.0 117.5 %collective-permute-start.61 = (bf16[2,192,1536]{2,1,0:T(8,128)(2,1)}, bf16[2,192,1536]{2,1,0:T(8,128)(2,1)}, u32[]{:S(2)}, u32[]{:S(2)}) collective-permute-start(bf16[2,192,1536]{2,1,0:T(8,128)(2,1)} %add_convert_fusion.2.refs_18_), channel_id=1, source_target_pairs={{0,32},{16,48},{32,0},{48,16},{1,33},{17,49},{33,1},{49,17},{2,34}... | collective-permute-start | bytes 3538952 | tf_op jit(solution)/shard_map/ppermute | solution.py:497
  846.0 56.2 %collective-permute-start.73 = (bf16[2,192,1536]{2,1,0:T(8,128)(2,1)}, bf16[2,192,1536]{2,1,0:T(8,128)(2,1)}, u32[]{:S(2)}, u32[]{:S(2)}) collective-permute-start(bf16[2,192,1536]{2,1,0:T(8,128)(2,1)} %get-tuple-element.281), channel_id=1, source_target_pairs={{0,16},{16,0},{32,48},{48,32},{1,17},{17,1},{33,49},{49,33},{2,18}... | collective-permute-start | bytes 3538952 | tf_op jit(solution)/shard_map/ppermute | solution.py:54
  854.2 41.1 %all-to-all-start.12 = ((bf16[16,96,384]{2,1,0:T(8,128)(2,1)}), bf16[16,96,384]{2,1,0:T(8,128)(2,1)}, u32[]{:S(2)}, u32[]{:S(2)}) async-start(bf16[16,96,384]{2,1,0:T(8,128)(2,1)} %bitcast.118), calls=%async_computation.12 | async-start | bytes 2359296 | tf_op jit(solution)/shard_map/all_to_all | solution.py:457
  865.2 41.1 %collective-permute-start.74 = (bf16[2,192,1536]{2,1,0:T(8,128)(2,1)}, bf16[2,192,1536]{2,1,0:T(8,128)(2,1)}, u32[]{:S(2)}, u32[]{:S(2)}) collective-permute-start(bf16[2,192,1536]{2,1,0:T(8,128)(2,1)} %copy-done.233), channel_id=1, source_target_pairs={{0,16},{16,0},{32,48},{48,32},{1,17},{17,1},{33,49},{49,33},{2,18}... | collective-permute-start | bytes 3538952 | tf_op jit(solution)/shard_map/ppermute | solution.py:54
  895.3 34.7 %all-to-all-start.13 = ((bf16[16,96,640]{2,1,0:T(8,128)(2,1)}), bf16[16,96,640]{2,1,0:T(8,128)(2,1)S(1)}, u32[]{:S(2)}, u32[]{:S(2)}) async-start(bf16[16,96,640]{2,1,0:T(8,128)(2,1)} %bitcast.116), calls=%async_computation.13 | async-start | bytes 3932160 | tf_op jit(solution)/shard_map/all_to_all | solution.py:457
  (317 other events, 3108.6 us)
Sparse Core Ops, SparseCore 0:
  11.7 97.3 all-gather.1

commit v4 on v3

--- a/solution.py
+++ b/solution.py
@@ -47,6 +47,21 @@
         ),
         name=body.func.__name__ if isinstance(body, functools.partial) else body.__name__,
     )(*scalars, *args, *far, *waits)
+
+
+def nothing(*refs):
+    pass
+
+
+def hold(value, *waits):
+    return pl.pallas_call(
+        nothing,
+        out_shape=like(value.shape, value.dtype),
+        in_specs=[pl.BlockSpec(memory_space=pl.ANY)] * (1 + len(waits)),
+        out_specs=pl.BlockSpec(memory_space=pl.ANY),
+        input_output_aliases={0: 0},
+        name="hold",
+    )(value, *waits)
 
 
 def swapped(value, step):
@@ -319,8 +334,9 @@
         kept[1][...] = jnp.broadcast_to(total, kept[1].shape)
         branch[...] = low
         share = width // 4
-        for s, out in enumerate(kept[2:]):
-            out[...] = branch[:, pl.ds(pl.multiple_of((row[0] ^ s) * share, LANES), share)]
+        for s, part in enumerate((part0, part1, part2, part3)):
+            begin = pl.multiple_of((row[0] ^ s) * share, LANES)
+            part[:, part.shape[1] - share :] = branch[:, pl.ds(begin, share)]
     copies[1].wait()
     mixed_grads = dot(low, weights[...], (1, 1)).astype(BF)
     pairs = jnp.concatenate([pair0[...], pair1[...], pair2[...], pair3[...]], 0)
@@ -366,8 +382,9 @@
     ]
     for copy in copies:
         copy.start()
-    total = sum(part[...].astype(F32) for part in (part0, part1, part2, part3))
-    keys = total.shape[1] // 2
+    pairs = weights.shape[1] - width
+    total = sum(part[:, :pairs].astype(F32) for part in (part0, part1, part2, part3))
+    keys = pairs // 2
     backs[:, :width] = query_back[...]
     backs[:, width : width + keys] = turned(total[:, :keys], cosine[...], -sine[...]).astype(BF)
     backs[:, width + keys :] = total[:, keys:].astype(BF)
@@ -398,6 +415,10 @@
         second[j] = total[size:].astype(BF)
 
 
+def add(one, other, total):
+    total[...] = (one[...].astype(F32) + other[...].astype(F32)).astype(BF)
+
+
 def pack(*refs):
     for k, value in enumerate(refs[:-1]):
         refs[-1][k] = value[...]
@@ -409,8 +430,10 @@
 
 def out_grads(*refs):
     lefts, rights, out = refs[:4], refs[4:12], refs[12]
+    share = out.shape[1]
     left = jnp.concatenate([one[k] for one in lefts for k in (2, 3)], 0)
-    out[...] = dot(left, stacked(rights), (0, 0)).astype(BF)
+    right = jnp.concatenate([r[:, r.shape[1] - share :] for r in rights], 0)
+    out[...] = dot(left, right, (0, 0)).astype(BF)
 
 
 def qkv_grads(*refs):
@@ -492,20 +515,12 @@
     gain_a = small[:, experts].astype(F32)[None, :]
     gain_f = small[:, experts + 1].astype(F32)[None, :]
 
-    def across(value, only):
-        lines = [(only * rows + r, only * rows + (r ^ 2)) for r in range(rows)]
-        return lax.ppermute(value, ("section", "row"), lines)
-
-    owns = (w_gate[0], w_up[0], w_down[0])
-    ones = [swapped(own, 1) for own in owns]
-    early_twos = [across(own, 0) for own in owns]
-    early_shards = [
-        (own, one, two, swapped(two, 1)) for own, one, two in zip(owns, ones, early_twos)
-    ]
-    twos = [two + across(own, 1) for own, two in zip(owns, early_twos)]
-    gate_shards, up_shards, down_shards = [
-        (own, one, two, swapped(two, 1)) for own, one, two in zip(owns, ones, twos)
-    ]
+    def shards_of(own):
+        two = swapped(own, 2)
+        return own, swapped(own, 1), two, swapped(two, 1)
+
+    gate_shards, up_shards = shards_of(w_gate[0]), shards_of(w_up[0])
+    down_shards = (w_down[0], swapped(w_down[0], 1), swapped(w_down[0], 2))
 
     lane = jnp.arange(LANES, dtype=jnp.int32)
     half = HEAD_DIM // 2
@@ -563,7 +578,7 @@
     per = slots // columns
     double_like = like((columns, 2 * per, width), BF)
 
-    def forward(came, entering, shards, targets, waits):
+    def forward(came, entering, targets, waits):
         projected, pairs = [], []
         for m in pieces:
             projected.append(
@@ -587,12 +602,24 @@
             for m in pieces
         ]
         arrived = [over_columns(a[4]) for a in attended]
+        lefts, rows_there, down_there = [], (), down_shards
+        if targets:
+            left = call(
+                pack, (like((2 * micro, tokens, width), BF),),
+                [p[1] for p in projected] + [a[0] for a in attended], 0,
+            )[0]
+            two = swapped(left, 2)
+            lefts = [left, swapped(left, 1), two, swapped(two, 1)]
+            rows_there = (two,)
+        else:
+            two = hold(down_shards[2], attended[1][4])
+            down_there = (*down_shards[:2], two, swapped(two, 1))
         applied = [
             call(
                 functools.partial(expert_forward, bool(targets)),
                 (double_like,) + (kept_like,) * 5 if targets else (block_like,), (arrived[m],),
-                (6 if targets else 3) * expert_flops, shards, expert_scratch,
-                waits=() if m else (attended[1][4],),
+                (6 if targets else 3) * expert_flops, (*gate_shards, *up_shards, *down_there),
+                expert_scratch, waits=rows_there if m else (attended[1][4],),
             )
             for m in pieces
         ]
@@ -605,7 +632,7 @@
             )
             for m in pieces
         ]
-        return projected, pairs, attended, arrived, applied, returned, results
+        return projected, pairs, attended, arrived, applied, returned, results, lefts, down_there
 
     def far_and_near(lefts, rights, begins, side):
         return [
@@ -617,23 +644,25 @@
             for left, right, begin in zip(lefts, rights, begins)
         ]
 
-    def merged(halves):
-        return [(h[0].astype(F32) + swapped(h[1], 1).astype(F32)).astype(BF) for h in halves]
+    def merged(half, waits):
+        return call(add, (like(half[0].shape, BF),), (half[0], swapped(half[1], 1)), 0, waits=waits)[0]
 
     def attention_back(keep, m, grad, token_grads, waits):
         return call(
             functools.partial(attend_back, keep),
-            (token_wide, token_low) + (pair_like,) * 4
-            + ((like((tokens, LANES), BF), sums_like) + (like((tokens, share), BF),) * rows
-               if keep else ()),
+            (token_wide, token_low)
+            + (like((tokens, 2 * kv_width + (share if keep else 0)), BF),) * rows
+            + ((like((tokens, LANES), BF), sums_like) if keep else ()),
             (token_grads, returned[m], attended[m][3], spread, places[m], attended[m][1], gain_f,
              grad, projected[m][2], *pairs[m], attended[m][5], cosine, sine),
             out_flops + 4 * score_flops, (dense,), [pltpu.VMEM((tokens, width), BF)] + out_scratch,
             scalars=(here,), waits=waits,
         )
 
-    def projection_back(keep, m, inner, waits):
-        parts = [inner[2]] + [swapped(inner[2 + s], s) for s in steps[1:]]
+    def parts_of(inner):
+        return [inner[2]] + [swapped(inner[2 + s], s) for s in steps[1:]]
+
+    def projection_back(keep, m, inner, parts, waits):
         return call(
             functools.partial(project_back, keep),
             (token_wide, token_low)
@@ -649,34 +678,21 @@
 
     entering = [inputs[m, 0] for m in pieces]
     targets = [cotangent[m, 0] for m in pieces]
-    shards = [one for line in early_shards for one in line]
-    here_by_now = [one for line in early_shards for one in line[1:3]]
-    results = forward(entering, entering, shards, (), (here_by_now, ()))[6]
+    here_by_now = (gate_shards[2], up_shards[2])
+    results, unused, down_shards = forward(entering, entering, (), (here_by_now, ()))[6:]
     came = [lax.ppermute(r[1], "section", [(0, 1)]) for r in results]
 
-    shards = (*gate_shards, *up_shards, *down_shards)
-    here_by_now = [line[3] for line in (gate_shards, up_shards, down_shards)]
-    kept = forward(came, entering, shards, targets, ((), here_by_now))
-    projected, pairs, attended, arrived, applied, returned, results = kept
-    left = call(
-        pack, (like((2 * micro, tokens, width), BF),),
-        [p[1] for p in projected] + [a[0] for a in attended], 0,
-    )[0]
-    two = swapped(left, 2)
-    lefts = [left, swapped(left, 1), two, swapped(two, 1)]
+    kept = forward(came, entering, targets, ((), ()))
+    projected, pairs, attended, arrived, applied, returned, results, lefts, unused = kept
     hidden = [a[1] for a in applied]
-
-    far = far_and_near(
-        (hidden, [a[4] for a in applied], [a[5] for a in applied]), (arrived,) * 3, (per, 0, 0), 1
-    )
-    between = merged(far)
+    done = [r[0] for r in results]
+
     inner, outer = [], []
     for m in pieces:
-        waits = (*between, *lefts[1:], outer[0][0]) if m else (applied[1][0], *(f[0] for f in far))
+        waits = (*done, *lefts[1:], outer[0][0]) if m else (applied[1][0],)
         inner.append(attention_back(False, m, targets[m], returned[m], waits))
-        outer.append(projection_back(False, m, inner[m], ()))
+        outer.append(projection_back(False, m, inner[m], parts_of(inner[m]), ()))
     came = [lax.ppermute(o[1], "section", [(1, 0)]) for o in outer]
-    early = [across(b, 1) for b in between]
 
     sent = [
         call(
@@ -701,36 +717,34 @@
         (hidden, [a[1] for a in moved], [a[2] for a in moved]), (arrived_grads, arrived, arrived),
         (0, 0, 0),
     )
-    far = far_and_near(*operands, 1)
-    between = merged(far)
-    late = [across(b, 0) for b in between]
-    near = far_and_near(*operands, 0)
-    done = [r[0] for r in results]
+    far, near = far_and_near(*operands, 1), far_and_near(*operands, 0)
+    crossed = [swapped(merged(far[0], ()), 2)]
 
     inner = [attention_back(
-        True, 0, sent[0][0], back[0], (moved[1][0], *(p[0] for p in far), *early, *done)
+        True, 0, sent[0][0], back[0], (moved[1][0], *(p[0] for p in far), near[0][0]),
     )]
-    outer = [projection_back(True, 0, inner[0], ())]
-    inner.append(attention_back(
-        True, 1, sent[1][0], back[1], (*between, outer[0][0], *(p[0] for p in near))
-    ))
-    branches = [[a[8]] + [swapped(a[8 + s], s) for s in steps[1:]] for a in inner]
+    parts = [parts_of(inner[0])]
+    outer = [projection_back(True, 0, inner[0], parts[0], ())]
+    inner.append(attention_back(True, 1, sent[1][0], back[1], (inner[0][0], crossed[0])))
+    parts.append(parts_of(inner[1]))
+    crossed.append(swapped(merged(far[1], parts[1][1:]), 2))
     o_grads = call(
         out_grads, (like((width, share), BF),),
-        (*lefts, *[b[s] for s in steps for b in branches]), 2 * width * length * micro * share,
-        waits=late,
+        (*lefts, *[p[s] for s in steps for p in parts]), 2 * width * length * micro * share,
+        waits=(outer[0][0],),
     )[0]
-    outer.append(projection_back(True, 1, inner[1], (o_grads,)))
+    outer.append(projection_back(True, 1, inner[1], parts[1], (o_grads,)))
     backs = [[o[3]] + [swapped(o[3 + s], s) for s in steps[1:]] for o in outer]
     w_grads = call(
         qkv_grads, (like((width, qkv_width // rows + LANES), BF),),
         (*lefts, *[b[s] for s in steps for b in backs], *[a[2] for a in attended],
          *[a[6] for a in inner], *[o[2] for o in outer], *[a[7] for a in inner]),
-        2 * width * length * micro * qkv_width // rows,
+        2 * width * length * micro * qkv_width // rows, waits=(near[1][0], crossed[1]),
     )[0]
+    crossed.append(swapped(merged(far[2], backs[1][1:]), 2))
     expert_grads = [
-        n[0].astype(F32) + swapped(n[1], 1).astype(F32) + e.astype(F32) + l.astype(F32)
-        for n, e, l in zip(near, early, late)
+        n[0].astype(F32) + swapped(n[1], 1).astype(F32) + c.astype(F32)
+        for n, c in zip(near, crossed)
     ]
 
     pieces_out = call(

time: 963 us -> 814 us (0.85)
  waiting for transfers between devices: 350 us -> 255 us
  starting transfers between devices: 211 us -> 174 us
  other arithmetic: 41.1 us -> 18.7 us
    ppermute x12 -> x0, waiting for transfers between devices: 104 us -> none  [across(): return lax.ppermute(value, ('section', 'row'), lines)]
    ppermute x60 -> x54, waiting for transfers between devices: 41.5 us -> 81.7 us  [swapped(): return lax.ppermute(value, 'row', [(r, r ^ step) for r in range(rows)])]
    ppermute x12 -> x0, starting transfers between devices: 30.3 us -> none  [across(): return lax.ppermute(value, ('section', 'row'), lines)]
    all_to_all x14, waiting for transfers between devices: 77.4 us -> 54.2 us  [over_columns(): return lax.all_to_all(value, 'col', split_axis=0, concat_axis=0, tiled=True)]
    ppermute x2, waiting for transfers between devices: 34 us -> 15.1 us  [on_device(): came = [lax.ppermute(r[1], 'section', [(0, 1)]) for r in results]]
    convert_element_type x6 -> x0, other arithmetic: 15.3 us -> none  [merged(): (h[0].astype(F32) + swapped(h[1], 1).astype(F32)).astype(BF)]
    unnamed x518 -> x456, local copies, waits for them, and re-layouts: 80.1 us -> 93.1 us
    all_gather x1, waiting for transfers between devices: 82.6 us -> 92.3 us  [on_device(): dense = lax.all_gather(dense, ('row', 'col'), axis=0, tiled=True)]
  transfers between devices with their start and end apart: 91 -> 73, of which waited for: 39 -> 28; matrix products, arithmetic and copies ran while one was open for 6% -> 3% of each run, Pallas kernels for 22% -> 27%
where the time goes in v4:
time: 814 us; the launch traced here: 799 us
  waiting for transfers between devices  255 us (31%)
  Pallas kernels  229 us (28%)
  starting transfers between devices  174 us (21%)
  local copies, waits for them, and re-layouts  105 us (13%)
  other arithmetic  18.7 us (2%)
  between operations  16.5 us (2%)
    pallas_call x42, Pallas kernels, call(): pl.pallas_call(run, out_shape=tuple(outs), in_specs=[pl.BlockSpec(memory_...  229 us
    unnamed x456, local copies, waits for them, and re-layouts  93.1 us
    all_gather x1, waiting for transfers between devices, on_device(): dense = lax.all_gather(dense, ('row', 'col'), axis=0, tiled=True)  92.3 us
    all_to_all x14, starting transfers between devices, over_columns(): return lax.all_to_all(value, 'col', split_axis=0, concat_axis=0, tiled=True)  89.4 us
    ppermute x54, waiting for transfers between devices, swapped(): return lax.ppermute(value, 'row', [(r, r ^ step) for r in range(rows)])  81.7 us
    ppermute x54, starting transfers between devices, swapped(): return lax.ppermute(value, 'row', [(r, r ^ step) for r in range(rows)])  76.2 us
    all_to_all x14, waiting for transfers between devices, over_columns(): return lax.all_to_all(value, 'col', split_axis=0, concat_axis=0, tiled=True)  54.2 us
  transfers between devices with their start and end apart: 73, of which 28 were waited for; matrix products, arithmetic and copies ran while one was open for 3% of the time, Pallas kernels for 27%

profile of v4, /device:TPU:9, one launch (start us, length us, event | category | flops | bytes accessed | tf_op | source)
XLA Modules:
  0.0 799.3 jit_solution(11490999971543420887)
XLA Ops:
  18.0 92.3 %all-gather.2.cloned.1.call-done.refs_6_.refs_10_.refs_11_.refs_17_ = bf16[1536,3712]{1,0:T(8,128)(2,1)} async-done(((bf16[24,3712]{1,0:T(8,128)(2,1)}), bf16[1536,3712]{1,0:T(8,128)(2,1)}) %all-gather.2.cloned.1.call-update) | async-done | bytes 11403280 | tf_op jit(solution)/shard_map/all_gather | solution.py:513
  127.2 6.6 attend.4
  159.3 15.0 %collective-permute-done.13.refs_5_ = bf16[96,512]{1,0:T(8,128)(2,1)} collective-permute-done((bf16[96,512]{1,0:T(8,128)(2,1)}, bf16[96,512]{1,0:T(8,128)(2,1)}, u32[]{:S(2)}, u32[]{:S(2)}) %collective-permute-start.13) | collective-permute-done | bytes 98336 | tf_op jit(solution)/shard_map/ppermute | solution.py:69
  180.9 6.6 attend.5
  190.7 6.6 all-to-all-start.2
  198.6 9.8 %expert_forward.4 = bf16[16,32,1536]{2,1,0:T(8,128)(2,1)} custom-call(bf16[16,32,1536]{2,1,0:T(8,128)(2,1)} %all-to-all-done.refs_0_, bf16[2,192,1536]{2,1,0:T(8,128)(2,1)S(1)} %bitcast.86, bf16[2,192,1536]{2,1,0:T(8,128)(2,1)} %collective-permute-done.5.refs_2_.refs_8_, bf16[2,192,1536]{2,1,0:T(8,128)(2,1)S(1)} %collective-permute-done.refs_7_.refs_3_.refs_9_, ...), custom_call_target="tpu_custom_call" | custom-call | flops 3623878656 | bytes 17301504 | tf_op jit(solution)/shard_map/expert_forward/pallas_call | solution.py:36
  208.4 10.8 %all-to-all-done.2.refs_0_ = bf16[16,32,1536]{2,1,0:T(8,128)(2,1)} async-done(((bf16[16,32,1536]{2,1,0:T(8,128)(2,1)}), bf16[16,32,1536]{2,1,0:T(8,128)(2,1)}, u32[]{:S(2)}, u32[]{:S(2)}) %all-to-all-start.2) | async-done | bytes 1572896 | tf_op jit(solution)/shard_map/all_to_all | solution.py:480
  224.9 9.8 %expert_forward.5.refs_5_ = bf16[16,32,1536]{2,1,0:T(8,128)(2,1)} custom-call(bf16[16,32,1536]{2,1,0:T(8,128)(2,1)} %all-to-all-done.2.refs_0_, bf16[2,192,1536]{2,1,0:T(8,128)(2,1)S(1)} %bitcast.87, bf16[2,192,1536]{2,1,0:T(8,128)(2,1)} %collective-permute-done.5.refs_2_.refs_8_, bf16[2,192,1536]{2,1,0:T(8,128)(2,1)S(1)} %collective-permute-done.refs_7_.refs_3_.refs_9_, ...), custom_call_target="tpu_custom_call" | custom-call | flops 3623878656 | bytes 17301504 | tf_op jit(solution)/shard_map/expert_forward/pallas_call | solution.py:36
  234.8 8.7 %all-to-all-done.1.refs_0_ = bf16[16,32,1536]{2,1,0:T(8,128)(2,1)} async-done(((bf16[16,32,1536]{2,1,0:T(8,128)(2,1)}), bf16[16,32,1536]{2,1,0:T(8,128)(2,1)}, u32[]{:S(2)}, u32[]{:S(2)}) %all-to-all-start.1) | async-done | bytes 1572896 | tf_op jit(solution)/shard_map/all_to_all | solution.py:480
  253.7 6.4 collective-permute-done.15.refs_1_
  276.2 7.1 attend.6
  289.8 7.0 all-to-all-start.3
  301.1 8.7 %collective-permute-done.19.refs_1_ = bf16[96,1536]{1,0:T(8,128)(2,1)S(1)} collective-permute-done((bf16[96,1536]{1,0:T(8,128)(2,1)S(1)}, bf16[96,1536]{1,0:T(8,128)(2,1)S(1)}, u32[]{:S(2)}, u32[]{:S(2)}) %collective-permute-start.19) | collective-permute-done | bytes 294944 | tf_op jit(solution)/shard_map/ppermute | solution.py:683
  323.2 7.0 attend.7
  337.6 11.6 %all-to-all-start.6 = ((bf16[16,64,1536]{2,1,0:T(8,128)(2,1)}), bf16[16,64,1536]{2,1,0:T(8,128)(2,1)}, u32[]{:S(2)}, u32[]{:S(2)}) async-start(bf16[16,64,1536]{2,1,0:T(8,128)(2,1)} %get-tuple-element.151.refs_13_), calls=%async_computation.6 | async-start | bytes 6291456 | tf_op jit(solution)/shard_map/all_to_all | solution.py:480
  349.2 16.2 %expert_forward.6 = (bf16[16,64,1536]{2,1,0:T(8,128)(2,1)}, bf16[2,256,768]{2,1,0:T(8,128)(2,1)S(1)}, bf16[2,256,768]{2,1,0:T(8,128)(2,1)S(1)}, bf16[2,256,768]{...) custom-call(bf16[16,64,1536]{2,1,0:T(8,128)(2,1)} %all-to-all-done.3.refs_0_.refs_2_, ...), custom_call_target="tpu_custom_call" | custom-call | flops 7247757312 | bytes 24379392 | tf_op jit(solution)/shard_map/expert_forward/pallas_call | solution.py:36
  368.1 21.0 %all-to-all-done.6.refs_0_.refs_3_ = bf16[16,64,1536]{2,1,0:T(8,128)(2,1)} async-done(((bf16[16,64,1536]{2,1,0:T(8,128)(2,1)}), bf16[16,64,1536]{2,1,0:T(8,128)(2,1)}, u32[]{:S(2)}, u32[]{:S(2)}) %all-to-all-start.6) | async-done | bytes 3145760 | tf_op jit(solution)/shard_map/all_to_all | solution.py:480
  400.7 22.7 %collective-permute-done.23.refs_13_.refs_21_.refs_2_ = bf16[4,96,1536]{2,1,0:T(8,128)(2,1)} collective-permute-done((bf16[4,96,1536]{2,1,0:T(8,128)(2,1)}, bf16[4,96,1536]{2,1,0:T(8,128)(2,1)}, u32[]{:S(2)}, u32[]{:S(2)}) %collective-permute-start.23) | collective-permute-done | bytes 1179680 | tf_op jit(solution)/shard_map/ppermute | solution.py:69
  423.4 16.1 %expert_forward.7 = (bf16[16,64,1536]{2,1,0:T(8,128)(2,1)}, bf16[2,256,768]{2,1,0:T(8,128)(2,1)S(1)}, bf16[2,256,768]{2,1,0:T(8,128)(2,1)S(1)}, bf16[2,256,768]{...) custom-call(bf16[16,64,1536]{2,1,0:T(8,128)(2,1)} %all-to-all-done.6.refs_0_.refs_3_, ...), custom_call_target="tpu_custom_call" | custom-call | flops 7247757312 | bytes 24379392 | tf_op jit(solution)/shard_map/expert_forward/pallas_call | solution.py:36
  443.8 6.4 all-to-all-start.7
  458.0 9.1 %attend_back.4 = (f32[96,1536]{1,0:T(8,128)S(1)}, bf16[96,1536]{1,0:T(8,128)(2,1)S(1)}, bf16[96,512]{1,0:T(8,128)(2,1)S(1)}, bf16[96,512]{1,0:T(8,128)(2,1)S(1)}...) custom-call(s32[1]{0:T(128)} %bitcast.33.refs_0_, bf16[16,64,1536]{2,1,0:T(8,128)(2,1)} %copy-done.1, ...), custom_call_target="tpu_custom_call" | custom-call | flops 1056964608 | bytes 21813248 | tf_op jit(solution)/shard_map/attend_back/pallas_call | solution.py:36
  497.0 7.5 all-to-all-start.8
  511.4 9.0 %attend_back.5 = (f32[96,1536]{1,0:T(8,128)S(1)}, bf16[96,1536]{1,0:T(8,128)(2,1)S(1)}, bf16[96,512]{1,0:T(8,128)(2,1)S(1)}, bf16[96,512]{1,0:T(8,128)(2,1)S(1)}...) custom-call(s32[1]{0:T(128)} %bitcast.33.refs_0_, bf16[16,64,1536]{2,1,0:T(8,128)(2,1)} %copy-done, ...), custom_call_target="tpu_custom_call" | custom-call | flops 1056964608 | bytes 21813248 | tf_op jit(solution)/shard_map/attend_back/pallas_call | solution.py:36
  547.6 7.5 all-to-all-start.10
  557.4 10.1 %expert_backward.2 = (bf16[16,32,1536]{2,1,0:T(8,128)(2,1)}, bf16[2,256,768]{2,1,0:T(8,128)(2,1)S(1)}, bf16[2,256,768]{2,1,0:T(8,128)(2,1)S(1)}) custom-call(bf16[16,32,1536]{2,1,0:T(8,128)(2,1)} %all-to-all-done.8.refs_0_.refs_2_, bf16[2,256,768]{2,1,0:T(8,128)(2,1)S(1)} %copy-done.140, bf16[2,256,768]{2,1,0:T(8,128)(2,1)S(1)} %copy-done.142, ...), custom_call_target="tpu_custom_call" | custom-call | flops 3623878656 | bytes 20447232 | tf_op jit(solution)/shard_map/expert_backward/pallas_call | solution.py:36
  568.4 7.2 all-to-all-done.10.refs_0_.refs_3_
  591.0 10.1 %expert_backward.3 = (bf16[16,32,1536]{2,1,0:T(8,128)(2,1)}, bf16[2,256,768]{2,1,0:T(8,128)(2,1)S(1)}, bf16[2,256,768]{2,1,0:T(8,128)(2,1)S(1)}) custom-call(bf16[16,32,1536]{2,1,0:T(8,128)(2,1)} %all-to-all-done.10.refs_0_.refs_3_, bf16[2,256,768]{2,1,0:T(8,128)(2,1)S(1)} %copy-done.144, bf16[2,256,768]{2,1,0:T(8,128)(2,1)S(1)} %copy-done.146, ...), custom_call_target="tpu_custom_call" | custom-call | flops 3623878656 | bytes 20447232 | tf_op jit(solution)/shard_map/expert_backward/pallas_call | solution.py:36
  602.9 6.9 all-to-all-start.11
  632.3 8.6 %attend_back.6 = (f32[96,1536]{1,0:T(8,128)S(1)}, bf16[96,1536]{1,0:T(8,128)(2,1)S(1)}, bf16[96,896]{1,0:T(8,128)(2,1)S(1)}, bf16[96,896]{1,0:T(8,128)(2,1)S(1)}...) custom-call(s32[1]{0:T(128)} %bitcast.33.refs_0_, ...), custom_call_target="tpu_custom_call" | custom-call | flops 1056964608 | bytes 20609024 | tf_op jit(solution)/shard_map/attend_back/pallas_call | solution.py:36
  654.1 8.7 %attend_back.7 = (f32[96,1536]{1,0:T(8,128)S(1)}, bf16[96,1536]{1,0:T(8,128)(2,1)S(1)}, bf16[96,896]{1,0:T(8,128)(2,1)S(1)}, bf16[96,896]{1,0:T(8,128)(2,1)S(1)}...) custom-call(s32[1]{0:T(128)} %bitcast.33.refs_0_, ...), custom_call_target="tpu_custom_call" | custom-call | flops 1056964608 | bytes 20609024 | tf_op jit(solution)/shard_map/attend_back/pallas_call | solution.py:36
  694.7 7.0 all-to-all-start.12
  778.5 6.6 collective-permute-done.56
  (665 shorter events, 387.9 us)
Async XLA Ops:
  7.2 103.1 %all-gather.2.cloned.1.call-start = ((), (), s32[]{:S(2)}) async-start(), calls=%async_computation.14 | async-start | bytes 11581440 | tf_op jit(solution)/shard_map/all_gather | solution.py:513
  10.5 101.5 %collective-permute-start = (bf16[2,192,1536]{2,1,0:T(8,128)(2,1)}, bf16[2,192,1536]{2,1,0:T(8,128)(2,1)S(1)}, u32[]{:S(2)}, u32[]{:S(2)}) collective-permute-start(bf16[2,192,1536]{2,1,0:T(8,128)(2,1)} %bitcast.82), channel_id=1, source_target_pairs={{0,32},{16,48},{32,0},{48,16},{1,33},{17,49},{33,1},{49,17},{2,34}... | collective-permute-start | bytes 3538952 | tf_op jit(solution)/shard_map/ppermute | solution.py:69
  12.6 99.5 %collective-permute-start.1 = (bf16[2,192,1536]{2,1,0:T(8,128)(2,1)}, bf16[2,192,1536]{2,1,0:T(8,128)(2,1)S(1)}, u32[]{:S(2)}, u32[]{:S(2)}) collective-permute-start(bf16[2,192,1536]{2,1,0:T(8,128)(2,1)} %bitcast.90), channel_id=1, source_target_pairs={{0,32},{16,48},{32,0},{48,16},{1,33},{17,49},{33,1},{49,17},{2,34}... | collective-permute-start | bytes 3538952 | tf_op jit(solution)/shard_map/ppermute | solution.py:69
  136.5 54.2 %all-to-all-start = ((bf16[16,32,1536]{2,1,0:T(8,128)(2,1)}), bf16[16,32,1536]{2,1,0:T(8,128)(2,1)}, u32[]{:S(2)}, u32[]{:S(2)}) async-start(bf16[16,32,1536]{2,1,0:T(8,128)(2,1)} %copy-done.103), calls=%async_computation | async-start | bytes 3145728 | tf_op jit(solution)/shard_map/all_to_all | solution.py:480
  141.6 48.5 %collective-permute-start.10 = (bf16[2,192,1536]{2,1,0:T(8,128)(2,1)}, bf16[2,192,1536]{2,1,0:T(8,128)(2,1)}, u32[]{:S(2)}, u32[]{:S(2)}) collective-permute-start(bf16[2,192,1536]{2,1,0:T(8,128)(2,1)} %bitcast.98), channel_id=1, source_target_pairs={{0,32},{16,48},{32,0},{48,16},{1,33},{17,49},{33,1},{49,17},{2,34}... | collective-permute-start | bytes 3538952 | tf_op jit(solution)/shard_map/ppermute | solution.py:69
  142.7 47.8 %collective-permute-start.5 = (bf16[2,192,1536]{2,1,0:T(8,128)(2,1)S(1)}, bf16[2,192,1536]{2,1,0:T(8,128)(2,1)}, u32[]{:S(2)}, u32[]{:S(2)}) collective-permute-start(bf16[2,192,1536]{2,1,0:T(8,128)(2,1)S(1)} %bitcast.85), channel_id=1, source_target_pairs={{0,16},{16,0},{32,48},{48,32},{1,17},{17,1},{33,49},{49,33},{2,18}... | collective-permute-start | bytes 3538952 | tf_op jit(solution)/shard_map/ppermute | solution.py:69
  174.3 22.9 %collective-permute-start.7 = (bf16[2,192,1536]{2,1,0:T(8,128)(2,1)}, bf16[2,192,1536]{2,1,0:T(8,128)(2,1)}, u32[]{:S(2)}, u32[]{:S(2)}) collective-permute-start(bf16[2,192,1536]{2,1,0:T(8,128)(2,1)} %bitcast.91), channel_id=1, source_target_pairs={{0,16},{16,0},{32,48},{48,32},{1,17},{17,1},{33,49},{49,33},{2,18}... | collective-permute-start | bytes 3538952 | tf_op jit(solution)/shard_map/ppermute | solution.py:69
  174.3 22.9 %collective-permute-start.9 = (bf16[2,192,1536]{2,1,0:T(8,128)(2,1)}, bf16[2,192,1536]{2,1,0:T(8,128)(2,1)}, u32[]{:S(2)}, u32[]{:S(2)}) collective-permute-start(bf16[2,192,1536]{2,1,0:T(8,128)(2,1)} %bitcast.99), channel_id=1, source_target_pairs={{0,16},{16,0},{32,48},{48,32},{1,17},{17,1},{33,49},{49,33},{2,18}... | collective-permute-start | bytes 3538952 | tf_op jit(solution)/shard_map/ppermute | solution.py:69
  190.7 28.6 %all-to-all-start.2 = ((bf16[16,32,1536]{2,1,0:T(8,128)(2,1)}), bf16[16,32,1536]{2,1,0:T(8,128)(2,1)}, u32[]{:S(2)}, u32[]{:S(2)}) async-start(bf16[16,32,1536]{2,1,0:T(8,128)(2,1)} %copy-done.11), calls=%async_computation.2 | async-start | bytes 3145728 | tf_op jit(solution)/shard_map/all_to_all | solution.py:480
  219.2 24.3 %all-to-all-start.1 = ((bf16[16,32,1536]{2,1,0:T(8,128)(2,1)}), bf16[16,32,1536]{2,1,0:T(8,128)(2,1)}, u32[]{:S(2)}, u32[]{:S(2)}) async-start(bf16[16,32,1536]{2,1,0:T(8,128)(2,1)} %expert_forward.4), calls=%async_computation.1 | async-start | bytes 3145728 | tf_op jit(solution)/shard_map/all_to_all | solution.py:480
  243.6 46.2 %all-to-all-start.4 = ((bf16[16,32,1536]{2,1,0:T(8,128)(2,1)}), bf16[16,32,1536]{2,1,0:T(8,128)(2,1)}, u32[]{:S(2)}, u32[]{:S(2)}) async-start(bf16[16,32,1536]{2,1,0:T(8,128)(2,1)} %expert_forward.5.refs_5_), calls=%async_computation.4 | async-start | bytes 3145728 | tf_op jit(solution)/shard_map/all_to_all | solution.py:480
  289.8 47.8 %all-to-all-start.3 = ((bf16[16,64,1536]{2,1,0:T(8,128)(2,1)}), bf16[16,64,1536]{2,1,0:T(8,128)(2,1)}, u32[]{:S(2)}, u32[]{:S(2)}) async-start(bf16[16,64,1536]{2,1,0:T(8,128)(2,1)} %get-tuple-element.144), calls=%async_computation.3 | async-start | bytes 6291456 | tf_op jit(solution)/shard_map/all_to_all | solution.py:480
  337.6 51.5 %all-to-all-start.6 = ((bf16[16,64,1536]{2,1,0:T(8,128)(2,1)}), bf16[16,64,1536]{2,1,0:T(8,128)(2,1)}, u32[]{:S(2)}, u32[]{:S(2)}) async-start(bf16[16,64,1536]{2,1,0:T(8,128)(2,1)} %get-tuple-element.151.refs_13_), calls=%async_computation.6 | async-start | bytes 6291456 | tf_op jit(solution)/shard_map/all_to_all | solution.py:480
  389.1 53.1 %all-to-all-start.5 = ((bf16[16,64,1536]{2,1,0:T(8,128)(2,1)}), bf16[16,64,1536]{2,1,0:T(8,128)(2,1)S(1)}, u32[]{:S(2)}, u32[]{:S(2)}) async-start(bf16[16,64,1536]{2,1,0:T(8,128)(2,1)} %get-tuple-element.152), calls=%async_computation.5 | async-start | bytes 6291456 | tf_op jit(solution)/shard_map/all_to_all | solution.py:480
  397.0 26.4 %collective-permute-start.23 = (bf16[4,96,1536]{2,1,0:T(8,128)(2,1)}, bf16[4,96,1536]{2,1,0:T(8,128)(2,1)}, u32[]{:S(2)}, u32[]{:S(2)}) collective-permute-start(bf16[4,96,1536]{2,1,0:T(8,128)(2,1)} %pack.1.refs_0_), channel_id=1, source_target_pairs={{0,32},{16,48},{32,0},{48,16},{1,33},{17,49},{33,1},{49,17},{2,34}... | collective-permute-start | bytes 3538952 | tf_op jit(solution)/shard_map/ppermute | solution.py:69
  443.8 53.1 %all-to-all-start.7 = ((bf16[16,64,1536]{2,1,0:T(8,128)(2,1)}), bf16[16,64,1536]{2,1,0:T(8,128)(2,1)S(1)}, u32[]{:S(2)}, u32[]{:S(2)}) async-start(bf16[16,64,1536]{2,1,0:T(8,128)(2,1)} %get-tuple-element.159.refs_5_.refs_18_), calls=%async_computation.7 | async-start | bytes 6291456 | tf_op jit(solution)/shard_map/all_to_all | solution.py:480
  488.2 22.6 %collective-permute-start.28 = (bf16[4,96,1536]{2,1,0:T(8,128)(2,1)}, bf16[4,96,1536]{2,1,0:T(8,128)(2,1)}, u32[]{:S(2)}, u32[]{:S(2)}) collective-permute-start(bf16[4,96,1536]{2,1,0:T(8,128)(2,1)} %pack.1.refs_0_), channel_id=1, source_target_pairs={{0,16},{16,0},{32,48},{48,32},{1,17},{17,1},{33,49},{49,33},{2,18}... | collective-permute-start | bytes 3538952 | tf_op jit(solution)/shard_map/ppermute | solution.py:69
  497.0 50.7 %all-to-all-start.8 = ((bf16[16,32,1536]{2,1,0:T(8,128)(2,1)}), bf16[16,32,1536]{2,1,0:T(8,128)(2,1)}, u32[]{:S(2)}, u32[]{:S(2)}) async-start(bf16[16,32,1536]{2,1,0:T(8,128)(2,1)} %copy-done.104), calls=%async_computation.8 | async-start | bytes 3145728 | tf_op jit(solution)/shard_map/all_to_all | solution.py:480
  547.6 28.0 %all-to-all-start.10 = ((bf16[16,32,1536]{2,1,0:T(8,128)(2,1)}), bf16[16,32,1536]{2,1,0:T(8,128)(2,1)}, u32[]{:S(2)}, u32[]{:S(2)}) async-start(bf16[16,32,1536]{2,1,0:T(8,128)(2,1)} %get-tuple-element.184.refs_15_), calls=%async_computation.10 | async-start | bytes 3145728 | tf_op jit(solution)/shard_map/all_to_all | solution.py:480
  575.7 27.3 %all-to-all-start.9 = ((bf16[16,32,1536]{2,1,0:T(8,128)(2,1)}), bf16[16,32,1536]{2,1,0:T(8,128)(2,1)}, u32[]{:S(2)}, u32[]{:S(2)}) async-start(bf16[16,32,1536]{2,1,0:T(8,128)(2,1)} %get-tuple-element.185), calls=%async_computation.9 | async-start | bytes 3145728 | tf_op jit(solution)/shard_map/all_to_all | solution.py:480
  586.9 22.9 %collective-permute-start.37 = (bf16[2,192,1536]{2,1,0:T(8,128)(2,1)}, bf16[2,192,1536]{2,1,0:T(8,128)(2,1)}, u32[]{:S(2)}, u32[]{:S(2)}) collective-permute-start(bf16[2,192,1536]{2,1,0:T(8,128)(2,1)} %get-tuple-element.208), channel_id=1, source_target_pairs={{0,16},{16,0},{32,48},{48,32},{1,17},{17,1},{33,49},{49,33},{2,18}... | collective-permute-start | bytes 3538952 | tf_op jit(solution)/shard_map/ppermute | solution.py:69
  602.9 43.4 %all-to-all-start.11 = ((bf16[16,32,1536]{2,1,0:T(8,128)(2,1)}), bf16[16,32,1536]{2,1,0:T(8,128)(2,1)}, u32[]{:S(2)}, u32[]{:S(2)}) async-start(bf16[16,32,1536]{2,1,0:T(8,128)(2,1)} %get-tuple-element.189.refs_18_), calls=%async_computation.11 | async-start | bytes 3145728 | tf_op jit(solution)/shard_map/all_to_all | solution.py:480
  612.5 33.9 %collective-permute-start.38 = (bf16[2,192,1536]{2,1,0:T(8,128)(2,1)}, bf16[2,192,1536]{2,1,0:T(8,128)(2,1)}, u32[]{:S(2)}, u32[]{:S(2)}) collective-permute-start(bf16[2,192,1536]{2,1,0:T(8,128)(2,1)} %add.136), channel_id=1, source_target_pairs={{0,32},{16,48},{32,0},{48,16},{1,33},{17,49},{33,1},{49,17},{2,34}... | collective-permute-start | bytes 3538952 | tf_op jit(solution)/shard_map/ppermute | solution.py:69
  620.4 48.9 %collective-permute-start.48 = (bf16[2,192,1536]{2,1,0:T(8,128)(2,1)}, bf16[2,192,1536]{2,1,0:T(8,128)(2,1)}, u32[]{:S(2)}, u32[]{:S(2)}) collective-permute-start(bf16[2,192,1536]{2,1,0:T(8,128)(2,1)} %get-tuple-element.233), channel_id=1, source_target_pairs={{0,16},{16,0},{32,48},{48,32},{1,17},{17,1},{33,49},{49,33},{2,18}... | collective-permute-start | bytes 3538952 | tf_op jit(solution)/shard_map/ppermute | solution.py:69
  680.4 49.7 %collective-permute-start.49 = (bf16[2,192,1536]{2,1,0:T(8,128)(2,1)}, bf16[2,192,1536]{2,1,0:T(8,128)(2,1)}, u32[]{:S(2)}, u32[]{:S(2)}) collective-permute-start(bf16[2,192,1536]{2,1,0:T(8,128)(2,1)} %add.137), channel_id=1, source_target_pairs={{0,32},{16,48},{32,0},{48,16},{1,33},{17,49},{33,1},{49,17},{2,34}... | collective-permute-start | bytes 3538952 | tf_op jit(solution)/shard_map/ppermute | solution.py:69
  694.7 43.8 %all-to-all-start.12 = ((bf16[16,96,384]{2,1,0:T(8,128)(2,1)}), bf16[16,96,384]{2,1,0:T(8,128)(2,1)S(1)}, u32[]{:S(2)}, u32[]{:S(2)}) async-start(bf16[16,96,384]{2,1,0:T(8,128)(2,1)} %bitcast.115), calls=%async_computation.12 | async-start | bytes 2359296 | tf_op jit(solution)/shard_map/all_to_all | solution.py:480
  701.7 52.1 %collective-permute-start.55 = (bf16[2,192,1536]{2,1,0:T(8,128)(2,1)}, bf16[2,192,1536]{2,1,0:T(8,128)(2,1)}, u32[]{:S(2)}, u32[]{:S(2)}) collective-permute-start(bf16[2,192,1536]{2,1,0:T(8,128)(2,1)} %copy-done.214), channel_id=1, source_target_pairs={{0,16},{16,0},{32,48},{48,32},{1,17},{17,1},{33,49},{49,33},{2,18}... | collective-permute-start | bytes 3538952 | tf_op jit(solution)/shard_map/ppermute | solution.py:69
  701.9 55.8 %collective-permute-start.57 = (bf16[2,192,1536]{2,1,0:T(8,128)(2,1)}, bf16[2,192,1536]{2,1,0:T(8,128)(2,1)}, u32[]{:S(2)}, u32[]{:S(2)}) collective-permute-start(bf16[2,192,1536]{2,1,0:T(8,128)(2,1)} %copy-done.213), channel_id=1, source_target_pairs={{0,16},{16,0},{32,48},{48,32},{1,17},{17,1},{33,49},{49,33},{2,18}... | collective-permute-start | bytes 3538952 | tf_op jit(solution)/shard_map/ppermute | solution.py:69
  730.1 32.2 %collective-permute-start.53 = (bf16[2,192,1536]{2,1,0:T(8,128)(2,1)}, bf16[2,192,1536]{2,1,0:T(8,128)(2,1)}, u32[]{:S(2)}, u32[]{:S(2)}) collective-permute-start(bf16[2,192,1536]{2,1,0:T(8,128)(2,1)} %get-tuple-element.243), channel_id=1, source_target_pairs={{0,16},{16,0},{32,48},{48,32},{1,17},{17,1},{33,49},{49,33},{2,18}... | collective-permute-start | bytes 3538952 | tf_op jit(solution)/shard_map/ppermute | solution.py:69
  738.5 33.3 %all-to-all-start.13 = ((bf16[16,96,640]{2,1,0:T(8,128)(2,1)}), bf16[16,96,640]{2,1,0:T(8,128)(2,1)S(1)}, u32[]{:S(2)}, u32[]{:S(2)}) async-start(bf16[16,96,640]{2,1,0:T(8,128)(2,1)} %bitcast.113), calls=%async_computation.13 | async-start | bytes 3932160 | tf_op jit(solution)/shard_map/all_to_all | solution.py:480
  752.7 25.8 %collective-permute-start.54 = (bf16[2,192,1536]{2,1,0:T(8,128)(2,1)}, bf16[2,192,1536]{2,1,0:T(8,128)(2,1)}, u32[]{:S(2)}, u32[]{:S(2)}) collective-permute-start(bf16[2,192,1536]{2,1,0:T(8,128)(2,1)} %get-tuple-element.245), channel_id=1, source_target_pairs={{0,16},{16,0},{32,48},{48,32},{1,17},{17,1},{33,49},{49,33},{2,18}... | collective-permute-start | bytes 3538952 | tf_op jit(solution)/shard_map/ppermute | solution.py:69
  756.3 28.8 %collective-permute-start.56 = (bf16[2,192,1536]{2,1,0:T(8,128)(2,1)}, bf16[2,192,1536]{2,1,0:T(8,128)(2,1)}, u32[]{:S(2)}, u32[]{:S(2)}) collective-permute-start(bf16[2,192,1536]{2,1,0:T(8,128)(2,1)} %add.138), channel_id=1, source_target_pairs={{0,32},{16,48},{32,0},{48,16},{1,33},{17,49},{33,1},{49,17},{2,34}... | collective-permute-start | bytes 3538952 | tf_op jit(solution)/shard_map/ppermute | solution.py:69
  (268 other events, 2309.2 us)
Sparse Core Ops, SparseCore 0:
  11.7 98.5 all-gather.1

commit v5 on v4

--- a/solution.py
+++ b/solution.py
@@ -26,27 +26,109 @@
     return jax.ShapeDtypeStruct(shape, dtype)
 
 
-def call(body, outs, args, flops, far=(), scratch=(), vmem=48, scalars=(), waits=()):
-    moved = sum(a.size * a.dtype.itemsize for a in (*args, *far, *outs))
-    used = len(scalars) + len(args) + len(far)
+class Late:
+    def __init__(self, source, target=None, sem=None):
+        self.source, self.target, self.copy = source, target, None
+        if target is not None:
+            self.copy = pltpu.make_async_copy(source, target, sem)
+            self.copy.start()
+            self.waiting = True
+
+    def ready(self):
+        if self.waiting:
+            self.copy.wait()
+            self.waiting = False
+        return self.target
+
+    def __getitem__(self, index):
+        return self.ready()[index]
+
+    @property
+    def shape(self):
+        return self.source.shape
+
+
+class Sent:
+    def __init__(self, source, target=None, sem=None):
+        self.source, self.target, self.sem, self.copy = source, target, sem, None
+
+    def __getitem__(self, index):
+        return self.source[index]
+
+    def __setitem__(self, index, value):
+        self.source[index] = value
+
+    def send(self):
+        self.copy = pltpu.make_async_copy(self.source, self.target, self.sem)
+        self.copy.start()
+
+    @property
+    def shape(self):
+        return self.source.shape
+
+
+def sent(out):
+    if isinstance(out, Sent):
+        out.send()
+
+
+def call(body, outs, args, flops, far=(), scratch=(), scalars=(), waits=()):
+    arrays = [a.source if isinstance(a, Late) else a for a in args]
+    shapes = [o.source if isinstance(o, Sent) else o for o in outs]
+    moved = sum(a.size * a.dtype.itemsize for a in (*arrays, *far, *shapes))
+    count = len(scalars) + len(args) + len(far)
+    kinds = [isinstance(a, Late) for a in args]
+    out_kinds = [isinstance(o, Sent) for o in outs]
+    buffers = [pltpu.VMEM(a.shape, a.dtype) for a, k in zip(arrays, kinds) if k]
+    buffers += [pltpu.VMEM(o.shape, o.dtype) for o, k in zip(shapes, out_kinds) if k]
 
     def run(*refs):
-        body(*refs[:used], *refs[used + len(waits) :])
-
+        given, refs = list(refs[:count]), refs[count + len(waits) :]
+        results, refs = list(refs[: len(outs)]), refs[len(outs) :]
+        own, rest = list(refs[: len(buffers)]), refs[len(buffers) :]
+        sems, rest = (rest[0], rest[1:]) if buffers else (None, rest)
+        used = 0
+        for k, late in enumerate(kinds):
+            if late:
+                at = len(scalars) + k
+                given[at] = Late(given[at], own[used], sems.at[used])
+                used += 1
+        for k, kind in enumerate(out_kinds):
+            if kind:
+                results[k] = Sent(own[used], results[k], sems.at[used])
+                used += 1
+        body(*given, *results, *rest)
+        for one in given:
+            if isinstance(one, Late):
+                one.ready()
+        for one in results:
+            if isinstance(one, Sent) and one.copy is None:
+                one.send()
+        for one in results:
+            if isinstance(one, Sent):
+                one.copy.wait()
+
+    anywhere, local = pl.BlockSpec(memory_space=pl.ANY), pl.BlockSpec(memory_space=pltpu.VMEM)
     return pl.pallas_call(
         run,
-        out_shape=tuple(outs),
+        out_shape=tuple(shapes),
         in_specs=[pl.BlockSpec(memory_space=pltpu.SMEM)] * len(scalars)
-        + [pl.BlockSpec(memory_space=pltpu.VMEM)] * len(args)
-        + [pl.BlockSpec(memory_space=pl.ANY)] * (len(far) + len(waits)),
-        out_specs=tuple(pl.BlockSpec(memory_space=pltpu.VMEM) for unused in outs),
-        scratch_shapes=list(scratch),
-        compiler_params=pltpu.CompilerParams(vmem_limit_bytes=vmem * MIB),
+        + [anywhere if k else local for k in kinds]
+        + [anywhere] * (len(far) + len(waits)),
+        out_specs=tuple(anywhere if k else local for k in out_kinds),
+        scratch_shapes=buffers
+        + ([pltpu.SemaphoreType.DMA((len(buffers),))] if buffers else [])
+        + list(scratch),
+        compiler_params=pltpu.CompilerParams(vmem_limit_bytes=60 * MIB),
         cost_estimate=pl.CostEstimate(
             flops=int(flops), bytes_accessed=int(moved), transcendentals=0
         ),
         name=body.func.__name__ if isinstance(body, functools.partial) else body.__name__,
-    )(*scalars, *args, *far, *waits)
+    )(*scalars, *arrays, *far, *waits)
+
+
+def late(values):
+    return [Late(v) for v in values]
 
 
 def nothing(*refs):
@@ -105,8 +187,9 @@
 
 
 def project(
-    flag, came, entering, gain, cosine, sine, dense, stream, normed, query, pair, weights, sems
+    keep, flag, came, entering, gain, cosine, sine, dense, stream, query, pair, *rest
 ):
+    kept, (weights, sems) = rest[:-2], rest[-2:]
     width = stream.shape[1]
     cuts = cuts_of(weights.shape[1])
     copies = [
@@ -120,7 +203,11 @@
     x = jnp.where(flag[0] > 0, came[...].astype(F32), entering[...].astype(F32))
     stream[...] = x
     low = (x * norm_parts(x) * gain[...]).astype(BF)
-    normed[...] = low
+    if keep:
+        kept[0][...] = low
+        kept[1][...] = x
+        sent(kept[0])
+        sent(kept[1])
     keys = pair.shape[1] // 2
     for copy, (at, size) in zip(copies, cuts):
         copy.wait()
@@ -129,25 +216,33 @@
             head = part[:, begin - at : begin - at + HEAD_DIM]
             if begin < width + keys:
                 head = turned(head, cosine[...], sine[...])
+            head = head.astype(BF)
             if begin < width:
-                query[:, begin : begin + HEAD_DIM] = head.astype(BF)
+                query[:, begin : begin + HEAD_DIM] = head
             else:
-                pair[:, begin - width : begin - width + HEAD_DIM] = head.astype(BF)
+                pair[:, begin - width : begin - width + HEAD_DIM] = head
+    if keep:
+        kept[2][...] = query[...]
+        kept[3][...] = pair[...]
+
+
+def slot_experts(slots):
+    own = lax.broadcasted_iota(jnp.int32, (slots, LANES), 0) // ROOMS
+    return own == lax.broadcasted_iota(jnp.int32, (slots, LANES), 1)
 
 
 def scaled_rows(dispatch, gates, low):
-    slots = dispatch.shape[0]
-    own = lax.broadcasted_iota(jnp.int32, (slots, LANES), 0) // ROOMS
-    here = own == lax.broadcasted_iota(jnp.int32, (slots, LANES), 1)
+    here = slot_experts(dispatch.shape[0])
     scale = jnp.sum(jnp.where(here, dot(dispatch, gates.astype(BF)), 0.0), -1, keepdims=True)
     return (dot(dispatch, low) * scale).astype(BF)
 
 
 def attend(
-    stream, query, pair0, pair1, pair2, pair3, bias, gain, chosen, dispatch, *rest,
+    keep, stream, query, pair0, pair1, pair2, pair3, bias, gain, chosen, dispatch, *rest,
 ):
-    targets, rest = rest[:-10], rest[-10:]
-    dense, mixed, middle, normed_ffn, gates, outgoing, probs, weights, router, sems = rest
+    targets, rest = (rest[:1], rest[1:]) if keep else ((), rest)
+    dense, middle, gates, outgoing = rest[:4]
+    kept, (mixed, weights, router, sems) = rest[4:-4], rest[-4:]
     width = stream.shape[1]
     block = (outgoing.shape[0], -1, width)
     per = dispatch.shape[0] // outgoing.shape[0]
@@ -170,25 +265,35 @@
         scores = dot(queries, keys, (1, 1)) * HEAD_DIM ** (-0.5) + biases
         expo = jnp.exp(scores - jnp.max(scores, -1, keepdims=True))
         weight = (expo * (1.0 / jnp.sum(expo, -1, keepdims=True))).astype(BF)
-        probs[h] = weight
+        if keep:
+            kept[0][h] = weight
         done = dot(weight, values).astype(BF)
         for j in range(group):
             begin = (h * group + j) * HEAD_DIM
             mixed[:, begin : begin + HEAD_DIM] = done[j * tokens : (j + 1) * tokens]
+    if keep:
+        kept[1][...] = mixed[...]
+        sent(kept[0])
+        sent(kept[1])
     copies[0].wait()
     x = stream[...] + dot(mixed[...], weights[...])
     middle[...] = x
+    sent(middle)
     low = (x * norm_parts(x) * gain[...]).astype(BF)
-    normed_ffn[...] = low
+    if keep:
+        kept[2][...] = low
+        sent(kept[2])
     copies[1].wait()
     taken = chosen[...] > 0
     logits = jnp.where(taken, dot(low, router[...]), -1e30)
     expo = jnp.where(taken, jnp.exp(logits - jnp.max(logits, -1, keepdims=True)), 0.0)
     share = expo / jnp.sum(expo, -1, keepdims=True)
     gates[...] = share
-    outgoing[:, :per, :] = dot(dispatch[...], low).astype(BF).reshape(block)
+    sent(gates)
+    slots = dispatch[...]
+    outgoing[:, :per, :] = dot(slots, low).astype(BF).reshape(block)
     if targets:
-        outgoing[:, per:, :] = scaled_rows(dispatch[...], share, targets[0][...]).reshape(block)
+        outgoing[:, per:, :] = scaled_rows(slots, share, targets[0][...]).reshape(block)
 
 
 def fetch(shards, weights, sems):
@@ -224,6 +329,15 @@
     columns, unused, width = value.shape
     at = begin + j * ROOMS
     return value[:, at : at + ROOMS, :].reshape(columns * ROOMS, width)
+
+
+def put_rows(out, j, rows, inner):
+    at, width = j * ROOMS, rows.shape[1]
+    out[:, at : at + ROOMS, :width] = rows.reshape(-1, ROOMS, width)
+    high = inner.astype(BF).astype(F32)
+    lane = lax.broadcasted_iota(jnp.int32, (rows.shape[0], LANES), 1)
+    both = jnp.where(lane == 0, high, jnp.where(lane == 1, inner - high, 0.0))
+    out[:, at : at + ROOMS, width:] = both.astype(BF).reshape(-1, ROOMS, LANES)
 
 
 def expert_forward(both, arrived, *refs):
@@ -256,35 +370,42 @@
             hidden_grads = dot(rows_of(arrived, j, per), weights[2, j], (1, 1))
             gate_part = (hidden_grads * bent).astype(BF)
             lifted_part = (hidden_grads * active).astype(BF)
-            outs[4][j] = gate_part
-            outs[5][j] = lifted_part
+            inner = jnp.sum(hidden_grads * hidden.astype(F32), -1, keepdims=True)
             back = dot(gate_part, weights[0, j]) + dot(lifted_part, weights[1, j])
-            outs[0][:, per + at : per + at + ROOMS, :] = back.astype(BF).reshape(
-                -1, ROOMS, back.shape[1]
-            )
-
-
-def first_rows(returned, places):
-    columns, unused, width = returned.shape
-    return returned[:, : places.shape[1] // columns, :].reshape(-1, width)
+            put_rows(outs[4], j, back.astype(BF), inner)
+    if both:
+        for out in outs[:4]:
+            sent(out)
 
 
 def combine(returned, middle, gates, spread, places, result, low):
-    weights = dot(gates[...].astype(BF), spread[...]) * places[...].astype(F32)
-    done = middle[...] + dot(weights.astype(BF), first_rows(returned, places))
+    weights = (dot(gates[...].astype(BF), spread[...]) * places[...].astype(F32)).astype(BF)
+    done = middle[...] + dot(weights, returned[...].reshape(-1, returned.shape[2]))
     result[...] = done
+    sent(result)
     low[...] = done.astype(BF)
+
+
+def last_outputs(flag, spread, *refs):
+    out = refs[-1]
+    width = out.shape[2]
+    for m in range(out.shape[0]):
+        returned, middle, gates, places, before = refs[5 * m : 5 * m + 5]
+        weights = (dot(gates[...].astype(BF), spread[...]) * places[...].astype(F32)).astype(BF)
+        rows = returned[:, :, :width].reshape(-1, width)
+        out[m] = jnp.where(flag[0] > 0, middle[...] + dot(weights, rows), before[...])
 
 
 def send_grads(flag, came, target, gates, dispatch, grad, outgoing):
     low = jnp.where(flag[0] > 0, came[...], target[...])
     grad[...] = low
+    sent(grad)
     outgoing[...] = scaled_rows(dispatch[...], gates[...], low).reshape(outgoing.shape)
 
 
-def expert_backward(arrived, active, bent, *refs):
+def expert_backward(flag, arrived, hidden, active, bent, produced, *refs):
     shards = [refs[4 * k : 4 * k + 4] for k in range(3)]
-    sent, gate_back, lifted_back, weights, sems = refs[12:]
+    out, gate_back, lifted_back, weights, sems = refs[12:]
     copies = fetch(shards, weights, sems)
     for j in range(weights.shape[1]):
         done_with(copies[j][0])
@@ -293,15 +414,18 @@
         lifted_part = (hidden_grads * active[j].astype(F32)).astype(BF)
         gate_back[j] = gate_part
         lifted_back[j] = lifted_part
+        inner = jnp.sum(hidden_grads * hidden[j].astype(F32), -1, keepdims=True)
         done_with(copies[j][1])
         done = dot(gate_part, weights[1, j])
         done_with(copies[j][2])
         done = (done + dot(lifted_part, weights[2, j])).astype(BF)
-        sent[:, j * ROOMS : (j + 1) * ROOMS, :] = done.reshape(-1, ROOMS, done.shape[1])
+        put_rows(out, j, jnp.where(flag[0] > 0, rows_of(produced, j), done), inner)
+    sent(gate_back)
+    sent(lifted_back)
 
 
 def attend_back(
-    keep, row, token_grads, returned, gates, spread, places, middle, gain, grad, query, pair0, pair1,
+    keep, row, flag, token_grads, before, gates, places, middle, gain, grad, query, pair0, pair1,
     pair2, pair3, probs, cosine, sine, dense, middle_grads, query_back, part0, part1, part2, part3,
     *rest,
 ):
@@ -314,15 +438,18 @@
     ]
     for copy in copies:
         copy.start()
-    inner = dot(grad[...], first_rows(returned, places), (1, 1)) * places[...].astype(F32)
-    gate_grads = dot(inner.astype(BF), spread[...], (1, 1))
-    chances = gates[...]
-    logit_grads = (
-        chances * (gate_grads - jnp.sum(chances * gate_grads, -1, keepdims=True))
-    ).astype(BF)
-    per = places.shape[1] // returned.shape[0]
-    came = token_grads[:, token_grads.shape[1] - per :, :].reshape(-1, width)
-    ffn_grads = dot(places[...], came)
+    came = token_grads[...]
+    if keep:
+        came = jnp.where(flag[0] > 0, before[...], came)
+    came = came.reshape(-1, came.shape[2])
+    place = places[...]
+    here = slot_experts(came.shape[0])
+    notes = came[:, width:].astype(F32)
+    high = jnp.where(here, notes[:, :1], 0.0).astype(BF)
+    rest_of = jnp.where(here, notes[:, 1:2], 0.0).astype(BF)
+    inner = dot(place, high) + dot(place, rest_of)
+    logit_grads = (inner - gates[...] * jnp.sum(inner, -1, keepdims=True)).astype(BF)
+    ffn_grads = dot(place, came[:, :width])
     copies[0].wait()
     ffn_grads = ffn_grads + dot(logit_grads, router[...], (1, 1))
     part, total = norm_back(ffn_grads, middle[...], gain[...])
@@ -332,6 +459,8 @@
     if keep:
         kept[0][...] = logit_grads
         kept[1][...] = jnp.broadcast_to(total, kept[1].shape)
+        sent(kept[0])
+        sent(kept[1])
         branch[...] = low
         share = width // 4
         for s, part in enumerate((part0, part1, part2, part3)):
@@ -369,7 +498,7 @@
 
 def project_back(
     keep, row, part0, part1, part2, part3, query_back, stream, gain, middle_grads, cosine, sine,
-    dense, grad, low, *rest,
+    dense, low, *rest,
 ):
     width = stream.shape[1]
     kept, (backs, weights, sems) = rest[:-3], rest[-3:]
@@ -388,18 +517,19 @@
     backs[:, :width] = query_back[...]
     backs[:, width : width + keys] = turned(total[:, :keys], cosine[...], -sine[...]).astype(BF)
     backs[:, width + keys :] = total[:, keys:].astype(BF)
+    if keep:
+        share = backs.shape[1] // 4
+        for s, out in enumerate(kept[2:]):
+            out[...] = backs[:, pl.ds(pl.multiple_of((row[0] ^ s) * share, LANES), share)]
     above = jnp.zeros(stream.shape, F32)
     for copy, (at, size) in zip(copies, cuts):
         copy.wait()
         above = above + dot(backs[:, at : at + size], weights[:, at : at + size], (1, 1))
     part, sums = norm_back(above, stream[...], gain[...])
+    done = middle_grads[...] + part
     if keep:
-        kept[0][...] = jnp.broadcast_to(sums, kept[0].shape)
-        share = backs.shape[1] // 4
-        for s, out in enumerate(kept[1:]):
-            out[...] = backs[:, pl.ds(pl.multiple_of((row[0] ^ s) * share, LANES), share)]
-    done = middle_grads[...] + part
-    grad[...] = done
+        kept[0][...] = done
+        kept[1][...] = jnp.broadcast_to(sums, kept[1].shape)
     low[...] = done.astype(BF)
 
 
@@ -428,28 +558,37 @@
     return jnp.concatenate([r[...] for r in refs], 0)
 
 
+def by_owner(out, grads, begin):
+    columns, lines, unused = out.shape
+    size = lines // 4
+    for c in range(columns):
+        some = [grads[(r * columns + c) * size : (r * columns + c + 1) * size] for r in range(4)]
+        out[c, :, begin : begin + grads.shape[1]] = jnp.concatenate(some, 0).astype(BF)
+
+
 def out_grads(*refs):
     lefts, rights, out = refs[:4], refs[4:12], refs[12]
-    share = out.shape[1]
+    share = out.shape[2]
     left = jnp.concatenate([one[k] for one in lefts for k in (2, 3)], 0)
     right = jnp.concatenate([r[:, r.shape[1] - share :] for r in rights], 0)
-    out[...] = dot(left, right, (0, 0)).astype(BF)
+    by_owner(out, dot(left, right, (0, 0)), 0)
 
 
 def qkv_grads(*refs):
     lefts, rights, normed, logits, gains, out = (
         refs[:4], refs[4:12], refs[12:14], refs[14:16], refs[16:20], refs[20],
     )
-    width, wide = out.shape
+    wide = out.shape[2]
     left = jnp.concatenate([one[k] for one in lefts for k in (0, 1)], 0)
-    out[:, : wide - LANES] = dot(left, stacked(rights), (0, 0)).astype(BF)
-    first = gains[0][:1] + gains[1][:1]
-    second = gains[2][:1] + gains[3][:1]
+    by_owner(out, dot(left, stacked(rights), (0, 0)), 0)
+    width = left.shape[1]
+    first = gains[0][:1, :] + gains[1][:1, :]
+    second = gains[2][:1, :] + gains[3][:1, :]
     line = lax.broadcasted_iota(jnp.int32, (LANES, width), 0)
     sums = jnp.where(
         line == LANES - 2, first, jnp.where(line == LANES - 1, second, jnp.zeros((1, 1), F32))
     )
-    out[:, wide - LANES :] = (dot(stacked(normed), stacked(logits), (0, 0)) + sums.T).astype(BF)
+    by_owner(out, dot(stacked(normed), stacked(logits), (0, 0)) + sums.T, wide - LANES)
 
 
 def fold(row, first, second, out0, out1, out2, out3, total):
@@ -576,87 +715,95 @@
     expert_flops = 2 * slots * hidden_width * width
 
     per = slots // columns
+    back_like = like((columns, per, width + LANES), BF)
     double_like = like((columns, 2 * per, width), BF)
-
-    def forward(came, entering, targets, waits):
+    lanes_like = like((tokens, LANES), F32)
+    tables = late([cosine, sine])
+    first_flag = (1 - second)
+
+    def forward(came, entering, targets, waits, down):
+        keep = bool(targets)
         projected, pairs = [], []
         for m in pieces:
             projected.append(
                 call(
-                    project, (token_wide, token_low, token_low, pair_like),
-                    (came[m], entering[m], gain_a, cosine, sine), qkv_flops, (dense,), qkv_scratch,
-                    scalars=(second,), waits=(*waits[m], *(p[0] for p in projected)),
+                    functools.partial(project, keep),
+                    (token_wide, token_low, pair_like)
+                    + ((Sent(token_low), Sent(token_wide), Sent(token_low), Sent(pair_like))
+                       if keep else ()),
+                    (came[m], Late(entering[m]), Late(gain_a), *tables), qkv_flops, (dense,),
+                    qkv_scratch, (second,), waits=(*waits, *(p[0] for p in projected)),
                 )
             )
-            pair = projected[m][3]
-            pairs.append([pair] + [swapped(pair, s) for s in steps[1:]])
+            pair = projected[m][2]
+            pairs.append([swapped(pair, s) for s in steps[1:]])
         attended = [
             call(
-                attend,
-                (token_low, token_wide, token_low, like((tokens, LANES), F32),
-                 double_like if targets else block_like, probs_like),
-                (projected[m][0], projected[m][2], *pairs[m], biases[m], gain_f, chosens[m],
-                 dispatches[m], *targets[m : m + 1]),
-                out_flops + 2 * score_flops, (dense,), out_scratch,
+                functools.partial(attend, keep),
+                (Sent(token_wide), Sent(lanes_like), Sent(double_like if keep else block_like))
+                + ((Sent(probs_like), Sent(token_low), Sent(token_low)) if keep else ()),
+                (*projected[m][:3], *late([*pairs[m], biases[m], gain_f, chosens[m], dispatches[m],
+                                           *targets[m : m + 1]])),
+                out_flops + 2 * score_flops, (dense,), [pltpu.VMEM((tokens, width), BF)] + out_scratch,
+                waits=() if keep or m else (projected[1][2],),
             )
             for m in pieces
         ]
-        arrived = [over_columns(a[4]) for a in attended]
-        lefts, rows_there, down_there = [], (), down_shards
-        if targets:
+        arrived = [over_columns(a[2]) for a in attended]
+        lefts, ready = [], ()
+        if keep:
             left = call(
-                pack, (like((2 * micro, tokens, width), BF),),
-                [p[1] for p in projected] + [a[0] for a in attended], 0,
+                pack, (Sent(like((2 * micro, tokens, width), BF)),),
+                late([p[3] for p in projected] + [a[4] for a in attended]), 0,
             )[0]
             two = swapped(left, 2)
             lefts = [left, swapped(left, 1), two, swapped(two, 1)]
-            rows_there = (two,)
+            ready = (two,)
         else:
-            two = hold(down_shards[2], attended[1][4])
-            down_there = (*down_shards[:2], two, swapped(two, 1))
+            two = hold(down[2], attended[1][2])
+            down = (*down[:2], two, swapped(two, 1))
         applied = [
             call(
-                functools.partial(expert_forward, bool(targets)),
-                (double_like,) + (kept_like,) * 5 if targets else (block_like,), (arrived[m],),
-                (6 if targets else 3) * expert_flops, (*gate_shards, *up_shards, *down_there),
-                expert_scratch, waits=rows_there if m else (attended[1][4],),
+                functools.partial(expert_forward, keep),
+                (Sent(block_like),)
+                + ((Sent(kept_like),) * 3 + (Sent(back_like),) if keep else ()),
+                late([arrived[m]]), (6 if keep else 3) * expert_flops,
+                (*gate_shards, *up_shards, *down), expert_scratch,
+                waits=ready if m else (attended[1][2],),
             )
             for m in pieces
         ]
-        returned = [over_columns(a[0]) for a in applied]
-        results = [
-            call(
-                combine, (token_wide, token_low),
-                (returned[m], attended[m][1], attended[m][3], spread, places[m]),
-                2 * slots * tokens * width, waits=() if m else (applied[1][0],),
-            )
-            for m in pieces
-        ]
-        return projected, pairs, attended, arrived, applied, returned, results, lefts, down_there
-
-    def far_and_near(lefts, rights, begins, side):
+        return projected, pairs, attended, arrived, applied, lefts, down
+
+    def far_and_near(side):
         return [
             call(
                 functools.partial(expert_weight_grads, side, begin),
-                (like((per_column, hidden_width // 4, width), BF),) * 2, (*left, *right),
-                expert_flops,
+                (Sent(like((per_column, hidden_width // 4, width), BF)),) * 2,
+                late([*left, *right]), expert_flops,
             )
-            for left, right, begin in zip(lefts, rights, begins)
+            for left, right, begin in (
+                (hidden, arrived_grads, 0), ([a[1] for a in moved], arrived, 0),
+                ([a[2] for a in moved], arrived, 0),
+            )
         ]
 
     def merged(half, waits):
-        return call(add, (like(half[0].shape, BF),), (half[0], swapped(half[1], 1)), 0, waits=waits)[0]
+        return call(
+            add, (Sent(half[0]),), late([half[0], swapped(half[1], 1)]), 0, waits=waits
+        )[0]
 
     def attention_back(keep, m, grad, token_grads, waits):
         return call(
             functools.partial(attend_back, keep),
             (token_wide, token_low)
             + (like((tokens, 2 * kv_width + (share if keep else 0)), BF),) * rows
-            + ((like((tokens, LANES), BF), sums_like) if keep else ()),
-            (token_grads, returned[m], attended[m][3], spread, places[m], attended[m][1], gain_f,
-             grad, projected[m][2], *pairs[m], attended[m][5], cosine, sine),
+            + ((Sent(like((tokens, LANES), BF)), Sent(sums_like)) if keep else ()),
+            late([token_grads, shared[m] if keep else spread, attended[m][1], places[m],
+                  attended[m][0], gain_f, grad, projected[m][5], projected[m][6], *pairs[m],
+                  attended[m][3], cosine, sine]),
             out_flops + 4 * score_flops, (dense,), [pltpu.VMEM((tokens, width), BF)] + out_scratch,
-            scalars=(here,), waits=waits,
+            (here, second), waits,
         )
 
     def parts_of(inner):
@@ -665,93 +812,103 @@
     def projection_back(keep, m, inner, parts, waits):
         return call(
             functools.partial(project_back, keep),
-            (token_wide, token_low)
-            + ((sums_like,) + (like((tokens, qkv_width // rows), BF),) * rows if keep else ()),
-            (*parts, inner[1], projected[m][0], gain_a, inner[0], cosine, sine),
+            (token_low,)
+            + ((Sent(token_wide), Sent(sums_like))
+               + (like((tokens, qkv_width // rows), BF),) * rows if keep else ()),
+            (parts[0], *late(parts[1:]), inner[1], Late(projected[m][4]), Late(gain_a), inner[0],
+             *tables),
             qkv_flops, (dense,), [pltpu.VMEM((tokens, qkv_width), BF)] + qkv_scratch,
-            scalars=(here,), waits=waits,
+            (here,), waits,
         )
-
-    def by_columns(value):
-        cut = value.reshape(rows, columns, shard, value.shape[1]).transpose(1, 0, 2, 3)
-        return over_columns(cut.reshape(columns, rows * shard, value.shape[1]))
 
     entering = [inputs[m, 0] for m in pieces]
     targets = [cotangent[m, 0] for m in pieces]
-    here_by_now = (gate_shards[2], up_shards[2])
-    results, unused, down_shards = forward(entering, entering, (), (here_by_now, ()))[6:]
-    came = [lax.ppermute(r[1], "section", [(0, 1)]) for r in results]
-
-    kept = forward(came, entering, targets, ((), ()))
-    projected, pairs, attended, arrived, applied, returned, results, lefts, unused = kept
-    hidden = [a[1] for a in applied]
-    done = [r[0] for r in results]
-
-    inner, outer = [], []
-    for m in pieces:
-        waits = (*done, *lefts[1:], outer[0][0]) if m else (applied[1][0],)
-        inner.append(attention_back(False, m, targets[m], returned[m], waits))
-        outer.append(projection_back(False, m, inner[m], parts_of(inner[m]), ()))
-    came = [lax.ppermute(o[1], "section", [(1, 0)]) for o in outer]
-
-    sent = [
+    kept = forward(entering, entering, (), (gate_shards[2], up_shards[2]), down_shards)
+    attended, applied, down_shards = kept[2], kept[4], kept[6]
+    returned = [over_columns(a[0]) for a in applied]
+    results = [
         call(
-            send_grads, (token_low, block_like),
-            (came[m], targets[m], attended[m][3], dispatches[m]),
-            2 * slots * tokens * width, scalars=(1 - second,),
+            combine, (Sent(token_wide), token_low),
+            late([returned[m], attended[m][0], attended[m][1], spread, places[m]]),
+            2 * slots * tokens * width, waits=() if m else (applied[1][0],),
         )
         for m in pieces
     ]
-    arrived_grads = [over_columns(s[1]) for s in sent]
+    came = [lax.ppermute(r[1], "section", [(0, 1)]) for r in results]
+
+    kept = forward(came, entering, targets, (), down_shards)
+    projected, pairs, attended, arrived, applied, lefts, down_shards = kept
+    hidden = [a[1] for a in applied]
+    shared = [over_columns(a[4]) for a in applied]
+    inner, outer = [], []
+    for m in pieces:
+        waits = (*lefts[1:], outer[0][0]) if m else (applied[1][4],)
+        inner.append(attention_back(False, m, targets[m], shared[m], waits))
+        outer.append(projection_back(False, m, inner[m], parts_of(inner[m]), ()))
+    came = [lax.ppermute(o[0], "section", [(1, 0)]) for o in outer]
+
+    given = [
+        call(
+            send_grads, (Sent(token_low), Sent(block_like)),
+            (came[m], *late([targets[m], attended[m][1], dispatches[m]])),
+            2 * slots * tokens * width, scalars=(first_flag,),
+        )
+        for m in pieces
+    ]
+    arrived_grads = [over_columns(g[1]) for g in given]
     moved = [
         call(
-            expert_backward, (block_like, kept_like, kept_like),
-            (arrived_grads[m], applied[m][2], applied[m][3]), 3 * expert_flops,
-            (*down_shards, *gate_shards, *up_shards), expert_scratch,
-            waits=() if m else (sent[1][1],),
+            expert_backward, (Sent(back_like), Sent(kept_like), Sent(kept_like)),
+            late([arrived_grads[m], hidden[m], applied[m][2], applied[m][3], applied[m][0]]),
+            3 * expert_flops, (*down_shards, *gate_shards, *up_shards), expert_scratch,
+            (second,), () if m else (given[1][1],),
         )
         for m in pieces
     ]
     back = [over_columns(a[0]) for a in moved]
-    operands = (
-        (hidden, [a[1] for a in moved], [a[2] for a in moved]), (arrived_grads, arrived, arrived),
-        (0, 0, 0),
-    )
-    far, near = far_and_near(*operands, 1), far_and_near(*operands, 0)
+    far, near = far_and_near(1), far_and_near(0)
     crossed = [swapped(merged(far[0], ()), 2)]
 
-    inner = [attention_back(
-        True, 0, sent[0][0], back[0], (moved[1][0], *(p[0] for p in far), near[0][0]),
-    )]
+    inner = [attention_back(True, 0, given[0][0], back[0], (moved[1][0],))]
     parts = [parts_of(inner[0])]
     outer = [projection_back(True, 0, inner[0], parts[0], ())]
-    inner.append(attention_back(True, 1, sent[1][0], back[1], (inner[0][0], crossed[0])))
+    inner.append(attention_back(
+        True, 1, given[1][0], back[1], (inner[0][0], *(f[0] for f in far), near[0][0])
+    ))
     parts.append(parts_of(inner[1]))
     crossed.append(swapped(merged(far[1], parts[1][1:]), 2))
     o_grads = call(
-        out_grads, (like((width, share), BF),),
-        (*lefts, *[p[s] for s in steps for p in parts]), 2 * width * length * micro * share,
-        waits=(outer[0][0],),
+        out_grads, (Sent(like((columns, rows * shard, share), BF)),),
+        late([*lefts, *[p[s] for s in steps for p in parts]]),
+        2 * width * length * micro * share, waits=(crossed[0],),
     )[0]
     outer.append(projection_back(True, 1, inner[1], parts[1], (o_grads,)))
     backs = [[o[3]] + [swapped(o[3 + s], s) for s in steps[1:]] for o in outer]
+    last = merged(far[2], backs[1][1:])
+    crossed.append(swapped(last, 2))
     w_grads = call(
-        qkv_grads, (like((width, qkv_width // rows + LANES), BF),),
-        (*lefts, *[b[s] for s in steps for b in backs], *[a[2] for a in attended],
-         *[a[6] for a in inner], *[o[2] for o in outer], *[a[7] for a in inner]),
-        2 * width * length * micro * qkv_width // rows, waits=(near[1][0], crossed[1]),
+        qkv_grads, (Sent(like((columns, rows * shard, qkv_width // rows + LANES), BF)),),
+        late([*lefts, *[b[s] for s in steps for b in backs], *[a[5] for a in attended],
+              *[a[6] for a in inner], *[o[2] for o in outer], *[a[7] for a in inner]]),
+        2 * width * length * micro * qkv_width // rows,
+        waits=(near[1][0], crossed[1], last),
     )[0]
-    crossed.append(swapped(merged(far[2], backs[1][1:]), 2))
     expert_grads = [
         n[0].astype(F32) + swapped(n[1], 1).astype(F32) + c.astype(F32)
         for n, c in zip(near, crossed)
     ]
-
+    layer_outputs = call(
+        last_outputs, (Sent(like((micro, tokens, width), F32)),),
+        late([spread] + [v for m in pieces for v in (
+            back[m], attended[m][0], attended[m][1], places[m], results[m][0])]),
+        4 * slots * tokens * width, scalars=(second,), waits=(w_grads,),
+    )[0]
+
+    wide = share + qkv_width // rows + LANES
     pieces_out = call(
-        fold, (like((shard, share + qkv_width // rows + LANES), F32),) * rows,
-        (by_columns(o_grads), by_columns(w_grads)), 0,
-        scratch=[pltpu.VMEM((rows * shard, share + qkv_width // rows + LANES), F32)],
-        scalars=(here,),
+        fold, (like((shard, wide), F32),) * rows,
+        late([over_columns(o_grads), over_columns(w_grads)]), 0,
+        scratch=[pltpu.VMEM((rows * shard, wide), F32)], scalars=(here,),
     )
     pieces_out = [pieces_out[0]] + [swapped(pieces_out[s], s) for s in steps[1:]]
     o_grad, q_grad, k_grad, v_grad, rest = call(
@@ -762,8 +919,8 @@
     )
 
     return (
-        jnp.stack(done)[None, :, None],
-        jnp.stack([o[0] for o in outer])[None, :, None],
+        layer_outputs[None, :, None],
+        jnp.stack([o[1] for o in outer])[None, :, None],
         rest[:, LANES - 2][None],
         q_grad[None],
         k_grad[None],

time: 814 us -> 771 us (0.947)
  local copies, waits for them, and re-layouts: 105 us -> 37.4 us
  Pallas kernels: 229 us -> 292 us
  waiting for transfers between devices: 255 us -> 226 us
    unnamed x456 -> x140, local copies, waits for them, and re-layouts: 93.1 us -> 25.7 us
    pallas_call x42 -> x41, Pallas kernels: 229 us -> 292 us  [call(): pl.pallas_call(run, out_shape=tuple(shapes), in_specs=[pl.BlockSpec(memor...]
    ppermute x54, waiting for transfers between devices: 81.7 us -> 56.5 us  [swapped(): return lax.ppermute(value, 'row', [(r, r ^ step) for r in range(rows)])]
  transfers between devices with their start and end apart: 73 -> 73, of which waited for: 28 -> 27; matrix products, arithmetic and copies ran while one was open for 3% -> 3% of each run, Pallas kernels for 27% -> 37%
where the time goes in v5:
time: 771 us; the launch traced here: 757 us
  Pallas kernels  292 us (38%)
  waiting for transfers between devices  226 us (29%)
  starting transfers between devices  168 us (22%)
  local copies, waits for them, and re-layouts  37.4 us (5%)
  other arithmetic  18.1 us (2%)
  between operations  15.7 us (2%)
    pallas_call x41, Pallas kernels, call(): pl.pallas_call(run, out_shape=tuple(shapes), in_specs=[pl.BlockSpec(memor...  292 us
    all_gather x1, waiting for transfers between devices, on_device(): dense = lax.all_gather(dense, ('row', 'col'), axis=0, tiled=True)  91.7 us
    all_to_all x14, starting transfers between devices, over_columns(): return lax.all_to_all(value, 'col', split_axis=0, concat_axis=0, tiled=True)  90.1 us
    ppermute x54, starting transfers between devices, swapped(): return lax.ppermute(value, 'row', [(r, r ^ step) for r in range(rows)])  69.4 us
    ppermute x54, waiting for transfers between devices, swapped(): return lax.ppermute(value, 'row', [(r, r ^ step) for r in range(rows)])  56.5 us
    all_to_all x14, waiting for transfers between devices, over_columns(): return lax.all_to_all(value, 'col', split_axis=0, concat_axis=0, tiled=True)  50.2 us
    unnamed x140, local copies, waits for them, and re-layouts  25.7 us
  transfers between devices with their start and end apart: 73, of which 27 were waited for; matrix products, arithmetic and copies ran while one was open for 3% of the time, Pallas kernels for 37%

profile of v5, /device:TPU:9, one launch (start us, length us, event | category | flops | bytes accessed | tf_op | source)
XLA Modules:
  0.0 757.3 jit_solution(9290095274142609315)
XLA Ops:
  18.6 91.7 %all-gather.2.cloned.1.call-done.refs_6_.refs_10_.refs_11_.refs_17_ = bf16[1536,3712]{1,0:T(8,128)(2,1)} async-done(((bf16[24,3712]{1,0:T(8,128)(2,1)}), bf16[1536,3712]{1,0:T(8,128)(2,1)}) %all-gather.2.cloned.1.call-update) | async-done | bytes 11403280 | tf_op jit(solution)/shard_map/all_gather | solution.py:652
  132.6 7.0 attend.4
  151.6 24.4 %collective-permute-done.12.refs_4_ = bf16[96,512]{1,0:T(8,128)(2,1)S(1)} collective-permute-done((bf16[96,512]{1,0:T(8,128)(2,1)S(1)}, bf16[96,512]{1,0:T(8,128)(2,1)S(1)}, u32[]{:S(2)}, u32[]{:S(2)}) %collective-permute-start.12) | collective-permute-done | bytes 98336 | tf_op jit(solution)/shard_map/ppermute | solution.py:151
  179.1 7.1 attend.5
  195.1 12.5 %expert_forward.4 = bf16[16,32,1536]{2,1,0:T(8,128)(2,1)} custom-call(bf16[16,32,1536]{2,1,0:T(8,128)(2,1)} %all-to-all-done.refs_0_, bf16[2,192,1536]{2,1,0:T(8,128)(2,1)} %bitcast.10.refs_1_.refs_10_, bf16[2,192,1536]{2,1,0:T(8,128)(2,1)} %collective-permute-done.5.refs_2_.refs_11_, bf16[2,192,1536]{2,1,0:T(8,128)(2,1)} %copy-done.1, ...), custom_call_target="tpu_custom_call" | custom-call | flops 3623878656 | bytes 17301504 | tf_op jit(solution)/shard_map/expert_forward/pallas_call | solution.py:112
  207.6 7.9 %all-to-all-done.2.refs_0_ = bf16[16,32,1536]{2,1,0:T(8,128)(2,1)} async-done(((bf16[16,32,1536]{2,1,0:T(8,128)(2,1)}), bf16[16,32,1536]{2,1,0:T(8,128)(2,1)}, u32[]{:S(2)}, u32[]{:S(2)}) %all-to-all-start.2) | async-done | bytes 1572896 | tf_op jit(solution)/shard_map/all_to_all | solution.py:619
  220.3 12.5 %expert_forward.5.refs_5_ = bf16[16,32,1536]{2,1,0:T(8,128)(2,1)} custom-call(bf16[16,32,1536]{2,1,0:T(8,128)(2,1)} %all-to-all-done.2.refs_0_, bf16[2,192,1536]{2,1,0:T(8,128)(2,1)} %bitcast.10.refs_1_.refs_10_, bf16[2,192,1536]{2,1,0:T(8,128)(2,1)} %collective-permute-done.5.refs_2_.refs_11_, bf16[2,192,1536]{2,1,0:T(8,128)(2,1)} %copy-done.1, ...), custom_call_target="tpu_custom_call" | custom-call | flops 3623878656 | bytes 17301504 | tf_op jit(solution)/shard_map/expert_forward/pallas_call | solution.py:112
  232.8 7.6 %all-to-all-done.1.refs_0_ = bf16[16,32,1536]{2,1,0:T(8,128)(2,1)S(1)} async-done(((bf16[16,32,1536]{2,1,0:T(8,128)(2,1)}), bf16[16,32,1536]{2,1,0:T(8,128)(2,1)S(1)}, u32[]{:S(2)}, u32[]{:S(2)}) %all-to-all-start.1) | async-done | bytes 1572896 | tf_op jit(solution)/shard_map/all_to_all | solution.py:619
  260.1 7.0 project.6
  279.8 8.3 %attend.6 = (f32[96,1536]{1,0:T(8,128)}, f32[96,128]{1,0:T(8,128)}, bf16[16,64,1536]{2,1,0:T(8,128)(2,1)}, bf16[2,576,384]{2,1,0:T(8,128)(2,1)}, bf16[96,1536]{1,0:T(8,128)(2,1)}, /*index=5*/bf16[96,1536]{1,0:T(8,128)(2,1)}) custom-call(f32[96,1536]{1,0:T(8,128)} %get-tuple-element.146.refs_0_.refs_7_, bf16[96,1536]{1,0:T(8,128)(2,1)} %get-tuple-element.147.refs_1_, ...), custom_call_target="tpu_custom_call" | custom-call | flops 830472192 | bytes 18536448 | tf_op jit(solution)/shard_map/attend/pallas_call | solution.py:112
  301.2 8.9 %collective-permute-done.19.refs_1_ = bf16[96,1536]{1,0:T(8,128)(2,1)S(1)} collective-permute-done((bf16[96,1536]{1,0:T(8,128)(2,1)}, bf16[96,1536]{1,0:T(8,128)(2,1)S(1)}, u32[]{:S(2)}, u32[]{:S(2)}) %collective-permute-start.19) | collective-permute-done | bytes 294944 | tf_op jit(solution)/shard_map/ppermute | solution.py:837
  310.8 6.9 project.7
  328.4 8.3 %attend.7 = (f32[96,1536]{1,0:T(8,128)}, f32[96,128]{1,0:T(8,128)}, bf16[16,64,1536]{2,1,0:T(8,128)(2,1)}, bf16[2,576,384]{2,1,0:T(8,128)(2,1)}, bf16[96,1536]{1,0:T(8,128)(2,1)}, /*index=5*/bf16[96,1536]{1,0:T(8,128)(2,1)}) custom-call(f32[96,1536]{1,0:T(8,128)} %get-tuple-element.153.refs_0_, bf16[96,1536]{1,0:T(8,128)(2,1)} %get-tuple-element.154.refs_1_, ...), custom_call_target="tpu_custom_call" | custom-call | flops 830472192 | bytes 18536448 | tf_op jit(solution)/shard_map/attend/pallas_call | solution.py:112
  339.0 11.0 %all-to-all-start.6 = ((bf16[16,64,1536]{2,1,0:T(8,128)(2,1)}), bf16[16,64,1536]{2,1,0:T(8,128)(2,1)}, u32[]{:S(2)}, u32[]{:S(2)}) async-start(bf16[16,64,1536]{2,1,0:T(8,128)(2,1)} %get-tuple-element.156.refs_13_), calls=%async_computation.6 | async-start | bytes 6291456 | tf_op jit(solution)/shard_map/all_to_all | solution.py:619
  353.4 18.9 %expert_forward.6 = (bf16[16,32,1536]{2,1,0:T(8,128)(2,1)}, bf16[2,256,768]{2,1,0:T(8,128)(2,1)}, bf16[2,256,768]{2,1,0:T(8,128)(2,1)}, bf16[2,256,768]{2,1,0:T(8,128)(2,1)}, bf16[16,32,1664]{2,1,0:T(8,128)(2,1)}) custom-call(bf16[16,64,1536]{2,1,0:T(8,128)(2,1)} %copy-done, bf16[2,192,1536]{2,1,0:T(8,128)(2,1)} %bitcast.10.refs_1_.refs_10_, ...), custom_call_target="tpu_custom_call" | custom-call | flops 7247757312 | bytes 22937600 | tf_op jit(solution)/shard_map/expert_forward/pallas_call | solution.py:112
  372.3 17.5 %all-to-all-done.6.refs_0_.refs_3_ = bf16[16,64,1536]{2,1,0:T(8,128)(2,1)} async-done(((bf16[16,64,1536]{2,1,0:T(8,128)(2,1)}), bf16[16,64,1536]{2,1,0:T(8,128)(2,1)}, u32[]{:S(2)}, u32[]{:S(2)}) %all-to-all-start.6) | async-done | bytes 3145760 | tf_op jit(solution)/shard_map/all_to_all | solution.py:619
  393.8 18.9 %expert_forward.7 = (bf16[16,32,1536]{2,1,0:T(8,128)(2,1)}, bf16[2,256,768]{2,1,0:T(8,128)(2,1)}, bf16[2,256,768]{2,1,0:T(8,128)(2,1)}, bf16[2,256,768]{2,1,0:T(8,128)(2,1)}, bf16[16,32,1664]{2,1,0:T(8,128)(2,1)}) custom-call(bf16[16,64,1536]{2,1,0:T(8,128)(2,1)} %all-to-all-done.6.refs_0_.refs_3_, bf16[2,192,1536]{2,1,0:T(8,128)(2,1)} %bitcast.10.refs_1_.refs_10_, ...), custom_call_target="tpu_custom_call" | custom-call | flops 7247757312 | bytes 22937600 | tf_op jit(solution)/shard_map/expert_forward/pallas_call | solution.py:112
  415.1 7.0 all-to-all-start.8
  422.1 8.3 %attend_back.4 = (f32[96,1536]{1,0:T(8,128)}, bf16[96,1536]{1,0:T(8,128)(2,1)}, bf16[96,512]{1,0:T(8,128)(2,1)}, bf16[96,512]{1,0:T(8,128)(2,1)}, bf16[96,512]{1,0:T(8,128)(2,1)}, /*index=5*/bf16[96,512]{1,0:T(8,128)(2,1)}) custom-call(s32[1]{0:T(128)} %bitcast.1.refs_0_, s32[1]{0:T(128)} %bitcast.refs_0_.refs_1_, bf16[16,32,1664]{2,1,0:T(8,128)(2,1)} %copy-done.11, ...), custom_call_target="tpu_custom_call" | custom-call | flops 1056964608 | bytes 17225728 | tf_op jit(solution)/shard_map/attend_back/pallas_call | solution.py:112
  443.1 7.3 project_back.4.refs_21_
  470.9 8.4 %attend_back.5 = (f32[96,1536]{1,0:T(8,128)}, bf16[96,1536]{1,0:T(8,128)(2,1)}, bf16[96,512]{1,0:T(8,128)(2,1)}, bf16[96,512]{1,0:T(8,128)(2,1)}, bf16[96,512]{1,0:T(8,128)(2,1)}, /*index=5*/bf16[96,512]{1,0:T(8,128)(2,1)}) custom-call(s32[1]{0:T(128)} %bitcast.1.refs_0_, s32[1]{0:T(128)} %bitcast.refs_0_.refs_1_, bf16[16,32,1664]{2,1,0:T(8,128)(2,1)} %copy-done.10, ...), custom_call_target="tpu_custom_call" | custom-call | flops 1056964608 | bytes 17225728 | tf_op jit(solution)/shard_map/attend_back/pallas_call | solution.py:112
  489.9 7.3 project_back.5
  513.0 7.6 %all-to-all-start.10 = ((bf16[16,32,1536]{2,1,0:T(8,128)(2,1)}), bf16[16,32,1536]{2,1,0:T(8,128)(2,1)S(1)}, u32[]{:S(2)}, u32[]{:S(2)}) async-start(bf16[16,32,1536]{2,1,0:T(8,128)(2,1)} %get-tuple-element.192.refs_18_), calls=%async_computation.10 | async-start | bytes 3145728 | tf_op jit(solution)/shard_map/all_to_all | solution.py:619
  520.6 12.5 %expert_backward.2 = (bf16[16,32,1664]{2,1,0:T(8,128)(2,1)}, bf16[2,256,768]{2,1,0:T(8,128)(2,1)}, bf16[2,256,768]{2,1,0:T(8,128)(2,1)}) custom-call(s32[1]{0:T(128)} %bitcast.refs_0_.refs_1_, bf16[16,32,1536]{2,1,0:T(8,128)(2,1)} %copy-done.6, bf16[2,256,768]{2,1,0:T(8,128)(2,1)} %get-tuple-element.176.refs_2_.refs_0_, ...), custom_call_target="tpu_custom_call" | custom-call | flops 3623878656 | bytes 22937600 | tf_op jit(solution)/shard_map/expert_backward/pallas_call | solution.py:112
  533.1 8.0 %all-to-all-done.10.refs_1_.refs_3_ = bf16[16,32,1536]{2,1,0:T(8,128)(2,1)S(1)} async-done(((bf16[16,32,1536]{2,1,0:T(8,128)(2,1)}), bf16[16,32,1536]{2,1,0:T(8,128)(2,1)S(1)}, u32[]{:S(2)}, u32[]{:S(2)}) %all-to-all-start.10) | async-done | bytes 1572896 | tf_op jit(solution)/shard_map/all_to_all | solution.py:619
  556.2 12.5 %expert_backward.3 = (bf16[16,32,1664]{2,1,0:T(8,128)(2,1)}, bf16[2,256,768]{2,1,0:T(8,128)(2,1)}, bf16[2,256,768]{2,1,0:T(8,128)(2,1)}) custom-call(s32[1]{0:T(128)} %bitcast.refs_0_.refs_1_, bf16[16,32,1536]{2,1,0:T(8,128)(2,1)} %copy-done.7, bf16[2,256,768]{2,1,0:T(8,128)(2,1)} %get-tuple-element.195.refs_2_.refs_1_, ...), custom_call_target="tpu_custom_call" | custom-call | flops 3623878656 | bytes 22937600 | tf_op jit(solution)/shard_map/expert_backward/pallas_call | solution.py:112
  601.5 9.0 %attend_back.6 = (f32[96,1536]{1,0:T(8,128)}, bf16[96,1536]{1,0:T(8,128)(2,1)}, bf16[96,896]{1,0:T(8,128)(2,1)}, bf16[96,896]{1,0:T(8,128)(2,1)}, bf16[96,896]{1...) custom-call(s32[1]{0:T(128)} %bitcast.1.refs_0_, s32[1]{0:T(128)} %bitcast.refs_0_.refs_1_, ...), custom_call_target="tpu_custom_call" | custom-call | flops 1056964608 | bytes 19167232 | tf_op jit(solution)/shard_map/attend_back/pallas_call | solution.py:112
  611.7 9.0 %attend_back.7 = (f32[96,1536]{1,0:T(8,128)}, bf16[96,1536]{1,0:T(8,128)(2,1)}, bf16[96,896]{1,0:T(8,128)(2,1)}, bf16[96,896]{1,0:T(8,128)(2,1)}, bf16[96,896]{1...) custom-call(s32[1]{0:T(128)} %bitcast.1.refs_0_, s32[1]{0:T(128)} %bitcast.refs_0_.refs_1_, ...), custom_call_target="tpu_custom_call" | custom-call | flops 1056964608 | bytes 19167232 | tf_op jit(solution)/shard_map/attend_back/pallas_call | solution.py:112
  646.2 7.0 all-to-all-start.12
  653.7 8.4 %project_back.7 = (bf16[96,1536]{1,0:T(8,128)(2,1)}, f32[96,1536]{1,0:T(8,128)}, f32[8,1536]{1,0:T(8,128)}, bf16[96,512]{1,0:T(8,128)(2,1)}, bf16[96,512]{1,0:T(...) custom-call(s32[1]{0:T(128)} %bitcast.1.refs_0_, bf16[96,896]{1,0:T(8,128)(2,1)} %get-tuple-element.218.refs_5_.refs_1_, ...), custom_call_target="tpu_custom_call" | custom-call | flops 603979776 | bytes 14997504 | tf_op jit(solution)/shard_map/project_back/pallas_call | solution.py:112
  665.8 8.4 %project_back.6 = (bf16[96,1536]{1,0:T(8,128)(2,1)}, f32[96,1536]{1,0:T(8,128)}, f32[8,1536]{1,0:T(8,128)}, bf16[96,512]{1,0:T(8,128)(2,1)}, bf16[96,512]{1,0:T(...) custom-call(s32[1]{0:T(128)} %bitcast.1.refs_0_, bf16[96,896]{1,0:T(8,128)(2,1)} %get-tuple-element.202.refs_1_.refs_4_, ...), custom_call_target="tpu_custom_call" | custom-call | flops 603979776 | bytes 14997504 | tf_op jit(solution)/shard_map/project_back/pallas_call | solution.py:112
  723.2 7.4 all-to-all-done.13.refs_2_
  (345 shorter events, 336.7 us)
Async XLA Ops:
  7.2 103.1 %all-gather.2.cloned.1.call-start = ((), (), s32[]{:S(2)}) async-start(), calls=%async_computation.14 | async-start | bytes 11581440 | tf_op jit(solution)/shard_map/all_gather | solution.py:652
  10.5 102.1 %collective-permute-start = (bf16[2,192,1536]{2,1,0:T(8,128)(2,1)}, bf16[2,192,1536]{2,1,0:T(8,128)(2,1)S(1)}, u32[]{:S(2)}, u32[]{:S(2)}) collective-permute-start(bf16[2,192,1536]{2,1,0:T(8,128)(2,1)} %bitcast.10.refs_1_.refs_10_), channel_id=1, source_target_pairs={{0,32},{16,48},{32,0},{48,16},{1,33},{17,49},{33,1},{49,17},{2,34}... | collective-permute-start | bytes 3538952 | tf_op jit(solution)/shard_map/ppermute | solution.py:151
  12.6 100.0 %collective-permute-start.1 = (bf16[2,192,1536]{2,1,0:T(8,128)(2,1)}, bf16[2,192,1536]{2,1,0:T(8,128)(2,1)S(1)}, u32[]{:S(2)}, u32[]{:S(2)}) collective-permute-start(bf16[2,192,1536]{2,1,0:T(8,128)(2,1)} %bitcast.11.refs_5_.refs_14_), channel_id=1, source_target_pairs={{0,32},{16,48},{32,0},{48,16},{1,33},{17,49},{33,1},{49,17},{2,34}... | collective-permute-start | bytes 3538952 | tf_op jit(solution)/shard_map/ppermute | solution.py:151
  139.7 47.7 %all-to-all-start = ((bf16[16,32,1536]{2,1,0:T(8,128)(2,1)}), bf16[16,32,1536]{2,1,0:T(8,128)(2,1)}, u32[]{:S(2)}, u32[]{:S(2)}) async-start(bf16[16,32,1536]{2,1,0:T(8,128)(2,1)} %get-tuple-element.139), calls=%async_computation | async-start | bytes 3145728 | tf_op jit(solution)/shard_map/all_to_all | solution.py:619
  144.8 41.5 %collective-permute-start.10 = (bf16[2,192,1536]{2,1,0:T(8,128)(2,1)}, bf16[2,192,1536]{2,1,0:T(8,128)(2,1)S(1)}, u32[]{:S(2)}, u32[]{:S(2)}) collective-permute-start(bf16[2,192,1536]{2,1,0:T(8,128)(2,1)} %bitcast.20.refs_9_.refs_6_), channel_id=1, source_target_pairs={{0,32},{16,48},{32,0},{48,16},{1,33},{17,49},{33,1},{49,17},{2,34}... | collective-permute-start | bytes 3538952 | tf_op jit(solution)/shard_map/ppermute | solution.py:151
  146.0 41.4 %collective-permute-start.5 = (bf16[2,192,1536]{2,1,0:T(8,128)(2,1)}, bf16[2,192,1536]{2,1,0:T(8,128)(2,1)}, u32[]{:S(2)}, u32[]{:S(2)}) collective-permute-start(bf16[2,192,1536]{2,1,0:T(8,128)(2,1)} %bitcast.10.refs_1_.refs_10_), channel_id=1, source_target_pairs={{0,16},{16,0},{32,48},{48,32},{1,17},{17,1},{33,49},{49,33},{2,18}... | collective-permute-start | bytes 3538952 | tf_op jit(solution)/shard_map/ppermute | solution.py:151
  146.6 29.5 %collective-permute-start.12 = (bf16[96,512]{1,0:T(8,128)(2,1)S(1)}, bf16[96,512]{1,0:T(8,128)(2,1)S(1)}, u32[]{:S(2)}, u32[]{:S(2)}) collective-permute-start(bf16[96,512]{1,0:T(8,128)(2,1)S(1)} %copy-done.39), channel_id=1, source_target_pairs={{0,32},{16,48},{32,0},{48,16},{1,33},{17,49},{33,1},{49,17},{2,34}... | collective-permute-start | bytes 294920 | tf_op jit(solution)/shard_map/ppermute | solution.py:151
  148.4 30.1 %collective-permute-start.13 = (bf16[96,512]{1,0:T(8,128)(2,1)S(1)}, bf16[96,512]{1,0:T(8,128)(2,1)S(1)}, u32[]{:S(2)}, u32[]{:S(2)}) collective-permute-start(bf16[96,512]{1,0:T(8,128)(2,1)S(1)} %copy-done.39), channel_id=1, source_target_pairs={{0,48},{16,32},{32,16},{48,0},{1,49},{17,33},{33,17},{49,1},{2,50}... | collective-permute-start | bytes 294920 | tf_op jit(solution)/shard_map/ppermute | solution.py:151
  151.6 42.4 %collective-permute-start.7 = (bf16[2,192,1536]{2,1,0:T(8,128)(2,1)}, bf16[2,192,1536]{2,1,0:T(8,128)(2,1)}, u32[]{:S(2)}, u32[]{:S(2)}) collective-permute-start(bf16[2,192,1536]{2,1,0:T(8,128)(2,1)} %bitcast.11.refs_5_.refs_14_), channel_id=1, source_target_pairs={{0,16},{16,0},{32,48},{48,32},{1,17},{17,1},{33,49},{49,33},{2,18}... | collective-permute-start | bytes 3538952 | tf_op jit(solution)/shard_map/ppermute | solution.py:151
  187.4 28.1 %all-to-all-start.2 = ((bf16[16,32,1536]{2,1,0:T(8,128)(2,1)}), bf16[16,32,1536]{2,1,0:T(8,128)(2,1)}, u32[]{:S(2)}, u32[]{:S(2)}) async-start(bf16[16,32,1536]{2,1,0:T(8,128)(2,1)} %get-tuple-element.142.refs_1_.refs_13_), calls=%async_computation.2 | async-start | bytes 3145728 | tf_op jit(solution)/shard_map/all_to_all | solution.py:619
  215.5 24.9 %all-to-all-start.1 = ((bf16[16,32,1536]{2,1,0:T(8,128)(2,1)}), bf16[16,32,1536]{2,1,0:T(8,128)(2,1)S(1)}, u32[]{:S(2)}, u32[]{:S(2)}) async-start(bf16[16,32,1536]{2,1,0:T(8,128)(2,1)} %expert_forward.4), calls=%async_computation.1 | async-start | bytes 3145728 | tf_op jit(solution)/shard_map/all_to_all | solution.py:619
  241.6 46.5 %all-to-all-start.4 = ((bf16[16,32,1536]{2,1,0:T(8,128)(2,1)}), bf16[16,32,1536]{2,1,0:T(8,128)(2,1)S(1)}, u32[]{:S(2)}, u32[]{:S(2)}) async-start(bf16[16,32,1536]{2,1,0:T(8,128)(2,1)} %expert_forward.5.refs_5_), calls=%async_computation.4 | async-start | bytes 3145728 | tf_op jit(solution)/shard_map/all_to_all | solution.py:619
  289.2 48.1 %all-to-all-start.3 = ((bf16[16,64,1536]{2,1,0:T(8,128)(2,1)}), bf16[16,64,1536]{2,1,0:T(8,128)(2,1)S(1)}, u32[]{:S(2)}, u32[]{:S(2)}) async-start(bf16[16,64,1536]{2,1,0:T(8,128)(2,1)} %get-tuple-element.149), calls=%async_computation.3 | async-start | bytes 6291456 | tf_op jit(solution)/shard_map/all_to_all | solution.py:619
  339.0 50.9 %all-to-all-start.6 = ((bf16[16,64,1536]{2,1,0:T(8,128)(2,1)}), bf16[16,64,1536]{2,1,0:T(8,128)(2,1)}, u32[]{:S(2)}, u32[]{:S(2)}) async-start(bf16[16,64,1536]{2,1,0:T(8,128)(2,1)} %get-tuple-element.156.refs_13_), calls=%async_computation.6 | async-start | bytes 6291456 | tf_op jit(solution)/shard_map/all_to_all | solution.py:619
  352.4 41.4 %collective-permute-start.23 = (bf16[4,96,1536]{2,1,0:T(8,128)(2,1)}, bf16[4,96,1536]{2,1,0:T(8,128)(2,1)}, u32[]{:S(2)}, u32[]{:S(2)}) collective-permute-start(bf16[4,96,1536]{2,1,0:T(8,128)(2,1)} %pack.1.refs_0_), channel_id=1, source_target_pairs={{0,32},{16,48},{32,0},{48,16},{1,33},{17,49},{33,1},{49,17},{2,34}... | collective-permute-start | bytes 3538952 | tf_op jit(solution)/shard_map/ppermute | solution.py:151
  389.8 24.0 %all-to-all-start.5 = ((bf16[16,32,1664]{2,1,0:T(8,128)(2,1)}), bf16[16,32,1664]{2,1,0:T(8,128)(2,1)S(1)}, u32[]{:S(2)}, u32[]{:S(2)}) async-start(bf16[16,32,1664]{2,1,0:T(8,128)(2,1)} %get-tuple-element.157), calls=%async_computation.5 | async-start | bytes 3407872 | tf_op jit(solution)/shard_map/all_to_all | solution.py:619
  415.1 48.0 %all-to-all-start.8 = ((bf16[16,32,1664]{2,1,0:T(8,128)(2,1)}), bf16[16,32,1664]{2,1,0:T(8,128)(2,1)S(1)}, u32[]{:S(2)}, u32[]{:S(2)}) async-start(bf16[16,32,1664]{2,1,0:T(8,128)(2,1)} %get-tuple-element.167.refs_18_), calls=%async_computation.8 | async-start | bytes 3407872 | tf_op jit(solution)/shard_map/all_to_all | solution.py:619
  451.9 19.0 %collective-permute-start.28 = (bf16[4,96,1536]{2,1,0:T(8,128)(2,1)}, bf16[4,96,1536]{2,1,0:T(8,128)(2,1)}, u32[]{:S(2)}, u32[]{:S(2)}) collective-permute-start(bf16[4,96,1536]{2,1,0:T(8,128)(2,1)} %pack.1.refs_0_), channel_id=1, source_target_pairs={{0,16},{16,0},{32,48},{48,32},{1,17},{17,1},{33,49},{49,33},{2,18}... | collective-permute-start | bytes 3538952 | tf_op jit(solution)/shard_map/ppermute | solution.py:151
  464.2 47.6 %all-to-all-start.7 = ((bf16[16,32,1536]{2,1,0:T(8,128)(2,1)}), bf16[16,32,1536]{2,1,0:T(8,128)(2,1)S(1)}, u32[]{:S(2)}, u32[]{:S(2)}) async-start(bf16[16,32,1536]{2,1,0:T(8,128)(2,1)} %get-tuple-element.175), calls=%async_computation.7 | async-start | bytes 3145728 | tf_op jit(solution)/shard_map/all_to_all | solution.py:619
  513.0 28.1 %all-to-all-start.10 = ((bf16[16,32,1536]{2,1,0:T(8,128)(2,1)}), bf16[16,32,1536]{2,1,0:T(8,128)(2,1)S(1)}, u32[]{:S(2)}, u32[]{:S(2)}) async-start(bf16[16,32,1536]{2,1,0:T(8,128)(2,1)} %get-tuple-element.192.refs_18_), calls=%async_computation.10 | async-start | bytes 3145728 | tf_op jit(solution)/shard_map/all_to_all | solution.py:619
  542.3 26.5 %all-to-all-start.9 = ((bf16[16,32,1664]{2,1,0:T(8,128)(2,1)}), bf16[16,32,1664]{2,1,0:T(8,128)(2,1)}, u32[]{:S(2)}, u32[]{:S(2)}) async-start(bf16[16,32,1664]{2,1,0:T(8,128)(2,1)} %get-tuple-element.193), calls=%async_computation.9 | async-start | bytes 3407872 | tf_op jit(solution)/shard_map/all_to_all | solution.py:619
  552.1 30.7 %collective-permute-start.40 = (bf16[2,192,1536]{2,1,0:T(8,128)(2,1)}, bf16[2,192,1536]{2,1,0:T(8,128)(2,1)S(1)}, u32[]{:S(2)}, u32[]{:S(2)}) collective-permute-start(bf16[2,192,1536]{2,1,0:T(8,128)(2,1)} %get-tuple-element.224), channel_id=1, source_target_pairs={{0,16},{16,0},{32,48},{48,32},{1,17},{17,1},{33,49},{49,33},{2,18}... | collective-permute-start | bytes 3538952 | tf_op jit(solution)/shard_map/ppermute | solution.py:151
  568.8 41.7 %all-to-all-start.11 = ((bf16[16,32,1664]{2,1,0:T(8,128)(2,1)}), bf16[16,32,1664]{2,1,0:T(8,128)(2,1)S(1)}, u32[]{:S(2)}, u32[]{:S(2)}) async-start(bf16[16,32,1664]{2,1,0:T(8,128)(2,1)} %get-tuple-element.199.refs_18_), calls=%async_computation.11 | async-start | bytes 3407872 | tf_op jit(solution)/shard_map/all_to_all | solution.py:619
  581.8 42.6 %collective-permute-start.48 = (bf16[2,192,1536]{2,1,0:T(8,128)(2,1)}, bf16[2,192,1536]{2,1,0:T(8,128)(2,1)}, u32[]{:S(2)}, u32[]{:S(2)}) collective-permute-start(bf16[2,192,1536]{2,1,0:T(8,128)(2,1)} %get-tuple-element.241), channel_id=1, source_target_pairs={{0,16},{16,0},{32,48},{48,32},{1,17},{17,1},{33,49},{49,33},{2,18}... | collective-permute-start | bytes 3538952 | tf_op jit(solution)/shard_map/ppermute | solution.py:151
  586.7 53.6 %collective-permute-start.41 = (bf16[2,192,1536]{2,1,0:T(8,128)(2,1)}, bf16[2,192,1536]{2,1,0:T(8,128)(2,1)}, u32[]{:S(2)}, u32[]{:S(2)}) collective-permute-start(bf16[2,192,1536]{2,1,0:T(8,128)(2,1)} %add.136), channel_id=1, source_target_pairs={{0,32},{16,48},{32,0},{48,16},{1,33},{17,49},{33,1},{49,17},{2,34}... | collective-permute-start | bytes 3538952 | tf_op jit(solution)/shard_map/ppermute | solution.py:151
  624.4 39.1 %collective-permute-start.50 = (bf16[2,192,1536]{2,1,0:T(8,128)(2,1)}, bf16[2,192,1536]{2,1,0:T(8,128)(2,1)}, u32[]{:S(2)}, u32[]{:S(2)}) collective-permute-start(bf16[2,192,1536]{2,1,0:T(8,128)(2,1)} %get-tuple-element.242), channel_id=1, source_target_pairs={{0,16},{16,0},{32,48},{48,32},{1,17},{17,1},{33,49},{49,33},{2,18}... | collective-permute-start | bytes 3538952 | tf_op jit(solution)/shard_map/ppermute | solution.py:151
  636.5 50.9 %collective-permute-start.49 = (bf16[2,192,1536]{2,1,0:T(8,128)(2,1)}, bf16[2,192,1536]{2,1,0:T(8,128)(2,1)S(1)}, u32[]{:S(2)}, u32[]{:S(2)}) collective-permute-start(bf16[2,192,1536]{2,1,0:T(8,128)(2,1)} %add.137), channel_id=1, source_target_pairs={{0,32},{16,48},{32,0},{48,16},{1,33},{17,49},{33,1},{49,17},{2,34}... | collective-permute-start | bytes 3538952 | tf_op jit(solution)/shard_map/ppermute | solution.py:151
  646.2 48.5 %all-to-all-start.12 = ((bf16[16,96,384]{2,1,0:T(8,128)(2,1)}), bf16[16,96,384]{2,1,0:T(8,128)(2,1)S(1)}, u32[]{:S(2)}, u32[]{:S(2)}) async-start(bf16[16,96,384]{2,1,0:T(8,128)(2,1)} %out_grads.1.refs_12_), calls=%async_computation.12 | async-start | bytes 2359296 | tf_op jit(solution)/shard_map/all_to_all | solution.py:619
  653.2 58.6 %collective-permute-start.57 = (bf16[2,192,1536]{2,1,0:T(8,128)(2,1)}, bf16[2,192,1536]{2,1,0:T(8,128)(2,1)}, u32[]{:S(2)}, u32[]{:S(2)}) collective-permute-start(bf16[2,192,1536]{2,1,0:T(8,128)(2,1)} %get-tuple-element.257), channel_id=1, source_target_pairs={{0,16},{16,0},{32,48},{48,32},{1,17},{17,1},{33,49},{49,33},{2,18}... | collective-permute-start | bytes 3538952 | tf_op jit(solution)/shard_map/ppermute | solution.py:151
  695.8 34.8 %all-to-all-start.13 = ((bf16[16,96,640]{2,1,0:T(8,128)(2,1)}), bf16[16,96,640]{2,1,0:T(8,128)(2,1)S(1)}, u32[]{:S(2)}, u32[]{:S(2)}) async-start(bf16[16,96,640]{2,1,0:T(8,128)(2,1)} %qkv_grads.1.refs_12_), calls=%async_computation.13 | async-start | bytes 3932160 | tf_op jit(solution)/shard_map/all_to_all | solution.py:619
  709.1 30.5 %collective-permute-start.55 = (bf16[2,192,1536]{2,1,0:T(8,128)(2,1)}, bf16[2,192,1536]{2,1,0:T(8,128)(2,1)}, u32[]{:S(2)}, u32[]{:S(2)}) collective-permute-start(bf16[2,192,1536]{2,1,0:T(8,128)(2,1)} %get-tuple-element.256), channel_id=1, source_target_pairs={{0,16},{16,0},{32,48},{48,32},{1,17},{17,1},{33,49},{49,33},{2,18}... | collective-permute-start | bytes 3538952 | tf_op jit(solution)/shard_map/ppermute | solution.py:151
  710.6 29.2 %collective-permute-start.56 = (bf16[2,192,1536]{2,1,0:T(8,128)(2,1)}, bf16[2,192,1536]{2,1,0:T(8,128)(2,1)}, u32[]{:S(2)}, u32[]{:S(2)}) collective-permute-start(bf16[2,192,1536]{2,1,0:T(8,128)(2,1)} %add.138.refs_22_), channel_id=1, source_target_pairs={{0,32},{16,48},{32,0},{48,16},{1,33},{17,49},{33,1},{49,17},{2,34}... | collective-permute-start | bytes 3538952 | tf_op jit(solution)/shard_map/ppermute | solution.py:151
  (110 other events, 942.7 us)
Sparse Core Ops, SparseCore 0:
  11.7 98.5 all-gather.1

commit v6 on v5

--- a/solution.py
+++ b/solution.py
@@ -49,8 +49,8 @@
 
 
 class Sent:
-    def __init__(self, source, target=None, sem=None):
-        self.source, self.target, self.sem, self.copy = source, target, sem, None
+    def __init__(self, source, target=None, sems=None):
+        self.source, self.target, self.sems, self.copies = source, target, sems, []
 
     def __getitem__(self, index):
         return self.source[index]
@@ -58,27 +58,44 @@
     def __setitem__(self, index, value):
         self.source[index] = value
 
-    def send(self):
-        self.copy = pltpu.make_async_copy(self.source, self.target, self.sem)
-        self.copy.start()
+    def send(self, *parts):
+        for part in parts or (...,):
+            at = len(self.copies)
+            whole = part is ...
+            copy = pltpu.make_async_copy(
+                self.source if whole else self.source.at[part],
+                self.target if whole else self.target.at[part],
+                self.sems.at[at],
+            )
+            copy.start()
+            self.copies.append(copy)
 
     @property
     def shape(self):
         return self.source.shape
 
 
-def sent(out):
+class Raw:
+    def __init__(self, source):
+        self.source = source
+
+
+PARTS = 4
+
+
+def sent(out, *parts):
     if isinstance(out, Sent):
-        out.send()
+        out.send(*parts)
 
 
 def call(body, outs, args, flops, far=(), scratch=(), scalars=(), waits=()):
     arrays = [a.source if isinstance(a, Late) else a for a in args]
-    shapes = [o.source if isinstance(o, Sent) else o for o in outs]
+    shapes = [o.source if isinstance(o, (Sent, Raw)) else o for o in outs]
     moved = sum(a.size * a.dtype.itemsize for a in (*arrays, *far, *shapes))
     count = len(scalars) + len(args) + len(far)
     kinds = [isinstance(a, Late) for a in args]
     out_kinds = [isinstance(o, Sent) for o in outs]
+    raw_kinds = [isinstance(o, Raw) for o in outs]
     buffers = [pltpu.VMEM(a.shape, a.dtype) for a, k in zip(arrays, kinds) if k]
     buffers += [pltpu.VMEM(o.shape, o.dtype) for o, k in zip(shapes, out_kinds) if k]
 
@@ -88,10 +105,10 @@
         own, rest = list(refs[: len(buffers)]), refs[len(buffers) :]
         sems, rest = (rest[0], rest[1:]) if buffers else (None, rest)
         used = 0
-        for k, late in enumerate(kinds):
-            if late:
+        for k, kind in enumerate(kinds):
+            if kind:
                 at = len(scalars) + k
-                given[at] = Late(given[at], own[used], sems.at[used])
+                given[at] = Late(given[at], own[used], sems.at[used, 0])
                 used += 1
         for k, kind in enumerate(out_kinds):
             if kind:
@@ -102,11 +119,11 @@
             if isinstance(one, Late):
                 one.ready()
         for one in results:
-            if isinstance(one, Sent) and one.copy is None:
+            if isinstance(one, Sent) and not one.copies:
                 one.send()
         for one in results:
             if isinstance(one, Sent):
-                one.copy.wait()
+                done_with(one.copies)
 
     anywhere, local = pl.BlockSpec(memory_space=pl.ANY), pl.BlockSpec(memory_space=pltpu.VMEM)
     return pl.pallas_call(
@@ -115,9 +132,11 @@
         in_specs=[pl.BlockSpec(memory_space=pltpu.SMEM)] * len(scalars)
         + [anywhere if k else local for k in kinds]
         + [anywhere] * (len(far) + len(waits)),
-        out_specs=tuple(anywhere if k else local for k in out_kinds),
+        out_specs=tuple(
+            anywhere if k or raw else local for k, raw in zip(out_kinds, raw_kinds)
+        ),
         scratch_shapes=buffers
-        + ([pltpu.SemaphoreType.DMA((len(buffers),))] if buffers else [])
+        + ([pltpu.SemaphoreType.DMA((len(buffers), PARTS))] if buffers else [])
         + list(scratch),
         compiler_params=pltpu.CompilerParams(vmem_limit_bytes=60 * MIB),
         cost_estimate=pl.CostEstimate(
@@ -187,9 +206,8 @@
 
 
 def project(
-    keep, flag, came, entering, gain, cosine, sine, dense, stream, query, pair, *rest
+    flag, came, entering, gain, cosine, sine, dense, stream, normed, query, pair, weights, sems
 ):
-    kept, (weights, sems) = rest[:-2], rest[-2:]
     width = stream.shape[1]
     cuts = cuts_of(weights.shape[1])
     copies = [
@@ -203,11 +221,7 @@
     x = jnp.where(flag[0] > 0, came[...].astype(F32), entering[...].astype(F32))
     stream[...] = x
     low = (x * norm_parts(x) * gain[...]).astype(BF)
-    if keep:
-        kept[0][...] = low
-        kept[1][...] = x
-        sent(kept[0])
-        sent(kept[1])
+    normed[...] = low
     keys = pair.shape[1] // 2
     for copy, (at, size) in zip(copies, cuts):
         copy.wait()
@@ -221,9 +235,6 @@
                 query[:, begin : begin + HEAD_DIM] = head
             else:
                 pair[:, begin - width : begin - width + HEAD_DIM] = head
-    if keep:
-        kept[2][...] = query[...]
-        kept[3][...] = pair[...]
 
 
 def slot_experts(slots):
@@ -240,7 +251,7 @@
 def attend(
     keep, stream, query, pair0, pair1, pair2, pair3, bias, gain, chosen, dispatch, *rest,
 ):
-    targets, rest = (rest[:1], rest[1:]) if keep else ((), rest)
+    (normed, target), rest = (rest[:2], rest[2:]) if keep else ((None, None), rest)
     dense, middle, gates, outgoing = rest[:4]
     kept, (mixed, weights, router, sems) = rest[4:-4], rest[-4:]
     width = stream.shape[1]
@@ -251,6 +262,10 @@
         pltpu.make_async_copy(dense.at[:, pl.ds(at + LANES, width)], weights, sems.at[0]),
         pltpu.make_async_copy(dense.at[:, pl.ds(at, LANES)], router, sems.at[1]),
     ]
+    if keep:
+        own = [(stream, kept[3]), (query, kept[4]), (normed, kept[5])]
+        own += [(p, kept[6].at[k]) for k, p in enumerate((pair0, pair1, pair2, pair3))]
+        copies += [pltpu.make_async_copy(a, b, sems.at[2 + k]) for k, (a, b) in enumerate(own)]
     for copy in copies:
         copy.start()
     pairs = jnp.concatenate([pair0[...], pair1[...], pair2[...], pair3[...]], 0)
@@ -292,32 +307,37 @@
     sent(gates)
     slots = dispatch[...]
     outgoing[:, :per, :] = dot(slots, low).astype(BF).reshape(block)
-    if targets:
-        outgoing[:, per:, :] = scaled_rows(slots, share, targets[0][...]).reshape(block)
-
-
-def fetch(shards, weights, sems):
-    copies = []
-    for j in range(weights.shape[1]):
-        line = []
-        for k in range(weights.shape[0]):
-            some = []
-            for p in range(4):
-                size = shards[k][p].shape[1]
-                some.append(
+    if keep:
+        sent(outgoing, (slice(None), pl.ds(0, per)))
+        outgoing[:, per:, :] = scaled_rows(slots, share, target[...]).reshape(block)
+        sent(outgoing, (slice(None), pl.ds(per, per)))
+    done_with(copies[2:])
+
+
+class Fetched:
+    def __init__(self, shards, weights, sems):
+        self.weights = weights
+        self.copies = {}
+        for j in range(weights.shape[1]):
+            for k in range(weights.shape[0]):
+                self.copies[k, j] = [
                     pltpu.make_async_copy(
                         shards[k][p].at[j],
-                        weights.at[k, j, pl.ds(p * size, size)],
+                        weights.at[k, j, pl.ds(p * shards[k][p].shape[1], shards[k][p].shape[1])],
                         sems.at[k, j, p],
                     )
-                )
-            line.append(some)
-        copies.append(line)
-    for line in copies:
-        for some in line:
-            for copy in some:
-                copy.start()
-    return copies
+                    for p in range(4)
+                ]
+        for k in range(weights.shape[0]):
+            self.start(k, 0)
+
+    def start(self, k, j):
+        for copy in self.copies.get((k, j), ()):
+            copy.start()
+
+    def ready(self, k, j):
+        done_with(self.copies[k, j])
+        self.start(k, j + 1)
 
 
 def done_with(copies):
@@ -343,22 +363,23 @@
 def expert_forward(both, arrived, *refs):
     shards = [refs[4 * k : 4 * k + 4] for k in range(3)]
     outs, weights, sems = refs[12:-2], refs[-2], refs[-1]
-    copies = fetch(shards, weights, sems)
+    fetched = Fetched(shards, weights, sems)
     per = weights.shape[1] * ROOMS
     for j in range(weights.shape[1]):
         at = j * ROOMS
         rows = rows_of(arrived, j)
-        done_with(copies[j][0])
+        fetched.ready(0, j)
         gate = dot(rows, weights[0, j], (1, 1))
-        done_with(copies[j][1])
+        fetched.ready(1, j)
         lifted = dot(rows, weights[1, j], (1, 1))
         square = gate * gate
         bend = jnp.tanh(0.7978845608028654 * gate * (1.0 + 0.044715 * square))
         active = 0.5 * gate * (1.0 + bend)
         hidden = (active * lifted).astype(BF)
-        done_with(copies[j][2])
+        fetched.ready(2, j)
         made = dot(hidden, weights[2, j]).astype(BF)
         outs[0][:, at : at + ROOMS, :] = made.reshape(-1, ROOMS, made.shape[1])
+        sent(outs[0], (slice(None), pl.ds(at, ROOMS)))
         if both:
             slope = 0.5 * (1.0 + bend) + 0.5 * gate * (1.0 - bend * bend) * (
                 0.7978845608028654 * (1.0 + 3 * 0.044715 * square)
@@ -373,9 +394,9 @@
             inner = jnp.sum(hidden_grads * hidden.astype(F32), -1, keepdims=True)
             back = dot(gate_part, weights[0, j]) + dot(lifted_part, weights[1, j])
             put_rows(outs[4], j, back.astype(BF), inner)
-    if both:
-        for out in outs[:4]:
-            sent(out)
+            sent(outs[4], (slice(None), pl.ds(at, ROOMS)))
+            for out in outs[1:4]:
+                sent(out, j)
 
 
 def combine(returned, middle, gates, spread, places, result, low):
@@ -406,28 +427,28 @@
 def expert_backward(flag, arrived, hidden, active, bent, produced, *refs):
     shards = [refs[4 * k : 4 * k + 4] for k in range(3)]
     out, gate_back, lifted_back, weights, sems = refs[12:]
-    copies = fetch(shards, weights, sems)
+    fetched = Fetched(shards, weights, sems)
     for j in range(weights.shape[1]):
-        done_with(copies[j][0])
+        fetched.ready(0, j)
         hidden_grads = dot(rows_of(arrived, j), weights[0, j], (1, 1))
         gate_part = (hidden_grads * bent[j].astype(F32)).astype(BF)
         lifted_part = (hidden_grads * active[j].astype(F32)).astype(BF)
         gate_back[j] = gate_part
         lifted_back[j] = lifted_part
         inner = jnp.sum(hidden_grads * hidden[j].astype(F32), -1, keepdims=True)
-        done_with(copies[j][1])
+        fetched.ready(1, j)
         done = dot(gate_part, weights[1, j])
-        done_with(copies[j][2])
+        fetched.ready(2, j)
         done = (done + dot(lifted_part, weights[2, j])).astype(BF)
         put_rows(out, j, jnp.where(flag[0] > 0, rows_of(produced, j), done), inner)
-    sent(gate_back)
-    sent(lifted_back)
+        sent(out, (slice(None), pl.ds(j * ROOMS, ROOMS)))
+        sent(gate_back, j)
+        sent(lifted_back, j)
 
 
 def attend_back(
-    keep, row, flag, token_grads, before, gates, places, middle, gain, grad, query, pair0, pair1,
-    pair2, pair3, probs, cosine, sine, dense, middle_grads, query_back, part0, part1, part2, part3,
-    *rest,
+    keep, row, flag, token_grads, before, gates, places, middle, gain, grad, query, pairs, probs,
+    cosine, sine, dense, middle_grads, query_back, part0, part1, part2, part3, *rest,
 ):
     tokens, width = middle.shape
     kept, (branch, weights, router, sems) = rest[:-4], rest[-4:]
@@ -468,7 +489,7 @@
             part[:, part.shape[1] - share :] = branch[:, pl.ds(begin, share)]
     copies[1].wait()
     mixed_grads = dot(low, weights[...], (1, 1)).astype(BF)
-    pairs = jnp.concatenate([pair0[...], pair1[...], pair2[...], pair3[...]], 0)
+    pairs = pairs[...].reshape(-1, pairs.shape[2])
     kv_heads = pairs.shape[1] // (2 * HEAD_DIM)
     group = width // HEAD_DIM // kv_heads
     scale = HEAD_DIM ** (-0.5)
@@ -600,7 +621,9 @@
         out[...] = total[pl.ds(pl.multiple_of((row[0] ^ s) * size, 8), size), :]
 
 
-def finish(row, in0, in1, in2, in3, o_grad, q_grad, k_grad, v_grad, rest, total):
+def finish(
+    row, in0, in1, in2, in3, o_grad, q_grad, k_grad, v_grad, r_grad, first, second, total
+):
     share = o_grad.shape[1] // 4
     piece = total.shape[1] // 4
     ins = (in0, in1, in2, in3)
@@ -608,7 +631,11 @@
         where = row[0] ^ s
         o_grad[:, pl.ds(pl.multiple_of(where * share, LANES), share)] = one[:, :share]
         total[:, pl.ds(pl.multiple_of(where * piece, LANES), piece)] = one[:, share : share + piece]
-    rest[...] = sum(one[:, share + piece :] for one in ins)
+    rest = sum(one[:, share + piece :] for one in ins)
+    r_grad[...] = rest[:, : r_grad.shape[1]]
+    turned_rest = rest.T
+    first[...] = turned_rest[LANES - 2 : LANES - 1, :]
+    second[...] = turned_rest[LANES - 1 :, :]
     begin = 0
     for out in (q_grad, k_grad, v_grad):
         out[...] = total[:, begin : begin + out.shape[1]]
@@ -703,7 +730,7 @@
     qkv_scratch = [pltpu.VMEM((width, qkv_width), BF), pltpu.SemaphoreType.DMA((8,))]
     out_scratch = [
         pltpu.VMEM((width, width), BF), pltpu.VMEM((width, LANES), BF),
-        pltpu.SemaphoreType.DMA((2,)),
+        pltpu.SemaphoreType.DMA((16,)),
     ]
     expert_scratch = [
         pltpu.VMEM((3, per_column, hidden_width, width), BF),
@@ -727,25 +754,25 @@
         for m in pieces:
             projected.append(
                 call(
-                    functools.partial(project, keep),
-                    (token_wide, token_low, pair_like)
-                    + ((Sent(token_low), Sent(token_wide), Sent(token_low), Sent(pair_like))
-                       if keep else ()),
+                    project, (token_wide, token_low, token_low, pair_like),
                     (came[m], Late(entering[m]), Late(gain_a), *tables), qkv_flops, (dense,),
                     qkv_scratch, (second,), waits=(*waits, *(p[0] for p in projected)),
                 )
             )
-            pair = projected[m][2]
+            pair = projected[m][3]
             pairs.append([swapped(pair, s) for s in steps[1:]])
         attended = [
             call(
                 functools.partial(attend, keep),
                 (Sent(token_wide), Sent(lanes_like), Sent(double_like if keep else block_like))
-                + ((Sent(probs_like), Sent(token_low), Sent(token_low)) if keep else ()),
-                (*projected[m][:3], *late([*pairs[m], biases[m], gain_f, chosens[m], dispatches[m],
-                                           *targets[m : m + 1]])),
+                + ((Sent(probs_like), Sent(token_low), Sent(token_low), Raw(token_wide),
+                    Raw(token_low), Raw(token_low), Raw(like((rows, tokens, 2 * kv_width), BF)))
+                   if keep else ()),
+                (projected[m][0], projected[m][2], projected[m][3], *pairs[m],
+                 *late([biases[m], gain_f, chosens[m], dispatches[m]]),
+                 *((projected[m][1], Late(targets[m])) if keep else ())),
                 out_flops + 2 * score_flops, (dense,), [pltpu.VMEM((tokens, width), BF)] + out_scratch,
-                waits=() if keep or m else (projected[1][2],),
+                waits=() if keep or m else pairs[1],
             )
             for m in pieces
         ]
@@ -754,7 +781,7 @@
         if keep:
             left = call(
                 pack, (Sent(like((2 * micro, tokens, width), BF)),),
-                late([p[3] for p in projected] + [a[4] for a in attended]), 0,
+                late([a[8] for a in attended] + [a[4] for a in attended]), 0,
             )[0]
             two = swapped(left, 2)
             lefts = [left, swapped(left, 1), two, swapped(two, 1)]
@@ -773,14 +800,14 @@
             )
             for m in pieces
         ]
-        return projected, pairs, attended, arrived, applied, lefts, down
-
-    def far_and_near(side):
+        return attended, arrived, applied, lefts, down
+
+    def far_and_near(side, waits):
         return [
             call(
                 functools.partial(expert_weight_grads, side, begin),
                 (Sent(like((per_column, hidden_width // 4, width), BF)),) * 2,
-                late([*left, *right]), expert_flops,
+                late([*left, *right]), expert_flops, waits=() if left is hidden else waits,
             )
             for left, right, begin in (
                 (hidden, arrived_grads, 0), ([a[1] for a in moved], arrived, 0),
@@ -800,8 +827,8 @@
             + (like((tokens, 2 * kv_width + (share if keep else 0)), BF),) * rows
             + ((Sent(like((tokens, LANES), BF)), Sent(sums_like)) if keep else ()),
             late([token_grads, shared[m] if keep else spread, attended[m][1], places[m],
-                  attended[m][0], gain_f, grad, projected[m][5], projected[m][6], *pairs[m],
-                  attended[m][3], cosine, sine]),
+                  attended[m][0], gain_f, grad, attended[m][7], attended[m][9], attended[m][3],
+                  cosine, sine]),
             out_flops + 4 * score_flops, (dense,), [pltpu.VMEM((tokens, width), BF)] + out_scratch,
             (here, second), waits,
         )
@@ -815,7 +842,7 @@
             (token_low,)
             + ((Sent(token_wide), Sent(sums_like))
                + (like((tokens, qkv_width // rows), BF),) * rows if keep else ()),
-            (parts[0], *late(parts[1:]), inner[1], Late(projected[m][4]), Late(gain_a), inner[0],
+            (*parts, inner[1], Late(attended[m][6]), Late(gain_a), inner[0],
              *tables),
             qkv_flops, (dense,), [pltpu.VMEM((tokens, qkv_width), BF)] + qkv_scratch,
             (here,), waits,
@@ -824,7 +851,7 @@
     entering = [inputs[m, 0] for m in pieces]
     targets = [cotangent[m, 0] for m in pieces]
     kept = forward(entering, entering, (), (gate_shards[2], up_shards[2]), down_shards)
-    attended, applied, down_shards = kept[2], kept[4], kept[6]
+    attended, applied, down_shards = kept[0], kept[2], kept[4]
     returned = [over_columns(a[0]) for a in applied]
     results = [
         call(
@@ -837,7 +864,7 @@
     came = [lax.ppermute(r[1], "section", [(0, 1)]) for r in results]
 
     kept = forward(came, entering, targets, (), down_shards)
-    projected, pairs, attended, arrived, applied, lefts, down_shards = kept
+    attended, arrived, applied, lefts, down_shards = kept
     hidden = [a[1] for a in applied]
     shared = [over_columns(a[4]) for a in applied]
     inner, outer = [], []
@@ -851,7 +878,7 @@
         call(
             send_grads, (Sent(token_low), Sent(block_like)),
             (came[m], *late([targets[m], attended[m][1], dispatches[m]])),
-            2 * slots * tokens * width, scalars=(first_flag,),
+            2 * slots * tokens * width, scalars=(first_flag,), waits=() if m else (inner[1][0],),
         )
         for m in pieces
     ]
@@ -866,17 +893,17 @@
         for m in pieces
     ]
     back = [over_columns(a[0]) for a in moved]
-    far, near = far_and_near(1), far_and_near(0)
-    crossed = [swapped(merged(far[0], ()), 2)]
-
     inner = [attention_back(True, 0, given[0][0], back[0], (moved[1][0],))]
     parts = [parts_of(inner[0])]
     outer = [projection_back(True, 0, inner[0], parts[0], ())]
+    far = far_and_near(1, (inner[0][0],))
+    crossed = [swapped(merged(far[0], parts[0][1:]), 2)]
     inner.append(attention_back(
-        True, 1, given[1][0], back[1], (inner[0][0], *(f[0] for f in far), near[0][0])
+        True, 1, given[1][0], back[1], (outer[0][0], *(f[0] for f in far))
     ))
     parts.append(parts_of(inner[1]))
     crossed.append(swapped(merged(far[1], parts[1][1:]), 2))
+    near = far_and_near(0, (inner[1][0],))
     o_grads = call(
         out_grads, (Sent(like((columns, rows * shard, share), BF)),),
         late([*lefts, *[p[s] for s in steps for p in parts]]),
@@ -891,7 +918,7 @@
         late([*lefts, *[b[s] for s in steps for b in backs], *[a[5] for a in attended],
               *[a[6] for a in inner], *[o[2] for o in outer], *[a[7] for a in inner]]),
         2 * width * length * micro * qkv_width // rows,
-        waits=(near[1][0], crossed[1], last),
+        waits=(near[0][0], crossed[1], last),
     )[0]
     expert_grads = [
         n[0].astype(F32) + swapped(n[1], 1).astype(F32) + c.astype(F32)
@@ -911,23 +938,24 @@
         scratch=[pltpu.VMEM((rows * shard, wide), F32)], scalars=(here,),
     )
     pieces_out = [pieces_out[0]] + [swapped(pieces_out[s], s) for s in steps[1:]]
-    o_grad, q_grad, k_grad, v_grad, rest = call(
+    o_grad, q_grad, k_grad, v_grad, r_grad, first, second_sum = call(
         finish,
         (like((shard, width), F32), like((shard, width), F32), like((shard, kv_width), F32),
-         like((shard, kv_width), F32), like((shard, LANES), F32)),
+         like((shard, kv_width), F32), like((shard, experts), F32), like((1, shard), F32),
+         like((1, shard), F32)),
         pieces_out, 0, scratch=[pltpu.VMEM((shard, qkv_width), F32)], scalars=(here,),
     )
 
     return (
         layer_outputs[None, :, None],
         jnp.stack([o[1] for o in outer])[None, :, None],
-        rest[:, LANES - 2][None],
+        first,
         q_grad[None],
         k_grad[None],
         v_grad[None],
         o_grad[None],
-        rest[:, LANES - 1][None],
-        rest[:, :experts][None],
+        second_sum,
+        r_grad[None],
         expert_grads[1][None],
         expert_grads[2][None],
         expert_grads[0][None],

time: 771 us -> 769 us (level)
    unnamed x140 -> x148, local copies, waits for them, and re-layouts: 25.7 us -> 26.2 us
  transfers between devices with their start and end apart: 73 -> 73, of which waited for: 27 -> 28; matrix products, arithmetic and copies ran while one was open for 3% -> 3% of each run, Pallas kernels for 37% -> 35%
where the time goes in v6:
time: 769 us; the launch traced here: 755 us
  Pallas kernels  287 us (37%)
  waiting for transfers between devices  229 us (30%)
  starting transfers between devices  171 us (22%)
  local copies, waits for them, and re-layouts  35.1 us (5%)
  other arithmetic  18.3 us (2%)
  between operations  15.5 us (2%)
    pallas_call x41, Pallas kernels, call(): pl.pallas_call(run, out_shape=tuple(shapes), in_specs=[pl.BlockSpec(memor...  287 us
    all_gather x1, waiting for transfers between devices, on_device(): dense = lax.all_gather(dense, ('row', 'col'), axis=0, tiled=True)  91.8 us
    all_to_all x14, starting transfers between devices, over_columns(): return lax.all_to_all(value, 'col', split_axis=0, concat_axis=0, tiled=True)  87.9 us
    ppermute x54, starting transfers between devices, swapped(): return lax.ppermute(value, 'row', [(r, r ^ step) for r in range(rows)])  76.4 us
    ppermute x54, waiting for transfers between devices, swapped(): return lax.ppermute(value, 'row', [(r, r ^ step) for r in range(rows)])  61.2 us
    all_to_all x14, waiting for transfers between devices, over_columns(): return lax.all_to_all(value, 'col', split_axis=0, concat_axis=0, tiled=True)  53.8 us
    unnamed x148, local copies, waits for them, and re-layouts  26.2 us
  transfers between devices with their start and end apart: 73, of which 28 were waited for; matrix products, arithmetic and copies ran while one was open for 3% of the time, Pallas kernels for 35%

profile of v6, /device:TPU:9, one launch (start us, length us, event | category | flops | bytes accessed | tf_op | source)
XLA Modules:
  0.0 755.3 jit_solution(15094948004329208702)
XLA Ops:
  18.5 91.8 %all-gather.2.cloned.1.call-done.refs_6_.refs_10_.refs_12_.refs_14_.refs_11_ = bf16[1536,3712]{1,0:T(8,128)(2,1)} async-done(((bf16[24,3712]{1,0:T(8,128)(2,1)}), bf16[1536,3712]{1,0:T(8,128)(2,1)}) %all-gather.2.cloned.1.call-update) | async-done | bytes 11403280 | tf_op jit(solution)/shard_map/all_gather | solution.py:679
  138.8 7.3 attend.4
  156.1 7.4 attend.5
  163.5 16.5 %collective-permute-done.13.refs_0_ = bf16[2,192,1536]{2,1,0:T(8,128)(2,1)S(1)} collective-permute-done((bf16[2,192,1536]{2,1,0:T(8,128)(2,1)}, bf16[2,192,1536]{2,1,0:T(8,128)(2,1)S(1)}, u32[]{:S(2)}, u32[]{:S(2)}) %collective-permute-start.13) | collective-permute-done | bytes 1179680 | tf_op jit(solution)/shard_map/ppermute | solution.py:170
  190.1 10.3 %expert_forward.4 = bf16[16,32,1536]{2,1,0:T(8,128)(2,1)} custom-call(bf16[16,32,1536]{2,1,0:T(8,128)(2,1)} %all-to-all-done.refs_0_, bf16[2,192,1536]{2,1,0:T(8,128)(2,1)} %bitcast.10.refs_1_.refs_10_, bf16[2,192,1536]{2,1,0:T(8,128)(2,1)} %collective-permute-done.8.refs_2_.refs_11_, bf16[2,192,1536]{2,1,0:T(8,128)(2,1)} %copy-done.1, ...), custom_call_target="tpu_custom_call" | custom-call | flops 3623878656 | bytes 17301504 | tf_op jit(solution)/shard_map/expert_forward/pallas_call | solution.py:129
  200.4 12.4 %all-to-all-done.2.refs_0_ = bf16[16,32,1536]{2,1,0:T(8,128)(2,1)} async-done(((bf16[16,32,1536]{2,1,0:T(8,128)(2,1)}), bf16[16,32,1536]{2,1,0:T(8,128)(2,1)}, u32[]{:S(2)}, u32[]{:S(2)}) %all-to-all-start.2) | async-done | bytes 1572896 | tf_op jit(solution)/shard_map/all_to_all | solution.py:646
  216.5 10.3 %expert_forward.5.refs_5_ = bf16[16,32,1536]{2,1,0:T(8,128)(2,1)} custom-call(bf16[16,32,1536]{2,1,0:T(8,128)(2,1)} %all-to-all-done.2.refs_0_, bf16[2,192,1536]{2,1,0:T(8,128)(2,1)} %bitcast.10.refs_1_.refs_10_, bf16[2,192,1536]{2,1,0:T(8,128)(2,1)} %collective-permute-done.8.refs_2_.refs_11_, bf16[2,192,1536]{2,1,0:T(8,128)(2,1)} %copy-done.1, ...), custom_call_target="tpu_custom_call" | custom-call | flops 3623878656 | bytes 17301504 | tf_op jit(solution)/shard_map/expert_forward/pallas_call | solution.py:129
  226.8 10.1 %all-to-all-done.1.refs_0_ = bf16[16,32,1536]{2,1,0:T(8,128)(2,1)S(1)} async-done(((bf16[16,32,1536]{2,1,0:T(8,128)(2,1)}), bf16[16,32,1536]{2,1,0:T(8,128)(2,1)S(1)}, u32[]{:S(2)}, u32[]{:S(2)}) %all-to-all-start.1) | async-done | bytes 1572896 | tf_op jit(solution)/shard_map/all_to_all | solution.py:646
  275.4 10.0 %attend.6 = (f32[96,1536]{1,0:T(8,128)}, f32[96,128]{1,0:T(8,128)}, bf16[16,64,1536]{2,1,0:T(8,128)(2,1)}, bf16[2,576,384]{2,1,0:T(8,128)(2,1)}, bf16[96,1536]{1...) custom-call(f32[96,1536]{1,0:T(8,128)} %get-tuple-element.151.refs_0, ...), custom_call_target="tpu_custom_call" | custom-call | flops 830472192 | bytes 20404224 | tf_op jit(solution)/shard_map/attend/pallas_call | solution.py:129
  286.6 6.9 all-to-all-start.3
  298.7 8.7 %collective-permute-done.19.refs_1_ = bf16[96,1536]{1,0:T(8,128)(2,1)S(1)} collective-permute-done((bf16[96,1536]{1,0:T(8,128)(2,1)}, bf16[96,1536]{1,0:T(8,128)(2,1)S(1)}, u32[]{:S(2)}, u32[]{:S(2)}) %collective-permute-start.19) | collective-permute-done | bytes 294944 | tf_op jit(solution)/shard_map/ppermute | solution.py:864
  324.8 10.1 %attend.7 = (f32[96,1536]{1,0:T(8,128)}, f32[96,128]{1,0:T(8,128)}, bf16[16,64,1536]{2,1,0:T(8,128)(2,1)}, bf16[2,576,384]{2,1,0:T(8,128)(2,1)}, bf16[96,1536]{1...) custom-call(f32[96,1536]{1,0:T(8,128)} %get-tuple-element.159.refs_0, ...), custom_call_target="tpu_custom_call" | custom-call | flops 830472192 | bytes 20404224 | tf_op jit(solution)/shard_map/attend/pallas_call | solution.py:129
  336.6 10.2 %all-to-all-start.6 = ((bf16[16,64,1536]{2,1,0:T(8,128)(2,1)}), bf16[16,64,1536]{2,1,0:T(8,128)(2,1)}, u32[]{:S(2)}, u32[]{:S(2)}) async-start(bf16[16,64,1536]{2,1,0:T(8,128)(2,1)} %get-tuple-element.163.refs_13_), calls=%async_computation.6 | async-start | bytes 6291456 | tf_op jit(solution)/shard_map/all_to_all | solution.py:646
  351.8 16.4 %expert_forward.6 = (bf16[16,32,1536]{2,1,0:T(8,128)(2,1)}, bf16[2,256,768]{2,1,0:T(8,128)(2,1)}, bf16[2,256,768]{2,1,0:T(8,128)(2,1)}, bf16[2,256,768]{2,1,0:T(8,128)(2,1)}, bf16[16,32,1664]{2,1,0:T(8,128)(2,1)}) custom-call(bf16[16,64,1536]{2,1,0:T(8,128)(2,1)} %copy-done, bf16[2,192,1536]{2,1,0:T(8,128)(2,1)} %bitcast.10.refs_1_.refs_10_, ...), custom_call_target="tpu_custom_call" | custom-call | flops 7247757312 | bytes 22937600 | tf_op jit(solution)/shard_map/expert_forward/pallas_call | solution.py:129
  368.2 17.1 %all-to-all-done.6.refs_0_.refs_3_ = bf16[16,64,1536]{2,1,0:T(8,128)(2,1)} async-done(((bf16[16,64,1536]{2,1,0:T(8,128)(2,1)}), bf16[16,64,1536]{2,1,0:T(8,128)(2,1)}, u32[]{:S(2)}, u32[]{:S(2)}) %all-to-all-start.6) | async-done | bytes 3145760 | tf_op jit(solution)/shard_map/all_to_all | solution.py:646
  391.4 16.4 %expert_forward.7 = (bf16[16,32,1536]{2,1,0:T(8,128)(2,1)}, bf16[2,256,768]{2,1,0:T(8,128)(2,1)}, bf16[2,256,768]{2,1,0:T(8,128)(2,1)}, bf16[2,256,768]{2,1,0:T(8,128)(2,1)}, bf16[16,32,1664]{2,1,0:T(8,128)(2,1)}) custom-call(bf16[16,64,1536]{2,1,0:T(8,128)(2,1)} %all-to-all-done.6.refs_0_.refs_3_, bf16[2,192,1536]{2,1,0:T(8,128)(2,1)} %bitcast.10.refs_1_.refs_10_, ...), custom_call_target="tpu_custom_call" | custom-call | flops 7247757312 | bytes 22937600 | tf_op jit(solution)/shard_map/expert_forward/pallas_call | solution.py:129
  411.8 7.2 all-to-all-start.7
  421.5 8.8 %attend_back.4 = (f32[96,1536]{1,0:T(8,128)}, bf16[96,1536]{1,0:T(8,128)(2,1)}, bf16[96,512]{1,0:T(8,128)(2,1)}, bf16[96,512]{1,0:T(8,128)(2,1)}, bf16[96,512]{1,0:T(8,128)(2,1)}, /*index=5*/bf16[96,512]{1,0:T(8,128)(2,1)}) custom-call(s32[1]{0:T(128)} %bitcast.1.refs_0_, s32[1]{0:T(128)} %bitcast.refs_0_.refs_1_, bf16[16,32,1664]{2,1,0:T(8,128)(2,1)} %copy-done.9, ...), custom_call_target="tpu_custom_call" | custom-call | flops 1056964608 | bytes 17225728 | tf_op jit(solution)/shard_map/attend_back/pallas_call | solution.py:129
  441.1 7.4 project_back.4.refs_18_
  451.9 8.8 %attend_back.5 = (f32[96,1536]{1,0:T(8,128)}, bf16[96,1536]{1,0:T(8,128)(2,1)}, bf16[96,512]{1,0:T(8,128)(2,1)}, bf16[96,512]{1,0:T(8,128)(2,1)}, bf16[96,512]{1,0:T(8,128)(2,1)}, /*index=5*/bf16[96,512]{1,0:T(8,128)(2,1)}) custom-call(s32[1]{0:T(128)} %bitcast.1.refs_0_, s32[1]{0:T(128)} %bitcast.refs_0_.refs_1_, bf16[16,32,1664]{2,1,0:T(8,128)(2,1)} %copy-done.11, ...), custom_call_target="tpu_custom_call" | custom-call | flops 1056964608 | bytes 17225728 | tf_op jit(solution)/shard_map/attend_back/pallas_call | solution.py:129
  482.2 7.4 project_back.5
  503.5 7.3 all-to-all-start.10
  510.8 10.8 %expert_backward.2 = (bf16[16,32,1664]{2,1,0:T(8,128)(2,1)}, bf16[2,256,768]{2,1,0:T(8,128)(2,1)}, bf16[2,256,768]{2,1,0:T(8,128)(2,1)}) custom-call(s32[1]{0:T(128)} %bitcast.refs_0_.refs_1_, bf16[16,32,1536]{2,1,0:T(8,128)(2,1)} %copy-done.6, bf16[2,256,768]{2,1,0:T(8,128)(2,1)} %get-tuple-element.189.refs_2_.refs_0_, ...), custom_call_target="tpu_custom_call" | custom-call | flops 3623878656 | bytes 22937600 | tf_op jit(solution)/shard_map/expert_backward/pallas_call | solution.py:129
  521.6 9.8 %all-to-all-done.10.refs_1_.refs_3_ = bf16[16,32,1536]{2,1,0:T(8,128)(2,1)S(1)} async-done(((bf16[16,32,1536]{2,1,0:T(8,128)(2,1)}), bf16[16,32,1536]{2,1,0:T(8,128)(2,1)S(1)}, u32[]{:S(2)}, u32[]{:S(2)}) %all-to-all-start.10) | async-done | bytes 1572896 | tf_op jit(solution)/shard_map/all_to_all | solution.py:646
  546.6 10.9 %expert_backward.3 = (bf16[16,32,1664]{2,1,0:T(8,128)(2,1)}, bf16[2,256,768]{2,1,0:T(8,128)(2,1)}, bf16[2,256,768]{2,1,0:T(8,128)(2,1)}) custom-call(s32[1]{0:T(128)} %bitcast.refs_0_.refs_1_, bf16[16,32,1536]{2,1,0:T(8,128)(2,1)} %copy-done.7, bf16[2,256,768]{2,1,0:T(8,128)(2,1)} %get-tuple-element.202.refs_2_.refs_1_, ...), custom_call_target="tpu_custom_call" | custom-call | flops 3623878656 | bytes 22937600 | tf_op jit(solution)/shard_map/expert_backward/pallas_call | solution.py:129
  564.5 9.4 %attend_back.6 = (f32[96,1536]{1,0:T(8,128)}, bf16[96,1536]{1,0:T(8,128)(2,1)}, bf16[96,896]{1,0:T(8,128)(2,1)}, bf16[96,896]{1,0:T(8,128)(2,1)}, bf16[96,896]{1...) custom-call(s32[1]{0:T(128)} %bitcast.1.refs_0_, s32[1]{0:T(128)} %bitcast.refs_0_.refs_1_, ...), custom_call_target="tpu_custom_call" | custom-call | flops 1056964608 | bytes 19167232 | tf_op jit(solution)/shard_map/attend_back/pallas_call | solution.py:129
  601.1 8.7 %project_back.6 = (bf16[96,1536]{1,0:T(8,128)(2,1)}, f32[96,1536]{1,0:T(8,128)}, f32[8,1536]{1,0:T(8,128)}, bf16[96,512]{1,0:T(8,128)(2,1)}, bf16[96,512]{1,0:T(...) custom-call(s32[1]{0:T(128)} %bitcast.1.refs_0_, bf16[96,896]{1,0:T(8,128)(2,1)} %get-tuple-element.209.refs_1_.refs_4_, ...), custom_call_target="tpu_custom_call" | custom-call | flops 603979776 | bytes 14997504 | tf_op jit(solution)/shard_map/project_back/pallas_call | solution.py:129
  610.9 9.5 %attend_back.7 = (f32[96,1536]{1,0:T(8,128)}, bf16[96,1536]{1,0:T(8,128)(2,1)}, bf16[96,896]{1,0:T(8,128)(2,1)}, bf16[96,896]{1,0:T(8,128)(2,1)}, bf16[96,896]{1...) custom-call(s32[1]{0:T(128)} %bitcast.1.refs_0_, s32[1]{0:T(128)} %bitcast.refs_0_.refs_1_, ...), custom_call_target="tpu_custom_call" | custom-call | flops 1056964608 | bytes 19167232 | tf_op jit(solution)/shard_map/attend_back/pallas_call | solution.py:129
  644.6 7.0 all-to-all-start.12
  657.7 8.6 %project_back.7 = (bf16[96,1536]{1,0:T(8,128)(2,1)}, f32[96,1536]{1,0:T(8,128)}, f32[8,1536]{1,0:T(8,128)}, bf16[96,512]{1,0:T(8,128)(2,1)}, bf16[96,512]{1,0:T(...) custom-call(s32[1]{0:T(128)} %bitcast.1.refs_0_, bf16[96,896]{1,0:T(8,128)(2,1)} %get-tuple-element.225.refs_5_.refs_1_, ...), custom_call_target="tpu_custom_call" | custom-call | flops 603979776 | bytes 14997504 | tf_op jit(solution)/shard_map/project_back/pallas_call | solution.py:129
  682.4 6.8 qkv_grads.1.refs_12_
  690.3 6.9 all-to-all-start.13
  (351 shorter events, 342.7 us)
Async XLA Ops:
  7.2 103.1 %all-gather.2.cloned.1.call-start = ((), (), s32[]{:S(2)}) async-start(), calls=%async_computation.14 | async-start | bytes 11581440 | tf_op jit(solution)/shard_map/all_gather | solution.py:679
  10.5 102.3 %collective-permute-start = (bf16[2,192,1536]{2,1,0:T(8,128)(2,1)}, bf16[2,192,1536]{2,1,0:T(8,128)(2,1)S(1)}, u32[]{:S(2)}, u32[]{:S(2)}) collective-permute-start(bf16[2,192,1536]{2,1,0:T(8,128)(2,1)} %bitcast.10.refs_1_.refs_10_), channel_id=1, source_target_pairs={{0,32},{16,48},{32,0},{48,16},{1,33},{17,49},{33,1},{49,17},{2,34}... | collective-permute-start | bytes 3538952 | tf_op jit(solution)/shard_map/ppermute | solution.py:170
  12.6 100.2 %collective-permute-start.1 = (bf16[2,192,1536]{2,1,0:T(8,128)(2,1)}, bf16[2,192,1536]{2,1,0:T(8,128)(2,1)S(1)}, u32[]{:S(2)}, u32[]{:S(2)}) collective-permute-start(bf16[2,192,1536]{2,1,0:T(8,128)(2,1)} %bitcast.11.refs_5_.refs_14_), channel_id=1, source_target_pairs={{0,32},{16,48},{32,0},{48,16},{1,33},{17,49},{33,1},{49,17},{2,34}... | collective-permute-start | bytes 3538952 | tf_op jit(solution)/shard_map/ppermute | solution.py:170
  146.1 36.3 %all-to-all-start = ((bf16[16,32,1536]{2,1,0:T(8,128)(2,1)}), bf16[16,32,1536]{2,1,0:T(8,128)(2,1)}, u32[]{:S(2)}, u32[]{:S(2)}) async-start(bf16[16,32,1536]{2,1,0:T(8,128)(2,1)} %get-tuple-element.144), calls=%async_computation | async-start | bytes 3145728 | tf_op jit(solution)/shard_map/all_to_all | solution.py:646
  151.2 28.8 %collective-permute-start.13 = (bf16[2,192,1536]{2,1,0:T(8,128)(2,1)}, bf16[2,192,1536]{2,1,0:T(8,128)(2,1)S(1)}, u32[]{:S(2)}, u32[]{:S(2)}) collective-permute-start(bf16[2,192,1536]{2,1,0:T(8,128)(2,1)} %bitcast.20.refs_9_.refs_6_), channel_id=1, source_target_pairs={{0,32},{16,48},{32,0},{48,16},{1,33},{17,49},{33,1},{49,17},{2,34}... | collective-permute-start | bytes 3538952 | tf_op jit(solution)/shard_map/ppermute | solution.py:170
  153.0 28.4 %collective-permute-start.8 = (bf16[2,192,1536]{2,1,0:T(8,128)(2,1)}, bf16[2,192,1536]{2,1,0:T(8,128)(2,1)}, u32[]{:S(2)}, u32[]{:S(2)}) collective-permute-start(bf16[2,192,1536]{2,1,0:T(8,128)(2,1)} %bitcast.10.refs_1_.refs_10_), channel_id=1, source_target_pairs={{0,16},{16,0},{32,48},{48,32},{1,17},{17,1},{33,49},{49,33},{2,18}... | collective-permute-start | bytes 3538952 | tf_op jit(solution)/shard_map/ppermute | solution.py:170
  154.0 35.0 %collective-permute-start.10 = (bf16[2,192,1536]{2,1,0:T(8,128)(2,1)}, bf16[2,192,1536]{2,1,0:T(8,128)(2,1)}, u32[]{:S(2)}, u32[]{:S(2)}) collective-permute-start(bf16[2,192,1536]{2,1,0:T(8,128)(2,1)} %bitcast.11.refs_5_.refs_14_), channel_id=1, source_target_pairs={{0,16},{16,0},{32,48},{48,32},{1,17},{17,1},{33,49},{49,33},{2,18}... | collective-permute-start | bytes 3538952 | tf_op jit(solution)/shard_map/ppermute | solution.py:170
  154.0 35.0 %collective-permute-start.12 = (bf16[2,192,1536]{2,1,0:T(8,128)(2,1)}, bf16[2,192,1536]{2,1,0:T(8,128)(2,1)}, u32[]{:S(2)}, u32[]{:S(2)}) collective-permute-start(bf16[2,192,1536]{2,1,0:T(8,128)(2,1)} %bitcast.20.refs_9_.refs_6_), channel_id=1, source_target_pairs={{0,16},{16,0},{32,48},{48,32},{1,17},{17,1},{33,49},{49,33},{2,18}... | collective-permute-start | bytes 3538952 | tf_op jit(solution)/shard_map/ppermute | solution.py:170
  155.9 33.1 %collective-permute-start.9 = (bf16[2,192,1536]{2,1,0:T(8,128)(2,1)S(1)}, bf16[2,192,1536]{2,1,0:T(8,128)(2,1)}, u32[]{:S(2)}, u32[]{:S(2)}) collective-permute-start(bf16[2,192,1536]{2,1,0:T(8,128)(2,1)S(1)} %copy-done.2), channel_id=1, source_target_pairs={{0,16},{16,0},{32,48},{48,32},{1,17},{17,1},{33,49},{49,33},{2,18}... | collective-permute-start | bytes 3538952 | tf_op jit(solution)/shard_map/ppermute | solution.py:170
  182.4 30.3 %all-to-all-start.2 = ((bf16[16,32,1536]{2,1,0:T(8,128)(2,1)}), bf16[16,32,1536]{2,1,0:T(8,128)(2,1)}, u32[]{:S(2)}, u32[]{:S(2)}) async-start(bf16[16,32,1536]{2,1,0:T(8,128)(2,1)} %get-tuple-element.147.refs_1_.refs_13_), calls=%async_computation.2 | async-start | bytes 3145728 | tf_op jit(solution)/shard_map/all_to_all | solution.py:646
  212.7 24.2 %all-to-all-start.1 = ((bf16[16,32,1536]{2,1,0:T(8,128)(2,1)}), bf16[16,32,1536]{2,1,0:T(8,128)(2,1)S(1)}, u32[]{:S(2)}, u32[]{:S(2)}) async-start(bf16[16,32,1536]{2,1,0:T(8,128)(2,1)} %expert_forward.4), calls=%async_computation.1 | async-start | bytes 3145728 | tf_op jit(solution)/shard_map/all_to_all | solution.py:646
  238.1 47.4 %all-to-all-start.4 = ((bf16[16,32,1536]{2,1,0:T(8,128)(2,1)}), bf16[16,32,1536]{2,1,0:T(8,128)(2,1)S(1)}, u32[]{:S(2)}, u32[]{:S(2)}) async-start(bf16[16,32,1536]{2,1,0:T(8,128)(2,1)} %expert_forward.5.refs_5_), calls=%async_computation.4 | async-start | bytes 3145728 | tf_op jit(solution)/shard_map/all_to_all | solution.py:646
  286.6 48.3 %all-to-all-start.3 = ((bf16[16,64,1536]{2,1,0:T(8,128)(2,1)}), bf16[16,64,1536]{2,1,0:T(8,128)(2,1)S(1)}, u32[]{:S(2)}, u32[]{:S(2)}) async-start(bf16[16,64,1536]{2,1,0:T(8,128)(2,1)} %get-tuple-element.155), calls=%async_computation.3 | async-start | bytes 6291456 | tf_op jit(solution)/shard_map/all_to_all | solution.py:646
  336.6 48.8 %all-to-all-start.6 = ((bf16[16,64,1536]{2,1,0:T(8,128)(2,1)}), bf16[16,64,1536]{2,1,0:T(8,128)(2,1)}, u32[]{:S(2)}, u32[]{:S(2)}) async-start(bf16[16,64,1536]{2,1,0:T(8,128)(2,1)} %get-tuple-element.163.refs_13_), calls=%async_computation.6 | async-start | bytes 6291456 | tf_op jit(solution)/shard_map/all_to_all | solution.py:646
  349.3 41.1 %collective-permute-start.23 = (bf16[4,96,1536]{2,1,0:T(8,128)(2,1)}, bf16[4,96,1536]{2,1,0:T(8,128)(2,1)S(1)}, u32[]{:S(2)}, u32[]{:S(2)}) collective-permute-start(bf16[4,96,1536]{2,1,0:T(8,128)(2,1)} %pack.1.refs_0_), channel_id=1, source_target_pairs={{0,32},{16,48},{32,0},{48,16},{1,33},{17,49},{33,1},{49,17},{2,34}... | collective-permute-start | bytes 3538952 | tf_op jit(solution)/shard_map/ppermute | solution.py:170
  385.3 25.2 %all-to-all-start.5 = ((bf16[16,32,1664]{2,1,0:T(8,128)(2,1)}), bf16[16,32,1664]{2,1,0:T(8,128)(2,1)S(1)}, u32[]{:S(2)}, u32[]{:S(2)}) async-start(bf16[16,32,1664]{2,1,0:T(8,128)(2,1)} %get-tuple-element.164), calls=%async_computation.5 | async-start | bytes 3407872 | tf_op jit(solution)/shard_map/all_to_all | solution.py:646
  411.8 38.6 %all-to-all-start.7 = ((bf16[16,32,1664]{2,1,0:T(8,128)(2,1)}), bf16[16,32,1664]{2,1,0:T(8,128)(2,1)S(1)}, u32[]{:S(2)}, u32[]{:S(2)}) async-start(bf16[16,32,1664]{2,1,0:T(8,128)(2,1)} %get-tuple-element.174.refs_15_), calls=%async_computation.7 | async-start | bytes 3407872 | tf_op jit(solution)/shard_map/all_to_all | solution.py:646
  418.9 31.4 %collective-permute-start.28 = (bf16[4,96,1536]{2,1,0:T(8,128)(2,1)}, bf16[4,96,1536]{2,1,0:T(8,128)(2,1)S(1)}, u32[]{:S(2)}, u32[]{:S(2)}) collective-permute-start(bf16[4,96,1536]{2,1,0:T(8,128)(2,1)} %pack.1.refs_0_), channel_id=1, source_target_pairs={{0,16},{16,0},{32,48},{48,32},{1,17},{17,1},{33,49},{49,33},{2,18}... | collective-permute-start | bytes 3538952 | tf_op jit(solution)/shard_map/ppermute | solution.py:170
  421.4 29.0 %collective-permute-start.29 = (bf16[4,96,1536]{2,1,0:T(8,128)(2,1)}, bf16[4,96,1536]{2,1,0:T(8,128)(2,1)}, u32[]{:S(2)}, u32[]{:S(2)}) collective-permute-start(bf16[4,96,1536]{2,1,0:T(8,128)(2,1)} %copy-done.12), channel_id=1, source_target_pairs={{0,16},{16,0},{32,48},{48,32},{1,17},{17,1},{33,49},{49,33},{2,18}... | collective-permute-start | bytes 3538952 | tf_op jit(solution)/shard_map/ppermute | solution.py:170
  465.5 36.7 %all-to-all-start.8 = ((bf16[16,32,1536]{2,1,0:T(8,128)(2,1)}), bf16[16,32,1536]{2,1,0:T(8,128)(2,1)S(1)}, u32[]{:S(2)}, u32[]{:S(2)}) async-start(bf16[16,32,1536]{2,1,0:T(8,128)(2,1)} %get-tuple-element.188), calls=%async_computation.8 | async-start | bytes 3145728 | tf_op jit(solution)/shard_map/all_to_all | solution.py:646
  503.5 27.9 %all-to-all-start.10 = ((bf16[16,32,1536]{2,1,0:T(8,128)(2,1)}), bf16[16,32,1536]{2,1,0:T(8,128)(2,1)S(1)}, u32[]{:S(2)}, u32[]{:S(2)}) async-start(bf16[16,32,1536]{2,1,0:T(8,128)(2,1)} %get-tuple-element.199.refs_18_), calls=%async_computation.10 | async-start | bytes 3145728 | tf_op jit(solution)/shard_map/all_to_all | solution.py:646
  532.6 26.6 %all-to-all-start.9 = ((bf16[16,32,1664]{2,1,0:T(8,128)(2,1)}), bf16[16,32,1664]{2,1,0:T(8,128)(2,1)}, u32[]{:S(2)}, u32[]{:S(2)}) async-start(bf16[16,32,1664]{2,1,0:T(8,128)(2,1)} %get-tuple-element.200), calls=%async_computation.9 | async-start | bytes 3407872 | tf_op jit(solution)/shard_map/all_to_all | solution.py:646
  543.3 44.3 %collective-permute-start.40 = (bf16[2,192,1536]{2,1,0:T(8,128)(2,1)}, bf16[2,192,1536]{2,1,0:T(8,128)(2,1)}, u32[]{:S(2)}, u32[]{:S(2)}) collective-permute-start(bf16[2,192,1536]{2,1,0:T(8,128)(2,1)} %get-tuple-element.231), channel_id=1, source_target_pairs={{0,16},{16,0},{32,48},{48,32},{1,17},{17,1},{33,49},{49,33},{2,18}... | collective-permute-start | bytes 3538952 | tf_op jit(solution)/shard_map/ppermute | solution.py:170
  559.2 50.6 %all-to-all-start.11 = ((bf16[16,32,1664]{2,1,0:T(8,128)(2,1)}), bf16[16,32,1664]{2,1,0:T(8,128)(2,1)S(1)}, u32[]{:S(2)}, u32[]{:S(2)}) async-start(bf16[16,32,1664]{2,1,0:T(8,128)(2,1)} %get-tuple-element.206.refs_15_), calls=%async_computation.11 | async-start | bytes 3407872 | tf_op jit(solution)/shard_map/all_to_all | solution.py:646
  587.4 45.1 %collective-permute-start.48 = (bf16[2,192,1536]{2,1,0:T(8,128)(2,1)}, bf16[2,192,1536]{2,1,0:T(8,128)(2,1)S(1)}, u32[]{:S(2)}, u32[]{:S(2)}) collective-permute-start(bf16[2,192,1536]{2,1,0:T(8,128)(2,1)} %get-tuple-element.248), channel_id=1, source_target_pairs={{0,16},{16,0},{32,48},{48,32},{1,17},{17,1},{33,49},{49,33},{2,18}... | collective-permute-start | bytes 3538952 | tf_op jit(solution)/shard_map/ppermute | solution.py:170
  593.0 46.0 %collective-permute-start.41 = (bf16[2,192,1536]{2,1,0:T(8,128)(2,1)}, bf16[2,192,1536]{2,1,0:T(8,128)(2,1)}, u32[]{:S(2)}, u32[]{:S(2)}) collective-permute-start(bf16[2,192,1536]{2,1,0:T(8,128)(2,1)} %add.134), channel_id=1, source_target_pairs={{0,32},{16,48},{32,0},{48,16},{1,33},{17,49},{33,1},{49,17},{2,34}... | collective-permute-start | bytes 3538952 | tf_op jit(solution)/shard_map/ppermute | solution.py:170
  621.0 46.8 %collective-permute-start.50 = (bf16[2,192,1536]{2,1,0:T(8,128)(2,1)}, bf16[2,192,1536]{2,1,0:T(8,128)(2,1)}, u32[]{:S(2)}, u32[]{:S(2)}) collective-permute-start(bf16[2,192,1536]{2,1,0:T(8,128)(2,1)} %get-tuple-element.249), channel_id=1, source_target_pairs={{0,16},{16,0},{32,48},{48,32},{1,17},{17,1},{33,49},{49,33},{2,18}... | collective-permute-start | bytes 3538952 | tf_op jit(solution)/shard_map/ppermute | solution.py:170
  637.2 44.2 %collective-permute-start.49 = (bf16[2,192,1536]{2,1,0:T(8,128)(2,1)}, bf16[2,192,1536]{2,1,0:T(8,128)(2,1)S(1)}, u32[]{:S(2)}, u32[]{:S(2)}) collective-permute-start(bf16[2,192,1536]{2,1,0:T(8,128)(2,1)} %add.135), channel_id=1, source_target_pairs={{0,32},{16,48},{32,0},{48,16},{1,33},{17,49},{33,1},{49,17},{2,34}... | collective-permute-start | bytes 3538952 | tf_op jit(solution)/shard_map/ppermute | solution.py:170
  644.6 44.6 %all-to-all-start.12 = ((bf16[16,96,384]{2,1,0:T(8,128)(2,1)}), bf16[16,96,384]{2,1,0:T(8,128)(2,1)S(1)}, u32[]{:S(2)}, u32[]{:S(2)}) async-start(bf16[16,96,384]{2,1,0:T(8,128)(2,1)} %out_grads.1.refs_12_), calls=%async_computation.12 | async-start | bytes 2359296 | tf_op jit(solution)/shard_map/all_to_all | solution.py:646
  657.0 56.9 %collective-permute-start.57 = (bf16[2,192,1536]{2,1,0:T(8,128)(2,1)}, bf16[2,192,1536]{2,1,0:T(8,128)(2,1)}, u32[]{:S(2)}, u32[]{:S(2)}) collective-permute-start(bf16[2,192,1536]{2,1,0:T(8,128)(2,1)} %get-tuple-element.267), channel_id=1, source_target_pairs={{0,16},{16,0},{32,48},{48,32},{1,17},{17,1},{33,49},{49,33},{2,18}... | collective-permute-start | bytes 3538952 | tf_op jit(solution)/shard_map/ppermute | solution.py:170
  690.3 35.4 %all-to-all-start.13 = ((bf16[16,96,640]{2,1,0:T(8,128)(2,1)}), bf16[16,96,640]{2,1,0:T(8,128)(2,1)S(1)}, u32[]{:S(2)}, u32[]{:S(2)}) async-start(bf16[16,96,640]{2,1,0:T(8,128)(2,1)} %qkv_grads.1.refs_12_), calls=%async_computation.13 | async-start | bytes 3932160 | tf_op jit(solution)/shard_map/all_to_all | solution.py:646
  712.0 29.1 %collective-permute-start.56 = (bf16[2,192,1536]{2,1,0:T(8,128)(2,1)}, bf16[2,192,1536]{2,1,0:T(8,128)(2,1)}, u32[]{:S(2)}, u32[]{:S(2)}) collective-permute-start(bf16[2,192,1536]{2,1,0:T(8,128)(2,1)} %add.136.refs_22_), channel_id=1, source_target_pairs={{0,32},{16,48},{32,0},{48,16},{1,33},{17,49},{33,1},{49,17},{2,34}... | collective-permute-start | bytes 3538952 | tf_op jit(solution)/shard_map/ppermute | solution.py:170
  (114 other events, 905.0 us)
Sparse Core Ops, SparseCore 0:
  11.7 98.5 all-gather.1

commit v7 on v6

--- a/solution.py
+++ b/solution.py
@@ -125,7 +125,7 @@
             if isinstance(one, Sent):
                 done_with(one.copies)
 
-    anywhere, local = pl.BlockSpec(memory_space=pl.ANY), pl.BlockSpec(memory_space=pltpu.VMEM)
+    anywhere, local = pl.BlockSpec(memory_space=pltpu.HBM), pl.BlockSpec(memory_space=pltpu.VMEM)
     return pl.pallas_call(
         run,
         out_shape=tuple(shapes),
@@ -237,6 +237,44 @@
                 pair[:, begin - width : begin - width + HEAD_DIM] = head
 
 
+def project_all(entering, gain, cosine, sine, dense, pair, *rest):
+    outs, (weights, sems) = rest[:-2], rest[-2:]
+    micro, tokens, width = entering.shape
+    cuts = cuts_of(weights.shape[1])
+    copies = [
+        pltpu.make_async_copy(
+            dense.at[:, pl.ds(at, size)], weights.at[:, pl.ds(at, size)], sems.at[k]
+        )
+        for k, (at, size) in enumerate(cuts)
+    ]
+    for copy in copies:
+        copy.start()
+    lows = []
+    for m in range(micro):
+        x = entering[m].astype(F32)
+        outs[2 * m][...] = x
+        lows.append((x * norm_parts(x) * gain[...]).astype(BF))
+    low = jnp.concatenate(lows, 0)
+    cosines = jnp.concatenate([cosine[...]] * micro, 0)
+    sines = jnp.concatenate([sine[...]] * micro, 0)
+    keys = pair.shape[1] // 2
+    for copy, (at, size) in zip(copies, cuts):
+        copy.wait()
+        part = dot(low, weights[:, at : at + size])
+        for begin in range(at, at + size, HEAD_DIM):
+            head = part[:, begin - at : begin - at + HEAD_DIM]
+            if begin < width + keys:
+                head = turned(head, cosines, sines)
+            head = head.astype(BF)
+            if begin < width:
+                for m in range(micro):
+                    outs[2 * m + 1][:, begin : begin + HEAD_DIM] = head[
+                        m * tokens : (m + 1) * tokens
+                    ]
+            else:
+                pair[:, begin - width : begin - width + HEAD_DIM] = head
+
+
 def slot_experts(slots):
     own = lax.broadcasted_iota(jnp.int32, (slots, LANES), 0) // ROOMS
     return own == lax.broadcasted_iota(jnp.int32, (slots, LANES), 1)
@@ -249,7 +287,7 @@
 
 
 def attend(
-    keep, stream, query, pair0, pair1, pair2, pair3, bias, gain, chosen, dispatch, *rest,
+    keep, m, stream, query, pair0, pair1, pair2, pair3, bias, gain, chosen, dispatch, *rest,
 ):
     (normed, target), rest = (rest[:2], rest[2:]) if keep else ((None, None), rest)
     dense, middle, gates, outgoing = rest[:4]
@@ -268,11 +306,13 @@
         copies += [pltpu.make_async_copy(a, b, sems.at[2 + k]) for k, (a, b) in enumerate(own)]
     for copy in copies:
         copy.start()
-    pairs = jnp.concatenate([pair0[...], pair1[...], pair2[...], pair3[...]], 0)
+    tokens = stream.shape[0]
+    pairs = jnp.concatenate(
+        [p[m * tokens : (m + 1) * tokens, :] for p in (pair0, pair1, pair2, pair3)], 0
+    )
     kv_heads = pairs.shape[1] // (2 * HEAD_DIM)
     group = width // HEAD_DIM // kv_heads
     biases = jnp.concatenate([bias[...]] * group, 0)
-    tokens = stream.shape[0]
     for h in range(kv_heads):
         keys = pairs[:, h * HEAD_DIM : (h + 1) * HEAD_DIM]
         values = pairs[:, (kv_heads + h) * HEAD_DIM : (kv_heads + h + 1) * HEAD_DIM]
@@ -540,17 +580,16 @@
     backs[:, width + keys :] = total[:, keys:].astype(BF)
     if keep:
         share = backs.shape[1] // 4
-        for s, out in enumerate(kept[2:]):
+        for s, out in enumerate(kept[1:]):
             out[...] = backs[:, pl.ds(pl.multiple_of((row[0] ^ s) * share, LANES), share)]
     above = jnp.zeros(stream.shape, F32)
     for copy, (at, size) in zip(copies, cuts):
         copy.wait()
         above = above + dot(backs[:, at : at + size], weights[:, at : at + size], (1, 1))
-    part, sums = norm_back(above, stream[...], gain[...])
+    part, unused = norm_back(above, stream[...], gain[...])
     done = middle_grads[...] + part
     if keep:
         kept[0][...] = done
-        kept[1][...] = jnp.broadcast_to(sums, kept[1].shape)
     low[...] = done.astype(BF)
 
 
@@ -588,28 +627,23 @@
 
 
 def out_grads(*refs):
-    lefts, rights, out = refs[:4], refs[4:12], refs[12]
-    share = out.shape[2]
+    lefts, rights, normed, logits, gains, out = (
+        refs[:4], refs[4:12], refs[12:14], refs[14:16], refs[16:18], refs[18],
+    )
+    share = out.shape[2] - LANES
     left = jnp.concatenate([one[k] for one in lefts for k in (2, 3)], 0)
     right = jnp.concatenate([r[:, r.shape[1] - share :] for r in rights], 0)
     by_owner(out, dot(left, right, (0, 0)), 0)
+    width = left.shape[1]
+    line = lax.broadcasted_iota(jnp.int32, (LANES, width), 0)
+    sums = jnp.where(line == LANES - 1, gains[0][:1, :] + gains[1][:1, :], 0.0)
+    by_owner(out, dot(stacked(normed), stacked(logits), (0, 0)) + sums.T, share)
 
 
 def qkv_grads(*refs):
-    lefts, rights, normed, logits, gains, out = (
-        refs[:4], refs[4:12], refs[12:14], refs[14:16], refs[16:20], refs[20],
-    )
-    wide = out.shape[2]
+    lefts, rights, out = refs[:4], refs[4:12], refs[12]
     left = jnp.concatenate([one[k] for one in lefts for k in (0, 1)], 0)
     by_owner(out, dot(left, stacked(rights), (0, 0)), 0)
-    width = left.shape[1]
-    first = gains[0][:1, :] + gains[1][:1, :]
-    second = gains[2][:1, :] + gains[3][:1, :]
-    line = lax.broadcasted_iota(jnp.int32, (LANES, width), 0)
-    sums = jnp.where(
-        line == LANES - 2, first, jnp.where(line == LANES - 1, second, jnp.zeros((1, 1), F32))
-    )
-    by_owner(out, dot(stacked(normed), stacked(logits), (0, 0)) + sums.T, wide - LANES)
 
 
 def fold(row, first, second, out0, out1, out2, out3, total):
@@ -622,7 +656,8 @@
 
 
 def finish(
-    row, in0, in1, in2, in3, o_grad, q_grad, k_grad, v_grad, r_grad, first, second, total
+    row, in0, in1, in2, in3, w_query, w_key, w_value, gain, o_grad, q_grad, k_grad, v_grad, r_grad,
+    first, second, total,
 ):
     share = o_grad.shape[1] // 4
     piece = total.shape[1] // 4
@@ -630,16 +665,18 @@
     for s, one in enumerate(ins):
         where = row[0] ^ s
         o_grad[:, pl.ds(pl.multiple_of(where * share, LANES), share)] = one[:, :share]
-        total[:, pl.ds(pl.multiple_of(where * piece, LANES), piece)] = one[:, share : share + piece]
-    rest = sum(one[:, share + piece :] for one in ins)
+        total[:, pl.ds(pl.multiple_of(where * piece, LANES), piece)] = one[:, share + LANES :]
+    rest = sum(one[:, share : share + LANES] for one in ins)
     r_grad[...] = rest[:, : r_grad.shape[1]]
-    turned_rest = rest.T
-    first[...] = turned_rest[LANES - 2 : LANES - 1, :]
-    second[...] = turned_rest[LANES - 1 :, :]
-    begin = 0
-    for out in (q_grad, k_grad, v_grad):
-        out[...] = total[:, begin : begin + out.shape[1]]
+    second[...] = rest.T[LANES - 1 :, :]
+    begin, inner = 0, jnp.zeros((total.shape[0], 1), F32)
+    for out, weight in ((q_grad, w_query), (k_grad, w_key), (v_grad, w_value)):
+        part = total[:, begin : begin + out.shape[1]]
+        out[...] = part
+        inner = inner + jnp.sum(part * weight[...].astype(F32), -1, keepdims=True)
         begin += out.shape[1]
+    line = jnp.broadcast_to(inner, (total.shape[0], LANES)).T[:1, :]
+    first[...] = line / gain[...].astype(F32)
 
 
 def over_columns(value):
@@ -751,28 +788,36 @@
     def forward(came, entering, targets, waits, down):
         keep = bool(targets)
         projected, pairs = [], []
-        for m in pieces:
-            projected.append(
-                call(
-                    project, (token_wide, token_low, token_low, pair_like),
-                    (came[m], Late(entering[m]), Late(gain_a), *tables), qkv_flops, (dense,),
-                    qkv_scratch, (second,), waits=(*waits, *(p[0] for p in projected)),
+        if keep:
+            for m in pieces:
+                projected.append(
+                    call(
+                        project, (token_wide, token_low, token_low, pair_like),
+                        (came[m], Late(entering[m]), Late(gain_a), *tables), qkv_flops, (dense,),
+                        qkv_scratch, (second,), waits=[p[0] for p in projected],
+                    )
                 )
+                pairs.append([projected[m][3]] + [swapped(projected[m][3], s) for s in steps[1:]])
+        else:
+            pair, *streams = call(
+                project_all,
+                (like((micro * tokens, 2 * kv_width), BF),) + (token_wide, token_low) * micro,
+                (Late(inputs[:, 0]), Late(gain_a), *tables), micro * qkv_flops, (dense,),
+                qkv_scratch, waits=waits,
             )
-            pair = projected[m][3]
-            pairs.append([swapped(pair, s) for s in steps[1:]])
+            projected = [(streams[2 * m], None, streams[2 * m + 1]) for m in pieces]
+            pairs = [[pair] + [swapped(pair, s) for s in steps[1:]]] * micro
         attended = [
             call(
-                functools.partial(attend, keep),
+                functools.partial(attend, keep, 0 if keep else m),
                 (Sent(token_wide), Sent(lanes_like), Sent(double_like if keep else block_like))
                 + ((Sent(probs_like), Sent(token_low), Sent(token_low), Raw(token_wide),
                     Raw(token_low), Raw(token_low), Raw(like((rows, tokens, 2 * kv_width), BF)))
                    if keep else ()),
-                (projected[m][0], projected[m][2], projected[m][3], *pairs[m],
+                (projected[m][0], projected[m][2], *pairs[m],
                  *late([biases[m], gain_f, chosens[m], dispatches[m]]),
                  *((projected[m][1], Late(targets[m])) if keep else ())),
                 out_flops + 2 * score_flops, (dense,), [pltpu.VMEM((tokens, width), BF)] + out_scratch,
-                waits=() if keep or m else pairs[1],
             )
             for m in pieces
         ]
@@ -787,7 +832,7 @@
             lefts = [left, swapped(left, 1), two, swapped(two, 1)]
             ready = (two,)
         else:
-            two = hold(down[2], attended[1][2])
+            two = hold(down[2], arrived[0], attended[1][2])
             down = (*down[:2], two, swapped(two, 1))
         applied = [
             call(
@@ -807,7 +852,7 @@
             call(
                 functools.partial(expert_weight_grads, side, begin),
                 (Sent(like((per_column, hidden_width // 4, width), BF)),) * 2,
-                late([*left, *right]), expert_flops, waits=() if left is hidden else waits,
+                late([*left, *right]), expert_flops, waits=waits,
             )
             for left, right, begin in (
                 (hidden, arrived_grads, 0), ([a[1] for a in moved], arrived, 0),
@@ -840,8 +885,7 @@
         return call(
             functools.partial(project_back, keep),
             (token_low,)
-            + ((Sent(token_wide), Sent(sums_like))
-               + (like((tokens, qkv_width // rows), BF),) * rows if keep else ()),
+            + ((Sent(token_wide),) + (like((tokens, qkv_width // rows), BF),) * rows if keep else ()),
             (*parts, inner[1], Late(attended[m][6]), Late(gain_a), inner[0],
              *tables),
             qkv_flops, (dense,), [pltpu.VMEM((tokens, qkv_width), BF)] + qkv_scratch,
@@ -893,33 +937,31 @@
         for m in pieces
     ]
     back = [over_columns(a[0]) for a in moved]
-    inner = [attention_back(True, 0, given[0][0], back[0], (moved[1][0],))]
+    far = far_and_near(1, ())
+    down_far = merged(far[0], ())
+    crossed = [swapped(down_far, 2)]
+    inner = [attention_back(True, 0, given[0][0], back[0], (moved[1][0], down_far))]
     parts = [parts_of(inner[0])]
-    outer = [projection_back(True, 0, inner[0], parts[0], ())]
-    far = far_and_near(1, (inner[0][0],))
-    crossed = [swapped(merged(far[0], parts[0][1:]), 2)]
-    inner.append(attention_back(
-        True, 1, given[1][0], back[1], (outer[0][0], *(f[0] for f in far))
-    ))
+    inner.append(attention_back(True, 1, given[1][0], back[1], (inner[0][0], far[1][0])))
     parts.append(parts_of(inner[1]))
-    crossed.append(swapped(merged(far[1], parts[1][1:]), 2))
-    near = far_and_near(0, (inner[1][0],))
+    outer = [projection_back(True, 0, inner[0], parts[0], (inner[1][0],))]
     o_grads = call(
-        out_grads, (Sent(like((columns, rows * shard, share), BF)),),
-        late([*lefts, *[p[s] for s in steps for p in parts]]),
-        2 * width * length * micro * share, waits=(crossed[0],),
+        out_grads, (Sent(like((columns, rows * shard, share + LANES), BF)),),
+        late([*lefts, *[p[s] for s in steps for p in parts], *[a[5] for a in attended],
+              *[a[6] for a in inner], *[a[7] for a in inner]]),
+        2 * width * length * micro * share, waits=(crossed[0], outer[0][0]),
     )[0]
     outer.append(projection_back(True, 1, inner[1], parts[1], (o_grads,)))
-    backs = [[o[3]] + [swapped(o[3 + s], s) for s in steps[1:]] for o in outer]
-    last = merged(far[2], backs[1][1:])
-    crossed.append(swapped(last, 2))
+    far[2] = far_and_near(1, (outer[1][0],))[2]
+    backs = [[o[2]] + [swapped(o[2 + s], s) for s in steps[1:]] for o in outer]
+    last = [merged(f, backs[1][1:]) for f in far[1:]]
+    crossed += [swapped(one, 2) for one in last]
     w_grads = call(
-        qkv_grads, (Sent(like((columns, rows * shard, qkv_width // rows + LANES), BF)),),
-        late([*lefts, *[b[s] for s in steps for b in backs], *[a[5] for a in attended],
-              *[a[6] for a in inner], *[o[2] for o in outer], *[a[7] for a in inner]]),
-        2 * width * length * micro * qkv_width // rows,
-        waits=(near[0][0], crossed[1], last),
+        qkv_grads, (Sent(like((columns, rows * shard, qkv_width // rows), BF)),),
+        late([*lefts, *[b[s] for s in steps for b in backs]]),
+        2 * width * length * micro * qkv_width // rows, waits=(last[0],),
     )[0]
+    near = far_and_near(0, (w_grads, last[1]))
     expert_grads = [
         n[0].astype(F32) + swapped(n[1], 1).astype(F32) + c.astype(F32)
         for n, c in zip(near, crossed)
@@ -943,7 +985,8 @@
         (like((shard, width), F32), like((shard, width), F32), like((shard, kv_width), F32),
          like((shard, kv_width), F32), like((shard, experts), F32), like((1, shard), F32),
          like((1, shard), F32)),
-        pieces_out, 0, scratch=[pltpu.VMEM((shard, qkv_width), F32)], scalars=(here,),
+        (*pieces_out, *late([w_query[0], w_key[0], w_value[0], attn_gain])), 0,
+        scratch=[pltpu.VMEM((shard, qkv_width), F32)], scalars=(here,),
     )
 
     return (

time: 769 us -> 765 us (level)
    pallas_call x41 -> x40, Pallas kernels: 287 us -> 282 us  [call(): pl.pallas_call(run, out_shape=tuple(shapes), in_specs=[pl.BlockSpec(memor...]
    ppermute x54 -> x51, starting transfers between devices: 76.4 us -> 72.8 us  [swapped(): return lax.ppermute(value, 'row', [(r, r ^ step) for r in range(rows)])]
    ppermute x54 -> x51, waiting for transfers between devices: 61.2 us -> 63.1 us  [swapped(): return lax.ppermute(value, 'row', [(r, r ^ step) for r in range(rows)])]
    unnamed x148 -> x158, local copies, waits for them, and re-layouts: 26.2 us -> 26.5 us
  transfers between devices with their start and end apart: 73 -> 70, of which waited for: 28 -> 25; matrix products, arithmetic and copies ran while one was open for 3% -> 3% of each run, Pallas kernels for 35% -> 34%
where the time goes in v7:
time: 765 us; the launch traced here: 754 us
  Pallas kernels  282 us (37%)
  waiting for transfers between devices  235 us (31%)
  starting transfers between devices  166 us (22%)
  local copies, waits for them, and re-layouts  35.3 us (5%)
  other arithmetic  17.9 us (2%)
  between operations  15.8 us (2%)
    pallas_call x40, Pallas kernels, call(): pl.pallas_call(run, out_shape=tuple(shapes), in_specs=[pl.BlockSpec(memor...  282 us
    all_gather x1, waiting for transfers between devices, on_device(): dense = lax.all_gather(dense, ('row', 'col'), axis=0, tiled=True)  91.3 us
    all_to_all x14, starting transfers between devices, over_columns(): return lax.all_to_all(value, 'col', split_axis=0, concat_axis=0, tiled=True)  87.9 us
    ppermute x51, starting transfers between devices, swapped(): return lax.ppermute(value, 'row', [(r, r ^ step) for r in range(rows)])  72.8 us
    ppermute x51, waiting for transfers between devices, swapped(): return lax.ppermute(value, 'row', [(r, r ^ step) for r in range(rows)])  63.1 us
    all_to_all x14, waiting for transfers between devices, over_columns(): return lax.all_to_all(value, 'col', split_axis=0, concat_axis=0, tiled=True)  59.9 us
    unnamed x158, local copies, waits for them, and re-layouts  26.5 us
  transfers between devices with their start and end apart: 70, of which 25 were waited for; matrix products, arithmetic and copies ran while one was open for 3% of the time, Pallas kernels for 34%

profile of v7, /device:TPU:9, one launch (start us, length us, event | category | flops | bytes accessed | tf_op | source)
XLA Modules:
  0.0 753.6 jit_solution(11437005788976301691)
XLA Ops:
  19.0 91.3 %all-gather.2.cloned.1.call-done.refs_4_.refs_10_.refs_6_.refs_12_.refs_14_.refs_11_ = bf16[1536,3712]{1,0:T(8,128)(2,1)} async-done(((bf16[24,3712]{1,0:T(8,128)(2,1)}), bf16[1536,3712]{1,0:T(8,128)(2,1)}) %all-gather.2.cloned.1.call-update) | async-done | bytes 11403280 | tf_op jit(solution)/shard_map/all_gather | solution.py:716
  133.4 7.4 attend.4
  149.8 7.5 attend.5
  157.3 17.7 %collective-permute-done.10.refs_0_ = bf16[2,192,1536]{2,1,0:T(8,128)(2,1)S(1)} collective-permute-done((bf16[2,192,1536]{2,1,0:T(8,128)(2,1)}, bf16[2,192,1536]{2,1,0:T(8,128)(2,1)S(1)}, u32[]{:S(2)}, u32[]{:S(2)}) %collective-permute-start.10) | collective-permute-done | bytes 1179680 | tf_op jit(solution)/shard_map/ppermute | solution.py:170
  184.9 10.3 %expert_forward.4 = bf16[16,32,1536]{2,1,0:T(8,128)(2,1)} custom-call(bf16[16,32,1536]{2,1,0:T(8,128)(2,1)} %all-to-all-done.refs_1_.refs_0_, bf16[2,192,1536]{2,1,0:T(8,128)(2,1)} %bitcast.10.refs_1_.refs_10_, bf16[2,192,1536]{2,1,0:T(8,128)(2,1)} %collective-permute-done.5.refs_2_.refs_11_, bf16[2,192,1536]{2,1,0:T(8,128)(2,1)} %copy-done.1, ...), custom_call_target="tpu_custom_call" | custom-call | flops 3623878656 | bytes 17301504 | tf_op jit(solution)/shard_map/expert_forward/pallas_call | solution.py:129
  195.2 12.4 %all-to-all-done.2.refs_0_ = bf16[16,32,1536]{2,1,0:T(8,128)(2,1)} async-done(((bf16[16,32,1536]{2,1,0:T(8,128)(2,1)}), bf16[16,32,1536]{2,1,0:T(8,128)(2,1)}, u32[]{:S(2)}, u32[]{:S(2)}) %all-to-all-start.2) | async-done | bytes 1572896 | tf_op jit(solution)/shard_map/all_to_all | solution.py:683
  211.4 10.3 %expert_forward.5.refs_5_ = bf16[16,32,1536]{2,1,0:T(8,128)(2,1)} custom-call(bf16[16,32,1536]{2,1,0:T(8,128)(2,1)} %all-to-all-done.2.refs_0_, bf16[2,192,1536]{2,1,0:T(8,128)(2,1)} %bitcast.10.refs_1_.refs_10_, bf16[2,192,1536]{2,1,0:T(8,128)(2,1)} %collective-permute-done.5.refs_2_.refs_11_, bf16[2,192,1536]{2,1,0:T(8,128)(2,1)} %copy-done.1, ...), custom_call_target="tpu_custom_call" | custom-call | flops 3623878656 | bytes 17301504 | tf_op jit(solution)/shard_map/expert_forward/pallas_call | solution.py:129
  221.7 10.1 %all-to-all-done.1.refs_0_ = bf16[16,32,1536]{2,1,0:T(8,128)(2,1)S(1)} async-done(((bf16[16,32,1536]{2,1,0:T(8,128)(2,1)}), bf16[16,32,1536]{2,1,0:T(8,128)(2,1)S(1)}, u32[]{:S(2)}, u32[]{:S(2)}) %all-to-all-start.1) | async-done | bytes 1572896 | tf_op jit(solution)/shard_map/all_to_all | solution.py:683
  270.1 10.1 %attend.6 = (f32[96,1536]{1,0:T(8,128)}, f32[96,128]{1,0:T(8,128)}, bf16[16,64,1536]{2,1,0:T(8,128)(2,1)}, bf16[2,576,384]{2,1,0:T(8,128)(2,1)}, bf16[96,1536]{1...) custom-call(f32[96,1536]{1,0:T(8,128)} %get-tuple-element.148.refs_0, ...), custom_call_target="tpu_custom_call" | custom-call | flops 830472192 | bytes 20404224 | tf_op jit(solution)/shard_map/attend/pallas_call | solution.py:129
  293.5 8.9 %collective-permute-done.16.refs_1_ = bf16[96,1536]{1,0:T(8,128)(2,1)S(1)} collective-permute-done((bf16[96,1536]{1,0:T(8,128)(2,1)}, bf16[96,1536]{1,0:T(8,128)(2,1)S(1)}, u32[]{:S(2)}, u32[]{:S(2)}) %collective-permute-start.16) | collective-permute-done | bytes 294944 | tf_op jit(solution)/shard_map/ppermute | solution.py:908
  319.6 10.1 %attend.7 = (f32[96,1536]{1,0:T(8,128)}, f32[96,128]{1,0:T(8,128)}, bf16[16,64,1536]{2,1,0:T(8,128)(2,1)}, bf16[2,576,384]{2,1,0:T(8,128)(2,1)}, bf16[96,1536]{1...) custom-call(f32[96,1536]{1,0:T(8,128)} %get-tuple-element.156.refs_0, ...), custom_call_target="tpu_custom_call" | custom-call | flops 830472192 | bytes 20404224 | tf_op jit(solution)/shard_map/attend/pallas_call | solution.py:129
  331.3 11.2 %all-to-all-start.6 = ((bf16[16,64,1536]{2,1,0:T(8,128)(2,1)}), bf16[16,64,1536]{2,1,0:T(8,128)(2,1)}, u32[]{:S(2)}, u32[]{:S(2)}) async-start(bf16[16,64,1536]{2,1,0:T(8,128)(2,1)} %get-tuple-element.160.refs_13_), calls=%async_computation.6 | async-start | bytes 6291456 | tf_op jit(solution)/shard_map/all_to_all | solution.py:683
  345.5 16.4 %expert_forward.6 = (bf16[16,32,1536]{2,1,0:T(8,128)(2,1)}, bf16[2,256,768]{2,1,0:T(8,128)(2,1)}, bf16[2,256,768]{2,1,0:T(8,128)(2,1)}, bf16[2,256,768]{2,1,0:T(8,128)(2,1)}, bf16[16,32,1664]{2,1,0:T(8,128)(2,1)}) custom-call(bf16[16,64,1536]{2,1,0:T(8,128)(2,1)} %copy-done, bf16[2,192,1536]{2,1,0:T(8,128)(2,1)} %bitcast.10.refs_1_.refs_10_, ...), custom_call_target="tpu_custom_call" | custom-call | flops 7247757312 | bytes 22937600 | tf_op jit(solution)/shard_map/expert_forward/pallas_call | solution.py:129
  361.9 20.4 %all-to-all-done.6.refs_0_.refs_3_ = bf16[16,64,1536]{2,1,0:T(8,128)(2,1)} async-done(((bf16[16,64,1536]{2,1,0:T(8,128)(2,1)}), bf16[16,64,1536]{2,1,0:T(8,128)(2,1)}, u32[]{:S(2)}, u32[]{:S(2)}) %all-to-all-start.6) | async-done | bytes 3145760 | tf_op jit(solution)/shard_map/all_to_all | solution.py:683
  387.2 16.4 %expert_forward.7 = (bf16[16,32,1536]{2,1,0:T(8,128)(2,1)}, bf16[2,256,768]{2,1,0:T(8,128)(2,1)}, bf16[2,256,768]{2,1,0:T(8,128)(2,1)}, bf16[2,256,768]{2,1,0:T(8,128)(2,1)}, bf16[16,32,1664]{2,1,0:T(8,128)(2,1)}) custom-call(bf16[16,64,1536]{2,1,0:T(8,128)(2,1)} %all-to-all-done.6.refs_0_.refs_3_, bf16[2,192,1536]{2,1,0:T(8,128)(2,1)} %bitcast.10.refs_1_.refs_10_, ...), custom_call_target="tpu_custom_call" | custom-call | flops 7247757312 | bytes 22937600 | tf_op jit(solution)/shard_map/expert_forward/pallas_call | solution.py:129
  407.5 7.1 all-to-all-start.7
  417.2 8.7 %attend_back.4 = (f32[96,1536]{1,0:T(8,128)}, bf16[96,1536]{1,0:T(8,128)(2,1)}, bf16[96,512]{1,0:T(8,128)(2,1)}, bf16[96,512]{1,0:T(8,128)(2,1)}, bf16[96,512]{1,0:T(8,128)(2,1)}, /*index=5*/bf16[96,512]{1,0:T(8,128)(2,1)}) custom-call(s32[1]{0:T(128)} %bitcast.1.refs_0_, s32[1]{0:T(128)} %bitcast.refs_0_.refs_1_, bf16[16,32,1664]{2,1,0:T(8,128)(2,1)} %copy-done.12, ...), custom_call_target="tpu_custom_call" | custom-call | flops 1056964608 | bytes 17225728 | tf_op jit(solution)/shard_map/attend_back/pallas_call | solution.py:129
  436.0 7.5 project_back.4.refs_18_
  446.4 8.7 %attend_back.5 = (f32[96,1536]{1,0:T(8,128)}, bf16[96,1536]{1,0:T(8,128)(2,1)}, bf16[96,512]{1,0:T(8,128)(2,1)}, bf16[96,512]{1,0:T(8,128)(2,1)}, bf16[96,512]{1,0:T(8,128)(2,1)}, /*index=5*/bf16[96,512]{1,0:T(8,128)(2,1)}) custom-call(s32[1]{0:T(128)} %bitcast.1.refs_0_, s32[1]{0:T(128)} %bitcast.refs_0_.refs_1_, bf16[16,32,1664]{2,1,0:T(8,128)(2,1)} %copy-done.10, ...), custom_call_target="tpu_custom_call" | custom-call | flops 1056964608 | bytes 17225728 | tf_op jit(solution)/shard_map/attend_back/pallas_call | solution.py:129
  459.8 6.9 all-to-all-start.8
  476.4 7.4 project_back.5
  497.7 7.5 %all-to-all-start.10 = ((bf16[16,32,1536]{2,1,0:T(8,128)(2,1)}), bf16[16,32,1536]{2,1,0:T(8,128)(2,1)S(1)}, u32[]{:S(2)}, u32[]{:S(2)}) async-start(bf16[16,32,1536]{2,1,0:T(8,128)(2,1)} %get-tuple-element.196.refs_18_), calls=%async_computation.10 | async-start | bytes 3145728 | tf_op jit(solution)/shard_map/all_to_all | solution.py:683
  505.3 10.8 %expert_backward.2 = (bf16[16,32,1664]{2,1,0:T(8,128)(2,1)}, bf16[2,256,768]{2,1,0:T(8,128)(2,1)}, bf16[2,256,768]{2,1,0:T(8,128)(2,1)}) custom-call(s32[1]{0:T(128)} %bitcast.refs_0_.refs_1_, bf16[16,32,1536]{2,1,0:T(8,128)(2,1)} %copy-done.6, bf16[2,256,768]{2,1,0:T(8,128)(2,1)} %get-tuple-element.186.refs_2_.refs_0_, ...), custom_call_target="tpu_custom_call" | custom-call | flops 3623878656 | bytes 22937600 | tf_op jit(solution)/shard_map/expert_backward/pallas_call | solution.py:129
  516.1 9.8 %all-to-all-done.10.refs_1_.refs_3_ = bf16[16,32,1536]{2,1,0:T(8,128)(2,1)S(1)} async-done(((bf16[16,32,1536]{2,1,0:T(8,128)(2,1)}), bf16[16,32,1536]{2,1,0:T(8,128)(2,1)S(1)}, u32[]{:S(2)}, u32[]{:S(2)}) %all-to-all-start.10) | async-done | bytes 1572896 | tf_op jit(solution)/shard_map/all_to_all | solution.py:683
  541.0 10.9 %expert_backward.3 = (bf16[16,32,1664]{2,1,0:T(8,128)(2,1)}, bf16[2,256,768]{2,1,0:T(8,128)(2,1)}, bf16[2,256,768]{2,1,0:T(8,128)(2,1)}) custom-call(s32[1]{0:T(128)} %bitcast.refs_0_.refs_1_, bf16[16,32,1536]{2,1,0:T(8,128)(2,1)} %copy-done.7, bf16[2,256,768]{2,1,0:T(8,128)(2,1)} %get-tuple-element.199.refs_2_.refs_1_, ...), custom_call_target="tpu_custom_call" | custom-call | flops 3623878656 | bytes 22937600 | tf_op jit(solution)/shard_map/expert_backward/pallas_call | solution.py:129
  564.1 9.4 %attend_back.6 = (f32[96,1536]{1,0:T(8,128)}, bf16[96,1536]{1,0:T(8,128)(2,1)}, bf16[96,896]{1,0:T(8,128)(2,1)}, bf16[96,896]{1,0:T(8,128)(2,1)}, bf16[96,896]{1...) custom-call(s32[1]{0:T(128)} %bitcast.1.refs_0_, s32[1]{0:T(128)} %bitcast.refs_0_.refs_1_, ...), custom_call_target="tpu_custom_call" | custom-call | flops 1056964608 | bytes 19167232 | tf_op jit(solution)/shard_map/attend_back/pallas_call | solution.py:129
  588.6 9.4 %attend_back.7 = (f32[96,1536]{1,0:T(8,128)}, bf16[96,1536]{1,0:T(8,128)(2,1)}, bf16[96,896]{1,0:T(8,128)(2,1)}, bf16[96,896]{1,0:T(8,128)(2,1)}, bf16[96,896]{1...) custom-call(s32[1]{0:T(128)} %bitcast.1.refs_0_, s32[1]{0:T(128)} %bitcast.refs_0_.refs_1_, ...), custom_call_target="tpu_custom_call" | custom-call | flops 1056964608 | bytes 19167232 | tf_op jit(solution)/shard_map/attend_back/pallas_call | solution.py:129
  602.6 8.7 %project_back.6 = (bf16[96,1536]{1,0:T(8,128)(2,1)}, f32[96,1536]{1,0:T(8,128)}, bf16[96,512]{1,0:T(8,128)(2,1)}, bf16[96,512]{1,0:T(8,128)(2,1)}, bf16[96,512]{1,0:T(8,128)(2,1)}, /*index=5*/bf16[96,512]{1,0:T(8,128)(2,1)}) custom-call(s32[1]{0:T(128)} %bitcast.1.refs_0_, bf16[96,896]{1,0:T(8,128)(2,1)} %get-tuple-element.208.refs_1_.refs_4_, ...), custom_call_target="tpu_custom_call" | custom-call | flops 603979776 | bytes 14948352 | tf_op jit(solution)/shard_map/project_back/pallas_call | solution.py:129
  619.3 6.9 all-to-all-start.12
  626.5 8.5 %project_back.7 = (bf16[96,1536]{1,0:T(8,128)(2,1)}, f32[96,1536]{1,0:T(8,128)}, bf16[96,512]{1,0:T(8,128)(2,1)}, bf16[96,512]{1,0:T(8,128)(2,1)}, bf16[96,512]{1,0:T(8,128)(2,1)}, /*index=5*/bf16[96,512]{1,0:T(8,128)(2,1)}) custom-call(s32[1]{0:T(128)} %bitcast.1.refs_0_, bf16[96,896]{1,0:T(8,128)(2,1)} %get-tuple-element.220.refs_5_.refs_1_, ...), custom_call_target="tpu_custom_call" | custom-call | flops 603979776 | bytes 14948352 | tf_op jit(solution)/shard_map/project_back/pallas_call | solution.py:129
  662.1 7.0 all-to-all-start.13
  725.9 17.0 %collective-permute-done.53 = bf16[2,192,1536]{2,1,0:T(8,128)(2,1)} collective-permute-done((bf16[2,192,1536]{2,1,0:T(8,128)(2,1)S(1)}, bf16[2,192,1536]{2,1,0:T(8,128)(2,1)}, u32[]{:S(2)}, u32[]{:S(2)}) %collective-permute-start.53) | collective-permute-done | bytes 1179680 | tf_op jit(solution)/shard_map/ppermute | solution.py:170
  (353 shorter events, 325.1 us)
Async XLA Ops:
  7.2 103.1 %all-gather.2.cloned.1.call-start = ((), (), s32[]{:S(2)}) async-start(), calls=%async_computation.14 | async-start | bytes 11581440 | tf_op jit(solution)/shard_map/all_gather | solution.py:716
  10.5 102.1 %collective-permute-start = (bf16[2,192,1536]{2,1,0:T(8,128)(2,1)}, bf16[2,192,1536]{2,1,0:T(8,128)(2,1)S(1)}, u32[]{:S(2)}, u32[]{:S(2)}) collective-permute-start(bf16[2,192,1536]{2,1,0:T(8,128)(2,1)} %bitcast.10.refs_1_.refs_10_), channel_id=1, source_target_pairs={{0,32},{16,48},{32,0},{48,16},{1,33},{17,49},{33,1},{49,17},{2,34}... | collective-permute-start | bytes 3538952 | tf_op jit(solution)/shard_map/ppermute | solution.py:170
  12.6 100.1 %collective-permute-start.1 = (bf16[2,192,1536]{2,1,0:T(8,128)(2,1)}, bf16[2,192,1536]{2,1,0:T(8,128)(2,1)S(1)}, u32[]{:S(2)}, u32[]{:S(2)}) collective-permute-start(bf16[2,192,1536]{2,1,0:T(8,128)(2,1)} %bitcast.11.refs_5_.refs_14_), channel_id=1, source_target_pairs={{0,32},{16,48},{32,0},{48,16},{1,33},{17,49},{33,1},{49,17},{2,34}... | collective-permute-start | bytes 3538952 | tf_op jit(solution)/shard_map/ppermute | solution.py:170
  140.8 35.3 %all-to-all-start = ((bf16[16,32,1536]{2,1,0:T(8,128)(2,1)}), bf16[16,32,1536]{2,1,0:T(8,128)(2,1)}, u32[]{:S(2)}, u32[]{:S(2)}) async-start(bf16[16,32,1536]{2,1,0:T(8,128)(2,1)} %get-tuple-element.141), calls=%async_computation | async-start | bytes 3145728 | tf_op jit(solution)/shard_map/all_to_all | solution.py:683
  145.9 29.1 %collective-permute-start.10 = (bf16[2,192,1536]{2,1,0:T(8,128)(2,1)}, bf16[2,192,1536]{2,1,0:T(8,128)(2,1)S(1)}, u32[]{:S(2)}, u32[]{:S(2)}) collective-permute-start(bf16[2,192,1536]{2,1,0:T(8,128)(2,1)} %bitcast.19.refs_9_.refs_6_), channel_id=1, source_target_pairs={{0,32},{16,48},{32,0},{48,16},{1,33},{17,49},{33,1},{49,17},{2,34}... | collective-permute-start | bytes 3538952 | tf_op jit(solution)/shard_map/ppermute | solution.py:170
  147.2 29.0 %collective-permute-start.5 = (bf16[2,192,1536]{2,1,0:T(8,128)(2,1)}, bf16[2,192,1536]{2,1,0:T(8,128)(2,1)}, u32[]{:S(2)}, u32[]{:S(2)}) collective-permute-start(bf16[2,192,1536]{2,1,0:T(8,128)(2,1)} %bitcast.10.refs_1_.refs_10_), channel_id=1, source_target_pairs={{0,16},{16,0},{32,48},{48,32},{1,17},{17,1},{33,49},{49,33},{2,18}... | collective-permute-start | bytes 3538952 | tf_op jit(solution)/shard_map/ppermute | solution.py:170
  147.7 36.1 %collective-permute-start.7 = (bf16[2,192,1536]{2,1,0:T(8,128)(2,1)}, bf16[2,192,1536]{2,1,0:T(8,128)(2,1)}, u32[]{:S(2)}, u32[]{:S(2)}) collective-permute-start(bf16[2,192,1536]{2,1,0:T(8,128)(2,1)} %bitcast.11.refs_5_.refs_14_), channel_id=1, source_target_pairs={{0,16},{16,0},{32,48},{48,32},{1,17},{17,1},{33,49},{49,33},{2,18}... | collective-permute-start | bytes 3538952 | tf_op jit(solution)/shard_map/ppermute | solution.py:170
  147.7 36.1 %collective-permute-start.9 = (bf16[2,192,1536]{2,1,0:T(8,128)(2,1)}, bf16[2,192,1536]{2,1,0:T(8,128)(2,1)}, u32[]{:S(2)}, u32[]{:S(2)}) collective-permute-start(bf16[2,192,1536]{2,1,0:T(8,128)(2,1)} %bitcast.19.refs_9_.refs_6_), channel_id=1, source_target_pairs={{0,16},{16,0},{32,48},{48,32},{1,17},{17,1},{33,49},{49,33},{2,18}... | collective-permute-start | bytes 3538952 | tf_op jit(solution)/shard_map/ppermute | solution.py:170
  149.6 34.2 %collective-permute-start.6 = (bf16[2,192,1536]{2,1,0:T(8,128)(2,1)S(1)}, bf16[2,192,1536]{2,1,0:T(8,128)(2,1)}, u32[]{:S(2)}, u32[]{:S(2)}) collective-permute-start(bf16[2,192,1536]{2,1,0:T(8,128)(2,1)S(1)} %copy-done.2), channel_id=1, source_target_pairs={{0,16},{16,0},{32,48},{48,32},{1,17},{17,1},{33,49},{49,33},{2,18}... | collective-permute-start | bytes 3538952 | tf_op jit(solution)/shard_map/ppermute | solution.py:170
  177.2 30.4 %all-to-all-start.2 = ((bf16[16,32,1536]{2,1,0:T(8,128)(2,1)}), bf16[16,32,1536]{2,1,0:T(8,128)(2,1)}, u32[]{:S(2)}, u32[]{:S(2)}) async-start(bf16[16,32,1536]{2,1,0:T(8,128)(2,1)} %get-tuple-element.144.refs_2_.refs_13_), calls=%async_computation.2 | async-start | bytes 3145728 | tf_op jit(solution)/shard_map/all_to_all | solution.py:683
  207.6 24.2 %all-to-all-start.1 = ((bf16[16,32,1536]{2,1,0:T(8,128)(2,1)}), bf16[16,32,1536]{2,1,0:T(8,128)(2,1)S(1)}, u32[]{:S(2)}, u32[]{:S(2)}) async-start(bf16[16,32,1536]{2,1,0:T(8,128)(2,1)} %expert_forward.4), calls=%async_computation.1 | async-start | bytes 3145728 | tf_op jit(solution)/shard_map/all_to_all | solution.py:683
  232.9 47.3 %all-to-all-start.4 = ((bf16[16,32,1536]{2,1,0:T(8,128)(2,1)}), bf16[16,32,1536]{2,1,0:T(8,128)(2,1)S(1)}, u32[]{:S(2)}, u32[]{:S(2)}) async-start(bf16[16,32,1536]{2,1,0:T(8,128)(2,1)} %expert_forward.5.refs_5_), calls=%async_computation.4 | async-start | bytes 3145728 | tf_op jit(solution)/shard_map/all_to_all | solution.py:683
  281.4 48.3 %all-to-all-start.3 = ((bf16[16,64,1536]{2,1,0:T(8,128)(2,1)}), bf16[16,64,1536]{2,1,0:T(8,128)(2,1)S(1)}, u32[]{:S(2)}, u32[]{:S(2)}) async-start(bf16[16,64,1536]{2,1,0:T(8,128)(2,1)} %get-tuple-element.152), calls=%async_computation.3 | async-start | bytes 6291456 | tf_op jit(solution)/shard_map/all_to_all | solution.py:683
  331.3 51.0 %all-to-all-start.6 = ((bf16[16,64,1536]{2,1,0:T(8,128)(2,1)}), bf16[16,64,1536]{2,1,0:T(8,128)(2,1)}, u32[]{:S(2)}, u32[]{:S(2)}) async-start(bf16[16,64,1536]{2,1,0:T(8,128)(2,1)} %get-tuple-element.160.refs_13_), calls=%async_computation.6 | async-start | bytes 6291456 | tf_op jit(solution)/shard_map/all_to_all | solution.py:683
  345.0 41.2 %collective-permute-start.20 = (bf16[4,96,1536]{2,1,0:T(8,128)(2,1)}, bf16[4,96,1536]{2,1,0:T(8,128)(2,1)S(1)}, u32[]{:S(2)}, u32[]{:S(2)}) collective-permute-start(bf16[4,96,1536]{2,1,0:T(8,128)(2,1)} %pack.1.refs_0_), channel_id=1, source_target_pairs={{0,32},{16,48},{32,0},{48,16},{1,33},{17,49},{33,1},{49,17},{2,34}... | collective-permute-start | bytes 3538952 | tf_op jit(solution)/shard_map/ppermute | solution.py:170
  407.5 37.3 %all-to-all-start.7 = ((bf16[16,32,1664]{2,1,0:T(8,128)(2,1)}), bf16[16,32,1664]{2,1,0:T(8,128)(2,1)S(1)}, u32[]{:S(2)}, u32[]{:S(2)}) async-start(bf16[16,32,1664]{2,1,0:T(8,128)(2,1)} %get-tuple-element.171.refs_15_), calls=%async_computation.7 | async-start | bytes 3407872 | tf_op jit(solution)/shard_map/all_to_all | solution.py:683
  414.6 30.2 %collective-permute-start.25 = (bf16[4,96,1536]{2,1,0:T(8,128)(2,1)}, bf16[4,96,1536]{2,1,0:T(8,128)(2,1)S(1)}, u32[]{:S(2)}, u32[]{:S(2)}) collective-permute-start(bf16[4,96,1536]{2,1,0:T(8,128)(2,1)} %pack.1.refs_0_), channel_id=1, source_target_pairs={{0,16},{16,0},{32,48},{48,32},{1,17},{17,1},{33,49},{49,33},{2,18}... | collective-permute-start | bytes 3538952 | tf_op jit(solution)/shard_map/ppermute | solution.py:170
  417.1 27.7 %collective-permute-start.26 = (bf16[4,96,1536]{2,1,0:T(8,128)(2,1)}, bf16[4,96,1536]{2,1,0:T(8,128)(2,1)}, u32[]{:S(2)}, u32[]{:S(2)}) collective-permute-start(bf16[4,96,1536]{2,1,0:T(8,128)(2,1)} %copy-done.13), channel_id=1, source_target_pairs={{0,16},{16,0},{32,48},{48,32},{1,17},{17,1},{33,49},{49,33},{2,18}... | collective-permute-start | bytes 3538952 | tf_op jit(solution)/shard_map/ppermute | solution.py:170
  459.8 36.7 %all-to-all-start.8 = ((bf16[16,32,1536]{2,1,0:T(8,128)(2,1)}), bf16[16,32,1536]{2,1,0:T(8,128)(2,1)S(1)}, u32[]{:S(2)}, u32[]{:S(2)}) async-start(bf16[16,32,1536]{2,1,0:T(8,128)(2,1)} %get-tuple-element.185), calls=%async_computation.8 | async-start | bytes 3145728 | tf_op jit(solution)/shard_map/all_to_all | solution.py:683
  497.7 28.1 %all-to-all-start.10 = ((bf16[16,32,1536]{2,1,0:T(8,128)(2,1)}), bf16[16,32,1536]{2,1,0:T(8,128)(2,1)S(1)}, u32[]{:S(2)}, u32[]{:S(2)}) async-start(bf16[16,32,1536]{2,1,0:T(8,128)(2,1)} %get-tuple-element.196.refs_18_), calls=%async_computation.10 | async-start | bytes 3145728 | tf_op jit(solution)/shard_map/all_to_all | solution.py:683
  527.0 26.6 %all-to-all-start.9 = ((bf16[16,32,1664]{2,1,0:T(8,128)(2,1)}), bf16[16,32,1664]{2,1,0:T(8,128)(2,1)}, u32[]{:S(2)}, u32[]{:S(2)}) async-start(bf16[16,32,1664]{2,1,0:T(8,128)(2,1)} %get-tuple-element.197), calls=%async_computation.9 | async-start | bytes 3407872 | tf_op jit(solution)/shard_map/all_to_all | solution.py:683
  553.6 33.8 %all-to-all-start.11 = ((bf16[16,32,1664]{2,1,0:T(8,128)(2,1)}), bf16[16,32,1664]{2,1,0:T(8,128)(2,1)S(1)}, u32[]{:S(2)}, u32[]{:S(2)}) async-start(bf16[16,32,1664]{2,1,0:T(8,128)(2,1)} %get-tuple-element.203.refs_15_), calls=%async_computation.11 | async-start | bytes 3407872 | tf_op jit(solution)/shard_map/all_to_all | solution.py:683
  562.7 48.7 %collective-permute-start.38 = (bf16[2,192,1536]{2,1,0:T(8,128)(2,1)}, bf16[2,192,1536]{2,1,0:T(8,128)(2,1)S(1)}, u32[]{:S(2)}, u32[]{:S(2)}) collective-permute-start(bf16[2,192,1536]{2,1,0:T(8,128)(2,1)} %add.134.refs_16_), channel_id=1, source_target_pairs={{0,32},{16,48},{32,0},{48,16},{1,33},{17,49},{33,1},{49,17},{2,34}... | collective-permute-start | bytes 3538952 | tf_op jit(solution)/shard_map/ppermute | solution.py:170
  573.5 24.8 %collective-permute-start.32 = (bf16[96,896]{1,0:T(8,128)(2,1)}, bf16[96,896]{1,0:T(8,128)(2,1)S(1)}, u32[]{:S(2)}, u32[]{:S(2)}) collective-permute-start(bf16[96,896]{1,0:T(8,128)(2,1)} %get-tuple-element.209), channel_id=1, source_target_pairs={{0,16},{16,0},{32,48},{48,32},{1,17},{17,1},{33,49},{49,33},{2,18}... | collective-permute-start | bytes 516104 | tf_op jit(solution)/shard_map/ppermute | solution.py:170
  619.3 41.7 %all-to-all-start.12 = ((bf16[16,96,512]{2,1,0:T(8,128)(2,1)}), bf16[16,96,512]{2,1,0:T(8,128)(2,1)S(1)}, u32[]{:S(2)}, u32[]{:S(2)}) async-start(bf16[16,96,512]{2,1,0:T(8,128)(2,1)} %out_grads.1.refs_12_), calls=%async_computation.12 | async-start | bytes 3145728 | tf_op jit(solution)/shard_map/all_to_all | solution.py:683
  641.5 27.6 %collective-permute-start.49 = (bf16[2,192,1536]{2,1,0:T(8,128)(2,1)}, bf16[2,192,1536]{2,1,0:T(8,128)(2,1)}, u32[]{:S(2)}, u32[]{:S(2)}) collective-permute-start(bf16[2,192,1536]{2,1,0:T(8,128)(2,1)} %get-tuple-element.257), channel_id=1, source_target_pairs={{0,16},{16,0},{32,48},{48,32},{1,17},{17,1},{33,49},{49,33},{2,18}... | collective-permute-start | bytes 3538952 | tf_op jit(solution)/shard_map/ppermute | solution.py:170
  662.1 27.7 %all-to-all-start.13 = ((bf16[16,96,512]{2,1,0:T(8,128)(2,1)}), bf16[16,96,512]{2,1,0:T(8,128)(2,1)S(1)}, u32[]{:S(2)}, u32[]{:S(2)}) async-start(bf16[16,96,512]{2,1,0:T(8,128)(2,1)} %qkv_grads.1.refs_12_.refs_4_), calls=%async_computation.13 | async-start | bytes 3145728 | tf_op jit(solution)/shard_map/all_to_all | solution.py:683
  677.5 41.6 %collective-permute-start.54 = (bf16[2,192,1536]{2,1,0:T(8,128)(2,1)}, bf16[2,192,1536]{2,1,0:T(8,128)(2,1)}, u32[]{:S(2)}, u32[]{:S(2)}) collective-permute-start(bf16[2,192,1536]{2,1,0:T(8,128)(2,1)} %get-tuple-element.263), channel_id=1, source_target_pairs={{0,16},{16,0},{32,48},{48,32},{1,17},{17,1},{33,49},{49,33},{2,18}... | collective-permute-start | bytes 3538952 | tf_op jit(solution)/shard_map/ppermute | solution.py:170
  678.4 43.9 %collective-permute-start.51 = (bf16[2,192,1536]{2,1,0:T(8,128)(2,1)}, bf16[2,192,1536]{2,1,0:T(8,128)(2,1)}, u32[]{:S(2)}, u32[]{:S(2)}) collective-permute-start(bf16[2,192,1536]{2,1,0:T(8,128)(2,1)} %add.135.refs_12_), channel_id=1, source_target_pairs={{0,32},{16,48},{32,0},{48,16},{1,33},{17,49},{33,1},{49,17},{2,34}... | collective-permute-start | bytes 3538952 | tf_op jit(solution)/shard_map/ppermute | solution.py:170
  686.6 35.7 %collective-permute-start.50 = (bf16[2,192,1536]{2,1,0:T(8,128)(2,1)}, bf16[2,192,1536]{2,1,0:T(8,128)(2,1)}, u32[]{:S(2)}, u32[]{:S(2)}) collective-permute-start(bf16[2,192,1536]{2,1,0:T(8,128)(2,1)} %get-tuple-element.259), channel_id=1, source_target_pairs={{0,16},{16,0},{32,48},{48,32},{1,17},{17,1},{33,49},{49,33},{2,18}... | collective-permute-start | bytes 3538952 | tf_op jit(solution)/shard_map/ppermute | solution.py:170
  713.8 29.1 %collective-permute-start.53 = (bf16[2,192,1536]{2,1,0:T(8,128)(2,1)S(1)}, bf16[2,192,1536]{2,1,0:T(8,128)(2,1)}, u32[]{:S(2)}, u32[]{:S(2)}) collective-permute-start(bf16[2,192,1536]{2,1,0:T(8,128)(2,1)S(1)} %copy-done.9), channel_id=1, source_target_pairs={{0,32},{16,48},{32,0},{48,16},{1,33},{17,49},{33,1},{49,17},{2,34}... | collective-permute-start | bytes 3538952 | tf_op jit(solution)/shard_map/ppermute | solution.py:170
  715.3 27.6 %collective-permute-start.52 = (bf16[2,192,1536]{2,1,0:T(8,128)(2,1)}, bf16[2,192,1536]{2,1,0:T(8,128)(2,1)}, u32[]{:S(2)}, u32[]{:S(2)}) collective-permute-start(bf16[2,192,1536]{2,1,0:T(8,128)(2,1)} %get-tuple-element.261), channel_id=1, source_target_pairs={{0,16},{16,0},{32,48},{48,32},{1,17},{17,1},{33,49},{49,33},{2,18}... | collective-permute-start | bytes 3538952 | tf_op jit(solution)/shard_map/ppermute | solution.py:170
  (116 other events, 940.8 us)
Sparse Core Ops, SparseCore 0:
  11.7 98.5 all-gather.1

commit v8 on v7

--- a/solution.py
+++ b/solution.py
@@ -27,9 +27,10 @@
 
 
 class Late:
-    def __init__(self, source, target=None, sem=None):
-        self.source, self.target, self.copy = source, target, None
+    def __init__(self, source, index=None, target=None, sem=None):
+        self.source, self.index, self.target, self.copy = source, index, target, None
         if target is not None:
+            source = source if index is None else source.at[index]
             self.copy = pltpu.make_async_copy(source, target, sem)
             self.copy.start()
             self.waiting = True
@@ -45,7 +46,7 @@
 
     @property
     def shape(self):
-        return self.source.shape
+        return self.source.shape[len(self.index or ()) :]
 
 
 class Sent:
@@ -75,11 +76,6 @@
         return self.source.shape
 
 
-class Raw:
-    def __init__(self, source):
-        self.source = source
-
-
 PARTS = 4
 
 
@@ -90,13 +86,12 @@
 
 def call(body, outs, args, flops, far=(), scratch=(), scalars=(), waits=()):
     arrays = [a.source if isinstance(a, Late) else a for a in args]
-    shapes = [o.source if isinstance(o, (Sent, Raw)) else o for o in outs]
+    shapes = [o.source if isinstance(o, Sent) else o for o in outs]
     moved = sum(a.size * a.dtype.itemsize for a in (*arrays, *far, *shapes))
     count = len(scalars) + len(args) + len(far)
     kinds = [isinstance(a, Late) for a in args]
     out_kinds = [isinstance(o, Sent) for o in outs]
-    raw_kinds = [isinstance(o, Raw) for o in outs]
-    buffers = [pltpu.VMEM(a.shape, a.dtype) for a, k in zip(arrays, kinds) if k]
+    buffers = [pltpu.VMEM(a.shape, a.source.dtype) for a in args if isinstance(a, Late)]
     buffers += [pltpu.VMEM(o.shape, o.dtype) for o, k in zip(shapes, out_kinds) if k]
 
     def run(*refs):
@@ -108,7 +103,7 @@
         for k, kind in enumerate(kinds):
             if kind:
                 at = len(scalars) + k
-                given[at] = Late(given[at], own[used], sems.at[used, 0])
+                given[at] = Late(given[at], args[k].index, own[used], sems.at[used, 0])
                 used += 1
         for k, kind in enumerate(out_kinds):
             if kind:
@@ -132,13 +127,11 @@
         in_specs=[pl.BlockSpec(memory_space=pltpu.SMEM)] * len(scalars)
         + [anywhere if k else local for k in kinds]
         + [anywhere] * (len(far) + len(waits)),
-        out_specs=tuple(
-            anywhere if k or raw else local for k, raw in zip(out_kinds, raw_kinds)
-        ),
+        out_specs=tuple(anywhere if k else local for k in out_kinds),
         scratch_shapes=buffers
         + ([pltpu.SemaphoreType.DMA((len(buffers), PARTS))] if buffers else [])
         + list(scratch),
-        compiler_params=pltpu.CompilerParams(vmem_limit_bytes=60 * MIB),
+        compiler_params=pltpu.CompilerParams(vmem_limit_bytes=64 * MIB),
         cost_estimate=pl.CostEstimate(
             flops=int(flops), bytes_accessed=int(moved), transcendentals=0
         ),
@@ -220,8 +213,10 @@
         copy.start()
     x = jnp.where(flag[0] > 0, came[...].astype(F32), entering[...].astype(F32))
     stream[...] = x
+    sent(stream)
     low = (x * norm_parts(x) * gain[...]).astype(BF)
     normed[...] = low
+    sent(normed)
     keys = pair.shape[1] // 2
     for copy, (at, size) in zip(copies, cuts):
         copy.wait()
@@ -235,11 +230,13 @@
                 query[:, begin : begin + HEAD_DIM] = head
             else:
                 pair[:, begin - width : begin - width + HEAD_DIM] = head
+            if begin + HEAD_DIM == width:
+                sent(query)
 
 
 def project_all(entering, gain, cosine, sine, dense, pair, *rest):
     outs, (weights, sems) = rest[:-2], rest[-2:]
-    micro, tokens, width = entering.shape
+    micro, unused, tokens, width = entering.shape
     cuts = cuts_of(weights.shape[1])
     copies = [
         pltpu.make_async_copy(
@@ -251,8 +248,9 @@
         copy.start()
     lows = []
     for m in range(micro):
-        x = entering[m].astype(F32)
+        x = entering[m, 0].astype(F32)
         outs[2 * m][...] = x
+        sent(outs[2 * m])
         lows.append((x * norm_parts(x) * gain[...]).astype(BF))
     low = jnp.concatenate(lows, 0)
     cosines = jnp.concatenate([cosine[...]] * micro, 0)
@@ -273,6 +271,9 @@
                     ]
             else:
                 pair[:, begin - width : begin - width + HEAD_DIM] = head
+            if begin + HEAD_DIM == width:
+                for m in range(micro):
+                    sent(outs[2 * m + 1])
 
 
 def slot_experts(slots):
@@ -289,7 +290,7 @@
 def attend(
     keep, m, stream, query, pair0, pair1, pair2, pair3, bias, gain, chosen, dispatch, *rest,
 ):
-    (normed, target), rest = (rest[:2], rest[2:]) if keep else ((None, None), rest)
+    (target,), rest = (rest[:1], rest[1:]) if keep else ((None,), rest)
     dense, middle, gates, outgoing = rest[:4]
     kept, (mixed, weights, router, sems) = rest[4:-4], rest[-4:]
     width = stream.shape[1]
@@ -300,10 +301,6 @@
         pltpu.make_async_copy(dense.at[:, pl.ds(at + LANES, width)], weights, sems.at[0]),
         pltpu.make_async_copy(dense.at[:, pl.ds(at, LANES)], router, sems.at[1]),
     ]
-    if keep:
-        own = [(stream, kept[3]), (query, kept[4]), (normed, kept[5])]
-        own += [(p, kept[6].at[k]) for k, p in enumerate((pair0, pair1, pair2, pair3))]
-        copies += [pltpu.make_async_copy(a, b, sems.at[2 + k]) for k, (a, b) in enumerate(own)]
     for copy in copies:
         copy.start()
     tokens = stream.shape[0]
@@ -351,7 +348,6 @@
         sent(outgoing, (slice(None), pl.ds(0, per)))
         outgoing[:, per:, :] = scaled_rows(slots, share, target[...]).reshape(block)
         sent(outgoing, (slice(None), pl.ds(per, per)))
-    done_with(copies[2:])
 
 
 class Fetched:
@@ -439,11 +435,9 @@
                 sent(out, j)
 
 
-def combine(returned, middle, gates, spread, places, result, low):
+def combine(returned, middle, gates, spread, places, low):
     weights = (dot(gates[...].astype(BF), spread[...]) * places[...].astype(F32)).astype(BF)
     done = middle[...] + dot(weights, returned[...].reshape(-1, returned.shape[2]))
-    result[...] = done
-    sent(result)
     low[...] = done.astype(BF)
 
 
@@ -454,7 +448,7 @@
         returned, middle, gates, places, before = refs[5 * m : 5 * m + 5]
         weights = (dot(gates[...].astype(BF), spread[...]) * places[...].astype(F32)).astype(BF)
         rows = returned[:, :, :width].reshape(-1, width)
-        out[m] = jnp.where(flag[0] > 0, middle[...] + dot(weights, rows), before[...])
+        out[m] = jnp.where(flag[0] > 0, middle[...] + dot(weights, rows), before[...].astype(F32))
 
 
 def send_grads(flag, came, target, gates, dispatch, grad, outgoing):
@@ -487,8 +481,9 @@
 
 
 def attend_back(
-    keep, row, flag, token_grads, before, gates, places, middle, gain, grad, query, pairs, probs,
-    cosine, sine, dense, middle_grads, query_back, part0, part1, part2, part3, *rest,
+    keep, row, flag, token_grads, before, gates, places, middle, gain, grad, query, pair0, pair1,
+    pair2, pair3, probs, cosine, sine, dense, middle_grads, query_back, part0, part1, part2, part3,
+    *rest,
 ):
     tokens, width = middle.shape
     kept, (branch, weights, router, sems) = rest[:-4], rest[-4:]
@@ -516,6 +511,7 @@
     part, total = norm_back(ffn_grads, middle[...], gain[...])
     above = grad[...].astype(F32) + part
     middle_grads[...] = above
+    sent(middle_grads)
     low = above.astype(BF)
     if keep:
         kept[0][...] = logit_grads
@@ -529,7 +525,7 @@
             part[:, part.shape[1] - share :] = branch[:, pl.ds(begin, share)]
     copies[1].wait()
     mixed_grads = dot(low, weights[...], (1, 1)).astype(BF)
-    pairs = pairs[...].reshape(-1, pairs.shape[2])
+    pairs = stacked((pair0, pair1, pair2, pair3))
     kv_heads = pairs.shape[1] // (2 * HEAD_DIM)
     group = width // HEAD_DIM // kv_heads
     scale = HEAD_DIM ** (-0.5)
@@ -582,6 +578,7 @@
         share = backs.shape[1] // 4
         for s, out in enumerate(kept[1:]):
             out[...] = backs[:, pl.ds(pl.multiple_of((row[0] ^ s) * share, LANES), share)]
+            sent(out)
     above = jnp.zeros(stream.shape, F32)
     for copy, (at, size) in zip(copies, cuts):
         copy.wait()
@@ -593,20 +590,56 @@
     low[...] = done.astype(BF)
 
 
-def expert_weight_grads(half, begin, left0, left1, right0, right1, first, second):
-    size = first.shape[1]
-    wide = 2 * size
-    for j in range(first.shape[0]):
-        total = dot(left0[j, :, half * wide : (half + 1) * wide], rows_of(right0, j, begin), (0, 0))
-        total = total + dot(
-            left1[j, :, half * wide : (half + 1) * wide], rows_of(right1, j, begin), (0, 0)
-        )
-        first[j] = total[:size].astype(BF)
-        second[j] = total[size:].astype(BF)
-
-
-def add(one, other, total):
-    total[...] = (one[...].astype(F32) + other[...].astype(F32)).astype(BF)
+def expert_weight_grads(begin_left, which, *refs):
+    count = len(which)
+    rights = sorted({w for w in which})
+    sources, outs = refs[: 2 * count + 2 * len(rights)], refs[2 * count + 2 * len(rights) : -3]
+    left, right, sems = refs[-3:]
+    experts, deep, wide = left.shape[1:]
+    columns, width = right.shape[2] // 2, right.shape[4]
+    copies = {}
+    for j in range(experts):
+        for m in range(2):
+            for r, (unused, begin) in enumerate(rights):
+                copies["right", r, j, m] = pltpu.make_async_copy(
+                    sources[2 * count + 2 * r + m].at[:, pl.ds(begin + j * ROOMS, ROOMS), :],
+                    right.at[r, j, pl.ds(m * columns, columns)],
+                    sems.at[1, r, j, m],
+                )
+            for k in range(count):
+                copies["left", k, j, m] = pltpu.make_async_copy(
+                    sources[2 * k + m].at[j, :, pl.ds(begin_left, wide)],
+                    left.at[k, j, pl.ds(m * (deep // 2), deep // 2)],
+                    sems.at[0, k, j, m],
+                )
+    for copy in copies.values():
+        copy.start()
+    waiting = dict(copies)
+
+    def there(*name):
+        for m in range(2):
+            copy = waiting.pop((*name, m), None)
+            if copy is not None:
+                copy.wait()
+
+    for j in range(experts):
+        for k, name in enumerate(which):
+            r = rights.index(name)
+            there("right", r, j)
+            there("left", k, j)
+            total = dot(left[k, j], right[r, j].reshape(deep, width), (0, 0))
+            some = len(outs) // count
+            size = wide // some
+            for q, out in enumerate(outs[some * k : some * (k + 1)]):
+                out[j] = total[q * size : (q + 1) * size].astype(BF)
+                sent(out, j)
+
+
+def add(*refs):
+    count = len(refs) // 3
+    for k in range(count):
+        one, other, total = refs[2 * k], refs[2 * k + 1], refs[2 * count + k]
+        total[...] = (one[...].astype(F32) + other[...].astype(F32)).astype(BF)
 
 
 def pack(*refs):
@@ -653,6 +686,7 @@
     for s, out in enumerate((out0, out1, out2, out3)):
         size = out.shape[0]
         out[...] = total[pl.ds(pl.multiple_of((row[0] ^ s) * size, 8), size), :]
+        sent(out)
 
 
 def finish(
@@ -722,8 +756,7 @@
         two = swapped(own, 2)
         return own, swapped(own, 1), two, swapped(two, 1)
 
-    gate_shards, up_shards = shards_of(w_gate[0]), shards_of(w_up[0])
-    down_shards = (w_down[0], swapped(w_down[0], 1), swapped(w_down[0], 2))
+    gate_shards, up_shards, down_shards = [shards_of(w[0]) for w in (w_gate, w_up, w_down)]
 
     lane = jnp.arange(LANES, dtype=jnp.int32)
     half = HEAD_DIM // 2
@@ -767,7 +800,7 @@
     qkv_scratch = [pltpu.VMEM((width, qkv_width), BF), pltpu.SemaphoreType.DMA((8,))]
     out_scratch = [
         pltpu.VMEM((width, width), BF), pltpu.VMEM((width, LANES), BF),
-        pltpu.SemaphoreType.DMA((16,)),
+        pltpu.SemaphoreType.DMA((2,)),
     ]
     expert_scratch = [
         pltpu.VMEM((3, per_column, hidden_width, width), BF),
@@ -785,15 +818,15 @@
     tables = late([cosine, sine])
     first_flag = (1 - second)
 
-    def forward(came, entering, targets, waits, down):
-        keep = bool(targets)
+    def forward(keep, came, waits, down):
         projected, pairs = [], []
         if keep:
             for m in pieces:
                 projected.append(
                     call(
-                        project, (token_wide, token_low, token_low, pair_like),
-                        (came[m], Late(entering[m]), Late(gain_a), *tables), qkv_flops, (dense,),
+                        project,
+                        (Sent(token_wide), Sent(token_low), Sent(token_low), Sent(pair_like)),
+                        (Late(came[m]), Late(inputs, (m, 0)), Late(gain_a), *tables), qkv_flops, (dense,),
                         qkv_scratch, (second,), waits=[p[0] for p in projected],
                     )
                 )
@@ -801,8 +834,9 @@
         else:
             pair, *streams = call(
                 project_all,
-                (like((micro * tokens, 2 * kv_width), BF),) + (token_wide, token_low) * micro,
-                (Late(inputs[:, 0]), Late(gain_a), *tables), micro * qkv_flops, (dense,),
+                (Sent(like((micro * tokens, 2 * kv_width), BF)),)
+                + (Sent(token_wide), Sent(token_low)) * micro,
+                (Late(inputs), Late(gain_a), *tables), micro * qkv_flops, (dense,),
                 qkv_scratch, waits=waits,
             )
             projected = [(streams[2 * m], None, streams[2 * m + 1]) for m in pieces]
@@ -811,12 +845,10 @@
             call(
                 functools.partial(attend, keep, 0 if keep else m),
                 (Sent(token_wide), Sent(lanes_like), Sent(double_like if keep else block_like))
-                + ((Sent(probs_like), Sent(token_low), Sent(token_low), Raw(token_wide),
-                    Raw(token_low), Raw(token_low), Raw(like((rows, tokens, 2 * kv_width), BF)))
-                   if keep else ()),
-                (projected[m][0], projected[m][2], *pairs[m],
-                 *late([biases[m], gain_f, chosens[m], dispatches[m]]),
-                 *((projected[m][1], Late(targets[m])) if keep else ())),
+                + ((Sent(probs_like), Sent(token_low), Sent(token_low)) if keep else ()),
+                (*late([projected[m][0], projected[m][2], *pairs[m], biases[m], gain_f, chosens[m],
+                        dispatches[m]]),
+                 *((Late(cotangent, (m, 0)),) if keep else ())),
                 out_flops + 2 * score_flops, (dense,), [pltpu.VMEM((tokens, width), BF)] + out_scratch,
             )
             for m in pieces
@@ -826,14 +858,11 @@
         if keep:
             left = call(
                 pack, (Sent(like((2 * micro, tokens, width), BF)),),
-                late([a[8] for a in attended] + [a[4] for a in attended]), 0,
+                late([p[1] for p in projected] + [a[4] for a in attended]), 0,
             )[0]
             two = swapped(left, 2)
             lefts = [left, swapped(left, 1), two, swapped(two, 1)]
             ready = (two,)
-        else:
-            two = hold(down[2], arrived[0], attended[1][2])
-            down = (*down[:2], two, swapped(two, 1))
         applied = [
             call(
                 functools.partial(expert_forward, keep),
@@ -845,35 +874,33 @@
             )
             for m in pieces
         ]
-        return attended, arrived, applied, lefts, down
-
-    def far_and_near(side, waits):
-        return [
-            call(
-                functools.partial(expert_weight_grads, side, begin),
-                (Sent(like((per_column, hidden_width // 4, width), BF)),) * 2,
-                late([*left, *right]), expert_flops, waits=waits,
-            )
-            for left, right, begin in (
-                (hidden, arrived_grads, 0), ([a[1] for a in moved], arrived, 0),
-                ([a[2] for a in moved], arrived, 0),
-            )
-        ]
-
-    def merged(half, waits):
+        return projected, pairs, attended, arrived, applied, lefts, down
+
+    def weight_call(quarters, which, lefts, rights, waits):
+        quarter, some = hidden_width // 4, len(quarters)
         return call(
-            add, (Sent(half[0]),), late([half[0], swapped(half[1], 1)]), 0, waits=waits
-        )[0]
+            functools.partial(expert_weight_grads, quarters[0] * quarter, which),
+            (Sent(like((per_column, quarter, width), BF)),) * (some * len(which)), (),
+            len(which) * expert_flops, [*lefts, *rights],
+            [pltpu.VMEM((len(which), per_column, 2 * columns * ROOMS, some * quarter), BF),
+             pltpu.VMEM((len(rights) // 2, per_column, 2 * columns, ROOMS, width), BF),
+             pltpu.SemaphoreType.DMA((2, len(which), per_column, 2))],
+            waits=waits,
+        )
+
+    def merged(halves, waits):
+        pairs = [v for a, b in halves for v in (a, swapped(b, 1))]
+        return call(add, [Sent(a) for a, unused in halves], late(pairs), 0, waits=waits)
 
     def attention_back(keep, m, grad, token_grads, waits):
         return call(
             functools.partial(attend_back, keep),
-            (token_wide, token_low)
-            + (like((tokens, 2 * kv_width + (share if keep else 0)), BF),) * rows
+            (Sent(token_wide), Sent(token_low))
+            + (Sent(like((tokens, 2 * kv_width + (share if keep else 0)), BF)),) * rows
             + ((Sent(like((tokens, LANES), BF)), Sent(sums_like)) if keep else ()),
-            late([token_grads, shared[m] if keep else spread, attended[m][1], places[m],
-                  attended[m][0], gain_f, grad, attended[m][7], attended[m][9], attended[m][3],
-                  cosine, sine]),
+            (*late([token_grads, shared[m] if keep else spread, attended[m][1], places[m],
+                                 attended[m][0], gain_f]), Late(*grad),
+             *late([projected[m][2], *pairs[m], attended[m][3], cosine, sine])),
             out_flops + 4 * score_flops, (dense,), [pltpu.VMEM((tokens, width), BF)] + out_scratch,
             (here, second), waits,
         )
@@ -884,44 +911,43 @@
     def projection_back(keep, m, inner, parts, waits):
         return call(
             functools.partial(project_back, keep),
-            (token_low,)
-            + ((Sent(token_wide),) + (like((tokens, qkv_width // rows), BF),) * rows if keep else ()),
-            (*parts, inner[1], Late(attended[m][6]), Late(gain_a), inner[0],
+            (Sent(token_low),)
+            + ((Sent(token_wide),) + (Sent(like((tokens, qkv_width // rows), BF)),) * rows
+               if keep else ()),
+            (*late([*parts, inner[1], projected[m][0], gain_a, inner[0]]),
              *tables),
             qkv_flops, (dense,), [pltpu.VMEM((tokens, qkv_width), BF)] + qkv_scratch,
             (here,), waits,
         )
 
-    entering = [inputs[m, 0] for m in pieces]
-    targets = [cotangent[m, 0] for m in pieces]
-    kept = forward(entering, entering, (), (gate_shards[2], up_shards[2]), down_shards)
-    attended, applied, down_shards = kept[0], kept[2], kept[4]
+    kept = forward(False, None, (gate_shards[2], up_shards[2], down_shards[2]), down_shards)
+    attended, applied, down_shards = kept[2], kept[4], kept[6]
     returned = [over_columns(a[0]) for a in applied]
     results = [
         call(
-            combine, (Sent(token_wide), token_low),
+            combine, (Sent(token_low),),
             late([returned[m], attended[m][0], attended[m][1], spread, places[m]]),
             2 * slots * tokens * width, waits=() if m else (applied[1][0],),
         )
         for m in pieces
     ]
-    came = [lax.ppermute(r[1], "section", [(0, 1)]) for r in results]
-
-    kept = forward(came, entering, targets, (), down_shards)
-    attended, arrived, applied, lefts, down_shards = kept
+    came = [lax.ppermute(r[0], "section", [(0, 1)]) for r in results]
+
+    kept = forward(True, came, (), down_shards)
+    projected, pairs, attended, arrived, applied, lefts, down_shards = kept
     hidden = [a[1] for a in applied]
     shared = [over_columns(a[4]) for a in applied]
     inner, outer = [], []
     for m in pieces:
         waits = (*lefts[1:], outer[0][0]) if m else (applied[1][4],)
-        inner.append(attention_back(False, m, targets[m], shared[m], waits))
+        inner.append(attention_back(False, m, (cotangent, (m, 0)), shared[m], waits))
         outer.append(projection_back(False, m, inner[m], parts_of(inner[m]), ()))
     came = [lax.ppermute(o[0], "section", [(1, 0)]) for o in outer]
 
     given = [
         call(
             send_grads, (Sent(token_low), Sent(block_like)),
-            (came[m], *late([targets[m], attended[m][1], dispatches[m]])),
+            (Late(came[m]), Late(cotangent, (m, 0)), *late([attended[m][1], dispatches[m]])),
             2 * slots * tokens * width, scalars=(first_flag,), waits=() if m else (inner[1][0],),
         )
         for m in pieces
@@ -937,34 +963,35 @@
         for m in pieces
     ]
     back = [over_columns(a[0]) for a in moved]
-    far = far_and_near(1, ())
-    down_far = merged(far[0], ())
+    gate_up = [a[1] for a in moved] + [a[2] for a in moved]
+    down_far = merged([weight_call((2, 3), ((0, 0),), hidden, arrived_grads, ())], ())[0]
     crossed = [swapped(down_far, 2)]
-    inner = [attention_back(True, 0, given[0][0], back[0], (moved[1][0], down_far))]
+    inner = [attention_back(True, 0, given[0][:1], back[0], (moved[1][0], down_far))]
     parts = [parts_of(inner[0])]
-    inner.append(attention_back(True, 1, given[1][0], back[1], (inner[0][0], far[1][0])))
+    both = weight_call((0, 1, 2, 3), ((0, 0), (0, 0)), gate_up, arrived, (inner[0][0],))
+    inner.append(attention_back(True, 1, given[1][:1], back[1], (both[0], crossed[0])))
     parts.append(parts_of(inner[1]))
+    sums = merged([both[2:4], both[6:]], (inner[1][0],))
+    crossed.append(swapped(hold(sums[0], *parts[1][1:]), 2))
     outer = [projection_back(True, 0, inner[0], parts[0], (inner[1][0],))]
     o_grads = call(
         out_grads, (Sent(like((columns, rows * shard, share + LANES), BF)),),
         late([*lefts, *[p[s] for s in steps for p in parts], *[a[5] for a in attended],
               *[a[6] for a in inner], *[a[7] for a in inner]]),
-        2 * width * length * micro * share, waits=(crossed[0], outer[0][0]),
+        2 * width * length * micro * share, waits=(crossed[0], outer[0][0], sums[0]),
     )[0]
     outer.append(projection_back(True, 1, inner[1], parts[1], (o_grads,)))
-    far[2] = far_and_near(1, (outer[1][0],))[2]
     backs = [[o[2]] + [swapped(o[2 + s], s) for s in steps[1:]] for o in outer]
-    last = [merged(f, backs[1][1:]) for f in far[1:]]
-    crossed += [swapped(one, 2) for one in last]
+    crossed.append(swapped(hold(sums[1], *backs[1][1:]), 2))
+    near = weight_call((0, 1), ((0, 0),), hidden, arrived_grads, (outer[1][0],))
     w_grads = call(
         qkv_grads, (Sent(like((columns, rows * shard, qkv_width // rows), BF)),),
         late([*lefts, *[b[s] for s in steps for b in backs]]),
-        2 * width * length * micro * qkv_width // rows, waits=(last[0],),
+        2 * width * length * micro * qkv_width // rows, waits=(crossed[1], near[0]),
     )[0]
-    near = far_and_near(0, (w_grads, last[1]))
     expert_grads = [
-        n[0].astype(F32) + swapped(n[1], 1).astype(F32) + c.astype(F32)
-        for n, c in zip(near, crossed)
+        one.astype(F32) + swapped(other, 1).astype(F32) + c.astype(F32)
+        for one, other, c in zip((near[0], both[0], both[4]), (near[1], both[1], both[5]), crossed)
     ]
     layer_outputs = call(
         last_outputs, (Sent(like((micro, tokens, width), F32)),),
@@ -975,7 +1002,7 @@
 
     wide = share + qkv_width // rows + LANES
     pieces_out = call(
-        fold, (like((shard, wide), F32),) * rows,
+        fold, (Sent(like((shard, wide), F32)),) * rows,
         late([over_columns(o_grads), over_columns(w_grads)]), 0,
         scratch=[pltpu.VMEM((rows * shard, wide), F32)], scalars=(here,),
     )
@@ -985,7 +1012,7 @@
         (like((shard, width), F32), like((shard, width), F32), like((shard, kv_width), F32),
          like((shard, kv_width), F32), like((shard, experts), F32), like((1, shard), F32),
          like((1, shard), F32)),
-        (*pieces_out, *late([w_query[0], w_key[0], w_value[0], attn_gain])), 0,
+        late([*pieces_out, w_query[0], w_key[0], w_value[0], attn_gain]), 0,
         scratch=[pltpu.VMEM((shard, qkv_width), F32)], scalars=(here,),
     )
 

time: 765 us -> 734 us (0.959)
  Pallas kernels: 282 us -> 246 us
  local copies, waits for them, and re-layouts: 35.3 us -> 9.3 us
  waiting for transfers between devices: 235 us -> 253 us
  starting transfers between devices: 166 us -> 175 us
    pallas_call x40 -> x36, Pallas kernels: 282 us -> 246 us  [call(): pl.pallas_call(run, out_shape=tuple(shapes), in_specs=[pl.BlockSpec(memor...]
    unnamed x158 -> x34, local copies, waits for them, and re-layouts: 26.5 us -> 1.52 us
    all_to_all x14, waiting for transfers between devices: 59.9 us -> 76.2 us  [over_columns(): return lax.all_to_all(value, 'col', split_axis=0, concat_axis=0, tiled=True)]
    all_gather x1, waiting for transfers between devices: 91.3 us -> 106 us  [on_device(): dense = lax.all_gather(dense, ('row', 'col'), axis=0, tiled=True)]
    ppermute x51, waiting for transfers between devices: 63.1 us -> 49.5 us  [swapped(): return lax.ppermute(value, 'row', [(r, r ^ step) for r in range(rows)])]
  transfers between devices with their start and end apart: 70 -> 70, of which waited for: 25 -> 29; matrix products, arithmetic and copies ran while one was open for 3% -> 4% of each run, Pallas kernels for 34% -> 31%
where the time goes in v8:
time: 734 us; the launch traced here: 722 us
  waiting for transfers between devices  253 us (34%)
  Pallas kernels  246 us (34%)
  starting transfers between devices  175 us (24%)
  other arithmetic  22.6 us (3%)
  between operations  15.4 us (2%)
  local copies, waits for them, and re-layouts  9.3 us (1%)
    pallas_call x36, Pallas kernels, call(): pl.pallas_call(run, out_shape=tuple(shapes), in_specs=[pl.BlockSpec(memor...  246 us
    all_gather x1, waiting for transfers between devices, on_device(): dense = lax.all_gather(dense, ('row', 'col'), axis=0, tiled=True)  106 us
    all_to_all x14, starting transfers between devices, over_columns(): return lax.all_to_all(value, 'col', split_axis=0, concat_axis=0, tiled=True)  88.7 us
    ppermute x51, starting transfers between devices, swapped(): return lax.ppermute(value, 'row', [(r, r ^ step) for r in range(rows)])  77.7 us
    all_to_all x14, waiting for transfers between devices, over_columns(): return lax.all_to_all(value, 'col', split_axis=0, concat_axis=0, tiled=True)  76.2 us
    ppermute x51, waiting for transfers between devices, swapped(): return lax.ppermute(value, 'row', [(r, r ^ step) for r in range(rows)])  49.5 us
    ppermute x2, waiting for transfers between devices, on_device(): came = [lax.ppermute(r[0], 'section', [(0, 1)]) for r in results]  15.3 us
  transfers between devices with their start and end apart: 70, of which 29 were waited for; matrix products, arithmetic and copies ran while one was open for 4% of the time, Pallas kernels for 31%

profile of v8, /device:TPU:9, one launch (start us, length us, event | category | flops | bytes accessed | tf_op | source)
XLA Modules:
  0.0 722.2 jit_solution(16001468050327881655)
XLA Ops:
  23.6 106.5 %all-gather.2.cloned.1.call-done.refs_4_.refs_10_.refs_6_.refs_11_.refs_17_ = bf16[1536,3712]{1,0:T(8,128)(2,1)} async-done(((bf16[24,3712]{1,0:T(8,128)(2,1)}), bf16[1536,3712]{1,0:T(8,128)(2,1)}) %all-gather.2.cloned.1.call-update) | async-done | bytes 11403280 | tf_op jit(solution)/shard_map/all_gather | solution.py:750
  175.1 12.8 %all-to-all-done.refs_0_ = bf16[16,32,1536]{2,1,0:T(8,128)(2,1)} async-done(((bf16[16,32,1536]{2,1,0:T(8,128)(2,1)}), bf16[16,32,1536]{2,1,0:T(8,128)(2,1)}, u32[]{:S(2)}, u32[]{:S(2)}) %all-to-all-start) | async-done | bytes 1572896 | tf_op jit(solution)/shard_map/all_to_all | solution.py:717
  192.3 10.3 %expert_forward.4 = bf16[16,32,1536]{2,1,0:T(8,128)(2,1)} custom-call(bf16[16,32,1536]{2,1,0:T(8,128)(2,1)} %all-to-all-done.refs_0_, bf16[2,192,1536]{2,1,0:T(8,128)(2,1)} %bitcast.61, bf16[2,192,1536]{2,1,0:T(8,128)(2,1)} %copy-done.1, bf16[2,192,1536]{2,1,0:T(8,128)(2,1)} %collective-permute-done.refs_5_.refs_3_.refs_12_, ...), custom_call_target="tpu_custom_call" | custom-call | flops 3623878656 | bytes 17301504 | tf_op jit(solution)/shard_map/expert_forward/pallas_call | solution.py:124
  202.6 10.1 %all-to-all-done.2.refs_0_ = bf16[16,32,1536]{2,1,0:T(8,128)(2,1)} async-done(((bf16[16,32,1536]{2,1,0:T(8,128)(2,1)}), bf16[16,32,1536]{2,1,0:T(8,128)(2,1)}, u32[]{:S(2)}, u32[]{:S(2)}) %all-to-all-start.2) | async-done | bytes 1572896 | tf_op jit(solution)/shard_map/all_to_all | solution.py:717
  217.2 10.3 %expert_forward.5.refs_5_ = bf16[16,32,1536]{2,1,0:T(8,128)(2,1)} custom-call(bf16[16,32,1536]{2,1,0:T(8,128)(2,1)} %all-to-all-done.2.refs_0_, bf16[2,192,1536]{2,1,0:T(8,128)(2,1)} %bitcast.62, bf16[2,192,1536]{2,1,0:T(8,128)(2,1)} %copy-done.1, bf16[2,192,1536]{2,1,0:T(8,128)(2,1)} %collective-permute-done.refs_5_.refs_3_.refs_12_, ...), custom_call_target="tpu_custom_call" | custom-call | flops 3623878656 | bytes 17301504 | tf_op jit(solution)/shard_map/expert_forward/pallas_call | solution.py:124
  227.5 8.8 %all-to-all-done.1.refs_0_ = bf16[16,32,1536]{2,1,0:T(8,128)(2,1)} async-done(((bf16[16,32,1536]{2,1,0:T(8,128)(2,1)}), bf16[16,32,1536]{2,1,0:T(8,128)(2,1)}, u32[]{:S(2)}, u32[]{:S(2)}) %all-to-all-start.1) | async-done | bytes 1572896 | tf_op jit(solution)/shard_map/all_to_all | solution.py:717
  236.3 7.0 all-to-all-start.4
  273.0 7.3 %attend.6 = (f32[96,1536]{1,0:T(8,128)}, f32[96,128]{1,0:T(8,128)}, bf16[16,64,1536]{2,1,0:T(8,128)(2,1)}, bf16[2,576,384]{2,1,0:T(8,128)(2,1)}, bf16[96,1536]{1,0:T(8,128)(2,1)}, /*index=5*/bf16[96,1536]{1,0:T(8,128)(2,1)}) custom-call(f32[96,1536]{1,0:T(8,128)} %get-tuple-element.137.refs_0_.refs_7_.refs_6_, ...), custom_call_target="tpu_custom_call" | custom-call | flops 830472192 | bytes 18831360 | tf_op jit(solution)/shard_map/attend/pallas_call | solution.py:124
  280.3 6.9 all-to-all-start.3
  291.6 8.8 %collective-permute-done.16.refs_1_ = bf16[96,1536]{1,0:T(8,128)(2,1)} collective-permute-done((bf16[96,1536]{1,0:T(8,128)(2,1)}, bf16[96,1536]{1,0:T(8,128)(2,1)}, u32[]{:S(2)}, u32[]{:S(2)}) %collective-permute-start.16) | collective-permute-done | bytes 294944 | tf_op jit(solution)/shard_map/ppermute | solution.py:934
  316.2 7.3 %attend.7 = (f32[96,1536]{1,0:T(8,128)}, f32[96,128]{1,0:T(8,128)}, bf16[16,64,1536]{2,1,0:T(8,128)(2,1)}, bf16[2,576,384]{2,1,0:T(8,128)(2,1)}, bf16[96,1536]{1,0:T(8,128)(2,1)}, /*index=5*/bf16[96,1536]{1,0:T(8,128)(2,1)}) custom-call(f32[96,1536]{1,0:T(8,128)} %get-tuple-element.143.refs_0_.refs_6_, bf16[96,1536]{1,0:T(8,128)(2,1)} %get-tuple-element.144.refs_1_.refs_9_, ...), custom_call_target="tpu_custom_call" | custom-call | flops 830472192 | bytes 18831360 | tf_op jit(solution)/shard_map/attend/pallas_call | solution.py:124
  327.8 11.3 %all-to-all-start.6 = ((bf16[16,64,1536]{2,1,0:T(8,128)(2,1)}), bf16[16,64,1536]{2,1,0:T(8,128)(2,1)}, u32[]{:S(2)}, u32[]{:S(2)}) async-start(bf16[16,64,1536]{2,1,0:T(8,128)(2,1)} %get-tuple-element.146.refs_13_), calls=%async_computation.6 | async-start | bytes 6291456 | tf_op jit(solution)/shard_map/all_to_all | solution.py:717
  344.0 16.4 %expert_forward.6 = (bf16[16,32,1536]{2,1,0:T(8,128)(2,1)}, bf16[2,256,768]{2,1,0:T(8,128)(2,1)}, bf16[2,256,768]{2,1,0:T(8,128)(2,1)}, bf16[2,256,768]{2,1,0:T(8,128)(2,1)}, bf16[16,32,1664]{2,1,0:T(8,128)(2,1)}) custom-call(bf16[16,64,1536]{2,1,0:T(8,128)(2,1)} %all-to-all-done.3.refs_0_.refs_4_, bf16[2,192,1536]{2,1,0:T(8,128)(2,1)} %bitcast.63, ...), custom_call_target="tpu_custom_call" | custom-call | flops 7247757312 | bytes 22937600 | tf_op jit(solution)/shard_map/expert_forward/pallas_call | solution.py:124
  360.4 16.8 %all-to-all-done.6.refs_0_.refs_5_ = bf16[16,64,1536]{2,1,0:T(8,128)(2,1)} async-done(((bf16[16,64,1536]{2,1,0:T(8,128)(2,1)}), bf16[16,64,1536]{2,1,0:T(8,128)(2,1)}, u32[]{:S(2)}, u32[]{:S(2)}) %all-to-all-start.6) | async-done | bytes 3145760 | tf_op jit(solution)/shard_map/all_to_all | solution.py:717
  382.7 16.4 %expert_forward.7 = (bf16[16,32,1536]{2,1,0:T(8,128)(2,1)}, bf16[2,256,768]{2,1,0:T(8,128)(2,1)}, bf16[2,256,768]{2,1,0:T(8,128)(2,1)}, bf16[2,256,768]{2,1,0:T(8,128)(2,1)}, bf16[16,32,1664]{2,1,0:T(8,128)(2,1)}) custom-call(bf16[16,64,1536]{2,1,0:T(8,128)(2,1)} %all-to-all-done.6.refs_0_.refs_5_, bf16[2,192,1536]{2,1,0:T(8,128)(2,1)} %bitcast.64, ...), custom_call_target="tpu_custom_call" | custom-call | flops 7247757312 | bytes 22937600 | tf_op jit(solution)/shard_map/expert_forward/pallas_call | solution.py:124
  402.6 6.9 all-to-all-start.7
  413.4 8.7 %attend_back.4 = (f32[96,1536]{1,0:T(8,128)}, bf16[96,1536]{1,0:T(8,128)(2,1)}, bf16[96,512]{1,0:T(8,128)(2,1)}, bf16[96,512]{1,0:T(8,128)(2,1)}, bf16[96,512]{1,0:T(8,128)(2,1)}, /*index=5*/bf16[96,512]{1,0:T(8,128)(2,1)}) custom-call(s32[1]{0:T(128)} %bitcast.1.refs_0_, s32[1]{0:T(128)} %bitcast.refs_0_.refs_1_, ...), custom_call_target="tpu_custom_call" | custom-call | flops 1056964608 | bytes 17520640 | tf_op jit(solution)/shard_map/attend_back/pallas_call | solution.py:124
  432.8 6.8 project_back.4.refs_21_
  442.2 8.8 %attend_back.5 = (f32[96,1536]{1,0:T(8,128)}, bf16[96,1536]{1,0:T(8,128)(2,1)}, bf16[96,512]{1,0:T(8,128)(2,1)}, bf16[96,512]{1,0:T(8,128)(2,1)}, bf16[96,512]{1,0:T(8,128)(2,1)}, /*index=5*/bf16[96,512]{1,0:T(8,128)(2,1)}) custom-call(s32[1]{0:T(128)} %bitcast.1.refs_0_, s32[1]{0:T(128)} %bitcast.refs_0_.refs_1_, ...), custom_call_target="tpu_custom_call" | custom-call | flops 1056964608 | bytes 17520640 | tf_op jit(solution)/shard_map/attend_back/pallas_call | solution.py:124
  470.3 6.8 project_back.5
  489.0 7.0 all-to-all-start.10
  496.0 10.9 %expert_backward.2 = (bf16[16,32,1664]{2,1,0:T(8,128)(2,1)}, bf16[2,256,768]{2,1,0:T(8,128)(2,1)}, bf16[2,256,768]{2,1,0:T(8,128)(2,1)}) custom-call(s32[1]{0:T(128)} %bitcast.refs_0_.refs_1_, bf16[16,32,1536]{2,1,0:T(8,128)(2,1)} %all-to-all-done.8.refs_1_.refs_2_, bf16[2,256,768]{2,1,0:T(8,128)(2,1)} %get-tuple-element.167.refs_2_.refs_0_, ...), custom_call_target="tpu_custom_call" | custom-call | flops 3623878656 | bytes 22937600 | tf_op jit(solution)/shard_map/expert_backward/pallas_call | solution.py:124
  506.8 9.7 %all-to-all-done.10.refs_1_.refs_3_ = bf16[16,32,1536]{2,1,0:T(8,128)(2,1)} async-done(((bf16[16,32,1536]{2,1,0:T(8,128)(2,1)}), bf16[16,32,1536]{2,1,0:T(8,128)(2,1)}, u32[]{:S(2)}, u32[]{:S(2)}) %all-to-all-start.10) | async-done | bytes 1572896 | tf_op jit(solution)/shard_map/all_to_all | solution.py:717
  529.5 10.8 %expert_backward.3 = (bf16[16,32,1664]{2,1,0:T(8,128)(2,1)}, bf16[2,256,768]{2,1,0:T(8,128)(2,1)}, bf16[2,256,768]{2,1,0:T(8,128)(2,1)}) custom-call(s32[1]{0:T(128)} %bitcast.refs_0_.refs_1_, bf16[16,32,1536]{2,1,0:T(8,128)(2,1)} %all-to-all-done.10.refs_1_.refs_3_, bf16[2,256,768]{2,1,0:T(8,128)(2,1)} %get-tuple-element.178.refs_2_.refs_1_, ...), custom_call_target="tpu_custom_call" | custom-call | flops 3623878656 | bytes 22937600 | tf_op jit(solution)/shard_map/expert_backward/pallas_call | solution.py:124
  552.2 9.4 %attend_back.6 = (f32[96,1536]{1,0:T(8,128)}, bf16[96,1536]{1,0:T(8,128)(2,1)}, bf16[96,896]{1,0:T(8,128)(2,1)}, bf16[96,896]{1,0:T(8,128)(2,1)}, bf16[96,896]{1...) custom-call(s32[1]{0:T(128)} %bitcast.1.refs_0_, s32[1]{0:T(128)} %bitcast.refs_0_.refs_1_, ...), custom_call_target="tpu_custom_call" | custom-call | flops 1056964608 | bytes 19167232 | tf_op jit(solution)/shard_map/attend_back/pallas_call | solution.py:124
  561.6 9.0 %expert_weight_grads.4 = (bf16[2,192,1536]{2,1,0:T(8,128)(2,1)}, bf16[2,192,1536]{2,1,0:T(8,128)(2,1)}, bf16[2,192,1536]{2,1,0:T(8,128)(2,1)}, bf16[2,192,1536]{...) custom-call(bf16[2,256,768]{2,1,0:T(8,128)(2,1)} %get-tuple-element., ...), custom_call_target="tpu_custom_call" | custom-call | flops 2415919104 | bytes 18874368 | tf_op jit(solution)/shard_map/expert_weight_grads/pallas_call | solution.py:124
  582.5 9.4 %attend_back.7 = (f32[96,1536]{1,0:T(8,128)}, bf16[96,1536]{1,0:T(8,128)(2,1)}, bf16[96,896]{1,0:T(8,128)(2,1)}, bf16[96,896]{1,0:T(8,128)(2,1)}, bf16[96,896]{1...) custom-call(s32[1]{0:T(128)} %bitcast.1.refs_0_, s32[1]{0:T(128)} %bitcast.refs_0_.refs_1_, ...), custom_call_target="tpu_custom_call" | custom-call | flops 1056964608 | bytes 19167232 | tf_op jit(solution)/shard_map/attend_back/pallas_call | solution.py:124
  595.6 7.3 %project_back.6 = (bf16[96,1536]{1,0:T(8,128)(2,1)}, f32[96,1536]{1,0:T(8,128)}, bf16[96,512]{1,0:T(8,128)(2,1)}, bf16[96,512]{1,0:T(8,128)(2,1)}, bf16[96,512]{1,0:T(8,128)(2,1)}, /*index=5*/bf16[96,512]{1,0:T(8,128)(2,1)}) custom-call(s32[1]{0:T(128)} %bitcast.1.refs_0_, bf16[96,896]{1,0:T(8,128)(2,1)} %get-tuple-element.186.refs_1_.refs_4_, ...), custom_call_target="tpu_custom_call" | custom-call | flops 603979776 | bytes 14948352 | tf_op jit(solution)/shard_map/project_back/pallas_call | solution.py:124
  607.0 6.8 out_grads.1.refs_12_
  627.2 7.5 %project_back.7 = (bf16[96,1536]{1,0:T(8,128)(2,1)}, f32[96,1536]{1,0:T(8,128)}, bf16[96,512]{1,0:T(8,128)(2,1)}, bf16[96,512]{1,0:T(8,128)(2,1)}, bf16[96,512]{1,0:T(8,128)(2,1)}, /*index=5*/bf16[96,512]{1,0:T(8,128)(2,1)}) custom-call(s32[1]{0:T(128)} %bitcast.1.refs_0_, bf16[96,896]{1,0:T(8,128)(2,1)} %get-tuple-element.200.refs_5_.refs_1_, ...), custom_call_target="tpu_custom_call" | custom-call | flops 603979776 | bytes 14948352 | tf_op jit(solution)/shard_map/project_back/pallas_call | solution.py:124
  639.0 13.0 %collective-permute-done.43.refs_8_ = bf16[96,512]{1,0:T(8,128)(2,1)} collective-permute-done((bf16[96,512]{1,0:T(8,128)(2,1)}, bf16[96,512]{1,0:T(8,128)(2,1)}, u32[]{:S(2)}, u32[]{:S(2)}) %collective-permute-start.43) | collective-permute-done | bytes 98336 | tf_op jit(solution)/shard_map/ppermute | solution.py:163
  690.7 7.8 %all-to-all-done.13.refs_2_ = bf16[16,96,512]{2,1,0:T(8,128)(2,1)} async-done(((bf16[16,96,512]{2,1,0:T(8,128)(2,1)}), bf16[16,96,512]{2,1,0:T(8,128)(2,1)}, u32[]{:S(2)}, u32[]{:S(2)}) %all-to-all-start.13) | async-done | bytes 1572896 | tf_op jit(solution)/shard_map/all_to_all | solution.py:717
  (224 shorter events, 303.2 us)
Async XLA Ops:
  7.2 122.9 %all-gather.2.cloned.1.call-start = ((), (), s32[]{:S(2)}) async-start(), calls=%async_computation.14 | async-start | bytes 11581440 | tf_op jit(solution)/shard_map/all_gather | solution.py:750
  10.5 122.5 %collective-permute-start = (bf16[2,192,1536]{2,1,0:T(8,128)(2,1)}, bf16[2,192,1536]{2,1,0:T(8,128)(2,1)}, u32[]{:S(2)}, u32[]{:S(2)}) collective-permute-start(bf16[2,192,1536]{2,1,0:T(8,128)(2,1)} %bitcast.60), channel_id=1, source_target_pairs={{0,32},{16,48},{32,0},{48,16},{1,33},{17,49},{33,1},{49,17},{2,34}... | collective-permute-start | bytes 3538952 | tf_op jit(solution)/shard_map/ppermute | solution.py:163
  12.6 120.4 %collective-permute-start.1 = (bf16[2,192,1536]{2,1,0:T(8,128)(2,1)}, bf16[2,192,1536]{2,1,0:T(8,128)(2,1)}, u32[]{:S(2)}, u32[]{:S(2)}) collective-permute-start(bf16[2,192,1536]{2,1,0:T(8,128)(2,1)} %bitcast.10.refs_5_.refs_14_), channel_id=1, source_target_pairs={{0,32},{16,48},{32,0},{48,16},{1,33},{17,49},{33,1},{49,17},{2,34}... | collective-permute-start | bytes 3538952 | tf_op jit(solution)/shard_map/ppermute | solution.py:163
  13.5 119.5 %collective-permute-start.2 = (bf16[2,192,1536]{2,1,0:T(8,128)(2,1)}, bf16[2,192,1536]{2,1,0:T(8,128)(2,1)}, u32[]{:S(2)}, u32[]{:S(2)}) collective-permute-start(bf16[2,192,1536]{2,1,0:T(8,128)(2,1)} %bitcast.11.refs_9_.refs_6_), channel_id=1, source_target_pairs={{0,32},{16,48},{32,0},{48,16},{1,33},{17,49},{33,1},{49,17},{2,34}... | collective-permute-start | bytes 3538952 | tf_op jit(solution)/shard_map/ppermute | solution.py:163
  159.0 28.9 %all-to-all-start = ((bf16[16,32,1536]{2,1,0:T(8,128)(2,1)}), bf16[16,32,1536]{2,1,0:T(8,128)(2,1)}, u32[]{:S(2)}, u32[]{:S(2)}) async-start(bf16[16,32,1536]{2,1,0:T(8,128)(2,1)} %get-tuple-element.131), calls=%async_computation | async-start | bytes 3145728 | tf_op jit(solution)/shard_map/all_to_all | solution.py:717
  164.5 27.8 %collective-permute-start.8 = (bf16[2,192,1536]{2,1,0:T(8,128)(2,1)}, bf16[2,192,1536]{2,1,0:T(8,128)(2,1)}, u32[]{:S(2)}, u32[]{:S(2)}) collective-permute-start(bf16[2,192,1536]{2,1,0:T(8,128)(2,1)} %bitcast.10.refs_5_.refs_14_), channel_id=1, source_target_pairs={{0,16},{16,0},{32,48},{48,32},{1,17},{17,1},{33,49},{49,33},{2,18}... | collective-permute-start | bytes 3538952 | tf_op jit(solution)/shard_map/ppermute | solution.py:163
  164.7 27.6 %collective-permute-start.10 = (bf16[2,192,1536]{2,1,0:T(8,128)(2,1)}, bf16[2,192,1536]{2,1,0:T(8,128)(2,1)}, u32[]{:S(2)}, u32[]{:S(2)}) collective-permute-start(bf16[2,192,1536]{2,1,0:T(8,128)(2,1)} %bitcast.11.refs_9_.refs_6_), channel_id=1, source_target_pairs={{0,16},{16,0},{32,48},{48,32},{1,17},{17,1},{33,49},{49,33},{2,18}... | collective-permute-start | bytes 3538952 | tf_op jit(solution)/shard_map/ppermute | solution.py:163
  166.4 25.9 %collective-permute-start.7 = (bf16[2,192,1536]{2,1,0:T(8,128)(2,1)}, bf16[2,192,1536]{2,1,0:T(8,128)(2,1)}, u32[]{:S(2)}, u32[]{:S(2)}) collective-permute-start(bf16[2,192,1536]{2,1,0:T(8,128)(2,1)} %collective-permute-done.refs_5_.refs_3_.refs_12_), channel_id=1, source_target_pairs={{0,16},{16,0},{32,48},{48,32},{1,17},{17,1},{33,49},{49,33},{2,18}... | collective-permute-start | bytes 3538952 | tf_op jit(solution)/shard_map/ppermute | solution.py:163
  166.6 25.7 %collective-permute-start.9 = (bf16[2,192,1536]{2,1,0:T(8,128)(2,1)}, bf16[2,192,1536]{2,1,0:T(8,128)(2,1)}, u32[]{:S(2)}, u32[]{:S(2)}) collective-permute-start(bf16[2,192,1536]{2,1,0:T(8,128)(2,1)} %collective-permute-done.1.refs_6_.refs_7_.refs_16_), channel_id=1, source_target_pairs={{0,16},{16,0},{32,48},{48,32},{1,17},{17,1},{33,49},{49,33},{2,18}... | collective-permute-start | bytes 3538952 | tf_op jit(solution)/shard_map/ppermute | solution.py:163
  236.3 44.0 %all-to-all-start.4 = ((bf16[16,32,1536]{2,1,0:T(8,128)(2,1)}), bf16[16,32,1536]{2,1,0:T(8,128)(2,1)}, u32[]{:S(2)}, u32[]{:S(2)}) async-start(bf16[16,32,1536]{2,1,0:T(8,128)(2,1)} %expert_forward.5.refs_5_), calls=%async_computation.4 | async-start | bytes 3145728 | tf_op jit(solution)/shard_map/all_to_all | solution.py:717
  280.3 47.5 %all-to-all-start.3 = ((bf16[16,64,1536]{2,1,0:T(8,128)(2,1)}), bf16[16,64,1536]{2,1,0:T(8,128)(2,1)}, u32[]{:S(2)}, u32[]{:S(2)}) async-start(bf16[16,64,1536]{2,1,0:T(8,128)(2,1)} %get-tuple-element.140), calls=%async_computation.3 | async-start | bytes 6291456 | tf_op jit(solution)/shard_map/all_to_all | solution.py:717
  327.8 49.4 %all-to-all-start.6 = ((bf16[16,64,1536]{2,1,0:T(8,128)(2,1)}), bf16[16,64,1536]{2,1,0:T(8,128)(2,1)}, u32[]{:S(2)}, u32[]{:S(2)}) async-start(bf16[16,64,1536]{2,1,0:T(8,128)(2,1)} %get-tuple-element.146.refs_13_), calls=%async_computation.6 | async-start | bytes 6291456 | tf_op jit(solution)/shard_map/all_to_all | solution.py:717
  341.5 41.1 %collective-permute-start.20 = (bf16[4,96,1536]{2,1,0:T(8,128)(2,1)}, bf16[4,96,1536]{2,1,0:T(8,128)(2,1)}, u32[]{:S(2)}, u32[]{:S(2)}) collective-permute-start(bf16[4,96,1536]{2,1,0:T(8,128)(2,1)} %pack.1.refs_0_), channel_id=1, source_target_pairs={{0,32},{16,48},{32,0},{48,16},{1,33},{17,49},{33,1},{49,17},{2,34}... | collective-permute-start | bytes 3538952 | tf_op jit(solution)/shard_map/ppermute | solution.py:163
  402.6 39.6 %all-to-all-start.7 = ((bf16[16,32,1664]{2,1,0:T(8,128)(2,1)}), bf16[16,32,1664]{2,1,0:T(8,128)(2,1)}, u32[]{:S(2)}, u32[]{:S(2)}) async-start(bf16[16,32,1664]{2,1,0:T(8,128)(2,1)} %get-tuple-element.155.refs_18_), calls=%async_computation.7 | async-start | bytes 3407872 | tf_op jit(solution)/shard_map/all_to_all | solution.py:717
  409.5 32.6 %collective-permute-start.25 = (bf16[4,96,1536]{2,1,0:T(8,128)(2,1)}, bf16[4,96,1536]{2,1,0:T(8,128)(2,1)}, u32[]{:S(2)}, u32[]{:S(2)}) collective-permute-start(bf16[4,96,1536]{2,1,0:T(8,128)(2,1)} %pack.1.refs_0_), channel_id=1, source_target_pairs={{0,16},{16,0},{32,48},{48,32},{1,17},{17,1},{33,49},{49,33},{2,18}... | collective-permute-start | bytes 3538952 | tf_op jit(solution)/shard_map/ppermute | solution.py:163
  413.1 29.1 %collective-permute-start.26 = (bf16[4,96,1536]{2,1,0:T(8,128)(2,1)}, bf16[4,96,1536]{2,1,0:T(8,128)(2,1)}, u32[]{:S(2)}, u32[]{:S(2)}) collective-permute-start(bf16[4,96,1536]{2,1,0:T(8,128)(2,1)} %collective-permute-done.20.refs_13_.refs_19_.refs_2_), channel_id=1, source_target_pairs={{0,16},{16,0},{32,48},{48,32},{1,17},{17,1},{33,49},{49,33},{2,18}... | collective-permute-start | bytes 3538952 | tf_op jit(solution)/shard_map/ppermute | solution.py:163
  454.1 34.9 %all-to-all-start.8 = ((bf16[16,32,1536]{2,1,0:T(8,128)(2,1)}), bf16[16,32,1536]{2,1,0:T(8,128)(2,1)}, u32[]{:S(2)}, u32[]{:S(2)}) async-start(bf16[16,32,1536]{2,1,0:T(8,128)(2,1)} %get-tuple-element.166), calls=%async_computation.8 | async-start | bytes 3145728 | tf_op jit(solution)/shard_map/all_to_all | solution.py:717
  489.0 27.6 %all-to-all-start.10 = ((bf16[16,32,1536]{2,1,0:T(8,128)(2,1)}), bf16[16,32,1536]{2,1,0:T(8,128)(2,1)}, u32[]{:S(2)}, u32[]{:S(2)}) async-start(bf16[16,32,1536]{2,1,0:T(8,128)(2,1)} %get-tuple-element.176.refs_18_), calls=%async_computation.10 | async-start | bytes 3145728 | tf_op jit(solution)/shard_map/all_to_all | solution.py:717
  516.6 25.9 %all-to-all-start.9 = ((bf16[16,32,1664]{2,1,0:T(8,128)(2,1)}), bf16[16,32,1664]{2,1,0:T(8,128)(2,1)}, u32[]{:S(2)}, u32[]{:S(2)}) async-start(bf16[16,32,1664]{2,1,0:T(8,128)(2,1)} %get-tuple-element.177), calls=%async_computation.9 | async-start | bytes 3407872 | tf_op jit(solution)/shard_map/all_to_all | solution.py:717
  542.5 40.0 %all-to-all-start.11 = ((bf16[16,32,1664]{2,1,0:T(8,128)(2,1)}), bf16[16,32,1664]{2,1,0:T(8,128)(2,1)}, u32[]{:S(2)}, u32[]{:S(2)}) async-start(bf16[16,32,1664]{2,1,0:T(8,128)(2,1)} %get-tuple-element.182.refs_18_), calls=%async_computation.11 | async-start | bytes 3407872 | tf_op jit(solution)/shard_map/all_to_all | solution.py:717
  551.1 26.5 %collective-permute-start.35 = (bf16[2,192,1536]{2,1,0:T(8,128)(2,1)}, bf16[2,192,1536]{2,1,0:T(8,128)(2,1)}, u32[]{:S(2)}, u32[]{:S(2)}) collective-permute-start(bf16[2,192,1536]{2,1,0:T(8,128)(2,1)} %add.133.refs_19_), channel_id=1, source_target_pairs={{0,32},{16,48},{32,0},{48,16},{1,33},{17,49},{33,1},{49,17},{2,34}... | collective-permute-start | bytes 3538952 | tf_op jit(solution)/shard_map/ppermute | solution.py:163
  570.7 32.3 %collective-permute-start.39 = (bf16[2,192,1536]{2,1,0:T(8,128)(2,1)}, bf16[2,192,1536]{2,1,0:T(8,128)(2,1)}, u32[]{:S(2)}, u32[]{:S(2)}) collective-permute-start(bf16[2,192,1536]{2,1,0:T(8,128)(2,1)} %get-tuple-element.213), channel_id=1, source_target_pairs={{0,16},{16,0},{32,48},{48,32},{1,17},{17,1},{33,49},{49,33},{2,18}... | collective-permute-start | bytes 3538952 | tf_op jit(solution)/shard_map/ppermute | solution.py:163
  575.4 27.5 %collective-permute-start.40 = (bf16[2,192,1536]{2,1,0:T(8,128)(2,1)}, bf16[2,192,1536]{2,1,0:T(8,128)(2,1)}, u32[]{:S(2)}, u32[]{:S(2)}) collective-permute-start(bf16[2,192,1536]{2,1,0:T(8,128)(2,1)} %get-tuple-element.215), channel_id=1, source_target_pairs={{0,16},{16,0},{32,48},{48,32},{1,17},{17,1},{33,49},{49,33},{2,18}... | collective-permute-start | bytes 3538952 | tf_op jit(solution)/shard_map/ppermute | solution.py:163
  613.7 55.3 %all-to-all-start.12 = ((bf16[16,96,512]{2,1,0:T(8,128)(2,1)}), bf16[16,96,512]{2,1,0:T(8,128)(2,1)}, u32[]{:S(2)}, u32[]{:S(2)}) async-start(bf16[16,96,512]{2,1,0:T(8,128)(2,1)} %out_grads.1.refs_12_), calls=%async_computation.12 | async-start | bytes 3145728 | tf_op jit(solution)/shard_map/all_to_all | solution.py:717
  620.4 43.1 %collective-permute-start.47 = (bf16[2,192,1536]{2,1,0:T(8,128)(2,1)}, bf16[2,192,1536]{2,1,0:T(8,128)(2,1)}, u32[]{:S(2)}, u32[]{:S(2)}) collective-permute-start(bf16[2,192,1536]{2,1,0:T(8,128)(2,1)} %hold.2), channel_id=1, source_target_pairs={{0,32},{16,48},{32,0},{48,16},{1,33},{17,49},{33,1},{49,17},{2,34}... | collective-permute-start | bytes 3538952 | tf_op jit(solution)/shard_map/ppermute | solution.py:163
  623.0 60.3 %collective-permute-start.51 = (bf16[2,192,1536]{2,1,0:T(8,128)(2,1)}, bf16[2,192,1536]{2,1,0:T(8,128)(2,1)}, u32[]{:S(2)}, u32[]{:S(2)}) collective-permute-start(bf16[2,192,1536]{2,1,0:T(8,128)(2,1)} %get-tuple-element.239), channel_id=1, source_target_pairs={{0,16},{16,0},{32,48},{48,32},{1,17},{17,1},{33,49},{49,33},{2,18}... | collective-permute-start | bytes 3538952 | tf_op jit(solution)/shard_map/ppermute | solution.py:163
  623.5 28.5 %collective-permute-start.43 = (bf16[96,512]{1,0:T(8,128)(2,1)}, bf16[96,512]{1,0:T(8,128)(2,1)}, u32[]{:S(2)}, u32[]{:S(2)}) collective-permute-start(bf16[96,512]{1,0:T(8,128)(2,1)} %get-tuple-element.220), channel_id=1, source_target_pairs={{0,32},{16,48},{32,0},{48,16},{1,33},{17,49},{33,1},{49,17},{2,34}... | collective-permute-start | bytes 294920 | tf_op jit(solution)/shard_map/ppermute | solution.py:163
  624.0 30.2 %collective-permute-start.45 = (bf16[96,512]{1,0:T(8,128)(2,1)}, bf16[96,512]{1,0:T(8,128)(2,1)}, u32[]{:S(2)}, u32[]{:S(2)}) collective-permute-start(bf16[96,512]{1,0:T(8,128)(2,1)} %get-tuple-element.222), channel_id=1, source_target_pairs={{0,48},{16,32},{32,16},{48,0},{1,49},{17,33},{33,17},{49,1},{2,50}... | collective-permute-start | bytes 294920 | tf_op jit(solution)/shard_map/ppermute | solution.py:163
  652.0 35.2 %collective-permute-start.54 = (bf16[2,192,1536]{2,1,0:T(8,128)(2,1)}, bf16[2,192,1536]{2,1,0:T(8,128)(2,1)}, u32[]{:S(2)}, u32[]{:S(2)}) collective-permute-start(bf16[2,192,1536]{2,1,0:T(8,128)(2,1)} %get-tuple-element.243), channel_id=1, source_target_pairs={{0,16},{16,0},{32,48},{48,32},{1,17},{17,1},{33,49},{49,33},{2,18}... | collective-permute-start | bytes 3538952 | tf_op jit(solution)/shard_map/ppermute | solution.py:163
  660.3 46.8 %collective-permute-start.52 = (bf16[2,192,1536]{2,1,0:T(8,128)(2,1)}, bf16[2,192,1536]{2,1,0:T(8,128)(2,1)}, u32[]{:S(2)}, u32[]{:S(2)}) collective-permute-start(bf16[2,192,1536]{2,1,0:T(8,128)(2,1)} %get-tuple-element.241), channel_id=1, source_target_pairs={{0,16},{16,0},{32,48},{48,32},{1,17},{17,1},{33,49},{49,33},{2,18}... | collective-permute-start | bytes 3538952 | tf_op jit(solution)/shard_map/ppermute | solution.py:163
  669.1 29.4 %all-to-all-start.13 = ((bf16[16,96,512]{2,1,0:T(8,128)(2,1)}), bf16[16,96,512]{2,1,0:T(8,128)(2,1)}, u32[]{:S(2)}, u32[]{:S(2)}) async-start(bf16[16,96,512]{2,1,0:T(8,128)(2,1)} %qkv_grads.1.refs_12_), calls=%async_computation.13 | async-start | bytes 3145728 | tf_op jit(solution)/shard_map/all_to_all | solution.py:717
  676.6 30.5 %collective-permute-start.53 = (bf16[2,192,1536]{2,1,0:T(8,128)(2,1)}, bf16[2,192,1536]{2,1,0:T(8,128)(2,1)}, u32[]{:S(2)}, u32[]{:S(2)}) collective-permute-start(bf16[2,192,1536]{2,1,0:T(8,128)(2,1)} %hold.3), channel_id=1, source_target_pairs={{0,32},{16,48},{32,0},{48,16},{1,33},{17,49},{33,1},{49,17},{2,34}... | collective-permute-start | bytes 3538952 | tf_op jit(solution)/shard_map/ppermute | solution.py:163
  (54 other events, 610.5 us)
Sparse Core Ops, SparseCore 0:
  11.7 118.3 all-gather.1

commit v9 on v8

--- a/solution.py
+++ b/solution.py
@@ -281,21 +281,18 @@
     return own == lax.broadcasted_iota(jnp.int32, (slots, LANES), 1)
 
 
-def scaled_rows(dispatch, gates, low):
+def slot_gates(dispatch, gates):
     here = slot_experts(dispatch.shape[0])
-    scale = jnp.sum(jnp.where(here, dot(dispatch, gates.astype(BF)), 0.0), -1, keepdims=True)
-    return (dot(dispatch, low) * scale).astype(BF)
+    return jnp.sum(jnp.where(here, dot(dispatch, gates.astype(BF)), 0.0), -1, keepdims=True)
 
 
 def attend(
-    keep, m, stream, query, pair0, pair1, pair2, pair3, bias, gain, chosen, dispatch, *rest,
+    keep, m, flag, stream, query, pair0, pair1, pair2, pair3, bias, gain, chosen, dispatch, target,
+    *rest,
 ):
-    (target,), rest = (rest[:1], rest[1:]) if keep else ((None,), rest)
     dense, middle, gates, outgoing = rest[:4]
     kept, (mixed, weights, router, sems) = rest[4:-4], rest[-4:]
     width = stream.shape[1]
-    block = (outgoing.shape[0], -1, width)
-    per = dispatch.shape[0] // outgoing.shape[0]
     at = dense.shape[1] - width - LANES
     copies = [
         pltpu.make_async_copy(dense.at[:, pl.ds(at + LANES, width)], weights, sems.at[0]),
@@ -343,11 +340,23 @@
     gates[...] = share
     sent(gates)
     slots = dispatch[...]
-    outgoing[:, :per, :] = dot(slots, low).astype(BF).reshape(block)
+    per, columns = outgoing.shape[1], outgoing.shape[0]
     if keep:
-        sent(outgoing, (slice(None), pl.ds(0, per)))
-        outgoing[:, per:, :] = scaled_rows(slots, share, target[...]).reshape(block)
-        sent(outgoing, (slice(None), pl.ds(per, per)))
+        outgoing[:, :, :width] = dot(slots, low).astype(BF).reshape(columns, per, width)
+        lane = lax.broadcasted_iota(jnp.int32, (slots.shape[0], LANES), 1)
+        notes = jnp.where(lane == 0, slot_gates(slots, share), 0.0).astype(BF)
+        outgoing[:, :, width:] = notes.reshape(columns, per, LANES)
+    else:
+        low = jnp.where(flag[0] > 0, target[...], low)
+        outgoing[...] = dot(slots, low).astype(BF).reshape(columns, per, width)
+
+
+def by_expert(refs, experts):
+    whole = [[[r.at[j] for j in range(experts)] for r in refs[at : at + 4]] for at in (0, 4)]
+    down = [[r.at[j] for j in range(experts)] for r in refs[8:10]]
+    for at in (10, 10 + experts):
+        down.append([r.at[0] for r in refs[at : at + experts]])
+    return [*whole, down]
 
 
 class Fetched:
@@ -358,8 +367,8 @@
             for k in range(weights.shape[0]):
                 self.copies[k, j] = [
                     pltpu.make_async_copy(
-                        shards[k][p].at[j],
-                        weights.at[k, j, pl.ds(p * shards[k][p].shape[1], shards[k][p].shape[1])],
+                        shards[k][p][j],
+                        weights.at[k, j, pl.ds(p * shards[k][p][j].shape[0], shards[k][p][j].shape[0])],
                         sems.at[k, j, p],
                     )
                     for p in range(4)
@@ -397,13 +406,17 @@
 
 
 def expert_forward(both, arrived, *refs):
-    shards = [refs[4 * k : 4 * k + 4] for k in range(3)]
-    outs, weights, sems = refs[12:-2], refs[-2], refs[-1]
-    fetched = Fetched(shards, weights, sems)
-    per = weights.shape[1] * ROOMS
+    early, refs = (refs[0], refs[1:]) if both else (None, refs)
+    weights, sems = refs[-2:]
+    experts = weights.shape[1]
+    count = 10 + 2 * experts
+    outs = refs[count:-2]
+    fetched = Fetched(by_expert(refs, experts), weights, sems)
+    width = weights.shape[3]
     for j in range(weights.shape[1]):
         at = j * ROOMS
-        rows = rows_of(arrived, j)
+        noted = rows_of(arrived, j)
+        rows = noted[:, :width]
         fetched.ready(0, j)
         gate = dot(rows, weights[0, j], (1, 1))
         fetched.ready(1, j)
@@ -424,7 +437,8 @@
             outs[1][j] = hidden
             outs[2][j] = active.astype(BF)
             outs[3][j] = bent.astype(BF)
-            hidden_grads = dot(rows_of(arrived, j, per), weights[2, j], (1, 1))
+            grads = (rows_of(early, j).astype(F32) * noted[:, width : width + 1].astype(F32)).astype(BF)
+            hidden_grads = dot(grads, weights[2, j], (1, 1))
             gate_part = (hidden_grads * bent).astype(BF)
             lifted_part = (hidden_grads * active).astype(BF)
             inner = jnp.sum(hidden_grads * hidden.astype(F32), -1, keepdims=True)
@@ -455,13 +469,15 @@
     low = jnp.where(flag[0] > 0, came[...], target[...])
     grad[...] = low
     sent(grad)
-    outgoing[...] = scaled_rows(dispatch[...], gates[...], low).reshape(outgoing.shape)
+    slots = dispatch[...]
+    rows = dot(slots, low) * slot_gates(slots, gates[...])
+    outgoing[...] = rows.astype(BF).reshape(outgoing.shape)
 
 
 def expert_backward(flag, arrived, hidden, active, bent, produced, *refs):
-    shards = [refs[4 * k : 4 * k + 4] for k in range(3)]
-    out, gate_back, lifted_back, weights, sems = refs[12:]
-    fetched = Fetched(shards, weights, sems)
+    out, gate_back, lifted_back, weights, sems = refs[-5:]
+    gate_shards, up_shards, down_shards = by_expert(refs, weights.shape[1])
+    fetched = Fetched([down_shards, gate_shards, up_shards], weights, sems)
     for j in range(weights.shape[1]):
         fetched.ready(0, j)
         hidden_grads = dot(rows_of(arrived, j), weights[0, j], (1, 1))
@@ -602,7 +618,9 @@
         for m in range(2):
             for r, (unused, begin) in enumerate(rights):
                 copies["right", r, j, m] = pltpu.make_async_copy(
-                    sources[2 * count + 2 * r + m].at[:, pl.ds(begin + j * ROOMS, ROOMS), :],
+                    sources[2 * count + 2 * r + m].at[
+                        :, pl.ds(begin + j * ROOMS, ROOMS), pl.ds(0, width)
+                    ],
                     right.at[r, j, pl.ds(m * columns, columns)],
                     sems.at[1, r, j, m],
                 )
@@ -756,7 +774,12 @@
         two = swapped(own, 2)
         return own, swapped(own, 1), two, swapped(two, 1)
 
-    gate_shards, up_shards, down_shards = [shards_of(w[0]) for w in (w_gate, w_up, w_down)]
+    gate_shards, up_shards = shards_of(w_gate[0]), shards_of(w_up[0])
+    down_twos = [swapped(w_down[0, j : j + 1], 2) for j in range(per_column)]
+    shards = (
+        *gate_shards, *up_shards, w_down[0], swapped(w_down[0], 1), *down_twos,
+        *[swapped(two, 1) for two in down_twos],
+    )
 
     lane = jnp.arange(LANES, dtype=jnp.int32)
     half = HEAD_DIM // 2
@@ -813,12 +836,11 @@
 
     per = slots // columns
     back_like = like((columns, per, width + LANES), BF)
-    double_like = like((columns, 2 * per, width), BF)
     lanes_like = like((tokens, LANES), F32)
     tables = late([cosine, sine])
     first_flag = (1 - second)
 
-    def forward(keep, came, waits, down):
+    def forward(keep, came, waits, early):
         projected, pairs = [], []
         if keep:
             for m in pieces:
@@ -844,12 +866,12 @@
         attended = [
             call(
                 functools.partial(attend, keep, 0 if keep else m),
-                (Sent(token_wide), Sent(lanes_like), Sent(double_like if keep else block_like))
+                (Sent(token_wide), Sent(lanes_like), Sent(back_like if keep else block_like))
                 + ((Sent(probs_like), Sent(token_low), Sent(token_low)) if keep else ()),
                 (*late([projected[m][0], projected[m][2], *pairs[m], biases[m], gain_f, chosens[m],
-                        dispatches[m]]),
-                 *((Late(cotangent, (m, 0)),) if keep else ())),
+                        dispatches[m]]), Late(cotangent, (m, 0))),
                 out_flops + 2 * score_flops, (dense,), [pltpu.VMEM((tokens, width), BF)] + out_scratch,
+                (second,),
             )
             for m in pieces
         ]
@@ -868,13 +890,13 @@
                 functools.partial(expert_forward, keep),
                 (Sent(block_like),)
                 + ((Sent(kept_like),) * 3 + (Sent(back_like),) if keep else ()),
-                late([arrived[m]]), (6 if keep else 3) * expert_flops,
-                (*gate_shards, *up_shards, *down), expert_scratch,
+                late([arrived[m], early[m]] if keep else [arrived[m]]),
+                (6 if keep else 3) * expert_flops, shards, expert_scratch,
                 waits=ready if m else (attended[1][2],),
             )
             for m in pieces
         ]
-        return projected, pairs, attended, arrived, applied, lefts, down
+        return projected, pairs, attended, arrived, applied, lefts
 
     def weight_call(quarters, which, lefts, rights, waits):
         quarter, some = hidden_width // 4, len(quarters)
@@ -920,8 +942,8 @@
             (here,), waits,
         )
 
-    kept = forward(False, None, (gate_shards[2], up_shards[2], down_shards[2]), down_shards)
-    attended, applied, down_shards = kept[2], kept[4], kept[6]
+    kept = forward(False, None, (gate_shards[2], up_shards[2], down_twos[0]), None)
+    attended, early, applied = kept[2:5]
     returned = [over_columns(a[0]) for a in applied]
     results = [
         call(
@@ -933,8 +955,7 @@
     ]
     came = [lax.ppermute(r[0], "section", [(0, 1)]) for r in results]
 
-    kept = forward(True, came, (), down_shards)
-    projected, pairs, attended, arrived, applied, lefts, down_shards = kept
+    projected, pairs, attended, arrived, applied, lefts = forward(True, came, (), early)
     hidden = [a[1] for a in applied]
     shared = [over_columns(a[4]) for a in applied]
     inner, outer = [], []
@@ -957,7 +978,7 @@
         call(
             expert_backward, (Sent(back_like), Sent(kept_like), Sent(kept_like)),
             late([arrived_grads[m], hidden[m], applied[m][2], applied[m][3], applied[m][0]]),
-            3 * expert_flops, (*down_shards, *gate_shards, *up_shards), expert_scratch,
+            3 * expert_flops, shards, expert_scratch,
             (second,), () if m else (given[1][1],),
         )
         for m in pieces
@@ -972,17 +993,18 @@
     inner.append(attention_back(True, 1, given[1][:1], back[1], (both[0], crossed[0])))
     parts.append(parts_of(inner[1]))
     sums = merged([both[2:4], both[6:]], (inner[1][0],))
-    crossed.append(swapped(hold(sums[0], *parts[1][1:]), 2))
-    outer = [projection_back(True, 0, inner[0], parts[0], (inner[1][0],))]
+    gate_far = hold(sums[0], *parts[1][1:])
+    crossed.append(swapped(gate_far, 2))
     o_grads = call(
         out_grads, (Sent(like((columns, rows * shard, share + LANES), BF)),),
         late([*lefts, *[p[s] for s in steps for p in parts], *[a[5] for a in attended],
               *[a[6] for a in inner], *[a[7] for a in inner]]),
-        2 * width * length * micro * share, waits=(crossed[0], outer[0][0], sums[0]),
+        2 * width * length * micro * share, waits=(crossed[0], gate_far),
     )[0]
-    outer.append(projection_back(True, 1, inner[1], parts[1], (o_grads,)))
+    last = projection_back(True, 1, inner[1], parts[1], (o_grads,))
+    outer = [projection_back(True, 0, inner[0], parts[0], (last[0],)), last]
     backs = [[o[2]] + [swapped(o[2 + s], s) for s in steps[1:]] for o in outer]
-    crossed.append(swapped(hold(sums[1], *backs[1][1:]), 2))
+    crossed.append(swapped(hold(sums[1], *backs[0][1:], *backs[1][1:]), 2))
     near = weight_call((0, 1), ((0, 0),), hidden, arrived_grads, (outer[1][0],))
     w_grads = call(
         qkv_grads, (Sent(like((columns, rows * shard, qkv_width // rows), BF)),),

time: 734 us -> 704 us (0.959)
  waiting for transfers between devices: 253 us -> 226 us
    all_to_all x14, waiting for transfers between devices: 76.2 us -> 45.8 us  [over_columns(): return lax.all_to_all(value, 'col', split_axis=0, concat_axis=0, tiled=True)]
    ppermute x51 -> x53, waiting for transfers between devices: 49.5 us -> 67 us  [swapped(): return lax.ppermute(value, 'row', [(r, r ^ step) for r in range(rows)])]
    all_gather x1, waiting for transfers between devices: 106 us -> 92.7 us  [on_device(): dense = lax.all_gather(dense, ('row', 'col'), axis=0, tiled=True)]
    ppermute x51 -> x53, starting transfers between devices: 77.7 us -> 81.6 us  [swapped(): return lax.ppermute(value, 'row', [(r, r ^ step) for r in range(rows)])]
  transfers between devices with their start and end apart: 70 -> 72, of which waited for: 29 -> 34; matrix products, arithmetic and copies ran while one was open for 4% -> 4% of each run, Pallas kernels for 31% -> 32%
where the time goes in v9:
time: 704 us; the launch traced here: 692 us
  Pallas kernels  246 us (35%)
  waiting for transfers between devices  226 us (32%)
  starting transfers between devices  171 us (24%)
  other arithmetic  22.7 us (3%)
  between operations  15.1 us (2%)
  local copies, waits for them, and re-layouts  9.73 us (1%)
    pallas_call x36, Pallas kernels, call(): pl.pallas_call(run, out_shape=tuple(shapes), in_specs=[pl.BlockSpec(memor...  246 us
    all_gather x1, waiting for transfers between devices, on_device(): dense = lax.all_gather(dense, ('row', 'col'), axis=0, tiled=True)  92.7 us
    all_to_all x14, starting transfers between devices, over_columns(): return lax.all_to_all(value, 'col', split_axis=0, concat_axis=0, tiled=True)  82.2 us
    ppermute x53, starting transfers between devices, swapped(): return lax.ppermute(value, 'row', [(r, r ^ step) for r in range(rows)])  81.6 us
    ppermute x53, waiting for transfers between devices, swapped(): return lax.ppermute(value, 'row', [(r, r ^ step) for r in range(rows)])  67 us
    all_to_all x14, waiting for transfers between devices, over_columns(): return lax.all_to_all(value, 'col', split_axis=0, concat_axis=0, tiled=True)  45.8 us
    ppermute x2, waiting for transfers between devices, on_device(): came = [lax.ppermute(r[0], 'section', [(0, 1)]) for r in results]  15.2 us
  transfers between devices with their start and end apart: 72, of which 34 were waited for; matrix products, arithmetic and copies ran while one was open for 4% of the time, Pallas kernels for 32%

profile of v9, /device:TPU:9, one launch (start us, length us, event | category | flops | bytes accessed | tf_op | source)
XLA Modules:
  0.0 691.9 jit_solution(119941233735980016)
XLA Ops:
  25.1 92.7 %all-gather.2.cloned.1.call-done.refs_4_.refs_12_.refs_6_.refs_17_.refs_11_ = bf16[1536,3712]{1,0:T(8,128)(2,1)} async-done(((bf16[24,3712]{1,0:T(8,128)(2,1)}), bf16[1536,3712]{1,0:T(8,128)(2,1)}) %all-gather.2.cloned.1.call-update) | async-done | bytes 11403280 | tf_op jit(solution)/shard_map/all_gather | solution.py:768
  140.1 6.7 attend.4
  156.5 11.7 %collective-permute-done.11.refs_12_.refs_13_.refs_17_ = bf16[1,192,1536]{2,1,0:T(8,128)(2,1)} collective-permute-done((bf16[1,192,1536]{2,1,0:T(8,128)(2,1)S(1)}, bf16[1,192,1536]{2,1,0:T(8,128)(2,1)}, u32[]{:S(2)}, u32[]{:S(2)}) %collective-permute-start.11) | collective-permute-done | bytes 589856 | tf_op jit(solution)/shard_map/ppermute | solution.py:163
  169.6 6.7 attend.5
  176.2 6.7 all-to-all-start.2
  186.2 10.3 %expert_forward.4 = bf16[16,32,1536]{2,1,0:T(8,128)(2,1)} custom-call(bf16[16,32,1536]{2,1,0:T(8,128)(2,1)} %all-to-all-done.refs_0_.refs_1_, bf16[2,192,1536]{2,1,0:T(8,128)(2,1)} %bitcast.9.refs_1_.refs_2_.refs_6_, bf16[2,192,1536]{2,1,0:T(8,128)(2,1)} %collective-permute-done.6.refs_2_.refs_3_.refs_7_, ...), custom_call_target="tpu_custom_call" | custom-call | flops 3623878656 | bytes 17301504 | tf_op jit(solution)/shard_map/expert_forward/pallas_call | solution.py:124
  196.5 10.1 %all-to-all-done.2.refs_0_.refs_1_ = bf16[16,32,1536]{2,1,0:T(8,128)(2,1)} async-done(((bf16[16,32,1536]{2,1,0:T(8,128)(2,1)}), bf16[16,32,1536]{2,1,0:T(8,128)(2,1)}, u32[]{:S(2)}, u32[]{:S(2)}) %all-to-all-start.2) | async-done | bytes 1572896 | tf_op jit(solution)/shard_map/all_to_all | solution.py:735
  211.0 10.3 %expert_forward.5.refs_5_ = bf16[16,32,1536]{2,1,0:T(8,128)(2,1)} custom-call(bf16[16,32,1536]{2,1,0:T(8,128)(2,1)} %all-to-all-done.2.refs_0_.refs_1_, bf16[2,192,1536]{2,1,0:T(8,128)(2,1)} %bitcast.9.refs_1_.refs_2_.refs_6_, bf16[2,192,1536]{2,1,0:T(8,128)(2,1)} %collective-permute-done.6.refs_2_.refs_3_.refs_7_, ...), custom_call_target="tpu_custom_call" | custom-call | flops 3623878656 | bytes 17301504 | tf_op jit(solution)/shard_map/expert_forward/pallas_call | solution.py:124
  221.3 10.2 %all-to-all-done.1.refs_0_ = bf16[16,32,1536]{2,1,0:T(8,128)(2,1)} async-done(((bf16[16,32,1536]{2,1,0:T(8,128)(2,1)}), bf16[16,32,1536]{2,1,0:T(8,128)(2,1)}, u32[]{:S(2)}, u32[]{:S(2)}) %all-to-all-start.1) | async-done | bytes 1572896 | tf_op jit(solution)/shard_map/all_to_all | solution.py:735
  267.0 6.8 attend.6
  273.8 6.9 all-to-all-start.3
  285.1 8.8 %collective-permute-done.18.refs_1_ = bf16[96,1536]{1,0:T(8,128)(2,1)} collective-permute-done((bf16[96,1536]{1,0:T(8,128)(2,1)}, bf16[96,1536]{1,0:T(8,128)(2,1)}, u32[]{:S(2)}, u32[]{:S(2)}) %collective-permute-start.18) | collective-permute-done | bytes 294944 | tf_op jit(solution)/shard_map/ppermute | solution.py:956
  309.4 6.8 attend.7
  316.2 6.7 all-to-all-start.6
  327.4 16.5 %expert_forward.6 = (bf16[16,32,1536]{2,1,0:T(8,128)(2,1)}, bf16[2,256,768]{2,1,0:T(8,128)(2,1)}, bf16[2,256,768]{2,1,0:T(8,128)(2,1)}, bf16[2,256,768]{2,1,0:T(8,128)(2,1)}, bf16[16,32,1664]{2,1,0:T(8,128)(2,1)}) custom-call(bf16[16,32,1664]{2,1,0:T(8,128)(2,1)} %all-to-all-done.3.refs_0_.refs_4_, bf16[16,32,1536]{2,1,0:T(8,128)(2,1)} %all-to-all-done.refs_0_.refs_1_, ...), custom_call_target="tpu_custom_call" | custom-call | flops 7247757312 | bytes 23068672 | tf_op jit(solution)/shard_map/expert_forward/pallas_call | solution.py:124
  354.3 16.5 %expert_forward.7 = (bf16[16,32,1536]{2,1,0:T(8,128)(2,1)}, bf16[2,256,768]{2,1,0:T(8,128)(2,1)}, bf16[2,256,768]{2,1,0:T(8,128)(2,1)}, bf16[2,256,768]{2,1,0:T(8,128)(2,1)}, bf16[16,32,1664]{2,1,0:T(8,128)(2,1)}) custom-call(bf16[16,32,1664]{2,1,0:T(8,128)(2,1)} %all-to-all-done.6.refs_0_.refs_5_, bf16[16,32,1536]{2,1,0:T(8,128)(2,1)} %all-to-all-done.2.refs_0_.refs_1_, ...), custom_call_target="tpu_custom_call" | custom-call | flops 7247757312 | bytes 23068672 | tf_op jit(solution)/shard_map/expert_forward/pallas_call | solution.py:124
  382.7 8.7 %attend_back.4 = (f32[96,1536]{1,0:T(8,128)}, bf16[96,1536]{1,0:T(8,128)(2,1)}, bf16[96,512]{1,0:T(8,128)(2,1)}, bf16[96,512]{1,0:T(8,128)(2,1)}, bf16[96,512]{1,0:T(8,128)(2,1)}, /*index=5*/bf16[96,512]{1,0:T(8,128)(2,1)}) custom-call(s32[1]{0:T(128)} %bitcast.1.refs_0_, s32[1]{0:T(128)} %bitcast.refs_0_.refs_1_, ...), custom_call_target="tpu_custom_call" | custom-call | flops 1056964608 | bytes 17520640 | tf_op jit(solution)/shard_map/attend_back/pallas_call | solution.py:124
  401.7 6.7 project_back.4.refs_21_
  410.9 8.8 %attend_back.5 = (f32[96,1536]{1,0:T(8,128)}, bf16[96,1536]{1,0:T(8,128)(2,1)}, bf16[96,512]{1,0:T(8,128)(2,1)}, bf16[96,512]{1,0:T(8,128)(2,1)}, bf16[96,512]{1,0:T(8,128)(2,1)}, /*index=5*/bf16[96,512]{1,0:T(8,128)(2,1)}) custom-call(s32[1]{0:T(128)} %bitcast.1.refs_0_, s32[1]{0:T(128)} %bitcast.refs_0_.refs_1_, ...), custom_call_target="tpu_custom_call" | custom-call | flops 1056964608 | bytes 17520640 | tf_op jit(solution)/shard_map/attend_back/pallas_call | solution.py:124
  439.4 6.7 project_back.5
  457.3 7.6 %all-to-all-start.10 = ((bf16[16,32,1536]{2,1,0:T(8,128)(2,1)}), bf16[16,32,1536]{2,1,0:T(8,128)(2,1)}, u32[]{:S(2)}, u32[]{:S(2)}) async-start(bf16[16,32,1536]{2,1,0:T(8,128)(2,1)} %get-tuple-element.175.refs_20_), calls=%async_computation.10 | async-start | bytes 3145728 | tf_op jit(solution)/shard_map/all_to_all | solution.py:735
  464.9 10.8 %expert_backward.2 = (bf16[16,32,1664]{2,1,0:T(8,128)(2,1)}, bf16[2,256,768]{2,1,0:T(8,128)(2,1)}, bf16[2,256,768]{2,1,0:T(8,128)(2,1)}) custom-call(s32[1]{0:T(128)} %bitcast.refs_0_.refs_1_, bf16[16,32,1536]{2,1,0:T(8,128)(2,1)} %all-to-all-done.8.refs_1_.refs_2_, bf16[2,256,768]{2,1,0:T(8,128)(2,1)} %get-tuple-element.166.refs_2_.refs_0_, ...), custom_call_target="tpu_custom_call" | custom-call | flops 3623878656 | bytes 22937600 | tf_op jit(solution)/shard_map/expert_backward/pallas_call | solution.py:124
  475.8 9.8 %all-to-all-done.10.refs_1_.refs_3_ = bf16[16,32,1536]{2,1,0:T(8,128)(2,1)} async-done(((bf16[16,32,1536]{2,1,0:T(8,128)(2,1)}), bf16[16,32,1536]{2,1,0:T(8,128)(2,1)}, u32[]{:S(2)}, u32[]{:S(2)}) %all-to-all-start.10) | async-done | bytes 1572896 | tf_op jit(solution)/shard_map/all_to_all | solution.py:735
  498.4 11.1 %expert_backward.3 = (bf16[16,32,1664]{2,1,0:T(8,128)(2,1)}, bf16[2,256,768]{2,1,0:T(8,128)(2,1)}, bf16[2,256,768]{2,1,0:T(8,128)(2,1)}) custom-call(s32[1]{0:T(128)} %bitcast.refs_0_.refs_1_, bf16[16,32,1536]{2,1,0:T(8,128)(2,1)} %all-to-all-done.10.refs_1_.refs_3_, bf16[2,256,768]{2,1,0:T(8,128)(2,1)} %get-tuple-element.177.refs_2_.refs_1_, ...), custom_call_target="tpu_custom_call" | custom-call | flops 3623878656 | bytes 22937600 | tf_op jit(solution)/shard_map/expert_backward/pallas_call | solution.py:124
  521.4 9.4 %attend_back.6 = (f32[96,1536]{1,0:T(8,128)}, bf16[96,1536]{1,0:T(8,128)(2,1)}, bf16[96,896]{1,0:T(8,128)(2,1)}, bf16[96,896]{1,0:T(8,128)(2,1)}, bf16[96,896]{1...) custom-call(s32[1]{0:T(128)} %bitcast.1.refs_0_, s32[1]{0:T(128)} %bitcast.refs_0_.refs_1_, ...), custom_call_target="tpu_custom_call" | custom-call | flops 1056964608 | bytes 19167232 | tf_op jit(solution)/shard_map/attend_back/pallas_call | solution.py:124
  530.9 9.1 %expert_weight_grads.4 = (bf16[2,192,1536]{2,1,0:T(8,128)(2,1)}, bf16[2,192,1536]{2,1,0:T(8,128)(2,1)}, bf16[2,192,1536]{2,1,0:T(8,128)(2,1)}, bf16[2,192,1536]{...) custom-call(bf16[2,256,768]{2,1,0:T(8,128)(2,1)} %get-tuple-element., ...), custom_call_target="tpu_custom_call" | custom-call | flops 2415919104 | bytes 15990784 | tf_op jit(solution)/shard_map/expert_weight_grads/pallas_call | solution.py:124
  545.5 9.4 %attend_back.7 = (f32[96,1536]{1,0:T(8,128)}, bf16[96,1536]{1,0:T(8,128)(2,1)}, bf16[96,896]{1,0:T(8,128)(2,1)}, bf16[96,896]{1,0:T(8,128)(2,1)}, bf16[96,896]{1...) custom-call(s32[1]{0:T(128)} %bitcast.1.refs_0_, s32[1]{0:T(128)} %bitcast.refs_0_.refs_1_, ...), custom_call_target="tpu_custom_call" | custom-call | flops 1056964608 | bytes 19167232 | tf_op jit(solution)/shard_map/attend_back/pallas_call | solution.py:124
  579.0 6.8 out_grads.1.refs_12_
  585.8 6.7 all-to-all-start.12
  594.2 7.3 %project_back.6 = (bf16[96,1536]{1,0:T(8,128)(2,1)}, f32[96,1536]{1,0:T(8,128)}, bf16[96,512]{1,0:T(8,128)(2,1)}, bf16[96,512]{1,0:T(8,128)(2,1)}, bf16[96,512]{1,0:T(8,128)(2,1)}, /*index=5*/bf16[96,512]{1,0:T(8,128)(2,1)}) custom-call(s32[1]{0:T(128)} %bitcast.1.refs_0_, bf16[96,896]{1,0:T(8,128)(2,1)} %get-tuple-element.197.refs_5_.refs_1_, ...), custom_call_target="tpu_custom_call" | custom-call | flops 603979776 | bytes 14948352 | tf_op jit(solution)/shard_map/project_back/pallas_call | solution.py:124
  601.5 7.3 %project_back.7 = (bf16[96,1536]{1,0:T(8,128)(2,1)}, f32[96,1536]{1,0:T(8,128)}, bf16[96,512]{1,0:T(8,128)(2,1)}, bf16[96,512]{1,0:T(8,128)(2,1)}, bf16[96,512]{1,0:T(8,128)(2,1)}, /*index=5*/bf16[96,512]{1,0:T(8,128)(2,1)}) custom-call(s32[1]{0:T(128)} %bitcast.1.refs_0_, bf16[96,896]{1,0:T(8,128)(2,1)} %get-tuple-element.185.refs_4_.refs_1_, ...), custom_call_target="tpu_custom_call" | custom-call | flops 603979776 | bytes 14948352 | tf_op jit(solution)/shard_map/project_back/pallas_call | solution.py:124
  659.9 8.1 %all-to-all-done.13.refs_2_ = bf16[16,96,512]{2,1,0:T(8,128)(2,1)} async-done(((bf16[16,96,512]{2,1,0:T(8,128)(2,1)}), bf16[16,96,512]{2,1,0:T(8,128)(2,1)}, u32[]{:S(2)}, u32[]{:S(2)}) %all-to-all-start.13) | async-done | bytes 1572896 | tf_op jit(solution)/shard_map/all_to_all | solution.py:735
  (229 shorter events, 308.3 us)
Async XLA Ops:
  7.2 110.6 %all-gather.2.cloned.1.call-start = ((), (), s32[]{:S(2)}) async-start(), calls=%async_computation.14 | async-start | bytes 11581440 | tf_op jit(solution)/shard_map/all_gather | solution.py:768
  10.5 110.2 %collective-permute-start = (bf16[2,192,1536]{2,1,0:T(8,128)(2,1)}, bf16[2,192,1536]{2,1,0:T(8,128)(2,1)}, u32[]{:S(2)}, u32[]{:S(2)}) collective-permute-start(bf16[2,192,1536]{2,1,0:T(8,128)(2,1)} %bitcast.9.refs_1_.refs_2_.refs_6_), channel_id=1, source_target_pairs={{0,32},{16,48},{32,0},{48,16},{1,33},{17,49},{33,1},{49,17},{2,34}... | collective-permute-start | bytes 3538952 | tf_op jit(solution)/shard_map/ppermute | solution.py:163
  12.6 108.2 %collective-permute-start.1 = (bf16[2,192,1536]{2,1,0:T(8,128)(2,1)}, bf16[2,192,1536]{2,1,0:T(8,128)(2,1)}, u32[]{:S(2)}, u32[]{:S(2)}) collective-permute-start(bf16[2,192,1536]{2,1,0:T(8,128)(2,1)} %bitcast.10.refs_5_.refs_6_.refs_10_), channel_id=1, source_target_pairs={{0,32},{16,48},{32,0},{48,16},{1,33},{17,49},{33,1},{49,17},{2,34}... | collective-permute-start | bytes 3538952 | tf_op jit(solution)/shard_map/ppermute | solution.py:163
  15.7 105.0 %collective-permute-start.2 = (bf16[1,192,1536]{2,1,0:T(8,128)(2,1)S(1)}, bf16[1,192,1536]{2,1,0:T(8,128)(2,1)}, u32[]{:S(2)}, u32[]{:S(2)}) collective-permute-start(bf16[1,192,1536]{2,1,0:T(8,128)(2,1)S(1)} %get-tuple-element.281), channel_id=1, source_target_pairs={{0,32},{16,48},{32,0},{48,16},{1,33},{17,49},{33,1},{49,17},{2,34}... | collective-permute-start | bytes 1769480 | tf_op jit(solution)/shard_map/ppermute | solution.py:163
  146.8 29.5 %all-to-all-start = ((bf16[16,32,1536]{2,1,0:T(8,128)(2,1)}), bf16[16,32,1536]{2,1,0:T(8,128)(2,1)}, u32[]{:S(2)}, u32[]{:S(2)}) async-start(bf16[16,32,1536]{2,1,0:T(8,128)(2,1)} %get-tuple-element.130), calls=%async_computation | async-start | bytes 3145728 | tf_op jit(solution)/shard_map/all_to_all | solution.py:735
  154.0 28.9 %collective-permute-start.6 = (bf16[2,192,1536]{2,1,0:T(8,128)(2,1)}, bf16[2,192,1536]{2,1,0:T(8,128)(2,1)}, u32[]{:S(2)}, u32[]{:S(2)}) collective-permute-start(bf16[2,192,1536]{2,1,0:T(8,128)(2,1)} %bitcast.9.refs_1_.refs_2_.refs_6_), channel_id=1, source_target_pairs={{0,16},{16,0},{32,48},{48,32},{1,17},{17,1},{33,49},{49,33},{2,18}... | collective-permute-start | bytes 3538952 | tf_op jit(solution)/shard_map/ppermute | solution.py:163
  154.6 28.7 %collective-permute-start.8 = (bf16[2,192,1536]{2,1,0:T(8,128)(2,1)}, bf16[2,192,1536]{2,1,0:T(8,128)(2,1)}, u32[]{:S(2)}, u32[]{:S(2)}) collective-permute-start(bf16[2,192,1536]{2,1,0:T(8,128)(2,1)} %bitcast.10.refs_5_.refs_6_.refs_10_), channel_id=1, source_target_pairs={{0,16},{16,0},{32,48},{48,32},{1,17},{17,1},{33,49},{49,33},{2,18}... | collective-permute-start | bytes 3538952 | tf_op jit(solution)/shard_map/ppermute | solution.py:163
  154.6 28.9 %collective-permute-start.10 = (bf16[2,192,1536]{2,1,0:T(8,128)(2,1)}, bf16[2,192,1536]{2,1,0:T(8,128)(2,1)}, u32[]{:S(2)}, u32[]{:S(2)}) collective-permute-start(bf16[2,192,1536]{2,1,0:T(8,128)(2,1)} %bitcast.19.refs_9_.refs_10_.refs_14_), channel_id=1, source_target_pairs={{0,16},{16,0},{32,48},{48,32},{1,17},{17,1},{33,49},{49,33},{2,18}... | collective-permute-start | bytes 3538952 | tf_op jit(solution)/shard_map/ppermute | solution.py:163
  156.5 29.7 %collective-permute-start.7 = (bf16[2,192,1536]{2,1,0:T(8,128)(2,1)}, bf16[2,192,1536]{2,1,0:T(8,128)(2,1)}, u32[]{:S(2)}, u32[]{:S(2)}) collective-permute-start(bf16[2,192,1536]{2,1,0:T(8,128)(2,1)} %collective-permute-done.refs_5_.refs_3_.refs_4_.refs_8_), channel_id=1, source_target_pairs={{0,16},{16,0},{32,48},{48,32},{1,17},{17,1},{33,49},{49,33},{2,18}... | collective-permute-start | bytes 3538952 | tf_op jit(solution)/shard_map/ppermute | solution.py:163
  176.2 30.4 %all-to-all-start.2 = ((bf16[16,32,1536]{2,1,0:T(8,128)(2,1)}), bf16[16,32,1536]{2,1,0:T(8,128)(2,1)}, u32[]{:S(2)}, u32[]{:S(2)}) async-start(bf16[16,32,1536]{2,1,0:T(8,128)(2,1)} %get-tuple-element.133.refs_15_), calls=%async_computation.2 | async-start | bytes 3145728 | tf_op jit(solution)/shard_map/all_to_all | solution.py:735
  206.6 24.9 %all-to-all-start.1 = ((bf16[16,32,1536]{2,1,0:T(8,128)(2,1)}), bf16[16,32,1536]{2,1,0:T(8,128)(2,1)}, u32[]{:S(2)}, u32[]{:S(2)}) async-start(bf16[16,32,1536]{2,1,0:T(8,128)(2,1)} %expert_forward.4), calls=%async_computation.1 | async-start | bytes 3145728 | tf_op jit(solution)/shard_map/all_to_all | solution.py:735
  231.6 42.2 %all-to-all-start.4 = ((bf16[16,32,1536]{2,1,0:T(8,128)(2,1)}), bf16[16,32,1536]{2,1,0:T(8,128)(2,1)}, u32[]{:S(2)}, u32[]{:S(2)}) async-start(bf16[16,32,1536]{2,1,0:T(8,128)(2,1)} %expert_forward.5.refs_5_), calls=%async_computation.4 | async-start | bytes 3145728 | tf_op jit(solution)/shard_map/all_to_all | solution.py:735
  273.8 42.4 %all-to-all-start.3 = ((bf16[16,32,1664]{2,1,0:T(8,128)(2,1)}), bf16[16,32,1664]{2,1,0:T(8,128)(2,1)}, u32[]{:S(2)}, u32[]{:S(2)}) async-start(bf16[16,32,1664]{2,1,0:T(8,128)(2,1)} %get-tuple-element.139), calls=%async_computation.3 | async-start | bytes 3407872 | tf_op jit(solution)/shard_map/all_to_all | solution.py:735
  316.2 30.8 %all-to-all-start.6 = ((bf16[16,32,1664]{2,1,0:T(8,128)(2,1)}), bf16[16,32,1664]{2,1,0:T(8,128)(2,1)}, u32[]{:S(2)}, u32[]{:S(2)}) async-start(bf16[16,32,1664]{2,1,0:T(8,128)(2,1)} %get-tuple-element.145.refs_16_), calls=%async_computation.6 | async-start | bytes 3407872 | tf_op jit(solution)/shard_map/all_to_all | solution.py:735
  325.3 28.9 %collective-permute-start.22 = (bf16[4,96,1536]{2,1,0:T(8,128)(2,1)}, bf16[4,96,1536]{2,1,0:T(8,128)(2,1)}, u32[]{:S(2)}, u32[]{:S(2)}) collective-permute-start(bf16[4,96,1536]{2,1,0:T(8,128)(2,1)} %pack.1.refs_0_), channel_id=1, source_target_pairs={{0,32},{16,48},{32,0},{48,16},{1,33},{17,49},{33,1},{49,17},{2,34}... | collective-permute-start | bytes 3538952 | tf_op jit(solution)/shard_map/ppermute | solution.py:163
  347.0 26.1 %all-to-all-start.5 = ((bf16[16,32,1664]{2,1,0:T(8,128)(2,1)}), bf16[16,32,1664]{2,1,0:T(8,128)(2,1)}, u32[]{:S(2)}, u32[]{:S(2)}) async-start(bf16[16,32,1664]{2,1,0:T(8,128)(2,1)} %get-tuple-element.146), calls=%async_computation.5 | async-start | bytes 3407872 | tf_op jit(solution)/shard_map/all_to_all | solution.py:735
  373.1 37.8 %all-to-all-start.7 = ((bf16[16,32,1664]{2,1,0:T(8,128)(2,1)}), bf16[16,32,1664]{2,1,0:T(8,128)(2,1)}, u32[]{:S(2)}, u32[]{:S(2)}) async-start(bf16[16,32,1664]{2,1,0:T(8,128)(2,1)} %get-tuple-element.154.refs_18_), calls=%async_computation.7 | async-start | bytes 3407872 | tf_op jit(solution)/shard_map/all_to_all | solution.py:735
  378.5 32.4 %collective-permute-start.27 = (bf16[4,96,1536]{2,1,0:T(8,128)(2,1)}, bf16[4,96,1536]{2,1,0:T(8,128)(2,1)}, u32[]{:S(2)}, u32[]{:S(2)}) collective-permute-start(bf16[4,96,1536]{2,1,0:T(8,128)(2,1)} %pack.1.refs_0_), channel_id=1, source_target_pairs={{0,16},{16,0},{32,48},{48,32},{1,17},{17,1},{33,49},{49,33},{2,18}... | collective-permute-start | bytes 3538952 | tf_op jit(solution)/shard_map/ppermute | solution.py:163
  382.2 28.8 %collective-permute-start.28 = (bf16[4,96,1536]{2,1,0:T(8,128)(2,1)}, bf16[4,96,1536]{2,1,0:T(8,128)(2,1)}, u32[]{:S(2)}, u32[]{:S(2)}) collective-permute-start(bf16[4,96,1536]{2,1,0:T(8,128)(2,1)} %collective-permute-done.22.refs_16_.refs_19_.refs_2_), channel_id=1, source_target_pairs={{0,16},{16,0},{32,48},{48,32},{1,17},{17,1},{33,49},{49,33},{2,18}... | collective-permute-start | bytes 3538952 | tf_op jit(solution)/shard_map/ppermute | solution.py:163
  423.2 34.1 %all-to-all-start.8 = ((bf16[16,32,1536]{2,1,0:T(8,128)(2,1)}), bf16[16,32,1536]{2,1,0:T(8,128)(2,1)}, u32[]{:S(2)}, u32[]{:S(2)}) async-start(bf16[16,32,1536]{2,1,0:T(8,128)(2,1)} %get-tuple-element.165), calls=%async_computation.8 | async-start | bytes 3145728 | tf_op jit(solution)/shard_map/all_to_all | solution.py:735
  457.3 28.2 %all-to-all-start.10 = ((bf16[16,32,1536]{2,1,0:T(8,128)(2,1)}), bf16[16,32,1536]{2,1,0:T(8,128)(2,1)}, u32[]{:S(2)}, u32[]{:S(2)}) async-start(bf16[16,32,1536]{2,1,0:T(8,128)(2,1)} %get-tuple-element.175.refs_20_), calls=%async_computation.10 | async-start | bytes 3145728 | tf_op jit(solution)/shard_map/all_to_all | solution.py:735
  485.5 26.1 %all-to-all-start.9 = ((bf16[16,32,1664]{2,1,0:T(8,128)(2,1)}), bf16[16,32,1664]{2,1,0:T(8,128)(2,1)}, u32[]{:S(2)}, u32[]{:S(2)}) async-start(bf16[16,32,1664]{2,1,0:T(8,128)(2,1)} %get-tuple-element.176), calls=%async_computation.9 | async-start | bytes 3407872 | tf_op jit(solution)/shard_map/all_to_all | solution.py:735
  511.6 33.6 %all-to-all-start.11 = ((bf16[16,32,1664]{2,1,0:T(8,128)(2,1)}), bf16[16,32,1664]{2,1,0:T(8,128)(2,1)}, u32[]{:S(2)}, u32[]{:S(2)}) async-start(bf16[16,32,1664]{2,1,0:T(8,128)(2,1)} %get-tuple-element.181.refs_18_), calls=%async_computation.11 | async-start | bytes 3407872 | tf_op jit(solution)/shard_map/all_to_all | solution.py:735
  520.0 25.5 %collective-permute-start.37 = (bf16[2,192,1536]{2,1,0:T(8,128)(2,1)}, bf16[2,192,1536]{2,1,0:T(8,128)(2,1)}, u32[]{:S(2)}, u32[]{:S(2)}) collective-permute-start(bf16[2,192,1536]{2,1,0:T(8,128)(2,1)} %add.133.refs_19_), channel_id=1, source_target_pairs={{0,32},{16,48},{32,0},{48,16},{1,33},{17,49},{33,1},{49,17},{2,34}... | collective-permute-start | bytes 3538952 | tf_op jit(solution)/shard_map/ppermute | solution.py:163
  540.0 23.6 %collective-permute-start.41 = (bf16[2,192,1536]{2,1,0:T(8,128)(2,1)}, bf16[2,192,1536]{2,1,0:T(8,128)(2,1)}, u32[]{:S(2)}, u32[]{:S(2)}) collective-permute-start(bf16[2,192,1536]{2,1,0:T(8,128)(2,1)} %get-tuple-element.210), channel_id=1, source_target_pairs={{0,16},{16,0},{32,48},{48,32},{1,17},{17,1},{33,49},{49,33},{2,18}... | collective-permute-start | bytes 3538952 | tf_op jit(solution)/shard_map/ppermute | solution.py:163
  585.8 53.2 %all-to-all-start.12 = ((bf16[16,96,512]{2,1,0:T(8,128)(2,1)}), bf16[16,96,512]{2,1,0:T(8,128)(2,1)}, u32[]{:S(2)}, u32[]{:S(2)}) async-start(bf16[16,96,512]{2,1,0:T(8,128)(2,1)} %out_grads.1.refs_12_), calls=%async_computation.12 | async-start | bytes 3145728 | tf_op jit(solution)/shard_map/all_to_all | solution.py:735
  592.5 40.9 %collective-permute-start.49 = (bf16[2,192,1536]{2,1,0:T(8,128)(2,1)}, bf16[2,192,1536]{2,1,0:T(8,128)(2,1)}, u32[]{:S(2)}, u32[]{:S(2)}) collective-permute-start(bf16[2,192,1536]{2,1,0:T(8,128)(2,1)} %hold.2.refs_19_), channel_id=1, source_target_pairs={{0,32},{16,48},{32,0},{48,16},{1,33},{17,49},{33,1},{49,17},{2,34}... | collective-permute-start | bytes 3538952 | tf_op jit(solution)/shard_map/ppermute | solution.py:163
  593.7 58.8 %collective-permute-start.53 = (bf16[2,192,1536]{2,1,0:T(8,128)(2,1)}, bf16[2,192,1536]{2,1,0:T(8,128)(2,1)}, u32[]{:S(2)}, u32[]{:S(2)}) collective-permute-start(bf16[2,192,1536]{2,1,0:T(8,128)(2,1)} %get-tuple-element.237), channel_id=1, source_target_pairs={{0,16},{16,0},{32,48},{48,32},{1,17},{17,1},{33,49},{49,33},{2,18}... | collective-permute-start | bytes 3538952 | tf_op jit(solution)/shard_map/ppermute | solution.py:163
  616.6 39.9 %collective-permute-start.56 = (bf16[2,192,1536]{2,1,0:T(8,128)(2,1)}, bf16[2,192,1536]{2,1,0:T(8,128)(2,1)}, u32[]{:S(2)}, u32[]{:S(2)}) collective-permute-start(bf16[2,192,1536]{2,1,0:T(8,128)(2,1)} %get-tuple-element.241), channel_id=1, source_target_pairs={{0,16},{16,0},{32,48},{48,32},{1,17},{17,1},{33,49},{49,33},{2,18}... | collective-permute-start | bytes 3538952 | tf_op jit(solution)/shard_map/ppermute | solution.py:163
  630.6 46.5 %collective-permute-start.54 = (bf16[2,192,1536]{2,1,0:T(8,128)(2,1)}, bf16[2,192,1536]{2,1,0:T(8,128)(2,1)}, u32[]{:S(2)}, u32[]{:S(2)}) collective-permute-start(bf16[2,192,1536]{2,1,0:T(8,128)(2,1)} %get-tuple-element.239), channel_id=1, source_target_pairs={{0,16},{16,0},{32,48},{48,32},{1,17},{17,1},{33,49},{49,33},{2,18}... | collective-permute-start | bytes 3538952 | tf_op jit(solution)/shard_map/ppermute | solution.py:163
  639.0 29.0 %all-to-all-start.13 = ((bf16[16,96,512]{2,1,0:T(8,128)(2,1)}), bf16[16,96,512]{2,1,0:T(8,128)(2,1)}, u32[]{:S(2)}, u32[]{:S(2)}) async-start(bf16[16,96,512]{2,1,0:T(8,128)(2,1)} %qkv_grads.1.refs_12_), calls=%async_computation.13 | async-start | bytes 3145728 | tf_op jit(solution)/shard_map/all_to_all | solution.py:735
  646.6 30.4 %collective-permute-start.55 = (bf16[2,192,1536]{2,1,0:T(8,128)(2,1)}, bf16[2,192,1536]{2,1,0:T(8,128)(2,1)}, u32[]{:S(2)}, u32[]{:S(2)}) collective-permute-start(bf16[2,192,1536]{2,1,0:T(8,128)(2,1)} %hold.3), channel_id=1, source_target_pairs={{0,32},{16,48},{32,0},{48,16},{1,33},{17,49},{33,1},{49,17},{2,34}... | collective-permute-start | bytes 3538952 | tf_op jit(solution)/shard_map/ppermute | solution.py:163
  (56 other events, 734.0 us)
Sparse Core Ops, SparseCore 0:
  11.7 105.9 all-gather.1

commit v10 on v9

--- a/solution.py
+++ b/solution.py
@@ -234,10 +234,14 @@
                 sent(query)
 
 
-def project_all(entering, gain, cosine, sine, dense, pair, *rest):
-    outs, (weights, sems) = rest[:-2], rest[-2:]
+def project_all(at_gain, entering, cosine, sine, dense, *rest):
+    outs, (weights, small, sems) = rest[:-3], rest[-3:]
     micro, unused, tokens, width = entering.shape
     cuts = cuts_of(weights.shape[1])
+    block = pltpu.make_async_copy(
+        dense.at[:, pl.ds(weights.shape[1], LANES)], small, sems.at[len(cuts)]
+    )
+    block.start()
     copies = [
         pltpu.make_async_copy(
             dense.at[:, pl.ds(at, size)], weights.at[:, pl.ds(at, size)], sems.at[k]
@@ -246,16 +250,19 @@
     ]
     for copy in copies:
         copy.start()
-    lows = []
+    scaled = []
     for m in range(micro):
         x = entering[m, 0].astype(F32)
-        outs[2 * m][...] = x
-        sent(outs[2 * m])
-        lows.append((x * norm_parts(x) * gain[...]).astype(BF))
+        outs[3 * m][...] = x
+        sent(outs[3 * m])
+        scaled.append(x * norm_parts(x))
+    block.wait()
+    gain = small[...].astype(F32).T[at_gain : at_gain + 1, :]
+    lows = [(x * gain).astype(BF) for x in scaled]
     low = jnp.concatenate(lows, 0)
     cosines = jnp.concatenate([cosine[...]] * micro, 0)
     sines = jnp.concatenate([sine[...]] * micro, 0)
-    keys = pair.shape[1] // 2
+    keys = outs[2].shape[1] // 2
     for copy, (at, size) in zip(copies, cuts):
         copy.wait()
         part = dot(low, weights[:, at : at + size])
@@ -264,16 +271,11 @@
             if begin < width + keys:
                 head = turned(head, cosines, sines)
             head = head.astype(BF)
-            if begin < width:
-                for m in range(micro):
-                    outs[2 * m + 1][:, begin : begin + HEAD_DIM] = head[
-                        m * tokens : (m + 1) * tokens
-                    ]
-            else:
-                pair[:, begin - width : begin - width + HEAD_DIM] = head
-            if begin + HEAD_DIM == width:
-                for m in range(micro):
-                    sent(outs[2 * m + 1])
+            for m in range(micro):
+                out, to = (outs[3 * m + 1], begin) if begin < width else (outs[3 * m + 2], begin - width)
+                out[:, to : to + HEAD_DIM] = head[m * tokens : (m + 1) * tokens]
+                if begin + HEAD_DIM == width:
+                    sent(out)
 
 
 def slot_experts(slots):
@@ -287,7 +289,7 @@
 
 
 def attend(
-    keep, m, flag, stream, query, pair0, pair1, pair2, pair3, bias, gain, chosen, dispatch, target,
+    keep, flag, stream, query, pair0, pair1, pair2, pair3, bias, gain, chosen, dispatch, target,
     *rest,
 ):
     dense, middle, gates, outgoing = rest[:4]
@@ -301,9 +303,7 @@
     for copy in copies:
         copy.start()
     tokens = stream.shape[0]
-    pairs = jnp.concatenate(
-        [p[m * tokens : (m + 1) * tokens, :] for p in (pair0, pair1, pair2, pair3)], 0
-    )
+    pairs = stacked((pair0, pair1, pair2, pair3))
     kv_heads = pairs.shape[1] // (2 * HEAD_DIM)
     group = width // HEAD_DIM // kv_heads
     biases = jnp.concatenate([bias[...]] * group, 0)
@@ -840,7 +840,7 @@
     tables = late([cosine, sine])
     first_flag = (1 - second)
 
-    def forward(keep, came, waits, early):
+    def forward(keep, came, waits, early, after):
         projected, pairs = [], []
         if keep:
             for m in pieces:
@@ -854,24 +854,25 @@
                 )
                 pairs.append([projected[m][3]] + [swapped(projected[m][3], s) for s in steps[1:]])
         else:
-            pair, *streams = call(
-                project_all,
-                (Sent(like((micro * tokens, 2 * kv_width), BF)),)
-                + (Sent(token_wide), Sent(token_low)) * micro,
-                (Late(inputs), Late(gain_a), *tables), micro * qkv_flops, (dense,),
-                qkv_scratch, waits=waits,
+            made = call(
+                functools.partial(project_all, experts),
+                (Sent(token_wide), Sent(token_low), Sent(pair_like)) * micro,
+                (Late(inputs), *tables), micro * qkv_flops, (dense,),
+                [qkv_scratch[0], pltpu.VMEM((width, LANES), BF), qkv_scratch[1]], waits=waits,
             )
-            projected = [(streams[2 * m], None, streams[2 * m + 1]) for m in pieces]
-            pairs = [[pair] + [swapped(pair, s) for s in steps[1:]]] * micro
+            projected = [(made[3 * m], None, made[3 * m + 1]) for m in pieces]
+            for m in pieces:
+                pair = made[3 * m + 2]
+                pairs.append([pair] + [swapped(pair, s) for s in steps[1:]])
         attended = [
             call(
-                functools.partial(attend, keep, 0 if keep else m),
+                functools.partial(attend, keep),
                 (Sent(token_wide), Sent(lanes_like), Sent(back_like if keep else block_like))
                 + ((Sent(probs_like), Sent(token_low), Sent(token_low)) if keep else ()),
                 (*late([projected[m][0], projected[m][2], *pairs[m], biases[m], gain_f, chosens[m],
                         dispatches[m]]), Late(cotangent, (m, 0))),
                 out_flops + 2 * score_flops, (dense,), [pltpu.VMEM((tokens, width), BF)] + out_scratch,
-                (second,),
+                (second,), () if m else after,
             )
             for m in pieces
         ]
@@ -942,7 +943,7 @@
             (here,), waits,
         )
 
-    kept = forward(False, None, (gate_shards[2], up_shards[2], down_twos[0]), None)
+    kept = forward(False, None, (gate_shards[2], up_shards[2], down_twos[0]), None, ())
     attended, early, applied = kept[2:5]
     returned = [over_columns(a[0]) for a in applied]
     results = [
@@ -955,7 +956,7 @@
     ]
     came = [lax.ppermute(r[0], "section", [(0, 1)]) for r in results]
 
-    projected, pairs, attended, arrived, applied, lefts = forward(True, came, (), early)
+    projected, pairs, attended, arrived, applied, lefts = forward(True, came, (), early, results[1])
     hidden = [a[1] for a in applied]
     shared = [over_columns(a[4]) for a in applied]
     inner, outer = [], []
@@ -983,14 +984,14 @@
         )
         for m in pieces
     ]
-    back = [over_columns(a[0]) for a in moved]
     gate_up = [a[1] for a in moved] + [a[2] for a in moved]
     down_far = merged([weight_call((2, 3), ((0, 0),), hidden, arrived_grads, ())], ())[0]
     crossed = [swapped(down_far, 2)]
+    back = [over_columns(moved[0][0]), over_columns(hold(moved[1][0], down_far))]
     inner = [attention_back(True, 0, given[0][:1], back[0], (moved[1][0], down_far))]
     parts = [parts_of(inner[0])]
     both = weight_call((0, 1, 2, 3), ((0, 0), (0, 0)), gate_up, arrived, (inner[0][0],))
-    inner.append(attention_back(True, 1, given[1][:1], back[1], (both[0], crossed[0])))
+    inner.append(attention_back(True, 1, given[1][:1], back[1], (both[0], crossed[0], *parts[0][1:])))
     parts.append(parts_of(inner[1]))
     sums = merged([both[2:4], both[6:]], (inner[1][0],))
     gate_far = hold(sums[0], *parts[1][1:])

time: 704 us -> 699 us (level)
    ppermute x53 -> x56, waiting for transfers between devices: 67 us -> 131 us  [swapped(): return lax.ppermute(value, 'row', [(r, r ^ step) for r in range(rows)])]
    all_gather x1, waiting for transfers between devices: 92.7 us -> 29.4 us  [on_device(): dense = lax.all_gather(dense, ('row', 'col'), axis=0, tiled=True)]
    ppermute x53 -> x56, starting transfers between devices: 81.6 us -> 79.7 us  [swapped(): return lax.ppermute(value, 'row', [(r, r ^ step) for r in range(rows)])]
  transfers between devices with their start and end apart: 72 -> 75, of which waited for: 34 -> 32; matrix products, arithmetic and copies ran while one was open for 4% -> 4% of each run, Pallas kernels for 32% -> 31%
where the time goes in v10:
time: 699 us; the launch traced here: 686 us
  Pallas kernels  246 us (35%)
  waiting for transfers between devices  221 us (32%)
  starting transfers between devices  172 us (25%)
  other arithmetic  20.2 us (3%)
  between operations  15.2 us (2%)
  local copies, waits for them, and re-layouts  12.2 us (2%)
    pallas_call x36, Pallas kernels, call(): pl.pallas_call(run, out_shape=tuple(shapes), in_specs=[pl.BlockSpec(memor...  246 us
    ppermute x56, waiting for transfers between devices, swapped(): return lax.ppermute(value, 'row', [(r, r ^ step) for r in range(rows)])  131 us
    all_to_all x14, starting transfers between devices, over_columns(): return lax.all_to_all(value, 'col', split_axis=0, concat_axis=0, tiled=True)  84.4 us
    ppermute x56, starting transfers between devices, swapped(): return lax.ppermute(value, 'row', [(r, r ^ step) for r in range(rows)])  79.7 us
    all_to_all x14, waiting for transfers between devices, over_columns(): return lax.all_to_all(value, 'col', split_axis=0, concat_axis=0, tiled=True)  41.2 us
    all_gather x1, waiting for transfers between devices, on_device(): dense = lax.all_gather(dense, ('row', 'col'), axis=0, tiled=True)  29.4 us
  transfers between devices with their start and end apart: 75, of which 32 were waited for; matrix products, arithmetic and copies ran while one was open for 4% of the time, Pallas kernels for 31%

profile of v10, /device:TPU:9, one launch (start us, length us, event | category | flops | bytes accessed | tf_op | source)
XLA Modules:
  0.0 686.5 jit_solution(11328742588478222489)
XLA Ops:
  24.0 64.4 %collective-permute-done.2.refs_6_.refs_11_.refs_12_.refs_16_ = bf16[1,192,1536]{2,1,0:T(8,128)(2,1)} collective-permute-done((bf16[1,192,1536]{2,1,0:T(8,128)(2,1)S(1)}, bf16[1,192,1536]{2,1,0:T(8,128)(2,1)}, u32[]{:S(2)}, u32[]{:S(2)}) %collective-permute-start.2) | collective-permute-done | bytes 589856 | tf_op jit(solution)/shard_map/ppermute | solution.py:163
  88.4 29.4 %all-gather.2.cloned.1.call-done.refs_3_.refs_12_.refs_6_.refs_17_.refs_11_ = bf16[1536,3712]{1,0:T(8,128)(2,1)} async-done(((bf16[24,3712]{1,0:T(8,128)(2,1)}), bf16[1536,3712]{1,0:T(8,128)(2,1)}) %all-gather.2.cloned.1.call-update) | async-done | bytes 11403280 | tf_op jit(solution)/shard_map/all_gather | solution.py:768
  149.3 11.3 %collective-permute-done.11.refs_12_.refs_13_.refs_17_ = bf16[1,192,1536]{2,1,0:T(8,128)(2,1)} collective-permute-done((bf16[1,192,1536]{2,1,0:T(8,128)(2,1)S(1)}, bf16[1,192,1536]{2,1,0:T(8,128)(2,1)}, u32[]{:S(2)}, u32[]{:S(2)}) %collective-permute-start.11) | collective-permute-done | bytes 589856 | tf_op jit(solution)/shard_map/ppermute | solution.py:163
  175.6 6.7 all-to-all-start.2
  185.9 10.3 %expert_forward.4 = bf16[16,32,1536]{2,1,0:T(8,128)(2,1)} custom-call(bf16[16,32,1536]{2,1,0:T(8,128)(2,1)} %all-to-all-done.refs_0_.refs_1_, bf16[2,192,1536]{2,1,0:T(8,128)(2,1)} %bitcast.9.refs_1_.refs_2_.refs_6_, bf16[2,192,1536]{2,1,0:T(8,128)(2,1)} %collective-permute-done.6.refs_2_.refs_3_.refs_7_, ...), custom_call_target="tpu_custom_call" | custom-call | flops 3623878656 | bytes 17301504 | tf_op jit(solution)/shard_map/expert_forward/pallas_call | solution.py:124
  196.2 7.7 %all-to-all-done.2.refs_0_.refs_1_ = bf16[16,32,1536]{2,1,0:T(8,128)(2,1)} async-done(((bf16[16,32,1536]{2,1,0:T(8,128)(2,1)}), bf16[16,32,1536]{2,1,0:T(8,128)(2,1)}, u32[]{:S(2)}, u32[]{:S(2)}) %all-to-all-start.2) | async-done | bytes 1572896 | tf_op jit(solution)/shard_map/all_to_all | solution.py:735
  208.6 10.3 %expert_forward.5.refs_5_ = bf16[16,32,1536]{2,1,0:T(8,128)(2,1)} custom-call(bf16[16,32,1536]{2,1,0:T(8,128)(2,1)} %all-to-all-done.2.refs_0_.refs_1_, bf16[2,192,1536]{2,1,0:T(8,128)(2,1)} %bitcast.9.refs_1_.refs_2_.refs_6_, bf16[2,192,1536]{2,1,0:T(8,128)(2,1)} %collective-permute-done.6.refs_2_.refs_3_.refs_7_, ...), custom_call_target="tpu_custom_call" | custom-call | flops 3623878656 | bytes 17301504 | tf_op jit(solution)/shard_map/expert_forward/pallas_call | solution.py:124
  218.9 9.6 %all-to-all-done.1.refs_0_ = bf16[16,32,1536]{2,1,0:T(8,128)(2,1)} async-done(((bf16[16,32,1536]{2,1,0:T(8,128)(2,1)}), bf16[16,32,1536]{2,1,0:T(8,128)(2,1)}, u32[]{:S(2)}, u32[]{:S(2)}) %all-to-all-start.1) | async-done | bytes 1572896 | tf_op jit(solution)/shard_map/all_to_all | solution.py:735
  263.9 6.8 attend.6
  270.7 7.0 %all-to-all-start.4 = ((bf16[16,32,1664]{2,1,0:T(8,128)(2,1)}), bf16[16,32,1664]{2,1,0:T(8,128)(2,1)}, u32[]{:S(2)}, u32[]{:S(2)}) async-start(bf16[16,32,1664]{2,1,0:T(8,128)(2,1)} %get-tuple-element.143), calls=%async_computation.4 | async-start | bytes 3407872 | tf_op jit(solution)/shard_map/all_to_all | solution.py:735
  279.1 8.6 %collective-permute-done.21.refs_1_ = bf16[96,1536]{1,0:T(8,128)(2,1)} collective-permute-done((bf16[96,1536]{1,0:T(8,128)(2,1)S(1)}, bf16[96,1536]{1,0:T(8,128)(2,1)}, u32[]{:S(2)}, u32[]{:S(2)}) %collective-permute-start.21) | collective-permute-done | bytes 294944 | tf_op jit(solution)/shard_map/ppermute | solution.py:957
  303.1 6.8 attend.7
  309.9 6.7 all-to-all-start.6
  320.9 16.4 %expert_forward.6 = (bf16[16,32,1536]{2,1,0:T(8,128)(2,1)}, bf16[2,256,768]{2,1,0:T(8,128)(2,1)}, bf16[2,256,768]{2,1,0:T(8,128)(2,1)}, bf16[2,256,768]{2,1,0:T(8,128)(2,1)}, bf16[16,32,1664]{2,1,0:T(8,128)(2,1)}) custom-call(bf16[16,32,1664]{2,1,0:T(8,128)(2,1)} %all-to-all-done.4.refs_0_.refs_4_, bf16[16,32,1536]{2,1,0:T(8,128)(2,1)} %all-to-all-done.refs_0_.refs_1_, ...), custom_call_target="tpu_custom_call" | custom-call | flops 7247757312 | bytes 23068672 | tf_op jit(solution)/shard_map/expert_forward/pallas_call | solution.py:124
  348.0 16.5 %expert_forward.7 = (bf16[16,32,1536]{2,1,0:T(8,128)(2,1)}, bf16[2,256,768]{2,1,0:T(8,128)(2,1)}, bf16[2,256,768]{2,1,0:T(8,128)(2,1)}, bf16[2,256,768]{2,1,0:T(8,128)(2,1)}, bf16[16,32,1664]{2,1,0:T(8,128)(2,1)}) custom-call(bf16[16,32,1664]{2,1,0:T(8,128)(2,1)} %all-to-all-done.6.refs_0_.refs_5_, bf16[16,32,1536]{2,1,0:T(8,128)(2,1)} %all-to-all-done.2.refs_0_.refs_1_, ...), custom_call_target="tpu_custom_call" | custom-call | flops 7247757312 | bytes 23068672 | tf_op jit(solution)/shard_map/expert_forward/pallas_call | solution.py:124
  376.2 8.8 %attend_back.4 = (f32[96,1536]{1,0:T(8,128)}, bf16[96,1536]{1,0:T(8,128)(2,1)}, bf16[96,512]{1,0:T(8,128)(2,1)}, bf16[96,512]{1,0:T(8,128)(2,1)}, bf16[96,512]{1,0:T(8,128)(2,1)}, /*index=5*/bf16[96,512]{1,0:T(8,128)(2,1)}) custom-call(s32[1]{0:T(128)} %bitcast.1.refs_0_, s32[1]{0:T(128)} %bitcast.refs_0_.refs_1_, ...), custom_call_target="tpu_custom_call" | custom-call | flops 1056964608 | bytes 17520640 | tf_op jit(solution)/shard_map/attend_back/pallas_call | solution.py:124
  394.7 6.7 project_back.4.refs_21_
  404.3 8.8 %attend_back.5 = (f32[96,1536]{1,0:T(8,128)}, bf16[96,1536]{1,0:T(8,128)(2,1)}, bf16[96,512]{1,0:T(8,128)(2,1)}, bf16[96,512]{1,0:T(8,128)(2,1)}, bf16[96,512]{1,0:T(8,128)(2,1)}, /*index=5*/bf16[96,512]{1,0:T(8,128)(2,1)}) custom-call(s32[1]{0:T(128)} %bitcast.1.refs_0_, s32[1]{0:T(128)} %bitcast.refs_0_.refs_1_, ...), custom_call_target="tpu_custom_call" | custom-call | flops 1056964608 | bytes 17520640 | tf_op jit(solution)/shard_map/attend_back/pallas_call | solution.py:124
  432.7 6.7 project_back.5
  450.5 7.6 %all-to-all-start.10 = ((bf16[16,32,1536]{2,1,0:T(8,128)(2,1)}), bf16[16,32,1536]{2,1,0:T(8,128)(2,1)}, u32[]{:S(2)}, u32[]{:S(2)}) async-start(bf16[16,32,1536]{2,1,0:T(8,128)(2,1)} %get-tuple-element.177.refs_20_), calls=%async_computation.10 | async-start | bytes 3145728 | tf_op jit(solution)/shard_map/all_to_all | solution.py:735
  458.1 10.9 %expert_backward.2 = (bf16[16,32,1664]{2,1,0:T(8,128)(2,1)}, bf16[2,256,768]{2,1,0:T(8,128)(2,1)}, bf16[2,256,768]{2,1,0:T(8,128)(2,1)}) custom-call(s32[1]{0:T(128)} %bitcast.refs_0_.refs_1_, bf16[16,32,1536]{2,1,0:T(8,128)(2,1)} %all-to-all-done.8.refs_1_.refs_2_, bf16[2,256,768]{2,1,0:T(8,128)(2,1)} %get-tuple-element.168.refs_2_.refs_0_, ...), custom_call_target="tpu_custom_call" | custom-call | flops 3623878656 | bytes 22937600 | tf_op jit(solution)/shard_map/expert_backward/pallas_call | solution.py:124
  469.0 9.7 %all-to-all-done.10.refs_1_.refs_3_ = bf16[16,32,1536]{2,1,0:T(8,128)(2,1)} async-done(((bf16[16,32,1536]{2,1,0:T(8,128)(2,1)}), bf16[16,32,1536]{2,1,0:T(8,128)(2,1)}, u32[]{:S(2)}, u32[]{:S(2)}) %all-to-all-start.10) | async-done | bytes 1572896 | tf_op jit(solution)/shard_map/all_to_all | solution.py:735
  491.6 10.9 %expert_backward.3 = (bf16[16,32,1664]{2,1,0:T(8,128)(2,1)}, bf16[2,256,768]{2,1,0:T(8,128)(2,1)}, bf16[2,256,768]{2,1,0:T(8,128)(2,1)}) custom-call(s32[1]{0:T(128)} %bitcast.refs_0_.refs_1_, bf16[16,32,1536]{2,1,0:T(8,128)(2,1)} %all-to-all-done.10.refs_1_.refs_3_, bf16[2,256,768]{2,1,0:T(8,128)(2,1)} %get-tuple-element.179.refs_2_.refs_1_, ...), custom_call_target="tpu_custom_call" | custom-call | flops 3623878656 | bytes 22937600 | tf_op jit(solution)/shard_map/expert_backward/pallas_call | solution.py:124
  508.3 6.9 %all-to-all-start.11 = ((bf16[16,32,1664]{2,1,0:T(8,128)(2,1)}), bf16[16,32,1664]{2,1,0:T(8,128)(2,1)}, u32[]{:S(2)}, u32[]{:S(2)}) async-start(bf16[16,32,1664]{2,1,0:T(8,128)(2,1)} %hold.3), calls=%async_computation.11 | async-start | bytes 3407872 | tf_op jit(solution)/shard_map/all_to_all | solution.py:735
  516.7 9.5 %attend_back.6 = (f32[96,1536]{1,0:T(8,128)}, bf16[96,1536]{1,0:T(8,128)(2,1)}, bf16[96,896]{1,0:T(8,128)(2,1)}, bf16[96,896]{1,0:T(8,128)(2,1)}, bf16[96,896]{1...) custom-call(s32[1]{0:T(128)} %bitcast.1.refs_0_, s32[1]{0:T(128)} %bitcast.refs_0_.refs_1_, ...), custom_call_target="tpu_custom_call" | custom-call | flops 1056964608 | bytes 19167232 | tf_op jit(solution)/shard_map/attend_back/pallas_call | solution.py:124
  526.2 9.1 %expert_weight_grads.4 = (bf16[2,192,1536]{2,1,0:T(8,128)(2,1)}, bf16[2,192,1536]{2,1,0:T(8,128)(2,1)}, bf16[2,192,1536]{2,1,0:T(8,128)(2,1)}, bf16[2,192,1536]{...) custom-call(bf16[2,256,768]{2,1,0:T(8,128)(2,1)} %get-tuple-element., ...), custom_call_target="tpu_custom_call" | custom-call | flops 2415919104 | bytes 15990784 | tf_op jit(solution)/shard_map/expert_weight_grads/pallas_call | solution.py:124
  552.4 9.5 %attend_back.7 = (f32[96,1536]{1,0:T(8,128)}, bf16[96,1536]{1,0:T(8,128)(2,1)}, bf16[96,896]{1,0:T(8,128)(2,1)}, bf16[96,896]{1,0:T(8,128)(2,1)}, bf16[96,896]{1...) custom-call(s32[1]{0:T(128)} %bitcast.1.refs_0_, s32[1]{0:T(128)} %bitcast.refs_0_.refs_1_, ...), custom_call_target="tpu_custom_call" | custom-call | flops 1056964608 | bytes 19167232 | tf_op jit(solution)/shard_map/attend_back/pallas_call | solution.py:124
  573.6 6.8 out_grads.1.refs_12_
  588.9 7.3 %project_back.6 = (bf16[96,1536]{1,0:T(8,128)(2,1)}, f32[96,1536]{1,0:T(8,128)}, bf16[96,512]{1,0:T(8,128)(2,1)}, bf16[96,512]{1,0:T(8,128)(2,1)}, bf16[96,512]{1,0:T(8,128)(2,1)}, /*index=5*/bf16[96,512]{1,0:T(8,128)(2,1)}) custom-call(s32[1]{0:T(128)} %bitcast.1.refs_0_, bf16[96,896]{1,0:T(8,128)(2,1)} %get-tuple-element.199.refs_5_.refs_1_, ...), custom_call_target="tpu_custom_call" | custom-call | flops 603979776 | bytes 14948352 | tf_op jit(solution)/shard_map/project_back/pallas_call | solution.py:124
  596.2 7.3 %project_back.7 = (bf16[96,1536]{1,0:T(8,128)(2,1)}, f32[96,1536]{1,0:T(8,128)}, bf16[96,512]{1,0:T(8,128)(2,1)}, bf16[96,512]{1,0:T(8,128)(2,1)}, bf16[96,512]{1,0:T(8,128)(2,1)}, /*index=5*/bf16[96,512]{1,0:T(8,128)(2,1)}) custom-call(s32[1]{0:T(128)} %bitcast.1.refs_0_, bf16[96,896]{1,0:T(8,128)(2,1)} %get-tuple-element.187.refs_4_.refs_1_, ...), custom_call_target="tpu_custom_call" | custom-call | flops 603979776 | bytes 14948352 | tf_op jit(solution)/shard_map/project_back/pallas_call | solution.py:124
  633.4 6.7 all-to-all-start.13
  654.6 8.6 %all-to-all-done.13.refs_2_ = bf16[16,96,512]{2,1,0:T(8,128)(2,1)} async-done(((bf16[16,96,512]{2,1,0:T(8,128)(2,1)}), bf16[16,96,512]{2,1,0:T(8,128)(2,1)}, u32[]{:S(2)}, u32[]{:S(2)}) %all-to-all-start.13) | async-done | bytes 1572896 | tf_op jit(solution)/shard_map/all_to_all | solution.py:735
  (242 shorter events, 311.2 us)
Async XLA Ops:
  7.2 110.6 %all-gather.2.cloned.1.call-start = ((), (), s32[]{:S(2)}) async-start(), calls=%async_computation.14 | async-start | bytes 11581440 | tf_op jit(solution)/shard_map/all_gather | solution.py:768
  10.5 77.9 %collective-permute-start = (bf16[2,192,1536]{2,1,0:T(8,128)(2,1)}, bf16[2,192,1536]{2,1,0:T(8,128)(2,1)}, u32[]{:S(2)}, u32[]{:S(2)}) collective-permute-start(bf16[2,192,1536]{2,1,0:T(8,128)(2,1)} %bitcast.9.refs_1_.refs_2_.refs_6_), channel_id=1, source_target_pairs={{0,32},{16,48},{32,0},{48,16},{1,33},{17,49},{33,1},{49,17},{2,34}... | collective-permute-start | bytes 3538952 | tf_op jit(solution)/shard_map/ppermute | solution.py:163
  12.6 75.8 %collective-permute-start.1 = (bf16[2,192,1536]{2,1,0:T(8,128)(2,1)}, bf16[2,192,1536]{2,1,0:T(8,128)(2,1)}, u32[]{:S(2)}, u32[]{:S(2)}) collective-permute-start(bf16[2,192,1536]{2,1,0:T(8,128)(2,1)} %bitcast.10.refs_5_.refs_6_.refs_10_), channel_id=1, source_target_pairs={{0,32},{16,48},{32,0},{48,16},{1,33},{17,49},{33,1},{49,17},{2,34}... | collective-permute-start | bytes 3538952 | tf_op jit(solution)/shard_map/ppermute | solution.py:163
  15.7 72.7 %collective-permute-start.2 = (bf16[1,192,1536]{2,1,0:T(8,128)(2,1)S(1)}, bf16[1,192,1536]{2,1,0:T(8,128)(2,1)}, u32[]{:S(2)}, u32[]{:S(2)}) collective-permute-start(bf16[1,192,1536]{2,1,0:T(8,128)(2,1)S(1)} %get-tuple-element.283), channel_id=1, source_target_pairs={{0,32},{16,48},{32,0},{48,16},{1,33},{17,49},{33,1},{49,17},{2,34}... | collective-permute-start | bytes 1769480 | tf_op jit(solution)/shard_map/ppermute | solution.py:163
  139.6 35.9 %all-to-all-start = ((bf16[16,32,1536]{2,1,0:T(8,128)(2,1)}), bf16[16,32,1536]{2,1,0:T(8,128)(2,1)}, u32[]{:S(2)}, u32[]{:S(2)}) async-start(bf16[16,32,1536]{2,1,0:T(8,128)(2,1)} %get-tuple-element.131), calls=%async_computation | async-start | bytes 3145728 | tf_op jit(solution)/shard_map/all_to_all | solution.py:735
  146.4 35.8 %collective-permute-start.6 = (bf16[2,192,1536]{2,1,0:T(8,128)(2,1)}, bf16[2,192,1536]{2,1,0:T(8,128)(2,1)}, u32[]{:S(2)}, u32[]{:S(2)}) collective-permute-start(bf16[2,192,1536]{2,1,0:T(8,128)(2,1)} %bitcast.9.refs_1_.refs_2_.refs_6_), channel_id=1, source_target_pairs={{0,16},{16,0},{32,48},{48,32},{1,17},{17,1},{33,49},{49,33},{2,18}... | collective-permute-start | bytes 3538952 | tf_op jit(solution)/shard_map/ppermute | solution.py:163
  147.0 36.1 %collective-permute-start.8 = (bf16[2,192,1536]{2,1,0:T(8,128)(2,1)}, bf16[2,192,1536]{2,1,0:T(8,128)(2,1)}, u32[]{:S(2)}, u32[]{:S(2)}) collective-permute-start(bf16[2,192,1536]{2,1,0:T(8,128)(2,1)} %bitcast.10.refs_5_.refs_6_.refs_10_), channel_id=1, source_target_pairs={{0,16},{16,0},{32,48},{48,32},{1,17},{17,1},{33,49},{49,33},{2,18}... | collective-permute-start | bytes 3538952 | tf_op jit(solution)/shard_map/ppermute | solution.py:163
  165.8 20.1 %collective-permute-start.7 = (bf16[2,192,1536]{2,1,0:T(8,128)(2,1)}, bf16[2,192,1536]{2,1,0:T(8,128)(2,1)}, u32[]{:S(2)}, u32[]{:S(2)}) collective-permute-start(bf16[2,192,1536]{2,1,0:T(8,128)(2,1)} %collective-permute-done.refs_4_.refs_3_.refs_8_), channel_id=1, source_target_pairs={{0,16},{16,0},{32,48},{48,32},{1,17},{17,1},{33,49},{49,33},{2,18}... | collective-permute-start | bytes 3538952 | tf_op jit(solution)/shard_map/ppermute | solution.py:163
  175.6 28.3 %all-to-all-start.2 = ((bf16[16,32,1536]{2,1,0:T(8,128)(2,1)}), bf16[16,32,1536]{2,1,0:T(8,128)(2,1)}, u32[]{:S(2)}, u32[]{:S(2)}) async-start(bf16[16,32,1536]{2,1,0:T(8,128)(2,1)} %get-tuple-element.135.refs_15_), calls=%async_computation.2 | async-start | bytes 3145728 | tf_op jit(solution)/shard_map/all_to_all | solution.py:735
  203.9 24.6 %all-to-all-start.1 = ((bf16[16,32,1536]{2,1,0:T(8,128)(2,1)}), bf16[16,32,1536]{2,1,0:T(8,128)(2,1)}, u32[]{:S(2)}, u32[]{:S(2)}) async-start(bf16[16,32,1536]{2,1,0:T(8,128)(2,1)} %expert_forward.4), calls=%async_computation.1 | async-start | bytes 3145728 | tf_op jit(solution)/shard_map/all_to_all | solution.py:735
  228.5 30.2 %all-to-all-start.3 = ((bf16[16,32,1536]{2,1,0:T(8,128)(2,1)}), bf16[16,32,1536]{2,1,0:T(8,128)(2,1)}, u32[]{:S(2)}, u32[]{:S(2)}) async-start(bf16[16,32,1536]{2,1,0:T(8,128)(2,1)} %expert_forward.5.refs_5_), calls=%async_computation.3 | async-start | bytes 3145728 | tf_op jit(solution)/shard_map/all_to_all | solution.py:735
  270.7 39.2 %all-to-all-start.4 = ((bf16[16,32,1664]{2,1,0:T(8,128)(2,1)}), bf16[16,32,1664]{2,1,0:T(8,128)(2,1)}, u32[]{:S(2)}, u32[]{:S(2)}) async-start(bf16[16,32,1664]{2,1,0:T(8,128)(2,1)} %get-tuple-element.143), calls=%async_computation.4 | async-start | bytes 3407872 | tf_op jit(solution)/shard_map/all_to_all | solution.py:735
  309.9 30.7 %all-to-all-start.6 = ((bf16[16,32,1664]{2,1,0:T(8,128)(2,1)}), bf16[16,32,1664]{2,1,0:T(8,128)(2,1)}, u32[]{:S(2)}, u32[]{:S(2)}) async-start(bf16[16,32,1664]{2,1,0:T(8,128)(2,1)} %get-tuple-element.147.refs_16_), calls=%async_computation.6 | async-start | bytes 3407872 | tf_op jit(solution)/shard_map/all_to_all | solution.py:735
  319.1 28.9 %collective-permute-start.25 = (bf16[4,96,1536]{2,1,0:T(8,128)(2,1)}, bf16[4,96,1536]{2,1,0:T(8,128)(2,1)}, u32[]{:S(2)}, u32[]{:S(2)}) collective-permute-start(bf16[4,96,1536]{2,1,0:T(8,128)(2,1)} %pack.1.refs_0_), channel_id=1, source_target_pairs={{0,32},{16,48},{32,0},{48,16},{1,33},{17,49},{33,1},{49,17},{2,34}... | collective-permute-start | bytes 3538952 | tf_op jit(solution)/shard_map/ppermute | solution.py:163
  340.6 26.0 %all-to-all-start.5 = ((bf16[16,32,1664]{2,1,0:T(8,128)(2,1)}), bf16[16,32,1664]{2,1,0:T(8,128)(2,1)}, u32[]{:S(2)}, u32[]{:S(2)}) async-start(bf16[16,32,1664]{2,1,0:T(8,128)(2,1)} %get-tuple-element.148), calls=%async_computation.5 | async-start | bytes 3407872 | tf_op jit(solution)/shard_map/all_to_all | solution.py:735
  366.7 37.6 %all-to-all-start.7 = ((bf16[16,32,1664]{2,1,0:T(8,128)(2,1)}), bf16[16,32,1664]{2,1,0:T(8,128)(2,1)}, u32[]{:S(2)}, u32[]{:S(2)}) async-start(bf16[16,32,1664]{2,1,0:T(8,128)(2,1)} %get-tuple-element.156.refs_18_), calls=%async_computation.7 | async-start | bytes 3407872 | tf_op jit(solution)/shard_map/all_to_all | solution.py:735
  372.2 32.0 %collective-permute-start.30 = (bf16[4,96,1536]{2,1,0:T(8,128)(2,1)}, bf16[4,96,1536]{2,1,0:T(8,128)(2,1)}, u32[]{:S(2)}, u32[]{:S(2)}) collective-permute-start(bf16[4,96,1536]{2,1,0:T(8,128)(2,1)} %pack.1.refs_0_), channel_id=1, source_target_pairs={{0,16},{16,0},{32,48},{48,32},{1,17},{17,1},{33,49},{49,33},{2,18}... | collective-permute-start | bytes 3538952 | tf_op jit(solution)/shard_map/ppermute | solution.py:163
  375.7 28.6 %collective-permute-start.31 = (bf16[4,96,1536]{2,1,0:T(8,128)(2,1)}, bf16[4,96,1536]{2,1,0:T(8,128)(2,1)}, u32[]{:S(2)}, u32[]{:S(2)}) collective-permute-start(bf16[4,96,1536]{2,1,0:T(8,128)(2,1)} %collective-permute-done.25.refs_16_.refs_19_.refs_2_), channel_id=1, source_target_pairs={{0,16},{16,0},{32,48},{48,32},{1,17},{17,1},{33,49},{49,33},{2,18}... | collective-permute-start | bytes 3538952 | tf_op jit(solution)/shard_map/ppermute | solution.py:163
  416.5 34.0 %all-to-all-start.8 = ((bf16[16,32,1536]{2,1,0:T(8,128)(2,1)}), bf16[16,32,1536]{2,1,0:T(8,128)(2,1)}, u32[]{:S(2)}, u32[]{:S(2)}) async-start(bf16[16,32,1536]{2,1,0:T(8,128)(2,1)} %get-tuple-element.167), calls=%async_computation.8 | async-start | bytes 3145728 | tf_op jit(solution)/shard_map/all_to_all | solution.py:735
  450.5 28.2 %all-to-all-start.10 = ((bf16[16,32,1536]{2,1,0:T(8,128)(2,1)}), bf16[16,32,1536]{2,1,0:T(8,128)(2,1)}, u32[]{:S(2)}, u32[]{:S(2)}) async-start(bf16[16,32,1536]{2,1,0:T(8,128)(2,1)} %get-tuple-element.177.refs_20_), calls=%async_computation.10 | async-start | bytes 3145728 | tf_op jit(solution)/shard_map/all_to_all | solution.py:735
  478.7 29.6 %all-to-all-start.9 = ((bf16[16,32,1664]{2,1,0:T(8,128)(2,1)}), bf16[16,32,1664]{2,1,0:T(8,128)(2,1)}, u32[]{:S(2)}, u32[]{:S(2)}) async-start(bf16[16,32,1664]{2,1,0:T(8,128)(2,1)} %get-tuple-element.178), calls=%async_computation.9 | async-start | bytes 3407872 | tf_op jit(solution)/shard_map/all_to_all | solution.py:735
  508.3 44.1 %all-to-all-start.11 = ((bf16[16,32,1664]{2,1,0:T(8,128)(2,1)}), bf16[16,32,1664]{2,1,0:T(8,128)(2,1)}, u32[]{:S(2)}, u32[]{:S(2)}) async-start(bf16[16,32,1664]{2,1,0:T(8,128)(2,1)} %hold.3), calls=%async_computation.11 | async-start | bytes 3407872 | tf_op jit(solution)/shard_map/all_to_all | solution.py:735
  515.2 37.2 %collective-permute-start.40 = (bf16[2,192,1536]{2,1,0:T(8,128)(2,1)}, bf16[2,192,1536]{2,1,0:T(8,128)(2,1)}, u32[]{:S(2)}, u32[]{:S(2)}) collective-permute-start(bf16[2,192,1536]{2,1,0:T(8,128)(2,1)} %add.133.refs_1_.refs_19_), channel_id=1, source_target_pairs={{0,32},{16,48},{32,0},{48,16},{1,33},{17,49},{33,1},{49,17},{2,34}... | collective-permute-start | bytes 3538952 | tf_op jit(solution)/shard_map/ppermute | solution.py:163
  535.3 30.2 %collective-permute-start.44 = (bf16[2,192,1536]{2,1,0:T(8,128)(2,1)}, bf16[2,192,1536]{2,1,0:T(8,128)(2,1)}, u32[]{:S(2)}, u32[]{:S(2)}) collective-permute-start(bf16[2,192,1536]{2,1,0:T(8,128)(2,1)} %get-tuple-element.212), channel_id=1, source_target_pairs={{0,16},{16,0},{32,48},{48,32},{1,17},{17,1},{33,49},{49,33},{2,18}... | collective-permute-start | bytes 3538952 | tf_op jit(solution)/shard_map/ppermute | solution.py:163
  536.0 29.6 %collective-permute-start.45 = (bf16[2,192,1536]{2,1,0:T(8,128)(2,1)}, bf16[2,192,1536]{2,1,0:T(8,128)(2,1)}, u32[]{:S(2)}, u32[]{:S(2)}) collective-permute-start(bf16[2,192,1536]{2,1,0:T(8,128)(2,1)} %get-tuple-element.214), channel_id=1, source_target_pairs={{0,16},{16,0},{32,48},{48,32},{1,17},{17,1},{33,49},{49,33},{2,18}... | collective-permute-start | bytes 3538952 | tf_op jit(solution)/shard_map/ppermute | solution.py:163
  580.4 53.0 %all-to-all-start.12 = ((bf16[16,96,512]{2,1,0:T(8,128)(2,1)}), bf16[16,96,512]{2,1,0:T(8,128)(2,1)}, u32[]{:S(2)}, u32[]{:S(2)}) async-start(bf16[16,96,512]{2,1,0:T(8,128)(2,1)} %out_grads.1.refs_12_), calls=%async_computation.12 | async-start | bytes 3145728 | tf_op jit(solution)/shard_map/all_to_all | solution.py:735
  587.0 40.8 %collective-permute-start.52 = (bf16[2,192,1536]{2,1,0:T(8,128)(2,1)}, bf16[2,192,1536]{2,1,0:T(8,128)(2,1)}, u32[]{:S(2)}, u32[]{:S(2)}) collective-permute-start(bf16[2,192,1536]{2,1,0:T(8,128)(2,1)} %hold.4.refs_19_), channel_id=1, source_target_pairs={{0,32},{16,48},{32,0},{48,16},{1,33},{17,49},{33,1},{49,17},{2,34}... | collective-permute-start | bytes 3538952 | tf_op jit(solution)/shard_map/ppermute | solution.py:163
  588.4 58.8 %collective-permute-start.56 = (bf16[2,192,1536]{2,1,0:T(8,128)(2,1)}, bf16[2,192,1536]{2,1,0:T(8,128)(2,1)}, u32[]{:S(2)}, u32[]{:S(2)}) collective-permute-start(bf16[2,192,1536]{2,1,0:T(8,128)(2,1)} %get-tuple-element.239), channel_id=1, source_target_pairs={{0,16},{16,0},{32,48},{48,32},{1,17},{17,1},{33,49},{49,33},{2,18}... | collective-permute-start | bytes 3538952 | tf_op jit(solution)/shard_map/ppermute | solution.py:163
  611.3 39.8 %collective-permute-start.59 = (bf16[2,192,1536]{2,1,0:T(8,128)(2,1)}, bf16[2,192,1536]{2,1,0:T(8,128)(2,1)}, u32[]{:S(2)}, u32[]{:S(2)}) collective-permute-start(bf16[2,192,1536]{2,1,0:T(8,128)(2,1)} %get-tuple-element.243), channel_id=1, source_target_pairs={{0,16},{16,0},{32,48},{48,32},{1,17},{17,1},{33,49},{49,33},{2,18}... | collective-permute-start | bytes 3538952 | tf_op jit(solution)/shard_map/ppermute | solution.py:163
  625.1 46.6 %collective-permute-start.57 = (bf16[2,192,1536]{2,1,0:T(8,128)(2,1)}, bf16[2,192,1536]{2,1,0:T(8,128)(2,1)}, u32[]{:S(2)}, u32[]{:S(2)}) collective-permute-start(bf16[2,192,1536]{2,1,0:T(8,128)(2,1)} %get-tuple-element.241), channel_id=1, source_target_pairs={{0,16},{16,0},{32,48},{48,32},{1,17},{17,1},{33,49},{49,33},{2,18}... | collective-permute-start | bytes 3538952 | tf_op jit(solution)/shard_map/ppermute | solution.py:163
  633.4 29.7 %all-to-all-start.13 = ((bf16[16,96,512]{2,1,0:T(8,128)(2,1)}), bf16[16,96,512]{2,1,0:T(8,128)(2,1)}, u32[]{:S(2)}, u32[]{:S(2)}) async-start(bf16[16,96,512]{2,1,0:T(8,128)(2,1)} %qkv_grads.1.refs_12_), calls=%async_computation.13 | async-start | bytes 3145728 | tf_op jit(solution)/shard_map/all_to_all | solution.py:735
  641.2 30.5 %collective-permute-start.58 = (bf16[2,192,1536]{2,1,0:T(8,128)(2,1)}, bf16[2,192,1536]{2,1,0:T(8,128)(2,1)}, u32[]{:S(2)}, u32[]{:S(2)}) collective-permute-start(bf16[2,192,1536]{2,1,0:T(8,128)(2,1)} %hold.5), channel_id=1, source_target_pairs={{0,32},{16,48},{32,0},{48,16},{1,33},{17,49},{33,1},{49,17},{2,34}... | collective-permute-start | bytes 3538952 | tf_op jit(solution)/shard_map/ppermute | solution.py:163
  (61 other events, 511.8 us)
Sparse Core Ops, SparseCore 0:
  11.7 105.9 all-gather.1

commit v11 on v10

--- a/solution.py
+++ b/solution.py
@@ -660,6 +660,19 @@
         total[...] = (one[...].astype(F32) + other[...].astype(F32)).astype(BF)
 
 
+def add_by_expert(gate, other_gate, up, other_up, up_sum, *gate_sums):
+    up_sum[...] = (up[...].astype(F32) + other_up[...].astype(F32)).astype(BF)
+    for j, out in enumerate(gate_sums):
+        out[0] = (gate[j].astype(F32) + other_gate[j].astype(F32)).astype(BF)
+
+
+def total_by_expert(one, other, *rest):
+    crossed, out = rest[:-1], rest[-1]
+    for j, far in enumerate(crossed):
+        out[j] = one[j].astype(F32) + other[j].astype(F32) + far[0].astype(F32)
+        sent(out, j)
+
+
 def pack(*refs):
     for k, value in enumerate(refs[:-1]):
         refs[-1][k] = value[...]
@@ -775,11 +788,14 @@
         return own, swapped(own, 1), two, swapped(two, 1)
 
     gate_shards, up_shards = shards_of(w_gate[0]), shards_of(w_up[0])
-    down_twos = [swapped(w_down[0, j : j + 1], 2) for j in range(per_column)]
-    shards = (
-        *gate_shards, *up_shards, w_down[0], swapped(w_down[0], 1), *down_twos,
-        *[swapped(two, 1) for two in down_twos],
-    )
+    down_one, down_first = swapped(w_down[0], 1), swapped(w_down[0, :1], 2)
+
+    def all_shards(waits):
+        twos = [down_first]
+        twos += [swapped(hold(w_down[0, j : j + 1], *waits), 2) for j in range(1, per_column)]
+        threes = [swapped(two, 1) for two in twos]
+        return (*gate_shards, *up_shards, w_down[0], down_one, *twos, *threes)
+
 
     lane = jnp.arange(LANES, dtype=jnp.int32)
     half = HEAD_DIM // 2
@@ -840,7 +856,7 @@
     tables = late([cosine, sine])
     first_flag = (1 - second)
 
-    def forward(keep, came, waits, early, after):
+    def forward(keep, came, waits, early, after, shards):
         projected, pairs = [], []
         if keep:
             for m in pieces:
@@ -864,6 +880,7 @@
             for m in pieces:
                 pair = made[3 * m + 2]
                 pairs.append([pair] + [swapped(pair, s) for s in steps[1:]])
+        shards = shards or all_shards(pairs[1][1:])
         attended = [
             call(
                 functools.partial(attend, keep),
@@ -897,7 +914,7 @@
             )
             for m in pieces
         ]
-        return projected, pairs, attended, arrived, applied, lefts
+        return projected, pairs, attended, arrived, applied, lefts, shards
 
     def weight_call(quarters, which, lefts, rights, waits):
         quarter, some = hidden_width // 4, len(quarters)
@@ -943,8 +960,8 @@
             (here,), waits,
         )
 
-    kept = forward(False, None, (gate_shards[2], up_shards[2], down_twos[0]), None, ())
-    attended, early, applied = kept[2:5]
+    kept = forward(False, None, (gate_shards[2], up_shards[2], down_first), None, (), ())
+    attended, early, applied, unused, shards = kept[2:]
     returned = [over_columns(a[0]) for a in applied]
     results = [
         call(
@@ -956,7 +973,8 @@
     ]
     came = [lax.ppermute(r[0], "section", [(0, 1)]) for r in results]
 
-    projected, pairs, attended, arrived, applied, lefts = forward(True, came, (), early, results[1])
+    kept = forward(True, came, (), early, results[1], shards)
+    projected, pairs, attended, arrived, applied, lefts, unused = kept
     hidden = [a[1] for a in applied]
     shared = [over_columns(a[4]) for a in applied]
     inner, outer = [], []
@@ -987,15 +1005,20 @@
     gate_up = [a[1] for a in moved] + [a[2] for a in moved]
     down_far = merged([weight_call((2, 3), ((0, 0),), hidden, arrived_grads, ())], ())[0]
     crossed = [swapped(down_far, 2)]
-    back = [over_columns(moved[0][0]), over_columns(hold(moved[1][0], down_far))]
+    back = [over_columns(moved[0][0]), over_columns(moved[1][0])]
     inner = [attention_back(True, 0, given[0][:1], back[0], (moved[1][0], down_far))]
     parts = [parts_of(inner[0])]
     both = weight_call((0, 1, 2, 3), ((0, 0), (0, 0)), gate_up, arrived, (inner[0][0],))
-    inner.append(attention_back(True, 1, given[1][:1], back[1], (both[0], crossed[0], *parts[0][1:])))
+    inner.append(attention_back(True, 1, given[1][:1], back[1], (both[0], crossed[0])))
     parts.append(parts_of(inner[1]))
-    sums = merged([both[2:4], both[6:]], (inner[1][0],))
-    gate_far = hold(sums[0], *parts[1][1:])
-    crossed.append(swapped(gate_far, 2))
+    quarter_like = like((1, hidden_width // 4, width), BF)
+    sums = call(
+        add_by_expert, (Sent(both[6]),) + (Sent(quarter_like),) * per_column,
+        late([both[2], swapped(both[3], 1), both[6], swapped(both[7], 1)]), 0,
+        waits=(inner[1][0],),
+    )
+    gate_far = hold(sums[1], *parts[1][1:])
+    gate_crossed = [swapped(gate_far, 2)]
     o_grads = call(
         out_grads, (Sent(like((columns, rows * shard, share + LANES), BF)),),
         late([*lefts, *[p[s] for s in steps for p in parts], *[a[5] for a in attended],
@@ -1005,17 +1028,23 @@
     last = projection_back(True, 1, inner[1], parts[1], (o_grads,))
     outer = [projection_back(True, 0, inner[0], parts[0], (last[0],)), last]
     backs = [[o[2]] + [swapped(o[2 + s], s) for s in steps[1:]] for o in outer]
-    crossed.append(swapped(hold(sums[1], *backs[0][1:], *backs[1][1:]), 2))
+    backs_there = (*backs[0][1:], *backs[1][1:])
+    gate_crossed += [swapped(hold(one, *backs_there), 2) for one in sums[2:]]
+    up_crossed = swapped(hold(sums[0], *backs_there), 2)
     near = weight_call((0, 1), ((0, 0),), hidden, arrived_grads, (outer[1][0],))
     w_grads = call(
         qkv_grads, (Sent(like((columns, rows * shard, qkv_width // rows), BF)),),
         late([*lefts, *[b[s] for s in steps for b in backs]]),
-        2 * width * length * micro * qkv_width // rows, waits=(crossed[1], near[0]),
+        2 * width * length * micro * qkv_width // rows, waits=(gate_crossed[0], near[0]),
     )[0]
     expert_grads = [
         one.astype(F32) + swapped(other, 1).astype(F32) + c.astype(F32)
-        for one, other, c in zip((near[0], both[0], both[4]), (near[1], both[1], both[5]), crossed)
+        for one, other, c in ((near[0], near[1], crossed[0]), (both[4], both[5], up_crossed))
     ]
+    gate_grad = call(
+        total_by_expert, (Sent(like(both[0].shape, F32)),),
+        late([both[0], swapped(both[1], 1), *gate_crossed]), 0,
+    )[0]
     layer_outputs = call(
         last_outputs, (Sent(like((micro, tokens, width), F32)),),
         late([spread] + [v for m in pieces for v in (
@@ -1049,8 +1078,8 @@
         o_grad[None],
         second_sum,
         r_grad[None],
+        gate_grad[None],
         expert_grads[1][None],
-        expert_grads[2][None],
         expert_grads[0][None],
     )
 

time: 699 us -> 695 us (level)
  waiting for transfers between devices: 221 us -> 210 us
    all_to_all x14, waiting for transfers between devices: 41.2 us -> 32.6 us  [over_columns(): return lax.all_to_all(value, 'col', split_axis=0, concat_axis=0, tiled=True)]
    ppermute x56 -> x57, starting transfers between devices: 79.7 us -> 86.2 us  [swapped(): return lax.ppermute(value, 'row', [(r, r ^ step) for r in range(rows)])]
    pallas_call x36 -> x37, Pallas kernels: 246 us -> 249 us  [call(): pl.pallas_call(run, out_shape=tuple(shapes), in_specs=[pl.BlockSpec(memor...]
    ppermute x56 -> x57, waiting for transfers between devices: 131 us -> 129 us  [swapped(): return lax.ppermute(value, 'row', [(r, r ^ step) for r in range(rows)])]
  transfers between devices with their start and end apart: 75 -> 76, of which waited for: 32 -> 37; matrix products, arithmetic and copies ran while one was open for 4% -> 3% of each run, Pallas kernels for 31% -> 32%
where the time goes in v11:
time: 695 us; the launch traced here: 681 us
  Pallas kernels  249 us (36%)
  waiting for transfers between devices  210 us (30%)
  starting transfers between devices  177 us (25%)
  other arithmetic  16.7 us (2%)
  between operations  15.1 us (2%)
  local copies, waits for them, and re-layouts  11.9 us (2%)
    pallas_call x37, Pallas kernels, call(): pl.pallas_call(run, out_shape=tuple(shapes), in_specs=[pl.BlockSpec(memor...  249 us
    ppermute x57, waiting for transfers between devices, swapped(): return lax.ppermute(value, 'row', [(r, r ^ step) for r in range(rows)])  129 us
    ppermute x57, starting transfers between devices, swapped(): return lax.ppermute(value, 'row', [(r, r ^ step) for r in range(rows)])  86.2 us
    all_to_all x14, starting transfers between devices, over_columns(): return lax.all_to_all(value, 'col', split_axis=0, concat_axis=0, tiled=True)  83.1 us
    all_to_all x14, waiting for transfers between devices, over_columns(): return lax.all_to_all(value, 'col', split_axis=0, concat_axis=0, tiled=True)  32.6 us
    all_gather x1, waiting for transfers between devices, on_device(): dense = lax.all_gather(dense, ('row', 'col'), axis=0, tiled=True)  29.4 us
  transfers between devices with their start and end apart: 76, of which 37 were waited for; matrix products, arithmetic and copies ran while one was open for 3% of the time, Pallas kernels for 32%

profile of v11, /device:TPU:9, one launch (start us, length us, event | category | flops | bytes accessed | tf_op | source)
XLA Modules:
  0.0 681.0 jit_solution(7768045803103510785)
XLA Ops:
  23.9 64.4 %collective-permute-done.2.refs_6_.refs_11_.refs_12_.refs_16_ = bf16[1,192,1536]{2,1,0:T(8,128)(2,1)} collective-permute-done((bf16[1,192,1536]{2,1,0:T(8,128)(2,1)S(1)}, bf16[1,192,1536]{2,1,0:T(8,128)(2,1)}, u32[]{:S(2)}, u32[]{:S(2)}) %collective-permute-start.2) | collective-permute-done | bytes 589856 | tf_op jit(solution)/shard_map/ppermute | solution.py:163
  88.4 29.4 %all-gather.2.cloned.1.call-done.refs_3_.refs_12_.refs_6_.refs_17_.refs_11_ = bf16[1536,3712]{1,0:T(8,128)(2,1)} async-done(((bf16[24,3712]{1,0:T(8,128)(2,1)}), bf16[1536,3712]{1,0:T(8,128)(2,1)}) %all-gather.2.cloned.1.call-update) | async-done | bytes 11403280 | tf_op jit(solution)/shard_map/all_gather | solution.py:781
  177.1 10.3 %expert_forward.4 = bf16[16,32,1536]{2,1,0:T(8,128)(2,1)} custom-call(bf16[16,32,1536]{2,1,0:T(8,128)(2,1)} %all-to-all-done.refs_0_.refs_1_, bf16[2,192,1536]{2,1,0:T(8,128)(2,1)} %bitcast.64, bf16[2,192,1536]{2,1,0:T(8,128)(2,1)} %copy-done.1, bf16[2,192,1536]{2,1,0:T(8,128)(2,1)} %collective-permute-done.refs_4_.refs_3_.refs_8_, ...), custom_call_target="tpu_custom_call" | custom-call | flops 3623878656 | bytes 17301504 | tf_op jit(solution)/shard_map/expert_forward/pallas_call | solution.py:124
  195.8 10.3 %expert_forward.5.refs_5_ = bf16[16,32,1536]{2,1,0:T(8,128)(2,1)} custom-call(bf16[16,32,1536]{2,1,0:T(8,128)(2,1)} %all-to-all-done.2.refs_0_.refs_1_, bf16[2,192,1536]{2,1,0:T(8,128)(2,1)} %bitcast.65, bf16[2,192,1536]{2,1,0:T(8,128)(2,1)} %copy-done.1, bf16[2,192,1536]{2,1,0:T(8,128)(2,1)} %collective-permute-done.refs_4_.refs_3_.refs_8_, ...), custom_call_target="tpu_custom_call" | custom-call | flops 3623878656 | bytes 17301504 | tf_op jit(solution)/shard_map/expert_forward/pallas_call | solution.py:124
  206.1 8.8 %all-to-all-done.1.refs_0_ = bf16[16,32,1536]{2,1,0:T(8,128)(2,1)} async-done(((bf16[16,32,1536]{2,1,0:T(8,128)(2,1)}), bf16[16,32,1536]{2,1,0:T(8,128)(2,1)}, u32[]{:S(2)}, u32[]{:S(2)}) %all-to-all-start.1) | async-done | bytes 1572896 | tf_op jit(solution)/shard_map/all_to_all | solution.py:748
  214.9 6.9 %all-to-all-start.3 = ((bf16[16,32,1536]{2,1,0:T(8,128)(2,1)}), bf16[16,32,1536]{2,1,0:T(8,128)(2,1)}, u32[]{:S(2)}, u32[]{:S(2)}) async-start(bf16[16,32,1536]{2,1,0:T(8,128)(2,1)} %expert_forward.5.refs_5_), calls=%async_computation.3 | async-start | bytes 3145728 | tf_op jit(solution)/shard_map/all_to_all | solution.py:748
  253.3 6.9 %attend.6 = (f32[96,1536]{1,0:T(8,128)}, f32[96,128]{1,0:T(8,128)}, bf16[16,32,1664]{2,1,0:T(8,128)(2,1)}, bf16[2,576,384]{2,1,0:T(8,128)(2,1)}, bf16[96,1536]{1,0:T(8,128)(2,1)}, /*index=5*/bf16[96,1536]{1,0:T(8,128)(2,1)}) custom-call(s32[1]{0:T(128)} %bitcast.refs_0_.refs_1_, f32[96,1536]{1,0:T(8,128)} %get-tuple-element.139.refs_1_.refs_7_.refs_6_, ...), custom_call_target="tpu_custom_call" | custom-call | flops 830472192 | bytes 17389568 | tf_op jit(solution)/shard_map/attend/pallas_call | solution.py:124
  260.2 7.0 %all-to-all-start.4 = ((bf16[16,32,1664]{2,1,0:T(8,128)(2,1)}), bf16[16,32,1664]{2,1,0:T(8,128)(2,1)}, u32[]{:S(2)}, u32[]{:S(2)}) async-start(bf16[16,32,1664]{2,1,0:T(8,128)(2,1)} %get-tuple-element.144), calls=%async_computation.4 | async-start | bytes 3407872 | tf_op jit(solution)/shard_map/all_to_all | solution.py:748
  268.5 8.6 %collective-permute-done.21.refs_1_ = bf16[96,1536]{1,0:T(8,128)(2,1)} collective-permute-done((bf16[96,1536]{1,0:T(8,128)(2,1)S(1)}, bf16[96,1536]{1,0:T(8,128)(2,1)}, u32[]{:S(2)}, u32[]{:S(2)}) %collective-permute-start.21) | collective-permute-done | bytes 294944 | tf_op jit(solution)/shard_map/ppermute | solution.py:974
  292.6 6.8 attend.7
  299.4 6.7 all-to-all-start.6
  310.6 16.4 %expert_forward.6 = (bf16[16,32,1536]{2,1,0:T(8,128)(2,1)}, bf16[2,256,768]{2,1,0:T(8,128)(2,1)}, bf16[2,256,768]{2,1,0:T(8,128)(2,1)}, bf16[2,256,768]{2,1,0:T(8,128)(2,1)}, bf16[16,32,1664]{2,1,0:T(8,128)(2,1)}) custom-call(bf16[16,32,1664]{2,1,0:T(8,128)(2,1)} %all-to-all-done.4.refs_0_.refs_4_, bf16[16,32,1536]{2,1,0:T(8,128)(2,1)} %all-to-all-done.refs_0_.refs_1_, ...), custom_call_target="tpu_custom_call" | custom-call | flops 7247757312 | bytes 23068672 | tf_op jit(solution)/shard_map/expert_forward/pallas_call | solution.py:124
  337.5 16.4 %expert_forward.7 = (bf16[16,32,1536]{2,1,0:T(8,128)(2,1)}, bf16[2,256,768]{2,1,0:T(8,128)(2,1)}, bf16[2,256,768]{2,1,0:T(8,128)(2,1)}, bf16[2,256,768]{2,1,0:T(8,128)(2,1)}, bf16[16,32,1664]{2,1,0:T(8,128)(2,1)}) custom-call(bf16[16,32,1664]{2,1,0:T(8,128)(2,1)} %all-to-all-done.6.refs_0_.refs_5_, bf16[16,32,1536]{2,1,0:T(8,128)(2,1)} %all-to-all-done.2.refs_0_.refs_1_, ...), custom_call_target="tpu_custom_call" | custom-call | flops 7247757312 | bytes 23068672 | tf_op jit(solution)/shard_map/expert_forward/pallas_call | solution.py:124
  365.9 8.7 %attend_back.4 = (f32[96,1536]{1,0:T(8,128)}, bf16[96,1536]{1,0:T(8,128)(2,1)}, bf16[96,512]{1,0:T(8,128)(2,1)}, bf16[96,512]{1,0:T(8,128)(2,1)}, bf16[96,512]{1,0:T(8,128)(2,1)}, /*index=5*/bf16[96,512]{1,0:T(8,128)(2,1)}) custom-call(s32[1]{0:T(128)} %bitcast.1.refs_0_, s32[1]{0:T(128)} %bitcast.refs_0_.refs_1_, ...), custom_call_target="tpu_custom_call" | custom-call | flops 1056964608 | bytes 17520640 | tf_op jit(solution)/shard_map/attend_back/pallas_call | solution.py:124
  384.9 6.7 project_back.4.refs_21_
  394.0 8.8 %attend_back.5 = (f32[96,1536]{1,0:T(8,128)}, bf16[96,1536]{1,0:T(8,128)(2,1)}, bf16[96,512]{1,0:T(8,128)(2,1)}, bf16[96,512]{1,0:T(8,128)(2,1)}, bf16[96,512]{1,0:T(8,128)(2,1)}, /*index=5*/bf16[96,512]{1,0:T(8,128)(2,1)}) custom-call(s32[1]{0:T(128)} %bitcast.1.refs_0_, s32[1]{0:T(128)} %bitcast.refs_0_.refs_1_, ...), custom_call_target="tpu_custom_call" | custom-call | flops 1056964608 | bytes 17520640 | tf_op jit(solution)/shard_map/attend_back/pallas_call | solution.py:124
  406.3 6.6 all-to-all-start.8
  422.4 6.7 project_back.5
  440.5 7.6 %all-to-all-start.10 = ((bf16[16,32,1536]{2,1,0:T(8,128)(2,1)}), bf16[16,32,1536]{2,1,0:T(8,128)(2,1)}, u32[]{:S(2)}, u32[]{:S(2)}) async-start(bf16[16,32,1536]{2,1,0:T(8,128)(2,1)} %get-tuple-element.178.refs_20_), calls=%async_computation.10 | async-start | bytes 3145728 | tf_op jit(solution)/shard_map/all_to_all | solution.py:748
  448.1 10.9 %expert_backward.2 = (bf16[16,32,1664]{2,1,0:T(8,128)(2,1)}, bf16[2,256,768]{2,1,0:T(8,128)(2,1)}, bf16[2,256,768]{2,1,0:T(8,128)(2,1)}) custom-call(s32[1]{0:T(128)} %bitcast.refs_0_.refs_1_, bf16[16,32,1536]{2,1,0:T(8,128)(2,1)} %all-to-all-done.8.refs_1_.refs_2_, bf16[2,256,768]{2,1,0:T(8,128)(2,1)} %get-tuple-element.169.refs_2_.refs_0_, ...), custom_call_target="tpu_custom_call" | custom-call | flops 3623878656 | bytes 22937600 | tf_op jit(solution)/shard_map/expert_backward/pallas_call | solution.py:124
  459.0 9.7 %all-to-all-done.10.refs_1_.refs_3_ = bf16[16,32,1536]{2,1,0:T(8,128)(2,1)} async-done(((bf16[16,32,1536]{2,1,0:T(8,128)(2,1)}), bf16[16,32,1536]{2,1,0:T(8,128)(2,1)}, u32[]{:S(2)}, u32[]{:S(2)}) %all-to-all-start.10) | async-done | bytes 1572896 | tf_op jit(solution)/shard_map/all_to_all | solution.py:748
  481.6 10.9 %expert_backward.3 = (bf16[16,32,1664]{2,1,0:T(8,128)(2,1)}, bf16[2,256,768]{2,1,0:T(8,128)(2,1)}, bf16[2,256,768]{2,1,0:T(8,128)(2,1)}) custom-call(s32[1]{0:T(128)} %bitcast.refs_0_.refs_1_, bf16[16,32,1536]{2,1,0:T(8,128)(2,1)} %all-to-all-done.10.refs_1_.refs_3_, bf16[2,256,768]{2,1,0:T(8,128)(2,1)} %get-tuple-element.180.refs_2_.refs_1_, ...), custom_call_target="tpu_custom_call" | custom-call | flops 3623878656 | bytes 22937600 | tf_op jit(solution)/shard_map/expert_backward/pallas_call | solution.py:124
  504.7 9.4 %attend_back.6 = (f32[96,1536]{1,0:T(8,128)}, bf16[96,1536]{1,0:T(8,128)(2,1)}, bf16[96,896]{1,0:T(8,128)(2,1)}, bf16[96,896]{1,0:T(8,128)(2,1)}, bf16[96,896]{1...) custom-call(s32[1]{0:T(128)} %bitcast.1.refs_0_, s32[1]{0:T(128)} %bitcast.refs_0_.refs_1_, ...), custom_call_target="tpu_custom_call" | custom-call | flops 1056964608 | bytes 19167232 | tf_op jit(solution)/shard_map/attend_back/pallas_call | solution.py:124
  514.1 9.1 %expert_weight_grads.4 = (bf16[2,192,1536]{2,1,0:T(8,128)(2,1)}, bf16[2,192,1536]{2,1,0:T(8,128)(2,1)}, bf16[2,192,1536]{2,1,0:T(8,128)(2,1)}, bf16[2,192,1536]{...) custom-call(bf16[2,256,768]{2,1,0:T(8,128)(2,1)} %get-tuple-element., ...), custom_call_target="tpu_custom_call" | custom-call | flops 2415919104 | bytes 15990784 | tf_op jit(solution)/shard_map/expert_weight_grads/pallas_call | solution.py:124
  528.8 9.4 %attend_back.7 = (f32[96,1536]{1,0:T(8,128)}, bf16[96,1536]{1,0:T(8,128)(2,1)}, bf16[96,896]{1,0:T(8,128)(2,1)}, bf16[96,896]{1,0:T(8,128)(2,1)}, bf16[96,896]{1...) custom-call(s32[1]{0:T(128)} %bitcast.1.refs_0_, s32[1]{0:T(128)} %bitcast.refs_0_.refs_1_, ...), custom_call_target="tpu_custom_call" | custom-call | flops 1056964608 | bytes 19167232 | tf_op jit(solution)/shard_map/attend_back/pallas_call | solution.py:124
  562.2 6.8 out_grads.1.refs_12_
  569.0 6.7 all-to-all-start.12
  577.5 7.3 %project_back.6 = (bf16[96,1536]{1,0:T(8,128)(2,1)}, f32[96,1536]{1,0:T(8,128)}, bf16[96,512]{1,0:T(8,128)(2,1)}, bf16[96,512]{1,0:T(8,128)(2,1)}, bf16[96,512]{1,0:T(8,128)(2,1)}, /*index=5*/bf16[96,512]{1,0:T(8,128)(2,1)}) custom-call(s32[1]{0:T(128)} %bitcast.1.refs_0_, bf16[96,896]{1,0:T(8,128)(2,1)} %get-tuple-element.200.refs_5_.refs_1_, ...), custom_call_target="tpu_custom_call" | custom-call | flops 603979776 | bytes 14948352 | tf_op jit(solution)/shard_map/project_back/pallas_call | solution.py:124
  584.8 7.3 %project_back.7 = (bf16[96,1536]{1,0:T(8,128)(2,1)}, f32[96,1536]{1,0:T(8,128)}, bf16[96,512]{1,0:T(8,128)(2,1)}, bf16[96,512]{1,0:T(8,128)(2,1)}, bf16[96,512]{1,0:T(8,128)(2,1)}, /*index=5*/bf16[96,512]{1,0:T(8,128)(2,1)}) custom-call(s32[1]{0:T(128)} %bitcast.1.refs_0_, bf16[96,896]{1,0:T(8,128)(2,1)} %get-tuple-element.188.refs_4_.refs_1_, ...), custom_call_target="tpu_custom_call" | custom-call | flops 603979776 | bytes 14948352 | tf_op jit(solution)/shard_map/project_back/pallas_call | solution.py:124
  618.1 6.8 %all-to-all-start.13 = ((bf16[16,96,512]{2,1,0:T(8,128)(2,1)}), bf16[16,96,512]{2,1,0:T(8,128)(2,1)}, u32[]{:S(2)}, u32[]{:S(2)}) async-start(bf16[16,96,512]{2,1,0:T(8,128)(2,1)} %qkv_grads.1.refs_12_), calls=%async_computation.13 | async-start | bytes 3145728 | tf_op jit(solution)/shard_map/all_to_all | solution.py:748
  634.8 7.1 %collective-permute-done.57.refs_3_ = bf16[1,192,1536]{2,1,0:T(8,128)(2,1)} collective-permute-done((bf16[1,192,1536]{2,1,0:T(8,128)(2,1)}, bf16[1,192,1536]{2,1,0:T(8,128)(2,1)}, u32[]{:S(2)}, u32[]{:S(2)}) %collective-permute-start.57) | collective-permute-done | bytes 589856 | tf_op jit(solution)/shard_map/ppermute | solution.py:163
  656.9 10.3 %collective-permute-done.59 = bf16[2,192,1536]{2,1,0:T(8,128)(2,1)} collective-permute-done((bf16[2,192,1536]{2,1,0:T(8,128)(2,1)}, bf16[2,192,1536]{2,1,0:T(8,128)(2,1)}, u32[]{:S(2)}, u32[]{:S(2)}) %collective-permute-start.59) | collective-permute-done | bytes 1179680 | tf_op jit(solution)/shard_map/ppermute | solution.py:163
  (244 shorter events, 310.2 us)
Async XLA Ops:
  7.2 110.6 %all-gather.2.cloned.1.call-start = ((), (), s32[]{:S(2)}) async-start(), calls=%async_computation.14 | async-start | bytes 11581440 | tf_op jit(solution)/shard_map/all_gather | solution.py:781
  10.5 77.9 %collective-permute-start = (bf16[2,192,1536]{2,1,0:T(8,128)(2,1)}, bf16[2,192,1536]{2,1,0:T(8,128)(2,1)}, u32[]{:S(2)}, u32[]{:S(2)}) collective-permute-start(bf16[2,192,1536]{2,1,0:T(8,128)(2,1)} %bitcast.63), channel_id=1, source_target_pairs={{0,32},{16,48},{32,0},{48,16},{1,33},{17,49},{33,1},{49,17},{2,34}... | collective-permute-start | bytes 3538952 | tf_op jit(solution)/shard_map/ppermute | solution.py:163
  12.6 75.8 %collective-permute-start.1 = (bf16[2,192,1536]{2,1,0:T(8,128)(2,1)}, bf16[2,192,1536]{2,1,0:T(8,128)(2,1)}, u32[]{:S(2)}, u32[]{:S(2)}) collective-permute-start(bf16[2,192,1536]{2,1,0:T(8,128)(2,1)} %bitcast.10.refs_5_.refs_6_.refs_10_), channel_id=1, source_target_pairs={{0,32},{16,48},{32,0},{48,16},{1,33},{17,49},{33,1},{49,17},{2,34}... | collective-permute-start | bytes 3538952 | tf_op jit(solution)/shard_map/ppermute | solution.py:163
  15.7 72.7 %collective-permute-start.2 = (bf16[1,192,1536]{2,1,0:T(8,128)(2,1)S(1)}, bf16[1,192,1536]{2,1,0:T(8,128)(2,1)}, u32[]{:S(2)}, u32[]{:S(2)}) collective-permute-start(bf16[1,192,1536]{2,1,0:T(8,128)(2,1)S(1)} %get-tuple-element.285), channel_id=1, source_target_pairs={{0,32},{16,48},{32,0},{48,16},{1,33},{17,49},{33,1},{49,17},{2,34}... | collective-permute-start | bytes 1769480 | tf_op jit(solution)/shard_map/ppermute | solution.py:163
  139.6 27.2 %all-to-all-start = ((bf16[16,32,1536]{2,1,0:T(8,128)(2,1)}), bf16[16,32,1536]{2,1,0:T(8,128)(2,1)}, u32[]{:S(2)}, u32[]{:S(2)}) async-start(bf16[16,32,1536]{2,1,0:T(8,128)(2,1)} %get-tuple-element.132), calls=%async_computation | async-start | bytes 3145728 | tf_op jit(solution)/shard_map/all_to_all | solution.py:748
  145.5 25.7 %collective-permute-start.8 = (bf16[2,192,1536]{2,1,0:T(8,128)(2,1)}, bf16[2,192,1536]{2,1,0:T(8,128)(2,1)}, u32[]{:S(2)}, u32[]{:S(2)}) collective-permute-start(bf16[2,192,1536]{2,1,0:T(8,128)(2,1)} %bitcast.10.refs_5_.refs_6_.refs_10_), channel_id=1, source_target_pairs={{0,16},{16,0},{32,48},{48,32},{1,17},{17,1},{33,49},{49,33},{2,18}... | collective-permute-start | bytes 3538952 | tf_op jit(solution)/shard_map/ppermute | solution.py:163
  150.7 23.7 %collective-permute-start.10 = (bf16[2,192,1536]{2,1,0:T(8,128)(2,1)}, bf16[2,192,1536]{2,1,0:T(8,128)(2,1)}, u32[]{:S(2)}, u32[]{:S(2)}) collective-permute-start(bf16[2,192,1536]{2,1,0:T(8,128)(2,1)} %bitcast.19.refs_9_.refs_10_.refs_14_), channel_id=1, source_target_pairs={{0,16},{16,0},{32,48},{48,32},{1,17},{17,1},{33,49},{49,33},{2,18}... | collective-permute-start | bytes 3538952 | tf_op jit(solution)/shard_map/ppermute | solution.py:163
  152.0 24.3 %collective-permute-start.7 = (bf16[2,192,1536]{2,1,0:T(8,128)(2,1)}, bf16[2,192,1536]{2,1,0:T(8,128)(2,1)}, u32[]{:S(2)}, u32[]{:S(2)}) collective-permute-start(bf16[2,192,1536]{2,1,0:T(8,128)(2,1)} %collective-permute-done.refs_4_.refs_3_.refs_8_), channel_id=1, source_target_pairs={{0,16},{16,0},{32,48},{48,32},{1,17},{17,1},{33,49},{49,33},{2,18}... | collective-permute-start | bytes 3538952 | tf_op jit(solution)/shard_map/ppermute | solution.py:163
  166.8 24.3 %all-to-all-start.2 = ((bf16[16,32,1536]{2,1,0:T(8,128)(2,1)}), bf16[16,32,1536]{2,1,0:T(8,128)(2,1)}, u32[]{:S(2)}, u32[]{:S(2)}) async-start(bf16[16,32,1536]{2,1,0:T(8,128)(2,1)} %get-tuple-element.136.refs_15_), calls=%async_computation.2 | async-start | bytes 3145728 | tf_op jit(solution)/shard_map/all_to_all | solution.py:748
  191.1 23.8 %all-to-all-start.1 = ((bf16[16,32,1536]{2,1,0:T(8,128)(2,1)}), bf16[16,32,1536]{2,1,0:T(8,128)(2,1)}, u32[]{:S(2)}, u32[]{:S(2)}) async-start(bf16[16,32,1536]{2,1,0:T(8,128)(2,1)} %expert_forward.4), calls=%async_computation.1 | async-start | bytes 3145728 | tf_op jit(solution)/shard_map/all_to_all | solution.py:748
  214.9 31.9 %all-to-all-start.3 = ((bf16[16,32,1536]{2,1,0:T(8,128)(2,1)}), bf16[16,32,1536]{2,1,0:T(8,128)(2,1)}, u32[]{:S(2)}, u32[]{:S(2)}) async-start(bf16[16,32,1536]{2,1,0:T(8,128)(2,1)} %expert_forward.5.refs_5_), calls=%async_computation.3 | async-start | bytes 3145728 | tf_op jit(solution)/shard_map/all_to_all | solution.py:748
  260.2 39.2 %all-to-all-start.4 = ((bf16[16,32,1664]{2,1,0:T(8,128)(2,1)}), bf16[16,32,1664]{2,1,0:T(8,128)(2,1)}, u32[]{:S(2)}, u32[]{:S(2)}) async-start(bf16[16,32,1664]{2,1,0:T(8,128)(2,1)} %get-tuple-element.144), calls=%async_computation.4 | async-start | bytes 3407872 | tf_op jit(solution)/shard_map/all_to_all | solution.py:748
  299.4 30.8 %all-to-all-start.6 = ((bf16[16,32,1664]{2,1,0:T(8,128)(2,1)}), bf16[16,32,1664]{2,1,0:T(8,128)(2,1)}, u32[]{:S(2)}, u32[]{:S(2)}) async-start(bf16[16,32,1664]{2,1,0:T(8,128)(2,1)} %get-tuple-element.148.refs_16_), calls=%async_computation.6 | async-start | bytes 3407872 | tf_op jit(solution)/shard_map/all_to_all | solution.py:748
  308.5 28.9 %collective-permute-start.25 = (bf16[4,96,1536]{2,1,0:T(8,128)(2,1)}, bf16[4,96,1536]{2,1,0:T(8,128)(2,1)}, u32[]{:S(2)}, u32[]{:S(2)}) collective-permute-start(bf16[4,96,1536]{2,1,0:T(8,128)(2,1)} %pack.1.refs_0_), channel_id=1, source_target_pairs={{0,32},{16,48},{32,0},{48,16},{1,33},{17,49},{33,1},{49,17},{2,34}... | collective-permute-start | bytes 3538952 | tf_op jit(solution)/shard_map/ppermute | solution.py:163
  330.2 26.1 %all-to-all-start.5 = ((bf16[16,32,1664]{2,1,0:T(8,128)(2,1)}), bf16[16,32,1664]{2,1,0:T(8,128)(2,1)}, u32[]{:S(2)}, u32[]{:S(2)}) async-start(bf16[16,32,1664]{2,1,0:T(8,128)(2,1)} %get-tuple-element.149), calls=%async_computation.5 | async-start | bytes 3407872 | tf_op jit(solution)/shard_map/all_to_all | solution.py:748
  356.3 37.7 %all-to-all-start.7 = ((bf16[16,32,1664]{2,1,0:T(8,128)(2,1)}), bf16[16,32,1664]{2,1,0:T(8,128)(2,1)}, u32[]{:S(2)}, u32[]{:S(2)}) async-start(bf16[16,32,1664]{2,1,0:T(8,128)(2,1)} %get-tuple-element.157.refs_18_), calls=%async_computation.7 | async-start | bytes 3407872 | tf_op jit(solution)/shard_map/all_to_all | solution.py:748
  361.7 32.3 %collective-permute-start.30 = (bf16[4,96,1536]{2,1,0:T(8,128)(2,1)}, bf16[4,96,1536]{2,1,0:T(8,128)(2,1)}, u32[]{:S(2)}, u32[]{:S(2)}) collective-permute-start(bf16[4,96,1536]{2,1,0:T(8,128)(2,1)} %pack.1.refs_0_), channel_id=1, source_target_pairs={{0,16},{16,0},{32,48},{48,32},{1,17},{17,1},{33,49},{49,33},{2,18}... | collective-permute-start | bytes 3538952 | tf_op jit(solution)/shard_map/ppermute | solution.py:163
  365.4 28.7 %collective-permute-start.31 = (bf16[4,96,1536]{2,1,0:T(8,128)(2,1)}, bf16[4,96,1536]{2,1,0:T(8,128)(2,1)}, u32[]{:S(2)}, u32[]{:S(2)}) collective-permute-start(bf16[4,96,1536]{2,1,0:T(8,128)(2,1)} %collective-permute-done.25.refs_16_.refs_19_.refs_2_), channel_id=1, source_target_pairs={{0,16},{16,0},{32,48},{48,32},{1,17},{17,1},{33,49},{49,33},{2,18}... | collective-permute-start | bytes 3538952 | tf_op jit(solution)/shard_map/ppermute | solution.py:163
  406.3 34.2 %all-to-all-start.8 = ((bf16[16,32,1536]{2,1,0:T(8,128)(2,1)}), bf16[16,32,1536]{2,1,0:T(8,128)(2,1)}, u32[]{:S(2)}, u32[]{:S(2)}) async-start(bf16[16,32,1536]{2,1,0:T(8,128)(2,1)} %get-tuple-element.168), calls=%async_computation.8 | async-start | bytes 3145728 | tf_op jit(solution)/shard_map/all_to_all | solution.py:748
  440.5 28.2 %all-to-all-start.10 = ((bf16[16,32,1536]{2,1,0:T(8,128)(2,1)}), bf16[16,32,1536]{2,1,0:T(8,128)(2,1)}, u32[]{:S(2)}, u32[]{:S(2)}) async-start(bf16[16,32,1536]{2,1,0:T(8,128)(2,1)} %get-tuple-element.178.refs_20_), calls=%async_computation.10 | async-start | bytes 3145728 | tf_op jit(solution)/shard_map/all_to_all | solution.py:748
  468.7 25.9 %all-to-all-start.9 = ((bf16[16,32,1664]{2,1,0:T(8,128)(2,1)}), bf16[16,32,1664]{2,1,0:T(8,128)(2,1)}, u32[]{:S(2)}, u32[]{:S(2)}) async-start(bf16[16,32,1664]{2,1,0:T(8,128)(2,1)} %get-tuple-element.179), calls=%async_computation.9 | async-start | bytes 3407872 | tf_op jit(solution)/shard_map/all_to_all | solution.py:748
  478.0 22.2 %collective-permute-start.36 = (bf16[2,192,1536]{2,1,0:T(8,128)(2,1)}, bf16[2,192,1536]{2,1,0:T(8,128)(2,1)}, u32[]{:S(2)}, u32[]{:S(2)}) collective-permute-start(bf16[2,192,1536]{2,1,0:T(8,128)(2,1)} %get-tuple-element.187), channel_id=1, source_target_pairs={{0,16},{16,0},{32,48},{48,32},{1,17},{17,1},{33,49},{49,33},{2,18}... | collective-permute-start | bytes 3538952 | tf_op jit(solution)/shard_map/ppermute | solution.py:163
  494.6 33.8 %all-to-all-start.11 = ((bf16[16,32,1664]{2,1,0:T(8,128)(2,1)}), bf16[16,32,1664]{2,1,0:T(8,128)(2,1)}, u32[]{:S(2)}, u32[]{:S(2)}) async-start(bf16[16,32,1664]{2,1,0:T(8,128)(2,1)} %get-tuple-element.184.refs_18_), calls=%async_computation.11 | async-start | bytes 3407872 | tf_op jit(solution)/shard_map/all_to_all | solution.py:748
  503.2 25.7 %collective-permute-start.40 = (bf16[2,192,1536]{2,1,0:T(8,128)(2,1)}, bf16[2,192,1536]{2,1,0:T(8,128)(2,1)}, u32[]{:S(2)}, u32[]{:S(2)}) collective-permute-start(bf16[2,192,1536]{2,1,0:T(8,128)(2,1)} %add.122.refs_19_), channel_id=1, source_target_pairs={{0,32},{16,48},{32,0},{48,16},{1,33},{17,49},{33,1},{49,17},{2,34}... | collective-permute-start | bytes 3538952 | tf_op jit(solution)/shard_map/ppermute | solution.py:163
  523.2 23.6 %collective-permute-start.44 = (bf16[2,192,1536]{2,1,0:T(8,128)(2,1)}, bf16[2,192,1536]{2,1,0:T(8,128)(2,1)}, u32[]{:S(2)}, u32[]{:S(2)}) collective-permute-start(bf16[2,192,1536]{2,1,0:T(8,128)(2,1)} %get-tuple-element.213), channel_id=1, source_target_pairs={{0,16},{16,0},{32,48},{48,32},{1,17},{17,1},{33,49},{49,33},{2,18}... | collective-permute-start | bytes 3538952 | tf_op jit(solution)/shard_map/ppermute | solution.py:163
  569.0 49.1 %all-to-all-start.12 = ((bf16[16,96,512]{2,1,0:T(8,128)(2,1)}), bf16[16,96,512]{2,1,0:T(8,128)(2,1)}, u32[]{:S(2)}, u32[]{:S(2)}) async-start(bf16[16,96,512]{2,1,0:T(8,128)(2,1)} %out_grads.1.refs_12_), calls=%async_computation.12 | async-start | bytes 3145728 | tf_op jit(solution)/shard_map/all_to_all | solution.py:748
  575.7 36.8 %collective-permute-start.52 = (bf16[1,192,1536]{2,1,0:T(8,128)(2,1)}, bf16[1,192,1536]{2,1,0:T(8,128)(2,1)}, u32[]{:S(2)}, u32[]{:S(2)}) collective-permute-start(bf16[1,192,1536]{2,1,0:T(8,128)(2,1)} %hold.5.refs_19_), channel_id=1, source_target_pairs={{0,32},{16,48},{32,0},{48,16},{1,33},{17,49},{33,1},{49,17},{2,34}... | collective-permute-start | bytes 1769480 | tf_op jit(solution)/shard_map/ppermute | solution.py:163
  577.0 57.8 %collective-permute-start.56 = (bf16[2,192,1536]{2,1,0:T(8,128)(2,1)}, bf16[2,192,1536]{2,1,0:T(8,128)(2,1)}, u32[]{:S(2)}, u32[]{:S(2)}) collective-permute-start(bf16[2,192,1536]{2,1,0:T(8,128)(2,1)} %get-tuple-element.240), channel_id=1, source_target_pairs={{0,16},{16,0},{32,48},{48,32},{1,17},{17,1},{33,49},{49,33},{2,18}... | collective-permute-start | bytes 3538952 | tf_op jit(solution)/shard_map/ppermute | solution.py:163
  596.9 48.7 %collective-permute-start.60 = (bf16[2,192,1536]{2,1,0:T(8,128)(2,1)}, bf16[2,192,1536]{2,1,0:T(8,128)(2,1)}, u32[]{:S(2)}, u32[]{:S(2)}) collective-permute-start(bf16[2,192,1536]{2,1,0:T(8,128)(2,1)} %get-tuple-element.245), channel_id=1, source_target_pairs={{0,16},{16,0},{32,48},{48,32},{1,17},{17,1},{33,49},{49,33},{2,18}... | collective-permute-start | bytes 3538952 | tf_op jit(solution)/shard_map/ppermute | solution.py:163
  618.1 31.4 %all-to-all-start.13 = ((bf16[16,96,512]{2,1,0:T(8,128)(2,1)}), bf16[16,96,512]{2,1,0:T(8,128)(2,1)}, u32[]{:S(2)}, u32[]{:S(2)}) async-start(bf16[16,96,512]{2,1,0:T(8,128)(2,1)} %qkv_grads.1.refs_12_), calls=%async_computation.13 | async-start | bytes 3145728 | tf_op jit(solution)/shard_map/all_to_all | solution.py:748
  627.0 29.9 %collective-permute-start.58 = (bf16[2,192,1536]{2,1,0:T(8,128)(2,1)}, bf16[2,192,1536]{2,1,0:T(8,128)(2,1)}, u32[]{:S(2)}, u32[]{:S(2)}) collective-permute-start(bf16[2,192,1536]{2,1,0:T(8,128)(2,1)} %get-tuple-element.243), channel_id=1, source_target_pairs={{0,16},{16,0},{32,48},{48,32},{1,17},{17,1},{33,49},{49,33},{2,18}... | collective-permute-start | bytes 3538952 | tf_op jit(solution)/shard_map/ppermute | solution.py:163
  627.9 39.2 %collective-permute-start.59 = (bf16[2,192,1536]{2,1,0:T(8,128)(2,1)}, bf16[2,192,1536]{2,1,0:T(8,128)(2,1)}, u32[]{:S(2)}, u32[]{:S(2)}) collective-permute-start(bf16[2,192,1536]{2,1,0:T(8,128)(2,1)} %hold.7), channel_id=1, source_target_pairs={{0,32},{16,48},{32,0},{48,16},{1,33},{17,49},{33,1},{49,17},{2,34}... | collective-permute-start | bytes 3538952 | tf_op jit(solution)/shard_map/ppermute | solution.py:163
  (62 other events, 486.4 us)
Sparse Core Ops, SparseCore 0:
  11.7 105.9 all-gather.1

commit v12 on v10

--- a/solution.py
+++ b/solution.py
@@ -292,13 +292,14 @@
     keep, flag, stream, query, pair0, pair1, pair2, pair3, bias, gain, chosen, dispatch, target,
     *rest,
 ):
-    dense, middle, gates, outgoing = rest[:4]
-    kept, (mixed, weights, router, sems) = rest[4:-4], rest[-4:]
+    dense, w_out, middle, gates, outgoing = rest[:5]
+    kept, (mixed, weights, router, sems) = rest[5:-4], rest[-4:]
     width = stream.shape[1]
-    at = dense.shape[1] - width - LANES
     copies = [
-        pltpu.make_async_copy(dense.at[:, pl.ds(at + LANES, width)], weights, sems.at[0]),
-        pltpu.make_async_copy(dense.at[:, pl.ds(at, LANES)], router, sems.at[1]),
+        pltpu.make_async_copy(w_out, weights, sems.at[0]),
+        pltpu.make_async_copy(
+            dense.at[:, pl.ds(dense.shape[1] - LANES, LANES)], router, sems.at[1]
+        ),
     ]
     for copy in copies:
         copy.start()
@@ -498,15 +499,16 @@
 
 def attend_back(
     keep, row, flag, token_grads, before, gates, places, middle, gain, grad, query, pair0, pair1,
-    pair2, pair3, probs, cosine, sine, dense, middle_grads, query_back, part0, part1, part2, part3,
+    pair2, pair3, probs, cosine, sine, dense, w_out, middle_grads, query_back, part0, part1, part2, part3,
     *rest,
 ):
     tokens, width = middle.shape
     kept, (branch, weights, router, sems) = rest[:-4], rest[-4:]
-    at = dense.shape[1] - width - LANES
     copies = [
-        pltpu.make_async_copy(dense.at[:, pl.ds(at, LANES)], router, sems.at[1]),
-        pltpu.make_async_copy(dense.at[:, pl.ds(at + LANES, width)], weights, sems.at[0]),
+        pltpu.make_async_copy(
+            dense.at[:, pl.ds(dense.shape[1] - LANES, LANES)], router, sems.at[1]
+        ),
+        pltpu.make_async_copy(w_out, weights, sems.at[0]),
     ]
     for copy in copies:
         copy.start()
@@ -763,10 +765,13 @@
 
     dense = jnp.concatenate(
         [w_query[0], w_key[0], w_value[0], w_router[0], attn_gain[0][:, None], ffn_gain[0][:, None],
-         jnp.zeros((shard, LANES - experts - 2), BF), w_out[0]], 1
+         jnp.zeros((shard, LANES - experts - 2), BF)], 1
     )
     dense = lax.all_gather(dense, ("row", "col"), axis=0, tiled=True)
-    small = dense[:, qkv_width : qkv_width + LANES]
+    w_o = lax.all_gather(w_out[0], "row", axis=0, tiled=True)
+    w_o = over_columns(jnp.broadcast_to(w_o[None], (columns, *w_o.shape)))
+    w_o = w_o.reshape(columns, rows, shard, width).transpose(1, 0, 2, 3).reshape(width, width)
+    small = dense[:, qkv_width:]
     gain_a = small[:, experts].astype(F32)[None, :]
     gain_f = small[:, experts + 1].astype(F32)[None, :]
 
@@ -775,11 +780,14 @@
         return own, swapped(own, 1), two, swapped(two, 1)
 
     gate_shards, up_shards = shards_of(w_gate[0]), shards_of(w_up[0])
-    down_twos = [swapped(w_down[0, j : j + 1], 2) for j in range(per_column)]
-    shards = (
-        *gate_shards, *up_shards, w_down[0], swapped(w_down[0], 1), *down_twos,
-        *[swapped(two, 1) for two in down_twos],
-    )
+    down_one, down_first = swapped(w_down[0], 1), swapped(w_down[0, :1], 2)
+
+    def all_shards(waits):
+        twos = [down_first]
+        twos += [swapped(hold(w_down[0, j : j + 1], *waits), 2) for j in range(1, per_column)]
+        threes = [swapped(two, 1) for two in twos]
+        return (*gate_shards, *up_shards, w_down[0], down_one, *twos, *threes)
+
 
     lane = jnp.arange(LANES, dtype=jnp.int32)
     half = HEAD_DIM // 2
@@ -840,7 +848,7 @@
     tables = late([cosine, sine])
     first_flag = (1 - second)
 
-    def forward(keep, came, waits, early, after):
+    def forward(keep, came, waits, early, after, shards):
         projected, pairs = [], []
         if keep:
             for m in pieces:
@@ -864,6 +872,7 @@
             for m in pieces:
                 pair = made[3 * m + 2]
                 pairs.append([pair] + [swapped(pair, s) for s in steps[1:]])
+        shards = shards or all_shards(pairs[1][1:])
         attended = [
             call(
                 functools.partial(attend, keep),
@@ -871,7 +880,7 @@
                 + ((Sent(probs_like), Sent(token_low), Sent(token_low)) if keep else ()),
                 (*late([projected[m][0], projected[m][2], *pairs[m], biases[m], gain_f, chosens[m],
                         dispatches[m]]), Late(cotangent, (m, 0))),
-                out_flops + 2 * score_flops, (dense,), [pltpu.VMEM((tokens, width), BF)] + out_scratch,
+                out_flops + 2 * score_flops, (dense, w_o), [pltpu.VMEM((tokens, width), BF)] + out_scratch,
                 (second,), () if m else after,
             )
             for m in pieces
@@ -897,7 +906,7 @@
             )
             for m in pieces
         ]
-        return projected, pairs, attended, arrived, applied, lefts
+        return projected, pairs, attended, arrived, applied, lefts, shards
 
     def weight_call(quarters, which, lefts, rights, waits):
         quarter, some = hidden_width // 4, len(quarters)
@@ -924,7 +933,7 @@
             (*late([token_grads, shared[m] if keep else spread, attended[m][1], places[m],
                                  attended[m][0], gain_f]), Late(*grad),
              *late([projected[m][2], *pairs[m], attended[m][3], cosine, sine])),
-            out_flops + 4 * score_flops, (dense,), [pltpu.VMEM((tokens, width), BF)] + out_scratch,
+            out_flops + 4 * score_flops, (dense, w_o), [pltpu.VMEM((tokens, width), BF)] + out_scratch,
             (here, second), waits,
         )
 
@@ -943,8 +952,8 @@
             (here,), waits,
         )
 
-    kept = forward(False, None, (gate_shards[2], up_shards[2], down_twos[0]), None, ())
-    attended, early, applied = kept[2:5]
+    kept = forward(False, None, (gate_shards[2], up_shards[2], down_first, w_o), None, (), ())
+    attended, early, applied, unused, shards = kept[2:]
     returned = [over_columns(a[0]) for a in applied]
     results = [
         call(
@@ -956,7 +965,8 @@
     ]
     came = [lax.ppermute(r[0], "section", [(0, 1)]) for r in results]
 
-    projected, pairs, attended, arrived, applied, lefts = forward(True, came, (), early, results[1])
+    kept = forward(True, came, (), early, results[1], shards)
+    projected, pairs, attended, arrived, applied, lefts, unused = kept
     hidden = [a[1] for a in applied]
     shared = [over_columns(a[4]) for a in applied]
     inner, outer = [], []
@@ -987,11 +997,11 @@
     gate_up = [a[1] for a in moved] + [a[2] for a in moved]
     down_far = merged([weight_call((2, 3), ((0, 0),), hidden, arrived_grads, ())], ())[0]
     crossed = [swapped(down_far, 2)]
-    back = [over_columns(moved[0][0]), over_columns(hold(moved[1][0], down_far))]
+    back = [over_columns(moved[0][0]), over_columns(moved[1][0])]
     inner = [attention_back(True, 0, given[0][:1], back[0], (moved[1][0], down_far))]
     parts = [parts_of(inner[0])]
     both = weight_call((0, 1, 2, 3), ((0, 0), (0, 0)), gate_up, arrived, (inner[0][0],))
-    inner.append(attention_back(True, 1, given[1][:1], back[1], (both[0], crossed[0], *parts[0][1:])))
+    inner.append(attention_back(True, 1, given[1][:1], back[1], (both[0], crossed[0])))
     parts.append(parts_of(inner[1]))
     sums = merged([both[2:4], both[6:]], (inner[1][0],))
     gate_far = hold(sums[0], *parts[1][1:])

time: 699 us -> 715 us (1.023)
  waiting for transfers between devices: 221 us -> 212 us
  blocking collectives: 0 us -> 8.1 us
  local copies, waits for them, and re-layouts: 12.2 us -> 20.2 us
  starting transfers between devices: 172 us -> 180 us
    ppermute x56, waiting for transfers between devices: 131 us -> 48.1 us  [swapped(): return lax.ppermute(value, 'row', [(r, r ^ step) for r in range(rows)])]
    all_to_all x14 -> x15, waiting for transfers between devices: 41.2 us -> 104 us  [over_columns(): return lax.all_to_all(value, 'col', split_axis=0, concat_axis=0, tiled=True)]
    all_gather x1, waiting for transfers between devices: 29.4 us -> 40.5 us  [on_device(): dense = lax.all_gather(dense, ('row', 'col'), axis=0, tiled=True)]
    all_gather x0 -> x1, blocking collectives: none -> 8.1 us  [on_device(): w_o = lax.all_gather(w_out[0], 'row', axis=0, tiled=True)]
    all_to_all x14 -> x15, starting transfers between devices: 84.4 us -> 89.3 us  [over_columns(): return lax.all_to_all(value, 'col', split_axis=0, concat_axis=0, tiled=True)]
  transfers between devices with their start and end apart: 75 -> 76, of which waited for: 32 -> 35; matrix products, arithmetic and copies ran while one was open for 4% -> 5% of each run, Pallas kernels for 31% -> 30%
where the time goes in v12:
time: 715 us; the launch traced here: 702 us
  Pallas kernels  245 us (34%)
  waiting for transfers between devices  212 us (30%)
  starting transfers between devices  180 us (25%)
  other arithmetic  20.4 us (3%)
  local copies, waits for them, and re-layouts  20.2 us (3%)
  between operations  15.2 us (2%)
  blocking collectives  8.1 us (1%)
    pallas_call x36, Pallas kernels, call(): pl.pallas_call(run, out_shape=tuple(shapes), in_specs=[pl.BlockSpec(memor...  245 us
    all_to_all x15, waiting for transfers between devices, over_columns(): return lax.all_to_all(value, 'col', split_axis=0, concat_axis=0, tiled=True)  104 us
    all_to_all x15, starting transfers between devices, over_columns(): return lax.all_to_all(value, 'col', split_axis=0, concat_axis=0, tiled=True)  89.3 us
    ppermute x56, starting transfers between devices, swapped(): return lax.ppermute(value, 'row', [(r, r ^ step) for r in range(rows)])  84.2 us
    ppermute x56, waiting for transfers between devices, swapped(): return lax.ppermute(value, 'row', [(r, r ^ step) for r in range(rows)])  48.1 us
    all_gather x1, waiting for transfers between devices, on_device(): dense = lax.all_gather(dense, ('row', 'col'), axis=0, tiled=True)  40.5 us
  transfers between devices with their start and end apart: 76, of which 35 were waited for; matrix products, arithmetic and copies ran while one was open for 5% of the time, Pallas kernels for 30%

profile of v12, /device:TPU:9, one launch (start us, length us, event | category | flops | bytes accessed | tf_op | source)
XLA Modules:
  0.0 702.1 jit_solution(17163921717500587089)
XLA Ops:
  10.4 8.1 %all-gather = bf16[1,96,1536]{2,1,0:T(8,128)(2,1)S(1)} all-gather(bf16[1,24,1536]{2,1,0:T(8,128)(2,1)} %param.22), channel_id=2, replica_groups=mesh['section'=2,'row'=4,'col'=16] {'row'}, dimensions={1}, use_global_device_ids=true | all-gather | bytes 368640 | tf_op jit(solution)/shard_map/all_gather | solution.py:771
  21.2 7.8 %all-to-all-start = ((bf16[16,96,1536]{2,1,0:T(8,128)(2,1)}), bf16[16,96,1536]{2,1,0:T(8,128)(2,1)}, u32[]{:S(2)}, u32[]{:S(2)}) async-start(bf16[16,96,1536]{2,1,0:T(8,128)(2,1)} %broadcast_in_dim.88), calls=%async_computation | async-start | bytes 9437184 | tf_op jit(solution)/shard_map/all_to_all | solution.py:737
  42.4 56.8 %all-to-all-done = bf16[16,96,1536]{2,1,0:T(8,128)(2,1)} async-done(((bf16[16,96,1536]{2,1,0:T(8,128)(2,1)}), bf16[16,96,1536]{2,1,0:T(8,128)(2,1)}, u32[]{:S(2)}, u32[]{:S(2)}) %all-to-all-start) | async-done | bytes 4718624 | tf_op jit(solution)/shard_map/all_to_all | solution.py:737
  105.0 40.5 %all-gather.3.cloned.1.call-done.refs_3_.refs_12_.refs_6_.refs_17_.refs_11_ = bf16[1536,2176]{1,0:T(8,128)(2,1)} async-done(((bf16[24,2176]{1,0:T(8,128)(2,1)}), bf16[1536,2176]{1,0:T(8,128)(2,1)}) %all-gather.3.cloned.1.call-update) | async-done | bytes 6684688 | tf_op jit(solution)/shard_map/all_gather | solution.py:770
  204.4 10.3 %expert_forward.4 = bf16[16,32,1536]{2,1,0:T(8,128)(2,1)} custom-call(bf16[16,32,1536]{2,1,0:T(8,128)(2,1)} %all-to-all-done.1.refs_0_.refs_1_, bf16[2,192,1536]{2,1,0:T(8,128)(2,1)} %bitcast.77, bf16[2,192,1536]{2,1,0:T(8,128)(2,1)} %copy-done.2, bf16[2,192,1536]{2,1,0:T(8,128)(2,1)} %collective-permute-done.refs_4_.refs_3_.refs_8_, ...), custom_call_target="tpu_custom_call" | custom-call | flops 3623878656 | bytes 17301504 | tf_op jit(solution)/shard_map/expert_forward/pallas_call | solution.py:124
  224.8 10.3 %expert_forward.5.refs_5_ = bf16[16,32,1536]{2,1,0:T(8,128)(2,1)} custom-call(bf16[16,32,1536]{2,1,0:T(8,128)(2,1)} %all-to-all-done.3.refs_0_.refs_1_, bf16[2,192,1536]{2,1,0:T(8,128)(2,1)} %bitcast.78, bf16[2,192,1536]{2,1,0:T(8,128)(2,1)} %copy-done.2, bf16[2,192,1536]{2,1,0:T(8,128)(2,1)} %collective-permute-done.refs_4_.refs_3_.refs_8_, ...), custom_call_target="tpu_custom_call" | custom-call | flops 3623878656 | bytes 17301504 | tf_op jit(solution)/shard_map/expert_forward/pallas_call | solution.py:124
  235.1 8.7 %all-to-all-done.2.refs_0_ = bf16[16,32,1536]{2,1,0:T(8,128)(2,1)} async-done(((bf16[16,32,1536]{2,1,0:T(8,128)(2,1)}), bf16[16,32,1536]{2,1,0:T(8,128)(2,1)}, u32[]{:S(2)}, u32[]{:S(2)}) %all-to-all-start.2) | async-done | bytes 1572896 | tf_op jit(solution)/shard_map/all_to_all | solution.py:737
  243.9 6.7 all-to-all-start.4
  281.0 6.8 attend.6
  287.8 7.0 all-to-all-start.5
  296.1 8.8 %collective-permute-done.21.refs_1_ = bf16[96,1536]{1,0:T(8,128)(2,1)} collective-permute-done((bf16[96,1536]{1,0:T(8,128)(2,1)S(1)}, bf16[96,1536]{1,0:T(8,128)(2,1)}, u32[]{:S(2)}, u32[]{:S(2)}) %collective-permute-start.21) | collective-permute-done | bytes 294944 | tf_op jit(solution)/shard_map/ppermute | solution.py:966
  320.2 6.8 attend.7
  327.0 6.9 all-to-all-start.7
  337.5 16.4 %expert_forward.6 = (bf16[16,32,1536]{2,1,0:T(8,128)(2,1)}, bf16[2,256,768]{2,1,0:T(8,128)(2,1)}, bf16[2,256,768]{2,1,0:T(8,128)(2,1)}, bf16[2,256,768]{2,1,0:T(8,128)(2,1)}, bf16[16,32,1664]{2,1,0:T(8,128)(2,1)}) custom-call(bf16[16,32,1664]{2,1,0:T(8,128)(2,1)} %all-to-all-done.5.refs_0_.refs_4_, bf16[16,32,1536]{2,1,0:T(8,128)(2,1)} %all-to-all-done.1.refs_0_.refs_1_, ...), custom_call_target="tpu_custom_call" | custom-call | flops 7247757312 | bytes 23068672 | tf_op jit(solution)/shard_map/expert_forward/pallas_call | solution.py:124
  365.3 16.4 %expert_forward.7 = (bf16[16,32,1536]{2,1,0:T(8,128)(2,1)}, bf16[2,256,768]{2,1,0:T(8,128)(2,1)}, bf16[2,256,768]{2,1,0:T(8,128)(2,1)}, bf16[2,256,768]{2,1,0:T(8,128)(2,1)}, bf16[16,32,1664]{2,1,0:T(8,128)(2,1)}) custom-call(bf16[16,32,1664]{2,1,0:T(8,128)(2,1)} %all-to-all-done.7.refs_0_.refs_5_, bf16[16,32,1536]{2,1,0:T(8,128)(2,1)} %all-to-all-done.3.refs_0_.refs_1_, ...), custom_call_target="tpu_custom_call" | custom-call | flops 7247757312 | bytes 23068672 | tf_op jit(solution)/shard_map/expert_forward/pallas_call | solution.py:124
  394.6 8.8 %attend_back.4 = (f32[96,1536]{1,0:T(8,128)}, bf16[96,1536]{1,0:T(8,128)(2,1)}, bf16[96,512]{1,0:T(8,128)(2,1)}, bf16[96,512]{1,0:T(8,128)(2,1)}, bf16[96,512]{1,0:T(8,128)(2,1)}, /*index=5*/bf16[96,512]{1,0:T(8,128)(2,1)}) custom-call(s32[1]{0:T(128)} %bitcast.1.refs_0_, s32[1]{0:T(128)} %bitcast.refs_0_.refs_1_, ...), custom_call_target="tpu_custom_call" | custom-call | flops 1056964608 | bytes 17520640 | tf_op jit(solution)/shard_map/attend_back/pallas_call | solution.py:124
  412.6 6.7 project_back.4.refs_22_
  421.4 8.8 %attend_back.5 = (f32[96,1536]{1,0:T(8,128)}, bf16[96,1536]{1,0:T(8,128)(2,1)}, bf16[96,512]{1,0:T(8,128)(2,1)}, bf16[96,512]{1,0:T(8,128)(2,1)}, bf16[96,512]{1,0:T(8,128)(2,1)}, /*index=5*/bf16[96,512]{1,0:T(8,128)(2,1)}) custom-call(s32[1]{0:T(128)} %bitcast.1.refs_0_, s32[1]{0:T(128)} %bitcast.refs_0_.refs_1_, ...), custom_call_target="tpu_custom_call" | custom-call | flops 1056964608 | bytes 17520640 | tf_op jit(solution)/shard_map/attend_back/pallas_call | solution.py:124
  449.5 6.8 project_back.5
  467.6 7.6 %all-to-all-start.11 = ((bf16[16,32,1536]{2,1,0:T(8,128)(2,1)}), bf16[16,32,1536]{2,1,0:T(8,128)(2,1)}, u32[]{:S(2)}, u32[]{:S(2)}) async-start(bf16[16,32,1536]{2,1,0:T(8,128)(2,1)} %get-tuple-element.177.refs_20_), calls=%async_computation.11 | async-start | bytes 3145728 | tf_op jit(solution)/shard_map/all_to_all | solution.py:737
  475.2 10.8 %expert_backward.2 = (bf16[16,32,1664]{2,1,0:T(8,128)(2,1)}, bf16[2,256,768]{2,1,0:T(8,128)(2,1)}, bf16[2,256,768]{2,1,0:T(8,128)(2,1)}) custom-call(s32[1]{0:T(128)} %bitcast.refs_0_.refs_1_, bf16[16,32,1536]{2,1,0:T(8,128)(2,1)} %all-to-all-done.9.refs_1_.refs_2_, bf16[2,256,768]{2,1,0:T(8,128)(2,1)} %get-tuple-element.168.refs_2_.refs_0_, ...), custom_call_target="tpu_custom_call" | custom-call | flops 3623878656 | bytes 22937600 | tf_op jit(solution)/shard_map/expert_backward/pallas_call | solution.py:124
  486.0 9.8 %all-to-all-done.11.refs_1_.refs_3_ = bf16[16,32,1536]{2,1,0:T(8,128)(2,1)} async-done(((bf16[16,32,1536]{2,1,0:T(8,128)(2,1)}), bf16[16,32,1536]{2,1,0:T(8,128)(2,1)}, u32[]{:S(2)}, u32[]{:S(2)}) %all-to-all-start.11) | async-done | bytes 1572896 | tf_op jit(solution)/shard_map/all_to_all | solution.py:737
  508.6 10.8 %expert_backward.3 = (bf16[16,32,1664]{2,1,0:T(8,128)(2,1)}, bf16[2,256,768]{2,1,0:T(8,128)(2,1)}, bf16[2,256,768]{2,1,0:T(8,128)(2,1)}) custom-call(s32[1]{0:T(128)} %bitcast.refs_0_.refs_1_, bf16[16,32,1536]{2,1,0:T(8,128)(2,1)} %all-to-all-done.11.refs_1_.refs_3_, bf16[2,256,768]{2,1,0:T(8,128)(2,1)} %get-tuple-element.179.refs_2_.refs_1_, ...), custom_call_target="tpu_custom_call" | custom-call | flops 3623878656 | bytes 22937600 | tf_op jit(solution)/shard_map/expert_backward/pallas_call | solution.py:124
  531.6 9.5 %attend_back.6 = (f32[96,1536]{1,0:T(8,128)}, bf16[96,1536]{1,0:T(8,128)(2,1)}, bf16[96,896]{1,0:T(8,128)(2,1)}, bf16[96,896]{1,0:T(8,128)(2,1)}, bf16[96,896]{1...) custom-call(s32[1]{0:T(128)} %bitcast.1.refs_0_, s32[1]{0:T(128)} %bitcast.refs_0_.refs_1_, ...), custom_call_target="tpu_custom_call" | custom-call | flops 1056964608 | bytes 19167232 | tf_op jit(solution)/shard_map/attend_back/pallas_call | solution.py:124
  541.0 9.1 %expert_weight_grads.4 = (bf16[2,192,1536]{2,1,0:T(8,128)(2,1)}, bf16[2,192,1536]{2,1,0:T(8,128)(2,1)}, bf16[2,192,1536]{2,1,0:T(8,128)(2,1)}, bf16[2,192,1536]{...) custom-call(bf16[2,256,768]{2,1,0:T(8,128)(2,1)} %get-tuple-element., ...), custom_call_target="tpu_custom_call" | custom-call | flops 2415919104 | bytes 15990784 | tf_op jit(solution)/shard_map/expert_weight_grads/pallas_call | solution.py:124
  555.9 9.4 %attend_back.7 = (f32[96,1536]{1,0:T(8,128)}, bf16[96,1536]{1,0:T(8,128)(2,1)}, bf16[96,896]{1,0:T(8,128)(2,1)}, bf16[96,896]{1,0:T(8,128)(2,1)}, bf16[96,896]{1...) custom-call(s32[1]{0:T(128)} %bitcast.1.refs_0_, s32[1]{0:T(128)} %bitcast.refs_0_.refs_1_, ...), custom_call_target="tpu_custom_call" | custom-call | flops 1056964608 | bytes 19167232 | tf_op jit(solution)/shard_map/attend_back/pallas_call | solution.py:124
  589.3 6.8 out_grads.1.refs_12_
  596.1 6.7 all-to-all-start.13
  604.4 7.3 %project_back.6 = (bf16[96,1536]{1,0:T(8,128)(2,1)}, f32[96,1536]{1,0:T(8,128)}, bf16[96,512]{1,0:T(8,128)(2,1)}, bf16[96,512]{1,0:T(8,128)(2,1)}, bf16[96,512]{1,0:T(8,128)(2,1)}, /*index=5*/bf16[96,512]{1,0:T(8,128)(2,1)}) custom-call(s32[1]{0:T(128)} %bitcast.1.refs_0_, bf16[96,896]{1,0:T(8,128)(2,1)} %get-tuple-element.199.refs_5_.refs_1_, ...), custom_call_target="tpu_custom_call" | custom-call | flops 603979776 | bytes 10229760 | tf_op jit(solution)/shard_map/project_back/pallas_call | solution.py:124
  611.7 7.3 %project_back.7 = (bf16[96,1536]{1,0:T(8,128)(2,1)}, f32[96,1536]{1,0:T(8,128)}, bf16[96,512]{1,0:T(8,128)(2,1)}, bf16[96,512]{1,0:T(8,128)(2,1)}, bf16[96,512]{1,0:T(8,128)(2,1)}, /*index=5*/bf16[96,512]{1,0:T(8,128)(2,1)}) custom-call(s32[1]{0:T(128)} %bitcast.1.refs_0_, bf16[96,896]{1,0:T(8,128)(2,1)} %get-tuple-element.187.refs_4_.refs_1_, ...), custom_call_target="tpu_custom_call" | custom-call | flops 603979776 | bytes 10229760 | tf_op jit(solution)/shard_map/project_back/pallas_call | solution.py:124
  627.6 6.7 collective-permute-done.48.refs_8_.refs_2_
  670.2 7.7 %all-to-all-done.14.refs_2_ = bf16[16,96,512]{2,1,0:T(8,128)(2,1)} async-done(((bf16[16,96,512]{2,1,0:T(8,128)(2,1)}), bf16[16,96,512]{2,1,0:T(8,128)(2,1)}, u32[]{:S(2)}, u32[]{:S(2)}) %all-to-all-start.14) | async-done | bytes 1572896 | tf_op jit(solution)/shard_map/all_to_all | solution.py:737
  (256 shorter events, 328.2 us)
Async XLA Ops:
  7.2 138.4 %all-gather.3.cloned.1.call-start = ((), (), s32[]{:S(2)}) async-start(), calls=%async_computation.15 | async-start | bytes 6789120 | tf_op jit(solution)/shard_map/all_gather | solution.py:770
  21.2 78.1 %all-to-all-start = ((bf16[16,96,1536]{2,1,0:T(8,128)(2,1)}), bf16[16,96,1536]{2,1,0:T(8,128)(2,1)}, u32[]{:S(2)}, u32[]{:S(2)}) async-start(bf16[16,96,1536]{2,1,0:T(8,128)(2,1)} %broadcast_in_dim.88), calls=%async_computation | async-start | bytes 9437184 | tf_op jit(solution)/shard_map/all_to_all | solution.py:737
  29.0 75.2 %collective-permute-start = (bf16[2,192,1536]{2,1,0:T(8,128)(2,1)S(1)}, bf16[2,192,1536]{2,1,0:T(8,128)(2,1)}, u32[]{:S(2)}, u32[]{:S(2)}) collective-permute-start(bf16[2,192,1536]{2,1,0:T(8,128)(2,1)S(1)} %bitcast.83), channel_id=1, source_target_pairs={{0,32},{16,48},{32,0},{48,16},{1,33},{17,49},{33,1},{49,17},{2,34}... | collective-permute-start | bytes 3538952 | tf_op jit(solution)/shard_map/ppermute | solution.py:163
  31.1 73.9 %collective-permute-start.1 = (bf16[2,192,1536]{2,1,0:T(8,128)(2,1)}, bf16[2,192,1536]{2,1,0:T(8,128)(2,1)}, u32[]{:S(2)}, u32[]{:S(2)}) collective-permute-start(bf16[2,192,1536]{2,1,0:T(8,128)(2,1)} %bitcast.9.refs_5_.refs_6_.refs_10_), channel_id=1, source_target_pairs={{0,32},{16,48},{32,0},{48,16},{1,33},{17,49},{33,1},{49,17},{2,34}... | collective-permute-start | bytes 3538952 | tf_op jit(solution)/shard_map/ppermute | solution.py:163
  34.2 70.0 %collective-permute-start.2 = (bf16[1,192,1536]{2,1,0:T(8,128)(2,1)S(1)}, bf16[1,192,1536]{2,1,0:T(8,128)(2,1)S(1)}, u32[]{:S(2)}, u32[]{:S(2)}) collective-permute-start(bf16[1,192,1536]{2,1,0:T(8,128)(2,1)S(1)} %get-tuple-element.283), channel_id=1, source_target_pairs={{0,32},{16,48},{32,0},{48,16},{1,33},{17,49},{33,1},{49,17},{2,34}... | collective-permute-start | bytes 1769480 | tf_op jit(solution)/shard_map/ppermute | solution.py:163
  167.0 28.3 %all-to-all-start.1 = ((bf16[16,32,1536]{2,1,0:T(8,128)(2,1)}), bf16[16,32,1536]{2,1,0:T(8,128)(2,1)}, u32[]{:S(2)}, u32[]{:S(2)}) async-start(bf16[16,32,1536]{2,1,0:T(8,128)(2,1)} %get-tuple-element.131), calls=%async_computation.1 | async-start | bytes 3145728 | tf_op jit(solution)/shard_map/all_to_all | solution.py:737
  172.3 27.6 %collective-permute-start.8 = (bf16[2,192,1536]{2,1,0:T(8,128)(2,1)}, bf16[2,192,1536]{2,1,0:T(8,128)(2,1)}, u32[]{:S(2)}, u32[]{:S(2)}) collective-permute-start(bf16[2,192,1536]{2,1,0:T(8,128)(2,1)} %bitcast.9.refs_5_.refs_6_.refs_10_), channel_id=1, source_target_pairs={{0,16},{16,0},{32,48},{48,32},{1,17},{17,1},{33,49},{49,33},{2,18}... | collective-permute-start | bytes 3538952 | tf_op jit(solution)/shard_map/ppermute | solution.py:163
  177.4 24.3 %collective-permute-start.10 = (bf16[2,192,1536]{2,1,0:T(8,128)(2,1)}, bf16[2,192,1536]{2,1,0:T(8,128)(2,1)}, u32[]{:S(2)}, u32[]{:S(2)}) collective-permute-start(bf16[2,192,1536]{2,1,0:T(8,128)(2,1)} %bitcast.22.refs_9_.refs_10_.refs_14_), channel_id=1, source_target_pairs={{0,16},{16,0},{32,48},{48,32},{1,17},{17,1},{33,49},{49,33},{2,18}... | collective-permute-start | bytes 3538952 | tf_op jit(solution)/shard_map/ppermute | solution.py:163
  178.7 25.4 %collective-permute-start.7 = (bf16[2,192,1536]{2,1,0:T(8,128)(2,1)}, bf16[2,192,1536]{2,1,0:T(8,128)(2,1)}, u32[]{:S(2)}, u32[]{:S(2)}) collective-permute-start(bf16[2,192,1536]{2,1,0:T(8,128)(2,1)} %collective-permute-done.refs_4_.refs_3_.refs_8_), channel_id=1, source_target_pairs={{0,16},{16,0},{32,48},{48,32},{1,17},{17,1},{33,49},{49,33},{2,18}... | collective-permute-start | bytes 3538952 | tf_op jit(solution)/shard_map/ppermute | solution.py:163
  195.3 25.2 %all-to-all-start.3 = ((bf16[16,32,1536]{2,1,0:T(8,128)(2,1)}), bf16[16,32,1536]{2,1,0:T(8,128)(2,1)}, u32[]{:S(2)}, u32[]{:S(2)}) async-start(bf16[16,32,1536]{2,1,0:T(8,128)(2,1)} %get-tuple-element.135.refs_15_), calls=%async_computation.3 | async-start | bytes 3145728 | tf_op jit(solution)/shard_map/all_to_all | solution.py:737
  220.4 23.4 %all-to-all-start.2 = ((bf16[16,32,1536]{2,1,0:T(8,128)(2,1)}), bf16[16,32,1536]{2,1,0:T(8,128)(2,1)}, u32[]{:S(2)}, u32[]{:S(2)}) async-start(bf16[16,32,1536]{2,1,0:T(8,128)(2,1)} %expert_forward.4), calls=%async_computation.2 | async-start | bytes 3145728 | tf_op jit(solution)/shard_map/all_to_all | solution.py:737
  243.9 31.9 %all-to-all-start.4 = ((bf16[16,32,1536]{2,1,0:T(8,128)(2,1)}), bf16[16,32,1536]{2,1,0:T(8,128)(2,1)}, u32[]{:S(2)}, u32[]{:S(2)}) async-start(bf16[16,32,1536]{2,1,0:T(8,128)(2,1)} %expert_forward.5.refs_5_), calls=%async_computation.4 | async-start | bytes 3145728 | tf_op jit(solution)/shard_map/all_to_all | solution.py:737
  287.8 39.2 %all-to-all-start.5 = ((bf16[16,32,1664]{2,1,0:T(8,128)(2,1)}), bf16[16,32,1664]{2,1,0:T(8,128)(2,1)}, u32[]{:S(2)}, u32[]{:S(2)}) async-start(bf16[16,32,1664]{2,1,0:T(8,128)(2,1)} %get-tuple-element.143), calls=%async_computation.5 | async-start | bytes 3407872 | tf_op jit(solution)/shard_map/all_to_all | solution.py:737
  327.0 31.8 %all-to-all-start.7 = ((bf16[16,32,1664]{2,1,0:T(8,128)(2,1)}), bf16[16,32,1664]{2,1,0:T(8,128)(2,1)}, u32[]{:S(2)}, u32[]{:S(2)}) async-start(bf16[16,32,1664]{2,1,0:T(8,128)(2,1)} %get-tuple-element.147.refs_16_), calls=%async_computation.7 | async-start | bytes 3407872 | tf_op jit(solution)/shard_map/all_to_all | solution.py:737
  336.3 28.9 %collective-permute-start.25 = (bf16[4,96,1536]{2,1,0:T(8,128)(2,1)}, bf16[4,96,1536]{2,1,0:T(8,128)(2,1)}, u32[]{:S(2)}, u32[]{:S(2)}) collective-permute-start(bf16[4,96,1536]{2,1,0:T(8,128)(2,1)} %pack.1.refs_0_), channel_id=1, source_target_pairs={{0,32},{16,48},{32,0},{48,16},{1,33},{17,49},{33,1},{49,17},{2,34}... | collective-permute-start | bytes 3538952 | tf_op jit(solution)/shard_map/ppermute | solution.py:163
  358.8 26.5 %all-to-all-start.6 = ((bf16[16,32,1664]{2,1,0:T(8,128)(2,1)}), bf16[16,32,1664]{2,1,0:T(8,128)(2,1)}, u32[]{:S(2)}, u32[]{:S(2)}) async-start(bf16[16,32,1664]{2,1,0:T(8,128)(2,1)} %get-tuple-element.148), calls=%async_computation.6 | async-start | bytes 3407872 | tf_op jit(solution)/shard_map/all_to_all | solution.py:737
  385.3 36.1 %all-to-all-start.8 = ((bf16[16,32,1664]{2,1,0:T(8,128)(2,1)}), bf16[16,32,1664]{2,1,0:T(8,128)(2,1)}, u32[]{:S(2)}, u32[]{:S(2)}) async-start(bf16[16,32,1664]{2,1,0:T(8,128)(2,1)} %get-tuple-element.156.refs_19_), calls=%async_computation.8 | async-start | bytes 3407872 | tf_op jit(solution)/shard_map/all_to_all | solution.py:737
  389.9 31.5 %collective-permute-start.30 = (bf16[4,96,1536]{2,1,0:T(8,128)(2,1)}, bf16[4,96,1536]{2,1,0:T(8,128)(2,1)}, u32[]{:S(2)}, u32[]{:S(2)}) collective-permute-start(bf16[4,96,1536]{2,1,0:T(8,128)(2,1)} %pack.1.refs_0_), channel_id=1, source_target_pairs={{0,16},{16,0},{32,48},{48,32},{1,17},{17,1},{33,49},{49,33},{2,18}... | collective-permute-start | bytes 3538952 | tf_op jit(solution)/shard_map/ppermute | solution.py:163
  394.1 27.2 %collective-permute-start.31 = (bf16[4,96,1536]{2,1,0:T(8,128)(2,1)}, bf16[4,96,1536]{2,1,0:T(8,128)(2,1)}, u32[]{:S(2)}, u32[]{:S(2)}) collective-permute-start(bf16[4,96,1536]{2,1,0:T(8,128)(2,1)} %collective-permute-done.25.refs_16_.refs_20_.refs_2_), channel_id=1, source_target_pairs={{0,16},{16,0},{32,48},{48,32},{1,17},{17,1},{33,49},{49,33},{2,18}... | collective-permute-start | bytes 3538952 | tf_op jit(solution)/shard_map/ppermute | solution.py:163
  433.6 34.0 %all-to-all-start.9 = ((bf16[16,32,1536]{2,1,0:T(8,128)(2,1)}), bf16[16,32,1536]{2,1,0:T(8,128)(2,1)}, u32[]{:S(2)}, u32[]{:S(2)}) async-start(bf16[16,32,1536]{2,1,0:T(8,128)(2,1)} %get-tuple-element.167), calls=%async_computation.9 | async-start | bytes 3145728 | tf_op jit(solution)/shard_map/all_to_all | solution.py:737
  467.6 28.2 %all-to-all-start.11 = ((bf16[16,32,1536]{2,1,0:T(8,128)(2,1)}), bf16[16,32,1536]{2,1,0:T(8,128)(2,1)}, u32[]{:S(2)}, u32[]{:S(2)}) async-start(bf16[16,32,1536]{2,1,0:T(8,128)(2,1)} %get-tuple-element.177.refs_20_), calls=%async_computation.11 | async-start | bytes 3145728 | tf_op jit(solution)/shard_map/all_to_all | solution.py:737
  495.8 26.0 %all-to-all-start.10 = ((bf16[16,32,1664]{2,1,0:T(8,128)(2,1)}), bf16[16,32,1664]{2,1,0:T(8,128)(2,1)}, u32[]{:S(2)}, u32[]{:S(2)}) async-start(bf16[16,32,1664]{2,1,0:T(8,128)(2,1)} %get-tuple-element.178), calls=%async_computation.10 | async-start | bytes 3407872 | tf_op jit(solution)/shard_map/all_to_all | solution.py:737
  521.7 33.7 %all-to-all-start.12 = ((bf16[16,32,1664]{2,1,0:T(8,128)(2,1)}), bf16[16,32,1664]{2,1,0:T(8,128)(2,1)}, u32[]{:S(2)}, u32[]{:S(2)}) async-start(bf16[16,32,1664]{2,1,0:T(8,128)(2,1)} %get-tuple-element.183.refs_19_), calls=%async_computation.12 | async-start | bytes 3407872 | tf_op jit(solution)/shard_map/all_to_all | solution.py:737
  530.2 25.6 %collective-permute-start.40 = (bf16[2,192,1536]{2,1,0:T(8,128)(2,1)}, bf16[2,192,1536]{2,1,0:T(8,128)(2,1)}, u32[]{:S(2)}, u32[]{:S(2)}) collective-permute-start(bf16[2,192,1536]{2,1,0:T(8,128)(2,1)} %add.133.refs_20_), channel_id=1, source_target_pairs={{0,32},{16,48},{32,0},{48,16},{1,33},{17,49},{33,1},{49,17},{2,34}... | collective-permute-start | bytes 3538952 | tf_op jit(solution)/shard_map/ppermute | solution.py:163
  550.1 23.7 %collective-permute-start.44 = (bf16[2,192,1536]{2,1,0:T(8,128)(2,1)}, bf16[2,192,1536]{2,1,0:T(8,128)(2,1)}, u32[]{:S(2)}, u32[]{:S(2)}) collective-permute-start(bf16[2,192,1536]{2,1,0:T(8,128)(2,1)} %get-tuple-element.212), channel_id=1, source_target_pairs={{0,16},{16,0},{32,48},{48,32},{1,17},{17,1},{33,49},{49,33},{2,18}... | collective-permute-start | bytes 3538952 | tf_op jit(solution)/shard_map/ppermute | solution.py:163
  596.1 53.3 %all-to-all-start.13 = ((bf16[16,96,512]{2,1,0:T(8,128)(2,1)}), bf16[16,96,512]{2,1,0:T(8,128)(2,1)}, u32[]{:S(2)}, u32[]{:S(2)}) async-start(bf16[16,96,512]{2,1,0:T(8,128)(2,1)} %out_grads.1.refs_12_), calls=%async_computation.13 | async-start | bytes 3145728 | tf_op jit(solution)/shard_map/all_to_all | solution.py:737
  602.7 41.0 %collective-permute-start.52 = (bf16[2,192,1536]{2,1,0:T(8,128)(2,1)}, bf16[2,192,1536]{2,1,0:T(8,128)(2,1)}, u32[]{:S(2)}, u32[]{:S(2)}) collective-permute-start(bf16[2,192,1536]{2,1,0:T(8,128)(2,1)} %hold.4.refs_19_), channel_id=1, source_target_pairs={{0,32},{16,48},{32,0},{48,16},{1,33},{17,49},{33,1},{49,17},{2,34}... | collective-permute-start | bytes 3538952 | tf_op jit(solution)/shard_map/ppermute | solution.py:163
  603.9 59.0 %collective-permute-start.56 = (bf16[2,192,1536]{2,1,0:T(8,128)(2,1)}, bf16[2,192,1536]{2,1,0:T(8,128)(2,1)}, u32[]{:S(2)}, u32[]{:S(2)}) collective-permute-start(bf16[2,192,1536]{2,1,0:T(8,128)(2,1)} %get-tuple-element.239), channel_id=1, source_target_pairs={{0,16},{16,0},{32,48},{48,32},{1,17},{17,1},{33,49},{49,33},{2,18}... | collective-permute-start | bytes 3538952 | tf_op jit(solution)/shard_map/ppermute | solution.py:163
  626.9 39.9 %collective-permute-start.59 = (bf16[2,192,1536]{2,1,0:T(8,128)(2,1)}, bf16[2,192,1536]{2,1,0:T(8,128)(2,1)}, u32[]{:S(2)}, u32[]{:S(2)}) collective-permute-start(bf16[2,192,1536]{2,1,0:T(8,128)(2,1)} %get-tuple-element.243), channel_id=1, source_target_pairs={{0,16},{16,0},{32,48},{48,32},{1,17},{17,1},{33,49},{49,33},{2,18}... | collective-permute-start | bytes 3538952 | tf_op jit(solution)/shard_map/ppermute | solution.py:163
  640.9 46.4 %collective-permute-start.57 = (bf16[2,192,1536]{2,1,0:T(8,128)(2,1)}, bf16[2,192,1536]{2,1,0:T(8,128)(2,1)}, u32[]{:S(2)}, u32[]{:S(2)}) collective-permute-start(bf16[2,192,1536]{2,1,0:T(8,128)(2,1)} %get-tuple-element.241), channel_id=1, source_target_pairs={{0,16},{16,0},{32,48},{48,32},{1,17},{17,1},{33,49},{49,33},{2,18}... | collective-permute-start | bytes 3538952 | tf_op jit(solution)/shard_map/ppermute | solution.py:163
  649.3 28.6 %all-to-all-start.14 = ((bf16[16,96,512]{2,1,0:T(8,128)(2,1)}), bf16[16,96,512]{2,1,0:T(8,128)(2,1)}, u32[]{:S(2)}, u32[]{:S(2)}) async-start(bf16[16,96,512]{2,1,0:T(8,128)(2,1)} %qkv_grads.1.refs_12_), calls=%async_computation.14 | async-start | bytes 3145728 | tf_op jit(solution)/shard_map/all_to_all | solution.py:737
  656.9 30.4 %collective-permute-start.58 = (bf16[2,192,1536]{2,1,0:T(8,128)(2,1)}, bf16[2,192,1536]{2,1,0:T(8,128)(2,1)}, u32[]{:S(2)}, u32[]{:S(2)}) collective-permute-start(bf16[2,192,1536]{2,1,0:T(8,128)(2,1)} %hold.5), channel_id=1, source_target_pairs={{0,32},{16,48},{32,0},{48,16},{1,33},{17,49},{33,1},{49,17},{2,34}... | collective-permute-start | bytes 3538952 | tf_op jit(solution)/shard_map/ppermute | solution.py:163
  (67 other events, 574.6 us)
Sparse Core Ops, SparseCore 0:
  11.7 133.7 all-gather.2

commit v13 on v10

--- a/solution.py
+++ b/solution.py
@@ -775,11 +775,14 @@
         return own, swapped(own, 1), two, swapped(two, 1)
 
     gate_shards, up_shards = shards_of(w_gate[0]), shards_of(w_up[0])
-    down_twos = [swapped(w_down[0, j : j + 1], 2) for j in range(per_column)]
-    shards = (
-        *gate_shards, *up_shards, w_down[0], swapped(w_down[0], 1), *down_twos,
-        *[swapped(two, 1) for two in down_twos],
-    )
+    down_one, down_first = swapped(w_down[0], 1), swapped(w_down[0, :1], 2)
+
+    def all_shards(waits):
+        twos = [down_first]
+        twos += [swapped(hold(w_down[0, j : j + 1], *waits), 2) for j in range(1, per_column)]
+        threes = [swapped(two, 1) for two in twos]
+        return (*gate_shards, *up_shards, w_down[0], down_one, *twos, *threes)
+
 
     lane = jnp.arange(LANES, dtype=jnp.int32)
     half = HEAD_DIM // 2
@@ -840,7 +843,7 @@
     tables = late([cosine, sine])
     first_flag = (1 - second)
 
-    def forward(keep, came, waits, early, after):
+    def forward(keep, came, waits, early, after, shards):
         projected, pairs = [], []
         if keep:
             for m in pieces:
@@ -864,6 +867,7 @@
             for m in pieces:
                 pair = made[3 * m + 2]
                 pairs.append([pair] + [swapped(pair, s) for s in steps[1:]])
+        shards = shards or all_shards(pairs[1][1:])
         attended = [
             call(
                 functools.partial(attend, keep),
@@ -897,7 +901,7 @@
             )
             for m in pieces
         ]
-        return projected, pairs, attended, arrived, applied, lefts
+        return projected, pairs, attended, arrived, applied, lefts, shards
 
     def weight_call(quarters, which, lefts, rights, waits):
         quarter, some = hidden_width // 4, len(quarters)
@@ -943,8 +947,8 @@
             (here,), waits,
         )
 
-    kept = forward(False, None, (gate_shards[2], up_shards[2], down_twos[0]), None, ())
-    attended, early, applied = kept[2:5]
+    kept = forward(False, None, (gate_shards[2], up_shards[2], down_first), None, (), ())
+    attended, early, applied, unused, shards = kept[2:]
     returned = [over_columns(a[0]) for a in applied]
     results = [
         call(
@@ -956,7 +960,8 @@
     ]
     came = [lax.ppermute(r[0], "section", [(0, 1)]) for r in results]
 
-    projected, pairs, attended, arrived, applied, lefts = forward(True, came, (), early, results[1])
+    kept = forward(True, came, (), early, results[1], shards)
+    projected, pairs, attended, arrived, applied, lefts, unused = kept
     hidden = [a[1] for a in applied]
     shared = [over_columns(a[4]) for a in applied]
     inner, outer = [], []
@@ -987,11 +992,11 @@
     gate_up = [a[1] for a in moved] + [a[2] for a in moved]
     down_far = merged([weight_call((2, 3), ((0, 0),), hidden, arrived_grads, ())], ())[0]
     crossed = [swapped(down_far, 2)]
-    back = [over_columns(moved[0][0]), over_columns(hold(moved[1][0], down_far))]
+    back = [over_columns(moved[0][0]), over_columns(moved[1][0])]
     inner = [attention_back(True, 0, given[0][:1], back[0], (moved[1][0], down_far))]
     parts = [parts_of(inner[0])]
     both = weight_call((0, 1, 2, 3), ((0, 0), (0, 0)), gate_up, arrived, (inner[0][0],))
-    inner.append(attention_back(True, 1, given[1][:1], back[1], (both[0], crossed[0], *parts[0][1:])))
+    inner.append(attention_back(True, 1, given[1][:1], back[1], (both[0], crossed[0])))
     parts.append(parts_of(inner[1]))
     sums = merged([both[2:4], both[6:]], (inner[1][0],))
     gate_far = hold(sums[0], *parts[1][1:])

time: 699 us -> 688 us (0.984)
  waiting for transfers between devices: 221 us -> 206 us
    ppermute x56, waiting for transfers between devices: 131 us -> 116 us  [swapped(): return lax.ppermute(value, 'row', [(r, r ^ step) for r in range(rows)])]
  transfers between devices with their start and end apart: 75 -> 75, of which waited for: 32 -> 36; matrix products, arithmetic and copies ran while one was open for 4% -> 4% of each run, Pallas kernels for 31% -> 32%
where the time goes in v13:
time: 688 us; the launch traced here: 675 us
  Pallas kernels  245 us (36%)
  waiting for transfers between devices  206 us (30%)
  starting transfers between devices  177 us (26%)
  other arithmetic  20.2 us (3%)
  between operations  15.1 us (2%)
  local copies, waits for them, and re-layouts  11.1 us (2%)
    pallas_call x36, Pallas kernels, call(): pl.pallas_call(run, out_shape=tuple(shapes), in_specs=[pl.BlockSpec(memor...  245 us
    ppermute x56, waiting for transfers between devices, swapped(): return lax.ppermute(value, 'row', [(r, r ^ step) for r in range(rows)])  116 us
    ppermute x56, starting transfers between devices, swapped(): return lax.ppermute(value, 'row', [(r, r ^ step) for r in range(rows)])  86.3 us
    all_to_all x14, starting transfers between devices, over_columns(): return lax.all_to_all(value, 'col', split_axis=0, concat_axis=0, tiled=True)  82.9 us
    all_to_all x14, waiting for transfers between devices, over_columns(): return lax.all_to_all(value, 'col', split_axis=0, concat_axis=0, tiled=True)  41 us
    all_gather x1, waiting for transfers between devices, on_device(): dense = lax.all_gather(dense, ('row', 'col'), axis=0, tiled=True)  29.4 us
  transfers between devices with their start and end apart: 75, of which 36 were waited for; matrix products, arithmetic and copies ran while one was open for 4% of the time, Pallas kernels for 32%

profile of v13, /device:TPU:9, one launch (start us, length us, event | category | flops | bytes accessed | tf_op | source)
XLA Modules:
  0.0 675.2 jit_solution(1576115970194985514)
XLA Ops:
  23.9 64.4 %collective-permute-done.2.refs_6_.refs_11_.refs_12_.refs_16_ = bf16[1,192,1536]{2,1,0:T(8,128)(2,1)} collective-permute-done((bf16[1,192,1536]{2,1,0:T(8,128)(2,1)S(1)}, bf16[1,192,1536]{2,1,0:T(8,128)(2,1)}, u32[]{:S(2)}, u32[]{:S(2)}) %collective-permute-start.2) | collective-permute-done | bytes 589856 | tf_op jit(solution)/shard_map/ppermute | solution.py:163
  88.4 29.4 %all-gather.2.cloned.1.call-done.refs_3_.refs_12_.refs_6_.refs_17_.refs_11_ = bf16[1536,3712]{1,0:T(8,128)(2,1)} async-done(((bf16[24,3712]{1,0:T(8,128)(2,1)}), bf16[1536,3712]{1,0:T(8,128)(2,1)}) %all-gather.2.cloned.1.call-update) | async-done | bytes 11403280 | tf_op jit(solution)/shard_map/all_gather | solution.py:768
  133.0 6.5 attend.4
  177.1 10.3 %expert_forward.4 = bf16[16,32,1536]{2,1,0:T(8,128)(2,1)} custom-call(bf16[16,32,1536]{2,1,0:T(8,128)(2,1)} %all-to-all-done.refs_0_.refs_1_, bf16[2,192,1536]{2,1,0:T(8,128)(2,1)} %bitcast.65, bf16[2,192,1536]{2,1,0:T(8,128)(2,1)} %copy-done.1, bf16[2,192,1536]{2,1,0:T(8,128)(2,1)} %collective-permute-done.refs_4_.refs_3_.refs_8_, ...), custom_call_target="tpu_custom_call" | custom-call | flops 3623878656 | bytes 17301504 | tf_op jit(solution)/shard_map/expert_forward/pallas_call | solution.py:124
  195.8 10.3 %expert_forward.5.refs_5_ = bf16[16,32,1536]{2,1,0:T(8,128)(2,1)} custom-call(bf16[16,32,1536]{2,1,0:T(8,128)(2,1)} %all-to-all-done.2.refs_0_.refs_1_, bf16[2,192,1536]{2,1,0:T(8,128)(2,1)} %bitcast.66, bf16[2,192,1536]{2,1,0:T(8,128)(2,1)} %copy-done.1, bf16[2,192,1536]{2,1,0:T(8,128)(2,1)} %collective-permute-done.refs_4_.refs_3_.refs_8_, ...), custom_call_target="tpu_custom_call" | custom-call | flops 3623878656 | bytes 17301504 | tf_op jit(solution)/shard_map/expert_forward/pallas_call | solution.py:124
  206.1 8.8 %all-to-all-done.1.refs_0_ = bf16[16,32,1536]{2,1,0:T(8,128)(2,1)} async-done(((bf16[16,32,1536]{2,1,0:T(8,128)(2,1)}), bf16[16,32,1536]{2,1,0:T(8,128)(2,1)}, u32[]{:S(2)}, u32[]{:S(2)}) %all-to-all-start.1) | async-done | bytes 1572896 | tf_op jit(solution)/shard_map/all_to_all | solution.py:735
  214.9 6.9 %all-to-all-start.3 = ((bf16[16,32,1536]{2,1,0:T(8,128)(2,1)}), bf16[16,32,1536]{2,1,0:T(8,128)(2,1)}, u32[]{:S(2)}, u32[]{:S(2)}) async-start(bf16[16,32,1536]{2,1,0:T(8,128)(2,1)} %expert_forward.5.refs_5_), calls=%async_computation.3 | async-start | bytes 3145728 | tf_op jit(solution)/shard_map/all_to_all | solution.py:735
  253.3 6.9 %attend.6 = (f32[96,1536]{1,0:T(8,128)}, f32[96,128]{1,0:T(8,128)}, bf16[16,32,1664]{2,1,0:T(8,128)(2,1)}, bf16[2,576,384]{2,1,0:T(8,128)(2,1)}, bf16[96,1536]{1,0:T(8,128)(2,1)}, /*index=5*/bf16[96,1536]{1,0:T(8,128)(2,1)}) custom-call(s32[1]{0:T(128)} %bitcast.refs_0_.refs_1_, f32[96,1536]{1,0:T(8,128)} %get-tuple-element.138.refs_1_.refs_7_.refs_6_, ...), custom_call_target="tpu_custom_call" | custom-call | flops 830472192 | bytes 17389568 | tf_op jit(solution)/shard_map/attend/pallas_call | solution.py:124
  260.2 7.0 %all-to-all-start.4 = ((bf16[16,32,1664]{2,1,0:T(8,128)(2,1)}), bf16[16,32,1664]{2,1,0:T(8,128)(2,1)}, u32[]{:S(2)}, u32[]{:S(2)}) async-start(bf16[16,32,1664]{2,1,0:T(8,128)(2,1)} %get-tuple-element.143), calls=%async_computation.4 | async-start | bytes 3407872 | tf_op jit(solution)/shard_map/all_to_all | solution.py:735
  268.5 8.6 %collective-permute-done.21.refs_1_ = bf16[96,1536]{1,0:T(8,128)(2,1)} collective-permute-done((bf16[96,1536]{1,0:T(8,128)(2,1)S(1)}, bf16[96,1536]{1,0:T(8,128)(2,1)}, u32[]{:S(2)}, u32[]{:S(2)}) %collective-permute-start.21) | collective-permute-done | bytes 294944 | tf_op jit(solution)/shard_map/ppermute | solution.py:961
  292.6 6.8 %attend.7 = (f32[96,1536]{1,0:T(8,128)}, f32[96,128]{1,0:T(8,128)}, bf16[16,32,1664]{2,1,0:T(8,128)(2,1)}, bf16[2,576,384]{2,1,0:T(8,128)(2,1)}, bf16[96,1536]{1,0:T(8,128)(2,1)}, /*index=5*/bf16[96,1536]{1,0:T(8,128)(2,1)}) custom-call(s32[1]{0:T(128)} %bitcast.refs_0_.refs_1_, f32[96,1536]{1,0:T(8,128)} %get-tuple-element.144.refs_1_.refs_6_, ...), custom_call_target="tpu_custom_call" | custom-call | flops 830472192 | bytes 17389568 | tf_op jit(solution)/shard_map/attend/pallas_call | solution.py:124
  299.4 6.7 all-to-all-start.6
  310.6 16.4 %expert_forward.6 = (bf16[16,32,1536]{2,1,0:T(8,128)(2,1)}, bf16[2,256,768]{2,1,0:T(8,128)(2,1)}, bf16[2,256,768]{2,1,0:T(8,128)(2,1)}, bf16[2,256,768]{2,1,0:T(8,128)(2,1)}, bf16[16,32,1664]{2,1,0:T(8,128)(2,1)}) custom-call(bf16[16,32,1664]{2,1,0:T(8,128)(2,1)} %all-to-all-done.4.refs_0_.refs_4_, bf16[16,32,1536]{2,1,0:T(8,128)(2,1)} %all-to-all-done.refs_0_.refs_1_, ...), custom_call_target="tpu_custom_call" | custom-call | flops 7247757312 | bytes 23068672 | tf_op jit(solution)/shard_map/expert_forward/pallas_call | solution.py:124
  337.5 16.4 %expert_forward.7 = (bf16[16,32,1536]{2,1,0:T(8,128)(2,1)}, bf16[2,256,768]{2,1,0:T(8,128)(2,1)}, bf16[2,256,768]{2,1,0:T(8,128)(2,1)}, bf16[2,256,768]{2,1,0:T(8,128)(2,1)}, bf16[16,32,1664]{2,1,0:T(8,128)(2,1)}) custom-call(bf16[16,32,1664]{2,1,0:T(8,128)(2,1)} %all-to-all-done.6.refs_0_.refs_5_, bf16[16,32,1536]{2,1,0:T(8,128)(2,1)} %all-to-all-done.2.refs_0_.refs_1_, ...), custom_call_target="tpu_custom_call" | custom-call | flops 7247757312 | bytes 23068672 | tf_op jit(solution)/shard_map/expert_forward/pallas_call | solution.py:124
  365.9 8.7 %attend_back.4 = (f32[96,1536]{1,0:T(8,128)}, bf16[96,1536]{1,0:T(8,128)(2,1)}, bf16[96,512]{1,0:T(8,128)(2,1)}, bf16[96,512]{1,0:T(8,128)(2,1)}, bf16[96,512]{1,0:T(8,128)(2,1)}, /*index=5*/bf16[96,512]{1,0:T(8,128)(2,1)}) custom-call(s32[1]{0:T(128)} %bitcast.1.refs_0_, s32[1]{0:T(128)} %bitcast.refs_0_.refs_1_, ...), custom_call_target="tpu_custom_call" | custom-call | flops 1056964608 | bytes 17520640 | tf_op jit(solution)/shard_map/attend_back/pallas_call | solution.py:124
  384.9 6.7 project_back.4.refs_21_
  394.1 8.8 %attend_back.5 = (f32[96,1536]{1,0:T(8,128)}, bf16[96,1536]{1,0:T(8,128)(2,1)}, bf16[96,512]{1,0:T(8,128)(2,1)}, bf16[96,512]{1,0:T(8,128)(2,1)}, bf16[96,512]{1,0:T(8,128)(2,1)}, /*index=5*/bf16[96,512]{1,0:T(8,128)(2,1)}) custom-call(s32[1]{0:T(128)} %bitcast.1.refs_0_, s32[1]{0:T(128)} %bitcast.refs_0_.refs_1_, ...), custom_call_target="tpu_custom_call" | custom-call | flops 1056964608 | bytes 17520640 | tf_op jit(solution)/shard_map/attend_back/pallas_call | solution.py:124
  406.3 6.6 all-to-all-start.8
  422.5 6.7 project_back.5
  440.6 7.6 %all-to-all-start.10 = ((bf16[16,32,1536]{2,1,0:T(8,128)(2,1)}), bf16[16,32,1536]{2,1,0:T(8,128)(2,1)}, u32[]{:S(2)}, u32[]{:S(2)}) async-start(bf16[16,32,1536]{2,1,0:T(8,128)(2,1)} %get-tuple-element.177.refs_20_), calls=%async_computation.10 | async-start | bytes 3145728 | tf_op jit(solution)/shard_map/all_to_all | solution.py:735
  448.1 10.9 %expert_backward.2 = (bf16[16,32,1664]{2,1,0:T(8,128)(2,1)}, bf16[2,256,768]{2,1,0:T(8,128)(2,1)}, bf16[2,256,768]{2,1,0:T(8,128)(2,1)}) custom-call(s32[1]{0:T(128)} %bitcast.refs_0_.refs_1_, bf16[16,32,1536]{2,1,0:T(8,128)(2,1)} %all-to-all-done.8.refs_1_.refs_2_, bf16[2,256,768]{2,1,0:T(8,128)(2,1)} %get-tuple-element.168.refs_2_.refs_0_, ...), custom_call_target="tpu_custom_call" | custom-call | flops 3623878656 | bytes 22937600 | tf_op jit(solution)/shard_map/expert_backward/pallas_call | solution.py:124
  459.0 9.7 %all-to-all-done.10.refs_1_.refs_3_ = bf16[16,32,1536]{2,1,0:T(8,128)(2,1)} async-done(((bf16[16,32,1536]{2,1,0:T(8,128)(2,1)}), bf16[16,32,1536]{2,1,0:T(8,128)(2,1)}, u32[]{:S(2)}, u32[]{:S(2)}) %all-to-all-start.10) | async-done | bytes 1572896 | tf_op jit(solution)/shard_map/all_to_all | solution.py:735
  481.6 10.9 %expert_backward.3 = (bf16[16,32,1664]{2,1,0:T(8,128)(2,1)}, bf16[2,256,768]{2,1,0:T(8,128)(2,1)}, bf16[2,256,768]{2,1,0:T(8,128)(2,1)}) custom-call(s32[1]{0:T(128)} %bitcast.refs_0_.refs_1_, bf16[16,32,1536]{2,1,0:T(8,128)(2,1)} %all-to-all-done.10.refs_1_.refs_3_, bf16[2,256,768]{2,1,0:T(8,128)(2,1)} %get-tuple-element.179.refs_2_.refs_1_, ...), custom_call_target="tpu_custom_call" | custom-call | flops 3623878656 | bytes 22937600 | tf_op jit(solution)/shard_map/expert_backward/pallas_call | solution.py:124
  504.7 9.4 %attend_back.6 = (f32[96,1536]{1,0:T(8,128)}, bf16[96,1536]{1,0:T(8,128)(2,1)}, bf16[96,896]{1,0:T(8,128)(2,1)}, bf16[96,896]{1,0:T(8,128)(2,1)}, bf16[96,896]{1...) custom-call(s32[1]{0:T(128)} %bitcast.1.refs_0_, s32[1]{0:T(128)} %bitcast.refs_0_.refs_1_, ...), custom_call_target="tpu_custom_call" | custom-call | flops 1056964608 | bytes 19167232 | tf_op jit(solution)/shard_map/attend_back/pallas_call | solution.py:124
  514.1 9.1 %expert_weight_grads.4 = (bf16[2,192,1536]{2,1,0:T(8,128)(2,1)}, bf16[2,192,1536]{2,1,0:T(8,128)(2,1)}, bf16[2,192,1536]{2,1,0:T(8,128)(2,1)}, bf16[2,192,1536]{...) custom-call(bf16[2,256,768]{2,1,0:T(8,128)(2,1)} %get-tuple-element., ...), custom_call_target="tpu_custom_call" | custom-call | flops 2415919104 | bytes 15990784 | tf_op jit(solution)/shard_map/expert_weight_grads/pallas_call | solution.py:124
  528.9 9.4 %attend_back.7 = (f32[96,1536]{1,0:T(8,128)}, bf16[96,1536]{1,0:T(8,128)(2,1)}, bf16[96,896]{1,0:T(8,128)(2,1)}, bf16[96,896]{1,0:T(8,128)(2,1)}, bf16[96,896]{1...) custom-call(s32[1]{0:T(128)} %bitcast.1.refs_0_, s32[1]{0:T(128)} %bitcast.refs_0_.refs_1_, ...), custom_call_target="tpu_custom_call" | custom-call | flops 1056964608 | bytes 19167232 | tf_op jit(solution)/shard_map/attend_back/pallas_call | solution.py:124
  562.3 6.8 %out_grads.1.refs_12_ = bf16[16,96,512]{2,1,0:T(8,128)(2,1)} custom-call(bf16[4,96,1536]{2,1,0:T(8,128)(2,1)} %pack.1.refs_0_, bf16[4,96,1536]{2,1,0:T(8,128)(2,1)} %collective-permute-done.30.refs_18_.refs_1_, bf16[4,96,1536]{2,1,0:T(8,128)(2,1)} %collective-permute-done.25.refs_16_.refs_19_.refs_2_, ...), custom_call_target="tpu_custom_call" | custom-call | flops 905969664 | bytes 8404992 | tf_op jit(solution)/shard_map/out_grads/pallas_call | solution.py:124
  569.1 6.7 all-to-all-start.12
  577.6 7.3 %project_back.6 = (bf16[96,1536]{1,0:T(8,128)(2,1)}, f32[96,1536]{1,0:T(8,128)}, bf16[96,512]{1,0:T(8,128)(2,1)}, bf16[96,512]{1,0:T(8,128)(2,1)}, bf16[96,512]{1,0:T(8,128)(2,1)}, /*index=5*/bf16[96,512]{1,0:T(8,128)(2,1)}) custom-call(s32[1]{0:T(128)} %bitcast.1.refs_0_, bf16[96,896]{1,0:T(8,128)(2,1)} %get-tuple-element.199.refs_5_.refs_1_, ...), custom_call_target="tpu_custom_call" | custom-call | flops 603979776 | bytes 14948352 | tf_op jit(solution)/shard_map/project_back/pallas_call | solution.py:124
  584.9 7.3 %project_back.7 = (bf16[96,1536]{1,0:T(8,128)(2,1)}, f32[96,1536]{1,0:T(8,128)}, bf16[96,512]{1,0:T(8,128)(2,1)}, bf16[96,512]{1,0:T(8,128)(2,1)}, bf16[96,512]{1,0:T(8,128)(2,1)}, /*index=5*/bf16[96,512]{1,0:T(8,128)(2,1)}) custom-call(s32[1]{0:T(128)} %bitcast.1.refs_0_, bf16[96,896]{1,0:T(8,128)(2,1)} %get-tuple-element.187.refs_4_.refs_1_, ...), custom_call_target="tpu_custom_call" | custom-call | flops 603979776 | bytes 14948352 | tf_op jit(solution)/shard_map/project_back/pallas_call | solution.py:124
  622.2 6.6 all-to-all-start.13
  643.3 8.4 %all-to-all-done.13.refs_2_ = bf16[16,96,512]{2,1,0:T(8,128)(2,1)} async-done(((bf16[16,96,512]{2,1,0:T(8,128)(2,1)}), bf16[16,96,512]{2,1,0:T(8,128)(2,1)}, u32[]{:S(2)}, u32[]{:S(2)}) %all-to-all-start.13) | async-done | bytes 1572896 | tf_op jit(solution)/shard_map/all_to_all | solution.py:735
  (243 shorter events, 307.1 us)
Async XLA Ops:
  7.2 110.6 %all-gather.2.cloned.1.call-start = ((), (), s32[]{:S(2)}) async-start(), calls=%async_computation.14 | async-start | bytes 11581440 | tf_op jit(solution)/shard_map/all_gather | solution.py:768
  10.5 77.9 %collective-permute-start = (bf16[2,192,1536]{2,1,0:T(8,128)(2,1)}, bf16[2,192,1536]{2,1,0:T(8,128)(2,1)}, u32[]{:S(2)}, u32[]{:S(2)}) collective-permute-start(bf16[2,192,1536]{2,1,0:T(8,128)(2,1)} %bitcast.64), channel_id=1, source_target_pairs={{0,32},{16,48},{32,0},{48,16},{1,33},{17,49},{33,1},{49,17},{2,34}... | collective-permute-start | bytes 3538952 | tf_op jit(solution)/shard_map/ppermute | solution.py:163
  12.6 75.8 %collective-permute-start.1 = (bf16[2,192,1536]{2,1,0:T(8,128)(2,1)}, bf16[2,192,1536]{2,1,0:T(8,128)(2,1)}, u32[]{:S(2)}, u32[]{:S(2)}) collective-permute-start(bf16[2,192,1536]{2,1,0:T(8,128)(2,1)} %bitcast.10.refs_5_.refs_6_.refs_10_), channel_id=1, source_target_pairs={{0,32},{16,48},{32,0},{48,16},{1,33},{17,49},{33,1},{49,17},{2,34}... | collective-permute-start | bytes 3538952 | tf_op jit(solution)/shard_map/ppermute | solution.py:163
  15.7 72.7 %collective-permute-start.2 = (bf16[1,192,1536]{2,1,0:T(8,128)(2,1)S(1)}, bf16[1,192,1536]{2,1,0:T(8,128)(2,1)}, u32[]{:S(2)}, u32[]{:S(2)}) collective-permute-start(bf16[1,192,1536]{2,1,0:T(8,128)(2,1)S(1)} %get-tuple-element.283), channel_id=1, source_target_pairs={{0,32},{16,48},{32,0},{48,16},{1,33},{17,49},{33,1},{49,17},{2,34}... | collective-permute-start | bytes 1769480 | tf_op jit(solution)/shard_map/ppermute | solution.py:163
  139.6 27.2 %all-to-all-start = ((bf16[16,32,1536]{2,1,0:T(8,128)(2,1)}), bf16[16,32,1536]{2,1,0:T(8,128)(2,1)}, u32[]{:S(2)}, u32[]{:S(2)}) async-start(bf16[16,32,1536]{2,1,0:T(8,128)(2,1)} %get-tuple-element.131), calls=%async_computation | async-start | bytes 3145728 | tf_op jit(solution)/shard_map/all_to_all | solution.py:735
  145.5 25.7 %collective-permute-start.8 = (bf16[2,192,1536]{2,1,0:T(8,128)(2,1)}, bf16[2,192,1536]{2,1,0:T(8,128)(2,1)}, u32[]{:S(2)}, u32[]{:S(2)}) collective-permute-start(bf16[2,192,1536]{2,1,0:T(8,128)(2,1)} %bitcast.10.refs_5_.refs_6_.refs_10_), channel_id=1, source_target_pairs={{0,16},{16,0},{32,48},{48,32},{1,17},{17,1},{33,49},{49,33},{2,18}... | collective-permute-start | bytes 3538952 | tf_op jit(solution)/shard_map/ppermute | solution.py:163
  150.7 23.7 %collective-permute-start.10 = (bf16[2,192,1536]{2,1,0:T(8,128)(2,1)}, bf16[2,192,1536]{2,1,0:T(8,128)(2,1)}, u32[]{:S(2)}, u32[]{:S(2)}) collective-permute-start(bf16[2,192,1536]{2,1,0:T(8,128)(2,1)} %bitcast.19.refs_9_.refs_10_.refs_14_), channel_id=1, source_target_pairs={{0,16},{16,0},{32,48},{48,32},{1,17},{17,1},{33,49},{49,33},{2,18}... | collective-permute-start | bytes 3538952 | tf_op jit(solution)/shard_map/ppermute | solution.py:163
  152.0 24.3 %collective-permute-start.7 = (bf16[2,192,1536]{2,1,0:T(8,128)(2,1)}, bf16[2,192,1536]{2,1,0:T(8,128)(2,1)}, u32[]{:S(2)}, u32[]{:S(2)}) collective-permute-start(bf16[2,192,1536]{2,1,0:T(8,128)(2,1)} %collective-permute-done.refs_4_.refs_3_.refs_8_), channel_id=1, source_target_pairs={{0,16},{16,0},{32,48},{48,32},{1,17},{17,1},{33,49},{49,33},{2,18}... | collective-permute-start | bytes 3538952 | tf_op jit(solution)/shard_map/ppermute | solution.py:163
  166.8 24.3 %all-to-all-start.2 = ((bf16[16,32,1536]{2,1,0:T(8,128)(2,1)}), bf16[16,32,1536]{2,1,0:T(8,128)(2,1)}, u32[]{:S(2)}, u32[]{:S(2)}) async-start(bf16[16,32,1536]{2,1,0:T(8,128)(2,1)} %get-tuple-element.135.refs_15_), calls=%async_computation.2 | async-start | bytes 3145728 | tf_op jit(solution)/shard_map/all_to_all | solution.py:735
  191.1 23.8 %all-to-all-start.1 = ((bf16[16,32,1536]{2,1,0:T(8,128)(2,1)}), bf16[16,32,1536]{2,1,0:T(8,128)(2,1)}, u32[]{:S(2)}, u32[]{:S(2)}) async-start(bf16[16,32,1536]{2,1,0:T(8,128)(2,1)} %expert_forward.4), calls=%async_computation.1 | async-start | bytes 3145728 | tf_op jit(solution)/shard_map/all_to_all | solution.py:735
  214.9 31.9 %all-to-all-start.3 = ((bf16[16,32,1536]{2,1,0:T(8,128)(2,1)}), bf16[16,32,1536]{2,1,0:T(8,128)(2,1)}, u32[]{:S(2)}, u32[]{:S(2)}) async-start(bf16[16,32,1536]{2,1,0:T(8,128)(2,1)} %expert_forward.5.refs_5_), calls=%async_computation.3 | async-start | bytes 3145728 | tf_op jit(solution)/shard_map/all_to_all | solution.py:735
  260.2 39.2 %all-to-all-start.4 = ((bf16[16,32,1664]{2,1,0:T(8,128)(2,1)}), bf16[16,32,1664]{2,1,0:T(8,128)(2,1)}, u32[]{:S(2)}, u32[]{:S(2)}) async-start(bf16[16,32,1664]{2,1,0:T(8,128)(2,1)} %get-tuple-element.143), calls=%async_computation.4 | async-start | bytes 3407872 | tf_op jit(solution)/shard_map/all_to_all | solution.py:735
  299.4 30.8 %all-to-all-start.6 = ((bf16[16,32,1664]{2,1,0:T(8,128)(2,1)}), bf16[16,32,1664]{2,1,0:T(8,128)(2,1)}, u32[]{:S(2)}, u32[]{:S(2)}) async-start(bf16[16,32,1664]{2,1,0:T(8,128)(2,1)} %get-tuple-element.147.refs_16_), calls=%async_computation.6 | async-start | bytes 3407872 | tf_op jit(solution)/shard_map/all_to_all | solution.py:735
  308.5 28.9 %collective-permute-start.25 = (bf16[4,96,1536]{2,1,0:T(8,128)(2,1)}, bf16[4,96,1536]{2,1,0:T(8,128)(2,1)}, u32[]{:S(2)}, u32[]{:S(2)}) collective-permute-start(bf16[4,96,1536]{2,1,0:T(8,128)(2,1)} %pack.1.refs_0_), channel_id=1, source_target_pairs={{0,32},{16,48},{32,0},{48,16},{1,33},{17,49},{33,1},{49,17},{2,34}... | collective-permute-start | bytes 3538952 | tf_op jit(solution)/shard_map/ppermute | solution.py:163
  330.2 26.1 %all-to-all-start.5 = ((bf16[16,32,1664]{2,1,0:T(8,128)(2,1)}), bf16[16,32,1664]{2,1,0:T(8,128)(2,1)}, u32[]{:S(2)}, u32[]{:S(2)}) async-start(bf16[16,32,1664]{2,1,0:T(8,128)(2,1)} %get-tuple-element.148), calls=%async_computation.5 | async-start | bytes 3407872 | tf_op jit(solution)/shard_map/all_to_all | solution.py:735
  356.3 37.7 %all-to-all-start.7 = ((bf16[16,32,1664]{2,1,0:T(8,128)(2,1)}), bf16[16,32,1664]{2,1,0:T(8,128)(2,1)}, u32[]{:S(2)}, u32[]{:S(2)}) async-start(bf16[16,32,1664]{2,1,0:T(8,128)(2,1)} %get-tuple-element.156.refs_18_), calls=%async_computation.7 | async-start | bytes 3407872 | tf_op jit(solution)/shard_map/all_to_all | solution.py:735
  361.7 32.3 %collective-permute-start.30 = (bf16[4,96,1536]{2,1,0:T(8,128)(2,1)}, bf16[4,96,1536]{2,1,0:T(8,128)(2,1)}, u32[]{:S(2)}, u32[]{:S(2)}) collective-permute-start(bf16[4,96,1536]{2,1,0:T(8,128)(2,1)} %pack.1.refs_0_), channel_id=1, source_target_pairs={{0,16},{16,0},{32,48},{48,32},{1,17},{17,1},{33,49},{49,33},{2,18}... | collective-permute-start | bytes 3538952 | tf_op jit(solution)/shard_map/ppermute | solution.py:163
  365.4 28.7 %collective-permute-start.31 = (bf16[4,96,1536]{2,1,0:T(8,128)(2,1)}, bf16[4,96,1536]{2,1,0:T(8,128)(2,1)}, u32[]{:S(2)}, u32[]{:S(2)}) collective-permute-start(bf16[4,96,1536]{2,1,0:T(8,128)(2,1)} %collective-permute-done.25.refs_16_.refs_19_.refs_2_), channel_id=1, source_target_pairs={{0,16},{16,0},{32,48},{48,32},{1,17},{17,1},{33,49},{49,33},{2,18}... | collective-permute-start | bytes 3538952 | tf_op jit(solution)/shard_map/ppermute | solution.py:163
  406.3 34.2 %all-to-all-start.8 = ((bf16[16,32,1536]{2,1,0:T(8,128)(2,1)}), bf16[16,32,1536]{2,1,0:T(8,128)(2,1)}, u32[]{:S(2)}, u32[]{:S(2)}) async-start(bf16[16,32,1536]{2,1,0:T(8,128)(2,1)} %get-tuple-element.167), calls=%async_computation.8 | async-start | bytes 3145728 | tf_op jit(solution)/shard_map/all_to_all | solution.py:735
  440.6 28.2 %all-to-all-start.10 = ((bf16[16,32,1536]{2,1,0:T(8,128)(2,1)}), bf16[16,32,1536]{2,1,0:T(8,128)(2,1)}, u32[]{:S(2)}, u32[]{:S(2)}) async-start(bf16[16,32,1536]{2,1,0:T(8,128)(2,1)} %get-tuple-element.177.refs_20_), calls=%async_computation.10 | async-start | bytes 3145728 | tf_op jit(solution)/shard_map/all_to_all | solution.py:735
  468.7 25.9 %all-to-all-start.9 = ((bf16[16,32,1664]{2,1,0:T(8,128)(2,1)}), bf16[16,32,1664]{2,1,0:T(8,128)(2,1)}, u32[]{:S(2)}, u32[]{:S(2)}) async-start(bf16[16,32,1664]{2,1,0:T(8,128)(2,1)} %get-tuple-element.178), calls=%async_computation.9 | async-start | bytes 3407872 | tf_op jit(solution)/shard_map/all_to_all | solution.py:735
  478.0 22.2 %collective-permute-start.36 = (bf16[2,192,1536]{2,1,0:T(8,128)(2,1)}, bf16[2,192,1536]{2,1,0:T(8,128)(2,1)}, u32[]{:S(2)}, u32[]{:S(2)}) collective-permute-start(bf16[2,192,1536]{2,1,0:T(8,128)(2,1)} %get-tuple-element.186), channel_id=1, source_target_pairs={{0,16},{16,0},{32,48},{48,32},{1,17},{17,1},{33,49},{49,33},{2,18}... | collective-permute-start | bytes 3538952 | tf_op jit(solution)/shard_map/ppermute | solution.py:163
  494.7 33.8 %all-to-all-start.11 = ((bf16[16,32,1664]{2,1,0:T(8,128)(2,1)}), bf16[16,32,1664]{2,1,0:T(8,128)(2,1)}, u32[]{:S(2)}, u32[]{:S(2)}) async-start(bf16[16,32,1664]{2,1,0:T(8,128)(2,1)} %get-tuple-element.183.refs_18_), calls=%async_computation.11 | async-start | bytes 3407872 | tf_op jit(solution)/shard_map/all_to_all | solution.py:735
  503.2 25.7 %collective-permute-start.40 = (bf16[2,192,1536]{2,1,0:T(8,128)(2,1)}, bf16[2,192,1536]{2,1,0:T(8,128)(2,1)}, u32[]{:S(2)}, u32[]{:S(2)}) collective-permute-start(bf16[2,192,1536]{2,1,0:T(8,128)(2,1)} %add.133.refs_19_), channel_id=1, source_target_pairs={{0,32},{16,48},{32,0},{48,16},{1,33},{17,49},{33,1},{49,17},{2,34}... | collective-permute-start | bytes 3538952 | tf_op jit(solution)/shard_map/ppermute | solution.py:163
  523.2 23.6 %collective-permute-start.44 = (bf16[2,192,1536]{2,1,0:T(8,128)(2,1)}, bf16[2,192,1536]{2,1,0:T(8,128)(2,1)}, u32[]{:S(2)}, u32[]{:S(2)}) collective-permute-start(bf16[2,192,1536]{2,1,0:T(8,128)(2,1)} %get-tuple-element.212), channel_id=1, source_target_pairs={{0,16},{16,0},{32,48},{48,32},{1,17},{17,1},{33,49},{49,33},{2,18}... | collective-permute-start | bytes 3538952 | tf_op jit(solution)/shard_map/ppermute | solution.py:163
  569.1 53.1 %all-to-all-start.12 = ((bf16[16,96,512]{2,1,0:T(8,128)(2,1)}), bf16[16,96,512]{2,1,0:T(8,128)(2,1)}, u32[]{:S(2)}, u32[]{:S(2)}) async-start(bf16[16,96,512]{2,1,0:T(8,128)(2,1)} %out_grads.1.refs_12_), calls=%async_computation.12 | async-start | bytes 3145728 | tf_op jit(solution)/shard_map/all_to_all | solution.py:735
  575.7 40.9 %collective-permute-start.52 = (bf16[2,192,1536]{2,1,0:T(8,128)(2,1)}, bf16[2,192,1536]{2,1,0:T(8,128)(2,1)}, u32[]{:S(2)}, u32[]{:S(2)}) collective-permute-start(bf16[2,192,1536]{2,1,0:T(8,128)(2,1)} %hold.4.refs_19_), channel_id=1, source_target_pairs={{0,32},{16,48},{32,0},{48,16},{1,33},{17,49},{33,1},{49,17},{2,34}... | collective-permute-start | bytes 3538952 | tf_op jit(solution)/shard_map/ppermute | solution.py:163
  577.1 58.8 %collective-permute-start.56 = (bf16[2,192,1536]{2,1,0:T(8,128)(2,1)}, bf16[2,192,1536]{2,1,0:T(8,128)(2,1)}, u32[]{:S(2)}, u32[]{:S(2)}) collective-permute-start(bf16[2,192,1536]{2,1,0:T(8,128)(2,1)} %get-tuple-element.239), channel_id=1, source_target_pairs={{0,16},{16,0},{32,48},{48,32},{1,17},{17,1},{33,49},{49,33},{2,18}... | collective-permute-start | bytes 3538952 | tf_op jit(solution)/shard_map/ppermute | solution.py:163
  600.0 39.8 %collective-permute-start.59 = (bf16[2,192,1536]{2,1,0:T(8,128)(2,1)}, bf16[2,192,1536]{2,1,0:T(8,128)(2,1)}, u32[]{:S(2)}, u32[]{:S(2)}) collective-permute-start(bf16[2,192,1536]{2,1,0:T(8,128)(2,1)} %get-tuple-element.243), channel_id=1, source_target_pairs={{0,16},{16,0},{32,48},{48,32},{1,17},{17,1},{33,49},{49,33},{2,18}... | collective-permute-start | bytes 3538952 | tf_op jit(solution)/shard_map/ppermute | solution.py:163
  613.9 46.5 %collective-permute-start.57 = (bf16[2,192,1536]{2,1,0:T(8,128)(2,1)}, bf16[2,192,1536]{2,1,0:T(8,128)(2,1)}, u32[]{:S(2)}, u32[]{:S(2)}) collective-permute-start(bf16[2,192,1536]{2,1,0:T(8,128)(2,1)} %get-tuple-element.241), channel_id=1, source_target_pairs={{0,16},{16,0},{32,48},{48,32},{1,17},{17,1},{33,49},{49,33},{2,18}... | collective-permute-start | bytes 3538952 | tf_op jit(solution)/shard_map/ppermute | solution.py:163
  622.2 29.4 %all-to-all-start.13 = ((bf16[16,96,512]{2,1,0:T(8,128)(2,1)}), bf16[16,96,512]{2,1,0:T(8,128)(2,1)}, u32[]{:S(2)}, u32[]{:S(2)}) async-start(bf16[16,96,512]{2,1,0:T(8,128)(2,1)} %qkv_grads.1.refs_12_), calls=%async_computation.13 | async-start | bytes 3145728 | tf_op jit(solution)/shard_map/all_to_all | solution.py:735
  629.9 30.5 %collective-permute-start.58 = (bf16[2,192,1536]{2,1,0:T(8,128)(2,1)}, bf16[2,192,1536]{2,1,0:T(8,128)(2,1)}, u32[]{:S(2)}, u32[]{:S(2)}) collective-permute-start(bf16[2,192,1536]{2,1,0:T(8,128)(2,1)} %hold.5), channel_id=1, source_target_pairs={{0,32},{16,48},{32,0},{48,16},{1,33},{17,49},{33,1},{49,17},{2,34}... | collective-permute-start | bytes 3538952 | tf_op jit(solution)/shard_map/ppermute | solution.py:163
  (62 other events, 472.3 us)
Sparse Core Ops, SparseCore 0:
  11.7 105.9 all-gather.1

commit v14 on v13

--- a/solution.py
+++ b/solution.py
@@ -999,24 +999,22 @@
     inner.append(attention_back(True, 1, given[1][:1], back[1], (both[0], crossed[0])))
     parts.append(parts_of(inner[1]))
     sums = merged([both[2:4], both[6:]], (inner[1][0],))
-    gate_far = hold(sums[0], *parts[1][1:])
-    crossed.append(swapped(gate_far, 2))
+    last = projection_back(True, 1, inner[1], parts[1], ())
+    outer = [projection_back(True, 0, inner[0], parts[0], (last[0],)), last]
+    backs = [[o[2]] + [swapped(o[2 + s], s) for s in steps[1:]] for o in outer]
+    w_grads = call(
+        qkv_grads, (Sent(like((columns, rows * shard, qkv_width // rows), BF)),),
+        late([*lefts, *[b[s] for s in steps for b in backs]]),
+        2 * width * length * micro * qkv_width // rows, waits=(sums[0],),
+    )[0]
+    crossed += [swapped(hold(one, *backs[0][1:], *backs[1][1:]), 2) for one in sums]
     o_grads = call(
         out_grads, (Sent(like((columns, rows * shard, share + LANES), BF)),),
         late([*lefts, *[p[s] for s in steps for p in parts], *[a[5] for a in attended],
               *[a[6] for a in inner], *[a[7] for a in inner]]),
-        2 * width * length * micro * share, waits=(crossed[0], gate_far),
+        2 * width * length * micro * share, waits=(w_grads,),
     )[0]
-    last = projection_back(True, 1, inner[1], parts[1], (o_grads,))
-    outer = [projection_back(True, 0, inner[0], parts[0], (last[0],)), last]
-    backs = [[o[2]] + [swapped(o[2 + s], s) for s in steps[1:]] for o in outer]
-    crossed.append(swapped(hold(sums[1], *backs[0][1:], *backs[1][1:]), 2))
-    near = weight_call((0, 1), ((0, 0),), hidden, arrived_grads, (outer[1][0],))
-    w_grads = call(
-        qkv_grads, (Sent(like((columns, rows * shard, qkv_width // rows), BF)),),
-        late([*lefts, *[b[s] for s in steps for b in backs]]),
-        2 * width * length * micro * qkv_width // rows, waits=(crossed[1], near[0]),
-    )[0]
+    near = weight_call((0, 1), ((0, 0),), hidden, arrived_grads, (o_grads,))
     expert_grads = [
         one.astype(F32) + swapped(other, 1).astype(F32) + c.astype(F32)
         for one, other, c in zip((near[0], both[0], both[4]), (near[1], both[1], both[5]), crossed)

time: 688 us -> 689 us (level)
    all_to_all x14, waiting for transfers between devices: 41 us -> 54.8 us  [over_columns(): return lax.all_to_all(value, 'col', split_axis=0, concat_axis=0, tiled=True)]
    ppermute x56, waiting for transfers between devices: 116 us -> 107 us  [swapped(): return lax.ppermute(value, 'row', [(r, r ^ step) for r in range(rows)])]
  transfers between devices with their start and end apart: 75 -> 75, of which waited for: 36 -> 34; matrix products, arithmetic and copies ran while one was open for 4% -> 4% of each run, Pallas kernels for 32% -> 31%
where the time goes in v14:
time: 689 us; the launch traced here: 677 us
  Pallas kernels  245 us (36%)
  waiting for transfers between devices  211 us (31%)
  starting transfers between devices  174 us (25%)
  other arithmetic  20.2 us (3%)
  between operations  15.4 us (2%)
  local copies, waits for them, and re-layouts  11.1 us (2%)
    pallas_call x36, Pallas kernels, call(): pl.pallas_call(run, out_shape=tuple(shapes), in_specs=[pl.BlockSpec(memor...  245 us
    ppermute x56, waiting for transfers between devices, swapped(): return lax.ppermute(value, 'row', [(r, r ^ step) for r in range(rows)])  107 us
    ppermute x56, starting transfers between devices, swapped(): return lax.ppermute(value, 'row', [(r, r ^ step) for r in range(rows)])  85.9 us
    all_to_all x14, starting transfers between devices, over_columns(): return lax.all_to_all(value, 'col', split_axis=0, concat_axis=0, tiled=True)  79.8 us
    all_to_all x14, waiting for transfers between devices, over_columns(): return lax.all_to_all(value, 'col', split_axis=0, concat_axis=0, tiled=True)  54.8 us
    all_gather x1, waiting for transfers between devices, on_device(): dense = lax.all_gather(dense, ('row', 'col'), axis=0, tiled=True)  29.4 us
    ppermute x2, waiting for transfers between devices, on_device(): came = [lax.ppermute(r[0], 'section', [(0, 1)]) for r in results]  13.9 us
  transfers between devices with their start and end apart: 75, of which 34 were waited for; matrix products, arithmetic and copies ran while one was open for 4% of the time, Pallas kernels for 31%

profile of v14, /device:TPU:9, one launch (start us, length us, event | category | flops | bytes accessed | tf_op | source)
XLA Modules:
  0.0 676.8 jit_solution(15607970946114312677)
XLA Ops:
  23.9 64.4 %collective-permute-done.2.refs_6_.refs_11_.refs_12_.refs_16_ = bf16[1,192,1536]{2,1,0:T(8,128)(2,1)} collective-permute-done((bf16[1,192,1536]{2,1,0:T(8,128)(2,1)S(1)}, bf16[1,192,1536]{2,1,0:T(8,128)(2,1)}, u32[]{:S(2)}, u32[]{:S(2)}) %collective-permute-start.2) | collective-permute-done | bytes 589856 | tf_op jit(solution)/shard_map/ppermute | solution.py:163
  88.4 29.4 %all-gather.2.cloned.1.call-done.refs_3_.refs_12_.refs_6_.refs_17_.refs_11_ = bf16[1536,3712]{1,0:T(8,128)(2,1)} async-done(((bf16[24,3712]{1,0:T(8,128)(2,1)}), bf16[1536,3712]{1,0:T(8,128)(2,1)}) %all-gather.2.cloned.1.call-update) | async-done | bytes 11403280 | tf_op jit(solution)/shard_map/all_gather | solution.py:768
  133.0 6.5 attend.4
  157.6 6.5 attend.5
  177.2 10.3 %expert_forward.4 = bf16[16,32,1536]{2,1,0:T(8,128)(2,1)} custom-call(bf16[16,32,1536]{2,1,0:T(8,128)(2,1)} %all-to-all-done.refs_0_.refs_1_, bf16[2,192,1536]{2,1,0:T(8,128)(2,1)} %bitcast.65, bf16[2,192,1536]{2,1,0:T(8,128)(2,1)} %copy-done.1, bf16[2,192,1536]{2,1,0:T(8,128)(2,1)} %collective-permute-done.refs_4_.refs_3_.refs_8_, ...), custom_call_target="tpu_custom_call" | custom-call | flops 3623878656 | bytes 17301504 | tf_op jit(solution)/shard_map/expert_forward/pallas_call | solution.py:124
  195.9 10.3 %expert_forward.5.refs_5_ = bf16[16,32,1536]{2,1,0:T(8,128)(2,1)} custom-call(bf16[16,32,1536]{2,1,0:T(8,128)(2,1)} %all-to-all-done.2.refs_0_.refs_1_, bf16[2,192,1536]{2,1,0:T(8,128)(2,1)} %bitcast.66, bf16[2,192,1536]{2,1,0:T(8,128)(2,1)} %copy-done.1, bf16[2,192,1536]{2,1,0:T(8,128)(2,1)} %collective-permute-done.refs_4_.refs_3_.refs_8_, ...), custom_call_target="tpu_custom_call" | custom-call | flops 3623878656 | bytes 17301504 | tf_op jit(solution)/shard_map/expert_forward/pallas_call | solution.py:124
  206.2 8.8 %all-to-all-done.1.refs_0_ = bf16[16,32,1536]{2,1,0:T(8,128)(2,1)} async-done(((bf16[16,32,1536]{2,1,0:T(8,128)(2,1)}), bf16[16,32,1536]{2,1,0:T(8,128)(2,1)}, u32[]{:S(2)}, u32[]{:S(2)}) %all-to-all-start.1) | async-done | bytes 1572896 | tf_op jit(solution)/shard_map/all_to_all | solution.py:735
  215.0 6.9 %all-to-all-start.3 = ((bf16[16,32,1536]{2,1,0:T(8,128)(2,1)}), bf16[16,32,1536]{2,1,0:T(8,128)(2,1)}, u32[]{:S(2)}, u32[]{:S(2)}) async-start(bf16[16,32,1536]{2,1,0:T(8,128)(2,1)} %expert_forward.5.refs_5_), calls=%async_computation.3 | async-start | bytes 3145728 | tf_op jit(solution)/shard_map/all_to_all | solution.py:735
  253.4 6.8 %attend.6 = (f32[96,1536]{1,0:T(8,128)}, f32[96,128]{1,0:T(8,128)}, bf16[16,32,1664]{2,1,0:T(8,128)(2,1)}, bf16[2,576,384]{2,1,0:T(8,128)(2,1)}, bf16[96,1536]{1,0:T(8,128)(2,1)}, /*index=5*/bf16[96,1536]{1,0:T(8,128)(2,1)}) custom-call(s32[1]{0:T(128)} %bitcast.refs_0_.refs_1_, f32[96,1536]{1,0:T(8,128)} %get-tuple-element.138.refs_1_.refs_7_.refs_6_, ...), custom_call_target="tpu_custom_call" | custom-call | flops 830472192 | bytes 17389568 | tf_op jit(solution)/shard_map/attend/pallas_call | solution.py:124
  260.2 7.0 %all-to-all-start.4 = ((bf16[16,32,1664]{2,1,0:T(8,128)(2,1)}), bf16[16,32,1664]{2,1,0:T(8,128)(2,1)}, u32[]{:S(2)}, u32[]{:S(2)}) async-start(bf16[16,32,1664]{2,1,0:T(8,128)(2,1)} %get-tuple-element.143), calls=%async_computation.4 | async-start | bytes 3407872 | tf_op jit(solution)/shard_map/all_to_all | solution.py:735
  268.5 8.6 %collective-permute-done.21.refs_1_ = bf16[96,1536]{1,0:T(8,128)(2,1)} collective-permute-done((bf16[96,1536]{1,0:T(8,128)(2,1)S(1)}, bf16[96,1536]{1,0:T(8,128)(2,1)}, u32[]{:S(2)}, u32[]{:S(2)}) %collective-permute-start.21) | collective-permute-done | bytes 294944 | tf_op jit(solution)/shard_map/ppermute | solution.py:961
  292.6 6.8 %attend.7 = (f32[96,1536]{1,0:T(8,128)}, f32[96,128]{1,0:T(8,128)}, bf16[16,32,1664]{2,1,0:T(8,128)(2,1)}, bf16[2,576,384]{2,1,0:T(8,128)(2,1)}, bf16[96,1536]{1,0:T(8,128)(2,1)}, /*index=5*/bf16[96,1536]{1,0:T(8,128)(2,1)}) custom-call(s32[1]{0:T(128)} %bitcast.refs_0_.refs_1_, f32[96,1536]{1,0:T(8,128)} %get-tuple-element.144.refs_1_.refs_6_, ...), custom_call_target="tpu_custom_call" | custom-call | flops 830472192 | bytes 17389568 | tf_op jit(solution)/shard_map/attend/pallas_call | solution.py:124
  299.4 6.7 all-to-all-start.6
  310.9 16.5 %expert_forward.6 = (bf16[16,32,1536]{2,1,0:T(8,128)(2,1)}, bf16[2,256,768]{2,1,0:T(8,128)(2,1)}, bf16[2,256,768]{2,1,0:T(8,128)(2,1)}, bf16[2,256,768]{2,1,0:T(8,128)(2,1)}, bf16[16,32,1664]{2,1,0:T(8,128)(2,1)}) custom-call(bf16[16,32,1664]{2,1,0:T(8,128)(2,1)} %all-to-all-done.4.refs_0_.refs_4_, bf16[16,32,1536]{2,1,0:T(8,128)(2,1)} %all-to-all-done.refs_0_.refs_1_, ...), custom_call_target="tpu_custom_call" | custom-call | flops 7247757312 | bytes 23068672 | tf_op jit(solution)/shard_map/expert_forward/pallas_call | solution.py:124
  337.7 16.4 %expert_forward.7 = (bf16[16,32,1536]{2,1,0:T(8,128)(2,1)}, bf16[2,256,768]{2,1,0:T(8,128)(2,1)}, bf16[2,256,768]{2,1,0:T(8,128)(2,1)}, bf16[2,256,768]{2,1,0:T(8,128)(2,1)}, bf16[16,32,1664]{2,1,0:T(8,128)(2,1)}) custom-call(bf16[16,32,1664]{2,1,0:T(8,128)(2,1)} %all-to-all-done.6.refs_0_.refs_5_, bf16[16,32,1536]{2,1,0:T(8,128)(2,1)} %all-to-all-done.2.refs_0_.refs_1_, ...), custom_call_target="tpu_custom_call" | custom-call | flops 7247757312 | bytes 23068672 | tf_op jit(solution)/shard_map/expert_forward/pallas_call | solution.py:124
  365.7 8.7 %attend_back.4 = (f32[96,1536]{1,0:T(8,128)}, bf16[96,1536]{1,0:T(8,128)(2,1)}, bf16[96,512]{1,0:T(8,128)(2,1)}, bf16[96,512]{1,0:T(8,128)(2,1)}, bf16[96,512]{1,0:T(8,128)(2,1)}, /*index=5*/bf16[96,512]{1,0:T(8,128)(2,1)}) custom-call(s32[1]{0:T(128)} %bitcast.1.refs_0_, s32[1]{0:T(128)} %bitcast.refs_0_.refs_1_, ...), custom_call_target="tpu_custom_call" | custom-call | flops 1056964608 | bytes 17520640 | tf_op jit(solution)/shard_map/attend_back/pallas_call | solution.py:124
  384.7 6.7 project_back.4.refs_21_
  393.8 8.8 %attend_back.5 = (f32[96,1536]{1,0:T(8,128)}, bf16[96,1536]{1,0:T(8,128)(2,1)}, bf16[96,512]{1,0:T(8,128)(2,1)}, bf16[96,512]{1,0:T(8,128)(2,1)}, bf16[96,512]{1,0:T(8,128)(2,1)}, /*index=5*/bf16[96,512]{1,0:T(8,128)(2,1)}) custom-call(s32[1]{0:T(128)} %bitcast.1.refs_0_, s32[1]{0:T(128)} %bitcast.refs_0_.refs_1_, ...), custom_call_target="tpu_custom_call" | custom-call | flops 1056964608 | bytes 17520640 | tf_op jit(solution)/shard_map/attend_back/pallas_call | solution.py:124
  406.1 6.6 all-to-all-start.8
  422.3 6.7 project_back.5
  441.2 6.9 %all-to-all-start.10 = ((bf16[16,32,1536]{2,1,0:T(8,128)(2,1)}), bf16[16,32,1536]{2,1,0:T(8,128)(2,1)}, u32[]{:S(2)}, u32[]{:S(2)}) async-start(bf16[16,32,1536]{2,1,0:T(8,128)(2,1)} %get-tuple-element.177.refs_20_), calls=%async_computation.10 | async-start | bytes 3145728 | tf_op jit(solution)/shard_map/all_to_all | solution.py:735
  448.1 10.8 %expert_backward.2 = (bf16[16,32,1664]{2,1,0:T(8,128)(2,1)}, bf16[2,256,768]{2,1,0:T(8,128)(2,1)}, bf16[2,256,768]{2,1,0:T(8,128)(2,1)}) custom-call(s32[1]{0:T(128)} %bitcast.refs_0_.refs_1_, bf16[16,32,1536]{2,1,0:T(8,128)(2,1)} %all-to-all-done.8.refs_1_.refs_2_, bf16[2,256,768]{2,1,0:T(8,128)(2,1)} %get-tuple-element.168.refs_2_.refs_0_, ...), custom_call_target="tpu_custom_call" | custom-call | flops 3623878656 | bytes 22937600 | tf_op jit(solution)/shard_map/expert_backward/pallas_call | solution.py:124
  458.9 9.8 %all-to-all-done.10.refs_1_.refs_3_ = bf16[16,32,1536]{2,1,0:T(8,128)(2,1)} async-done(((bf16[16,32,1536]{2,1,0:T(8,128)(2,1)}), bf16[16,32,1536]{2,1,0:T(8,128)(2,1)}, u32[]{:S(2)}, u32[]{:S(2)}) %all-to-all-start.10) | async-done | bytes 1572896 | tf_op jit(solution)/shard_map/all_to_all | solution.py:735
  481.6 10.8 %expert_backward.3 = (bf16[16,32,1664]{2,1,0:T(8,128)(2,1)}, bf16[2,256,768]{2,1,0:T(8,128)(2,1)}, bf16[2,256,768]{2,1,0:T(8,128)(2,1)}) custom-call(s32[1]{0:T(128)} %bitcast.refs_0_.refs_1_, bf16[16,32,1536]{2,1,0:T(8,128)(2,1)} %all-to-all-done.10.refs_1_.refs_3_, bf16[2,256,768]{2,1,0:T(8,128)(2,1)} %get-tuple-element.179.refs_2_.refs_1_, ...), custom_call_target="tpu_custom_call" | custom-call | flops 3623878656 | bytes 22937600 | tf_op jit(solution)/shard_map/expert_backward/pallas_call | solution.py:124
  504.4 9.4 %attend_back.6 = (f32[96,1536]{1,0:T(8,128)}, bf16[96,1536]{1,0:T(8,128)(2,1)}, bf16[96,896]{1,0:T(8,128)(2,1)}, bf16[96,896]{1,0:T(8,128)(2,1)}, bf16[96,896]{1...) custom-call(s32[1]{0:T(128)} %bitcast.1.refs_0_, s32[1]{0:T(128)} %bitcast.refs_0_.refs_1_, ...), custom_call_target="tpu_custom_call" | custom-call | flops 1056964608 | bytes 19167232 | tf_op jit(solution)/shard_map/attend_back/pallas_call | solution.py:124
  513.9 9.1 %expert_weight_grads.4 = (bf16[2,192,1536]{2,1,0:T(8,128)(2,1)}, bf16[2,192,1536]{2,1,0:T(8,128)(2,1)}, bf16[2,192,1536]{2,1,0:T(8,128)(2,1)}, bf16[2,192,1536]{...) custom-call(bf16[2,256,768]{2,1,0:T(8,128)(2,1)} %get-tuple-element., ...), custom_call_target="tpu_custom_call" | custom-call | flops 2415919104 | bytes 15990784 | tf_op jit(solution)/shard_map/expert_weight_grads/pallas_call | solution.py:124
  528.8 9.4 %attend_back.7 = (f32[96,1536]{1,0:T(8,128)}, bf16[96,1536]{1,0:T(8,128)(2,1)}, bf16[96,896]{1,0:T(8,128)(2,1)}, bf16[96,896]{1,0:T(8,128)(2,1)}, bf16[96,896]{1...) custom-call(s32[1]{0:T(128)} %bitcast.1.refs_0_, s32[1]{0:T(128)} %bitcast.refs_0_.refs_1_, ...), custom_call_target="tpu_custom_call" | custom-call | flops 1056964608 | bytes 19167232 | tf_op jit(solution)/shard_map/attend_back/pallas_call | solution.py:124
  555.8 7.3 %project_back.6 = (bf16[96,1536]{1,0:T(8,128)(2,1)}, f32[96,1536]{1,0:T(8,128)}, bf16[96,512]{1,0:T(8,128)(2,1)}, bf16[96,512]{1,0:T(8,128)(2,1)}, bf16[96,512]{1,0:T(8,128)(2,1)}, /*index=5*/bf16[96,512]{1,0:T(8,128)(2,1)}) custom-call(s32[1]{0:T(128)} %bitcast.1.refs_0_, bf16[96,896]{1,0:T(8,128)(2,1)} %get-tuple-element.199.refs_1_.refs_5_, ...), custom_call_target="tpu_custom_call" | custom-call | flops 603979776 | bytes 14948352 | tf_op jit(solution)/shard_map/project_back/pallas_call | solution.py:124
  563.2 7.3 %project_back.7 = (bf16[96,1536]{1,0:T(8,128)(2,1)}, f32[96,1536]{1,0:T(8,128)}, bf16[96,512]{1,0:T(8,128)(2,1)}, bf16[96,512]{1,0:T(8,128)(2,1)}, bf16[96,512]{1,0:T(8,128)(2,1)}, /*index=5*/bf16[96,512]{1,0:T(8,128)(2,1)}) custom-call(s32[1]{0:T(128)} %bitcast.1.refs_0_, bf16[96,896]{1,0:T(8,128)(2,1)} %get-tuple-element.187.refs_1_.refs_4_, ...), custom_call_target="tpu_custom_call" | custom-call | flops 603979776 | bytes 14948352 | tf_op jit(solution)/shard_map/project_back/pallas_call | solution.py:124
  589.3 6.8 %out_grads.1.refs_4_ = bf16[16,96,512]{2,1,0:T(8,128)(2,1)} custom-call(bf16[4,96,1536]{2,1,0:T(8,128)(2,1)} %pack.1.refs_0_, bf16[4,96,1536]{2,1,0:T(8,128)(2,1)} %collective-permute-done.30.refs_18_.refs_1_, bf16[4,96,1536]{2,1,0:T(8,128)(2,1)} %collective-permute-done.25.refs_16_.refs_19_.refs_2_, ...), custom_call_target="tpu_custom_call" | custom-call | flops 905969664 | bytes 8404992 | tf_op jit(solution)/shard_map/out_grads/pallas_call | solution.py:124
  596.1 6.7 all-to-all-start.12
  610.1 16.0 %all-to-all-done.12.refs_1_ = bf16[16,96,512]{2,1,0:T(8,128)(2,1)} async-done(((bf16[16,96,512]{2,1,0:T(8,128)(2,1)}), bf16[16,96,512]{2,1,0:T(8,128)(2,1)}, u32[]{:S(2)}, u32[]{:S(2)}) %all-to-all-start.12) | async-done | bytes 1572896 | tf_op jit(solution)/shard_map/all_to_all | solution.py:735
  (243 shorter events, 301.6 us)
Async XLA Ops:
  7.2 110.6 %all-gather.2.cloned.1.call-start = ((), (), s32[]{:S(2)}) async-start(), calls=%async_computation.14 | async-start | bytes 11581440 | tf_op jit(solution)/shard_map/all_gather | solution.py:768
  10.5 77.9 %collective-permute-start = (bf16[2,192,1536]{2,1,0:T(8,128)(2,1)}, bf16[2,192,1536]{2,1,0:T(8,128)(2,1)}, u32[]{:S(2)}, u32[]{:S(2)}) collective-permute-start(bf16[2,192,1536]{2,1,0:T(8,128)(2,1)} %bitcast.64), channel_id=1, source_target_pairs={{0,32},{16,48},{32,0},{48,16},{1,33},{17,49},{33,1},{49,17},{2,34}... | collective-permute-start | bytes 3538952 | tf_op jit(solution)/shard_map/ppermute | solution.py:163
  12.6 75.8 %collective-permute-start.1 = (bf16[2,192,1536]{2,1,0:T(8,128)(2,1)}, bf16[2,192,1536]{2,1,0:T(8,128)(2,1)}, u32[]{:S(2)}, u32[]{:S(2)}) collective-permute-start(bf16[2,192,1536]{2,1,0:T(8,128)(2,1)} %bitcast.10.refs_5_.refs_6_.refs_10_), channel_id=1, source_target_pairs={{0,32},{16,48},{32,0},{48,16},{1,33},{17,49},{33,1},{49,17},{2,34}... | collective-permute-start | bytes 3538952 | tf_op jit(solution)/shard_map/ppermute | solution.py:163
  15.7 72.7 %collective-permute-start.2 = (bf16[1,192,1536]{2,1,0:T(8,128)(2,1)S(1)}, bf16[1,192,1536]{2,1,0:T(8,128)(2,1)}, u32[]{:S(2)}, u32[]{:S(2)}) collective-permute-start(bf16[1,192,1536]{2,1,0:T(8,128)(2,1)S(1)} %get-tuple-element.283), channel_id=1, source_target_pairs={{0,32},{16,48},{32,0},{48,16},{1,33},{17,49},{33,1},{49,17},{2,34}... | collective-permute-start | bytes 1769480 | tf_op jit(solution)/shard_map/ppermute | solution.py:163
  139.6 27.4 %all-to-all-start = ((bf16[16,32,1536]{2,1,0:T(8,128)(2,1)}), bf16[16,32,1536]{2,1,0:T(8,128)(2,1)}, u32[]{:S(2)}, u32[]{:S(2)}) async-start(bf16[16,32,1536]{2,1,0:T(8,128)(2,1)} %get-tuple-element.131), calls=%async_computation | async-start | bytes 3145728 | tf_op jit(solution)/shard_map/all_to_all | solution.py:735
  145.6 25.8 %collective-permute-start.8 = (bf16[2,192,1536]{2,1,0:T(8,128)(2,1)}, bf16[2,192,1536]{2,1,0:T(8,128)(2,1)}, u32[]{:S(2)}, u32[]{:S(2)}) collective-permute-start(bf16[2,192,1536]{2,1,0:T(8,128)(2,1)} %bitcast.10.refs_5_.refs_6_.refs_10_), channel_id=1, source_target_pairs={{0,16},{16,0},{32,48},{48,32},{1,17},{17,1},{33,49},{49,33},{2,18}... | collective-permute-start | bytes 3538952 | tf_op jit(solution)/shard_map/ppermute | solution.py:163
  150.7 23.8 %collective-permute-start.10 = (bf16[2,192,1536]{2,1,0:T(8,128)(2,1)}, bf16[2,192,1536]{2,1,0:T(8,128)(2,1)}, u32[]{:S(2)}, u32[]{:S(2)}) collective-permute-start(bf16[2,192,1536]{2,1,0:T(8,128)(2,1)} %bitcast.19.refs_9_.refs_10_.refs_14_), channel_id=1, source_target_pairs={{0,16},{16,0},{32,48},{48,32},{1,17},{17,1},{33,49},{49,33},{2,18}... | collective-permute-start | bytes 3538952 | tf_op jit(solution)/shard_map/ppermute | solution.py:163
  152.0 24.3 %collective-permute-start.7 = (bf16[2,192,1536]{2,1,0:T(8,128)(2,1)}, bf16[2,192,1536]{2,1,0:T(8,128)(2,1)}, u32[]{:S(2)}, u32[]{:S(2)}) collective-permute-start(bf16[2,192,1536]{2,1,0:T(8,128)(2,1)} %collective-permute-done.refs_4_.refs_3_.refs_8_), channel_id=1, source_target_pairs={{0,16},{16,0},{32,48},{48,32},{1,17},{17,1},{33,49},{49,33},{2,18}... | collective-permute-start | bytes 3538952 | tf_op jit(solution)/shard_map/ppermute | solution.py:163
  167.0 24.4 %all-to-all-start.2 = ((bf16[16,32,1536]{2,1,0:T(8,128)(2,1)}), bf16[16,32,1536]{2,1,0:T(8,128)(2,1)}, u32[]{:S(2)}, u32[]{:S(2)}) async-start(bf16[16,32,1536]{2,1,0:T(8,128)(2,1)} %get-tuple-element.135.refs_15_), calls=%async_computation.2 | async-start | bytes 3145728 | tf_op jit(solution)/shard_map/all_to_all | solution.py:735
  191.3 23.7 %all-to-all-start.1 = ((bf16[16,32,1536]{2,1,0:T(8,128)(2,1)}), bf16[16,32,1536]{2,1,0:T(8,128)(2,1)}, u32[]{:S(2)}, u32[]{:S(2)}) async-start(bf16[16,32,1536]{2,1,0:T(8,128)(2,1)} %expert_forward.4), calls=%async_computation.1 | async-start | bytes 3145728 | tf_op jit(solution)/shard_map/all_to_all | solution.py:735
  215.0 31.9 %all-to-all-start.3 = ((bf16[16,32,1536]{2,1,0:T(8,128)(2,1)}), bf16[16,32,1536]{2,1,0:T(8,128)(2,1)}, u32[]{:S(2)}, u32[]{:S(2)}) async-start(bf16[16,32,1536]{2,1,0:T(8,128)(2,1)} %expert_forward.5.refs_5_), calls=%async_computation.3 | async-start | bytes 3145728 | tf_op jit(solution)/shard_map/all_to_all | solution.py:735
  260.2 39.2 %all-to-all-start.4 = ((bf16[16,32,1664]{2,1,0:T(8,128)(2,1)}), bf16[16,32,1664]{2,1,0:T(8,128)(2,1)}, u32[]{:S(2)}, u32[]{:S(2)}) async-start(bf16[16,32,1664]{2,1,0:T(8,128)(2,1)} %get-tuple-element.143), calls=%async_computation.4 | async-start | bytes 3407872 | tf_op jit(solution)/shard_map/all_to_all | solution.py:735
  299.4 30.9 %all-to-all-start.6 = ((bf16[16,32,1664]{2,1,0:T(8,128)(2,1)}), bf16[16,32,1664]{2,1,0:T(8,128)(2,1)}, u32[]{:S(2)}, u32[]{:S(2)}) async-start(bf16[16,32,1664]{2,1,0:T(8,128)(2,1)} %get-tuple-element.147.refs_16_), calls=%async_computation.6 | async-start | bytes 3407872 | tf_op jit(solution)/shard_map/all_to_all | solution.py:735
  308.5 29.2 %collective-permute-start.25 = (bf16[4,96,1536]{2,1,0:T(8,128)(2,1)}, bf16[4,96,1536]{2,1,0:T(8,128)(2,1)}, u32[]{:S(2)}, u32[]{:S(2)}) collective-permute-start(bf16[4,96,1536]{2,1,0:T(8,128)(2,1)} %pack.1.refs_0_), channel_id=1, source_target_pairs={{0,32},{16,48},{32,0},{48,16},{1,33},{17,49},{33,1},{49,17},{2,34}... | collective-permute-start | bytes 3538952 | tf_op jit(solution)/shard_map/ppermute | solution.py:163
  330.3 26.1 %all-to-all-start.5 = ((bf16[16,32,1664]{2,1,0:T(8,128)(2,1)}), bf16[16,32,1664]{2,1,0:T(8,128)(2,1)}, u32[]{:S(2)}, u32[]{:S(2)}) async-start(bf16[16,32,1664]{2,1,0:T(8,128)(2,1)} %get-tuple-element.148), calls=%async_computation.5 | async-start | bytes 3407872 | tf_op jit(solution)/shard_map/all_to_all | solution.py:735
  356.4 37.4 %all-to-all-start.7 = ((bf16[16,32,1664]{2,1,0:T(8,128)(2,1)}), bf16[16,32,1664]{2,1,0:T(8,128)(2,1)}, u32[]{:S(2)}, u32[]{:S(2)}) async-start(bf16[16,32,1664]{2,1,0:T(8,128)(2,1)} %get-tuple-element.156.refs_18_), calls=%async_computation.7 | async-start | bytes 3407872 | tf_op jit(solution)/shard_map/all_to_all | solution.py:735
  361.7 32.2 %collective-permute-start.30 = (bf16[4,96,1536]{2,1,0:T(8,128)(2,1)}, bf16[4,96,1536]{2,1,0:T(8,128)(2,1)}, u32[]{:S(2)}, u32[]{:S(2)}) collective-permute-start(bf16[4,96,1536]{2,1,0:T(8,128)(2,1)} %pack.1.refs_0_), channel_id=1, source_target_pairs={{0,16},{16,0},{32,48},{48,32},{1,17},{17,1},{33,49},{49,33},{2,18}... | collective-permute-start | bytes 3538952 | tf_op jit(solution)/shard_map/ppermute | solution.py:163
  365.4 28.4 %collective-permute-start.31 = (bf16[4,96,1536]{2,1,0:T(8,128)(2,1)}, bf16[4,96,1536]{2,1,0:T(8,128)(2,1)}, u32[]{:S(2)}, u32[]{:S(2)}) collective-permute-start(bf16[4,96,1536]{2,1,0:T(8,128)(2,1)} %collective-permute-done.25.refs_16_.refs_19_.refs_2_), channel_id=1, source_target_pairs={{0,16},{16,0},{32,48},{48,32},{1,17},{17,1},{33,49},{49,33},{2,18}... | collective-permute-start | bytes 3538952 | tf_op jit(solution)/shard_map/ppermute | solution.py:163
  406.1 35.1 %all-to-all-start.8 = ((bf16[16,32,1536]{2,1,0:T(8,128)(2,1)}), bf16[16,32,1536]{2,1,0:T(8,128)(2,1)}, u32[]{:S(2)}, u32[]{:S(2)}) async-start(bf16[16,32,1536]{2,1,0:T(8,128)(2,1)} %get-tuple-element.167), calls=%async_computation.8 | async-start | bytes 3145728 | tf_op jit(solution)/shard_map/all_to_all | solution.py:735
  441.2 27.6 %all-to-all-start.10 = ((bf16[16,32,1536]{2,1,0:T(8,128)(2,1)}), bf16[16,32,1536]{2,1,0:T(8,128)(2,1)}, u32[]{:S(2)}, u32[]{:S(2)}) async-start(bf16[16,32,1536]{2,1,0:T(8,128)(2,1)} %get-tuple-element.177.refs_20_), calls=%async_computation.10 | async-start | bytes 3145728 | tf_op jit(solution)/shard_map/all_to_all | solution.py:735
  468.7 25.9 %all-to-all-start.9 = ((bf16[16,32,1664]{2,1,0:T(8,128)(2,1)}), bf16[16,32,1664]{2,1,0:T(8,128)(2,1)}, u32[]{:S(2)}, u32[]{:S(2)}) async-start(bf16[16,32,1664]{2,1,0:T(8,128)(2,1)} %get-tuple-element.178), calls=%async_computation.9 | async-start | bytes 3407872 | tf_op jit(solution)/shard_map/all_to_all | solution.py:735
  494.7 33.3 %all-to-all-start.11 = ((bf16[16,32,1664]{2,1,0:T(8,128)(2,1)}), bf16[16,32,1664]{2,1,0:T(8,128)(2,1)}, u32[]{:S(2)}, u32[]{:S(2)}) async-start(bf16[16,32,1664]{2,1,0:T(8,128)(2,1)} %get-tuple-element.183.refs_18_), calls=%async_computation.11 | async-start | bytes 3407872 | tf_op jit(solution)/shard_map/all_to_all | solution.py:735
  503.2 25.6 %collective-permute-start.40 = (bf16[2,192,1536]{2,1,0:T(8,128)(2,1)}, bf16[2,192,1536]{2,1,0:T(8,128)(2,1)}, u32[]{:S(2)}, u32[]{:S(2)}) collective-permute-start(bf16[2,192,1536]{2,1,0:T(8,128)(2,1)} %add.133.refs_19_), channel_id=1, source_target_pairs={{0,32},{16,48},{32,0},{48,16},{1,33},{17,49},{33,1},{49,17},{2,34}... | collective-permute-start | bytes 3538952 | tf_op jit(solution)/shard_map/ppermute | solution.py:163
  523.0 51.2 %collective-permute-start.50 = (bf16[2,192,1536]{2,1,0:T(8,128)(2,1)}, bf16[2,192,1536]{2,1,0:T(8,128)(2,1)}, u32[]{:S(2)}, u32[]{:S(2)}) collective-permute-start(bf16[2,192,1536]{2,1,0:T(8,128)(2,1)} %get-tuple-element.215), channel_id=1, source_target_pairs={{0,16},{16,0},{32,48},{48,32},{1,17},{17,1},{33,49},{49,33},{2,18}... | collective-permute-start | bytes 3538952 | tf_op jit(solution)/shard_map/ppermute | solution.py:163
  527.7 49.1 %collective-permute-start.51 = (bf16[2,192,1536]{2,1,0:T(8,128)(2,1)}, bf16[2,192,1536]{2,1,0:T(8,128)(2,1)}, u32[]{:S(2)}, u32[]{:S(2)}) collective-permute-start(bf16[2,192,1536]{2,1,0:T(8,128)(2,1)} %get-tuple-element.217), channel_id=1, source_target_pairs={{0,16},{16,0},{32,48},{48,32},{1,17},{17,1},{33,49},{49,33},{2,18}... | collective-permute-start | bytes 3538952 | tf_op jit(solution)/shard_map/ppermute | solution.py:163
  596.1 30.1 %all-to-all-start.12 = ((bf16[16,96,512]{2,1,0:T(8,128)(2,1)}), bf16[16,96,512]{2,1,0:T(8,128)(2,1)}, u32[]{:S(2)}, u32[]{:S(2)}) async-start(bf16[16,96,512]{2,1,0:T(8,128)(2,1)} %out_grads.1.refs_4_), calls=%async_computation.12 | async-start | bytes 3145728 | tf_op jit(solution)/shard_map/all_to_all | solution.py:735
  602.8 35.0 %collective-permute-start.55 = (bf16[2,192,1536]{2,1,0:T(8,128)(2,1)}, bf16[2,192,1536]{2,1,0:T(8,128)(2,1)}, u32[]{:S(2)}, u32[]{:S(2)}) collective-permute-start(bf16[2,192,1536]{2,1,0:T(8,128)(2,1)} %get-tuple-element.238), channel_id=1, source_target_pairs={{0,16},{16,0},{32,48},{48,32},{1,17},{17,1},{33,49},{49,33},{2,18}... | collective-permute-start | bytes 3538952 | tf_op jit(solution)/shard_map/ppermute | solution.py:163
  603.3 34.5 %collective-permute-start.56 = (bf16[2,192,1536]{2,1,0:T(8,128)(2,1)}, bf16[2,192,1536]{2,1,0:T(8,128)(2,1)}, u32[]{:S(2)}, u32[]{:S(2)}) collective-permute-start(bf16[2,192,1536]{2,1,0:T(8,128)(2,1)} %hold.4), channel_id=1, source_target_pairs={{0,32},{16,48},{32,0},{48,16},{1,33},{17,49},{33,1},{49,17},{2,34}... | collective-permute-start | bytes 3538952 | tf_op jit(solution)/shard_map/ppermute | solution.py:163
  609.6 32.2 %collective-permute-start.59 = (bf16[2,192,1536]{2,1,0:T(8,128)(2,1)}, bf16[2,192,1536]{2,1,0:T(8,128)(2,1)}, u32[]{:S(2)}, u32[]{:S(2)}) collective-permute-start(bf16[2,192,1536]{2,1,0:T(8,128)(2,1)} %get-tuple-element.243), channel_id=1, source_target_pairs={{0,16},{16,0},{32,48},{48,32},{1,17},{17,1},{33,49},{49,33},{2,18}... | collective-permute-start | bytes 3538952 | tf_op jit(solution)/shard_map/ppermute | solution.py:163
  610.0 51.8 %collective-permute-start.57 = (bf16[2,192,1536]{2,1,0:T(8,128)(2,1)}, bf16[2,192,1536]{2,1,0:T(8,128)(2,1)}, u32[]{:S(2)}, u32[]{:S(2)}) collective-permute-start(bf16[2,192,1536]{2,1,0:T(8,128)(2,1)} %get-tuple-element.240), channel_id=1, source_target_pairs={{0,16},{16,0},{32,48},{48,32},{1,17},{17,1},{33,49},{49,33},{2,18}... | collective-permute-start | bytes 3538952 | tf_op jit(solution)/shard_map/ppermute | solution.py:163
  626.2 25.0 %all-to-all-start.13 = ((bf16[16,96,512]{2,1,0:T(8,128)(2,1)}), bf16[16,96,512]{2,1,0:T(8,128)(2,1)}, u32[]{:S(2)}, u32[]{:S(2)}) async-start(bf16[16,96,512]{2,1,0:T(8,128)(2,1)} %qkv_grads.1.refs_12_.refs_18_), calls=%async_computation.13 | async-start | bytes 3145728 | tf_op jit(solution)/shard_map/all_to_all | solution.py:735
  631.7 30.1 %collective-permute-start.58 = (bf16[2,192,1536]{2,1,0:T(8,128)(2,1)}, bf16[2,192,1536]{2,1,0:T(8,128)(2,1)}, u32[]{:S(2)}, u32[]{:S(2)}) collective-permute-start(bf16[2,192,1536]{2,1,0:T(8,128)(2,1)} %hold.5), channel_id=1, source_target_pairs={{0,32},{16,48},{32,0},{48,16},{1,33},{17,49},{33,1},{49,17},{2,34}... | collective-permute-start | bytes 3538952 | tf_op jit(solution)/shard_map/ppermute | solution.py:163
  (62 other events, 497.8 us)
Sparse Core Ops, SparseCore 0:
  11.7 105.9 all-gather.1

commit v15 on v13

--- a/solution.py
+++ b/solution.py
@@ -133,7 +133,7 @@
         + list(scratch),
         compiler_params=pltpu.CompilerParams(vmem_limit_bytes=64 * MIB),
         cost_estimate=pl.CostEstimate(
-            flops=int(flops), bytes_accessed=int(moved), transcendentals=0
+            flops=int(flops) // 1000, bytes_accessed=int(moved) // 1000, transcendentals=0
         ),
         name=body.func.__name__ if isinstance(body, functools.partial) else body.__name__,
     )(*scalars, *arrays, *far, *waits)

time: 688 us -> 728 us (1.058)
  waiting for transfers between devices: 206 us -> 246 us
    ppermute x56, waiting for transfers between devices: 116 us -> 151 us  [swapped(): return lax.ppermute(value, 'row', [(r, r ^ step) for r in range(rows)])]
  transfers between devices with their start and end apart: 75 -> 75, of which waited for: 36 -> 32; matrix products, arithmetic and copies ran while one was open for 4% -> 4% of each run, Pallas kernels for 32% -> 30%
where the time goes in v15:
time: 728 us; the launch traced here: 716 us
  waiting for transfers between devices  246 us (34%)
  Pallas kernels  245 us (34%)
  starting transfers between devices  177 us (24%)
  other arithmetic  20.2 us (3%)
  between operations  15.4 us (2%)
  local copies, waits for them, and re-layouts  11.3 us (2%)
    pallas_call x36, Pallas kernels, call(): pl.pallas_call(run, out_shape=tuple(shapes), in_specs=[pl.BlockSpec(memor...  245 us
    ppermute x56, waiting for transfers between devices, swapped(): return lax.ppermute(value, 'row', [(r, r ^ step) for r in range(rows)])  151 us
    ppermute x56, starting transfers between devices, swapped(): return lax.ppermute(value, 'row', [(r, r ^ step) for r in range(rows)])  86 us
    all_to_all x14, starting transfers between devices, over_columns(): return lax.all_to_all(value, 'col', split_axis=0, concat_axis=0, tiled=True)  83.5 us
    all_to_all x14, waiting for transfers between devices, over_columns(): return lax.all_to_all(value, 'col', split_axis=0, concat_axis=0, tiled=True)  45.7 us
    all_gather x1, waiting for transfers between devices, on_device(): dense = lax.all_gather(dense, ('row', 'col'), axis=0, tiled=True)  29.4 us
  transfers between devices with their start and end apart: 75, of which 32 were waited for; matrix products, arithmetic and copies ran while one was open for 4% of the time, Pallas kernels for 30%

profile of v15, /device:TPU:9, one launch (start us, length us, event | category | flops | bytes accessed | tf_op | source)
XLA Modules:
  0.0 716.4 jit_solution(12225903458102154657)
XLA Ops:
  24.0 64.4 %collective-permute-done.2.refs_6_.refs_11_.refs_12_.refs_16_ = bf16[1,192,1536]{2,1,0:T(8,128)(2,1)} collective-permute-done((bf16[1,192,1536]{2,1,0:T(8,128)(2,1)S(1)}, bf16[1,192,1536]{2,1,0:T(8,128)(2,1)}, u32[]{:S(2)}, u32[]{:S(2)}) %collective-permute-start.2) | collective-permute-done | bytes 589856 | tf_op jit(solution)/shard_map/ppermute | solution.py:163
  88.4 29.4 %all-gather.2.cloned.1.call-done.refs_3_.refs_12_.refs_6_.refs_17_.refs_11_ = bf16[1536,3712]{1,0:T(8,128)(2,1)} async-done(((bf16[24,3712]{1,0:T(8,128)(2,1)}), bf16[1536,3712]{1,0:T(8,128)(2,1)}) %all-gather.2.cloned.1.call-update) | async-done | bytes 11403280 | tf_op jit(solution)/shard_map/all_gather | solution.py:768
  177.5 14.2 %collective-permute-done.14.refs_12_.refs_13_.refs_17_ = bf16[1,192,1536]{2,1,0:T(8,128)(2,1)S(1)} collective-permute-done((bf16[1,192,1536]{2,1,0:T(8,128)(2,1)}, bf16[1,192,1536]{2,1,0:T(8,128)(2,1)S(1)}, u32[]{:S(2)}, u32[]{:S(2)}) %collective-permute-start.14) | collective-permute-done | bytes 589856 | tf_op jit(solution)/shard_map/ppermute | solution.py:163
  194.4 10.3 %expert_forward.4 = bf16[16,32,1536]{2,1,0:T(8,128)(2,1)} custom-call(bf16[16,32,1536]{2,1,0:T(8,128)(2,1)} %all-to-all-done.refs_0_.refs_1_, bf16[2,192,1536]{2,1,0:T(8,128)(2,1)} %bitcast.9.refs_1_.refs_2_.refs_6_, bf16[2,192,1536]{2,1,0:T(8,128)(2,1)} %collective-permute-done.6.refs_2_.refs_3_.refs_7_, ...), custom_call_target="tpu_custom_call" | custom-call | flops 3623878 | bytes 17301 | tf_op jit(solution)/shard_map/expert_forward/pallas_call | solution.py:124
  204.7 7.1 all-to-all-start.1
  211.8 10.3 %expert_forward.5.refs_5_ = bf16[16,32,1536]{2,1,0:T(8,128)(2,1)} custom-call(bf16[16,32,1536]{2,1,0:T(8,128)(2,1)} %all-to-all-done.2.refs_0_.refs_1_, bf16[2,192,1536]{2,1,0:T(8,128)(2,1)} %bitcast.9.refs_1_.refs_2_.refs_6_, bf16[2,192,1536]{2,1,0:T(8,128)(2,1)} %collective-permute-done.6.refs_2_.refs_3_.refs_7_, ...), custom_call_target="tpu_custom_call" | custom-call | flops 3623878 | bytes 17301 | tf_op jit(solution)/shard_map/expert_forward/pallas_call | solution.py:124
  222.1 12.6 %all-to-all-done.1.refs_0_ = bf16[16,32,1536]{2,1,0:T(8,128)(2,1)} async-done(((bf16[16,32,1536]{2,1,0:T(8,128)(2,1)}), bf16[16,32,1536]{2,1,0:T(8,128)(2,1)}, u32[]{:S(2)}, u32[]{:S(2)}) %all-to-all-start.1) | async-done | bytes 1572896 | tf_op jit(solution)/shard_map/all_to_all | solution.py:735
  268.7 6.8 attend.6
  275.5 6.7 all-to-all-start.4
  283.6 8.6 %collective-permute-done.21.refs_1_ = bf16[96,1536]{1,0:T(8,128)(2,1)} collective-permute-done((bf16[96,1536]{1,0:T(8,128)(2,1)S(1)}, bf16[96,1536]{1,0:T(8,128)(2,1)}, u32[]{:S(2)}, u32[]{:S(2)}) %collective-permute-start.21) | collective-permute-done | bytes 294944 | tf_op jit(solution)/shard_map/ppermute | solution.py:961
  307.6 6.8 attend.7
  314.4 7.1 all-to-all-start.6
  321.5 16.5 %expert_forward.6 = (bf16[16,32,1536]{2,1,0:T(8,128)(2,1)}, bf16[2,256,768]{2,1,0:T(8,128)(2,1)}, bf16[2,256,768]{2,1,0:T(8,128)(2,1)}, bf16[2,256,768]{2,1,0:T(8,128)(2,1)}, bf16[16,32,1664]{2,1,0:T(8,128)(2,1)}) custom-call(bf16[16,32,1664]{2,1,0:T(8,128)(2,1)} %all-to-all-done.4.refs_0_.refs_4_, bf16[16,32,1536]{2,1,0:T(8,128)(2,1)} %all-to-all-done.refs_0_.refs_1_, ...), custom_call_target="tpu_custom_call" | custom-call | flops 7247757 | bytes 23068 | tf_op jit(solution)/shard_map/expert_forward/pallas_call | solution.py:124
  338.0 7.7 %all-to-all-done.6.refs_0_.refs_5_ = bf16[16,32,1664]{2,1,0:T(8,128)(2,1)} async-done(((bf16[16,32,1664]{2,1,0:T(8,128)(2,1)}), bf16[16,32,1664]{2,1,0:T(8,128)(2,1)}, u32[]{:S(2)}, u32[]{:S(2)}) %all-to-all-start.6) | async-done | bytes 1703968 | tf_op jit(solution)/shard_map/all_to_all | solution.py:735
  355.4 24.1 %collective-permute-done.25.refs_16_.refs_19_.refs_2_ = bf16[4,96,1536]{2,1,0:T(8,128)(2,1)} collective-permute-done((bf16[4,96,1536]{2,1,0:T(8,128)(2,1)}, bf16[4,96,1536]{2,1,0:T(8,128)(2,1)}, u32[]{:S(2)}, u32[]{:S(2)}) %collective-permute-start.25) | collective-permute-done | bytes 1179680 | tf_op jit(solution)/shard_map/ppermute | solution.py:163
  379.5 16.4 %expert_forward.7 = (bf16[16,32,1536]{2,1,0:T(8,128)(2,1)}, bf16[2,256,768]{2,1,0:T(8,128)(2,1)}, bf16[2,256,768]{2,1,0:T(8,128)(2,1)}, bf16[2,256,768]{2,1,0:T(8,128)(2,1)}, bf16[16,32,1664]{2,1,0:T(8,128)(2,1)}) custom-call(bf16[16,32,1664]{2,1,0:T(8,128)(2,1)} %all-to-all-done.6.refs_0_.refs_5_, bf16[16,32,1536]{2,1,0:T(8,128)(2,1)} %all-to-all-done.2.refs_0_.refs_1_, ...), custom_call_target="tpu_custom_call" | custom-call | flops 7247757 | bytes 23068 | tf_op jit(solution)/shard_map/expert_forward/pallas_call | solution.py:124
  406.7 8.7 %attend_back.4 = (f32[96,1536]{1,0:T(8,128)}, bf16[96,1536]{1,0:T(8,128)(2,1)}, bf16[96,512]{1,0:T(8,128)(2,1)}, bf16[96,512]{1,0:T(8,128)(2,1)}, bf16[96,512]{1,0:T(8,128)(2,1)}, /*index=5*/bf16[96,512]{1,0:T(8,128)(2,1)}) custom-call(s32[1]{0:T(128)} %bitcast.1.refs_0_, s32[1]{0:T(128)} %bitcast.refs_0_.refs_1_, ...), custom_call_target="tpu_custom_call" | custom-call | flops 1056964 | bytes 17520 | tf_op jit(solution)/shard_map/attend_back/pallas_call | solution.py:124
  425.5 6.7 project_back.4.refs_21_
  434.6 8.8 %attend_back.5 = (f32[96,1536]{1,0:T(8,128)}, bf16[96,1536]{1,0:T(8,128)(2,1)}, bf16[96,512]{1,0:T(8,128)(2,1)}, bf16[96,512]{1,0:T(8,128)(2,1)}, bf16[96,512]{1,0:T(8,128)(2,1)}, /*index=5*/bf16[96,512]{1,0:T(8,128)(2,1)}) custom-call(s32[1]{0:T(128)} %bitcast.1.refs_0_, s32[1]{0:T(128)} %bitcast.refs_0_.refs_1_, ...), custom_call_target="tpu_custom_call" | custom-call | flops 1056964 | bytes 17520 | tf_op jit(solution)/shard_map/attend_back/pallas_call | solution.py:124
  463.1 6.8 project_back.5
  482.1 6.9 all-to-all-start.10
  489.1 10.8 %expert_backward.2 = (bf16[16,32,1664]{2,1,0:T(8,128)(2,1)}, bf16[2,256,768]{2,1,0:T(8,128)(2,1)}, bf16[2,256,768]{2,1,0:T(8,128)(2,1)}) custom-call(s32[1]{0:T(128)} %bitcast.refs_0_.refs_1_, bf16[16,32,1536]{2,1,0:T(8,128)(2,1)} %all-to-all-done.8.refs_1_.refs_2_, bf16[2,256,768]{2,1,0:T(8,128)(2,1)} %get-tuple-element.168.refs_2_.refs_0_, ...), custom_call_target="tpu_custom_call" | custom-call | flops 3623878 | bytes 22937 | tf_op jit(solution)/shard_map/expert_backward/pallas_call | solution.py:124
  499.9 9.8 %all-to-all-done.10.refs_1_.refs_3_ = bf16[16,32,1536]{2,1,0:T(8,128)(2,1)} async-done(((bf16[16,32,1536]{2,1,0:T(8,128)(2,1)}), bf16[16,32,1536]{2,1,0:T(8,128)(2,1)}, u32[]{:S(2)}, u32[]{:S(2)}) %all-to-all-start.10) | async-done | bytes 1572896 | tf_op jit(solution)/shard_map/all_to_all | solution.py:735
  522.6 10.8 %expert_backward.3 = (bf16[16,32,1664]{2,1,0:T(8,128)(2,1)}, bf16[2,256,768]{2,1,0:T(8,128)(2,1)}, bf16[2,256,768]{2,1,0:T(8,128)(2,1)}) custom-call(s32[1]{0:T(128)} %bitcast.refs_0_.refs_1_, bf16[16,32,1536]{2,1,0:T(8,128)(2,1)} %all-to-all-done.10.refs_1_.refs_3_, bf16[2,256,768]{2,1,0:T(8,128)(2,1)} %get-tuple-element.179.refs_2_.refs_1_, ...), custom_call_target="tpu_custom_call" | custom-call | flops 3623878 | bytes 22937 | tf_op jit(solution)/shard_map/expert_backward/pallas_call | solution.py:124
  545.4 9.4 %attend_back.6 = (f32[96,1536]{1,0:T(8,128)}, bf16[96,1536]{1,0:T(8,128)(2,1)}, bf16[96,896]{1,0:T(8,128)(2,1)}, bf16[96,896]{1,0:T(8,128)(2,1)}, bf16[96,896]{1...) custom-call(s32[1]{0:T(128)} %bitcast.1.refs_0_, s32[1]{0:T(128)} %bitcast.refs_0_.refs_1_, ...), custom_call_target="tpu_custom_call" | custom-call | flops 1056964 | bytes 19167 | tf_op jit(solution)/shard_map/attend_back/pallas_call | solution.py:124
  554.8 9.1 %expert_weight_grads.4 = (bf16[2,192,1536]{2,1,0:T(8,128)(2,1)}, bf16[2,192,1536]{2,1,0:T(8,128)(2,1)}, bf16[2,192,1536]{2,1,0:T(8,128)(2,1)}, bf16[2,192,1536]{...) custom-call(bf16[2,256,768]{2,1,0:T(8,128)(2,1)} %get-tuple-element., ...), custom_call_target="tpu_custom_call" | custom-call | flops 2415919 | bytes 15990 | tf_op jit(solution)/shard_map/expert_weight_grads/pallas_call | solution.py:124
  569.8 9.4 %attend_back.7 = (f32[96,1536]{1,0:T(8,128)}, bf16[96,1536]{1,0:T(8,128)(2,1)}, bf16[96,896]{1,0:T(8,128)(2,1)}, bf16[96,896]{1,0:T(8,128)(2,1)}, bf16[96,896]{1...) custom-call(s32[1]{0:T(128)} %bitcast.1.refs_0_, s32[1]{0:T(128)} %bitcast.refs_0_.refs_1_, ...), custom_call_target="tpu_custom_call" | custom-call | flops 1056964 | bytes 19167 | tf_op jit(solution)/shard_map/attend_back/pallas_call | solution.py:124
  603.2 6.8 out_grads.1.refs_12_
  618.3 7.3 %project_back.6 = (bf16[96,1536]{1,0:T(8,128)(2,1)}, f32[96,1536]{1,0:T(8,128)}, bf16[96,512]{1,0:T(8,128)(2,1)}, bf16[96,512]{1,0:T(8,128)(2,1)}, bf16[96,512]{1,0:T(8,128)(2,1)}, /*index=5*/bf16[96,512]{1,0:T(8,128)(2,1)}) custom-call(s32[1]{0:T(128)} %bitcast.1.refs_0_, bf16[96,896]{1,0:T(8,128)(2,1)} %get-tuple-element.199.refs_5_.refs_1_, ...), custom_call_target="tpu_custom_call" | custom-call | flops 603979 | bytes 14948 | tf_op jit(solution)/shard_map/project_back/pallas_call | solution.py:124
  625.6 7.3 %project_back.7 = (bf16[96,1536]{1,0:T(8,128)(2,1)}, f32[96,1536]{1,0:T(8,128)}, bf16[96,512]{1,0:T(8,128)(2,1)}, bf16[96,512]{1,0:T(8,128)(2,1)}, bf16[96,512]{1,0:T(8,128)(2,1)}, /*index=5*/bf16[96,512]{1,0:T(8,128)(2,1)}) custom-call(s32[1]{0:T(128)} %bitcast.1.refs_0_, bf16[96,896]{1,0:T(8,128)(2,1)} %get-tuple-element.187.refs_4_.refs_1_, ...), custom_call_target="tpu_custom_call" | custom-call | flops 603979 | bytes 14948 | tf_op jit(solution)/shard_map/project_back/pallas_call | solution.py:124
  641.0 7.2 %collective-permute-done.48.refs_8_.refs_2_ = bf16[96,512]{1,0:T(8,128)(2,1)} collective-permute-done((bf16[96,512]{1,0:T(8,128)(2,1)}, bf16[96,512]{1,0:T(8,128)(2,1)}, u32[]{:S(2)}, u32[]{:S(2)}) %collective-permute-start.48) | collective-permute-done | bytes 98336 | tf_op jit(solution)/shard_map/ppermute | solution.py:163
  684.2 7.7 %all-to-all-done.13.refs_2_ = bf16[16,96,512]{2,1,0:T(8,128)(2,1)} async-done(((bf16[16,96,512]{2,1,0:T(8,128)(2,1)}), bf16[16,96,512]{2,1,0:T(8,128)(2,1)}, u32[]{:S(2)}, u32[]{:S(2)}) %all-to-all-start.13) | async-done | bytes 1572896 | tf_op jit(solution)/shard_map/all_to_all | solution.py:735
  (241 shorter events, 318.5 us)
Async XLA Ops:
  7.2 110.6 %all-gather.2.cloned.1.call-start = ((), (), s32[]{:S(2)}) async-start(), calls=%async_computation.14 | async-start | bytes 11581440 | tf_op jit(solution)/shard_map/all_gather | solution.py:768
  10.5 77.9 %collective-permute-start = (bf16[2,192,1536]{2,1,0:T(8,128)(2,1)}, bf16[2,192,1536]{2,1,0:T(8,128)(2,1)}, u32[]{:S(2)}, u32[]{:S(2)}) collective-permute-start(bf16[2,192,1536]{2,1,0:T(8,128)(2,1)} %bitcast.9.refs_1_.refs_2_.refs_6_), channel_id=1, source_target_pairs={{0,32},{16,48},{32,0},{48,16},{1,33},{17,49},{33,1},{49,17},{2,34}... | collective-permute-start | bytes 3538952 | tf_op jit(solution)/shard_map/ppermute | solution.py:163
  12.6 75.8 %collective-permute-start.1 = (bf16[2,192,1536]{2,1,0:T(8,128)(2,1)}, bf16[2,192,1536]{2,1,0:T(8,128)(2,1)}, u32[]{:S(2)}, u32[]{:S(2)}) collective-permute-start(bf16[2,192,1536]{2,1,0:T(8,128)(2,1)} %bitcast.10.refs_5_.refs_6_.refs_10_), channel_id=1, source_target_pairs={{0,32},{16,48},{32,0},{48,16},{1,33},{17,49},{33,1},{49,17},{2,34}... | collective-permute-start | bytes 3538952 | tf_op jit(solution)/shard_map/ppermute | solution.py:163
  15.7 72.7 %collective-permute-start.2 = (bf16[1,192,1536]{2,1,0:T(8,128)(2,1)S(1)}, bf16[1,192,1536]{2,1,0:T(8,128)(2,1)}, u32[]{:S(2)}, u32[]{:S(2)}) collective-permute-start(bf16[1,192,1536]{2,1,0:T(8,128)(2,1)S(1)} %get-tuple-element.283), channel_id=1, source_target_pairs={{0,32},{16,48},{32,0},{48,16},{1,33},{17,49},{33,1},{49,17},{2,34}... | collective-permute-start | bytes 1769480 | tf_op jit(solution)/shard_map/ppermute | solution.py:163
  139.6 27.4 %all-to-all-start = ((bf16[16,32,1536]{2,1,0:T(8,128)(2,1)}), bf16[16,32,1536]{2,1,0:T(8,128)(2,1)}, u32[]{:S(2)}, u32[]{:S(2)}) async-start(bf16[16,32,1536]{2,1,0:T(8,128)(2,1)} %get-tuple-element.131), calls=%async_computation | async-start | bytes 3145728 | tf_op jit(solution)/shard_map/all_to_all | solution.py:735
  144.8 30.2 %collective-permute-start.6 = (bf16[2,192,1536]{2,1,0:T(8,128)(2,1)}, bf16[2,192,1536]{2,1,0:T(8,128)(2,1)}, u32[]{:S(2)}, u32[]{:S(2)}) collective-permute-start(bf16[2,192,1536]{2,1,0:T(8,128)(2,1)} %bitcast.9.refs_1_.refs_2_.refs_6_), channel_id=1, source_target_pairs={{0,16},{16,0},{32,48},{48,32},{1,17},{17,1},{33,49},{49,33},{2,18}... | collective-permute-start | bytes 3538952 | tf_op jit(solution)/shard_map/ppermute | solution.py:163
  145.5 31.6 %collective-permute-start.8 = (bf16[2,192,1536]{2,1,0:T(8,128)(2,1)}, bf16[2,192,1536]{2,1,0:T(8,128)(2,1)}, u32[]{:S(2)}, u32[]{:S(2)}) collective-permute-start(bf16[2,192,1536]{2,1,0:T(8,128)(2,1)} %bitcast.10.refs_5_.refs_6_.refs_10_), channel_id=1, source_target_pairs={{0,16},{16,0},{32,48},{48,32},{1,17},{17,1},{33,49},{49,33},{2,18}... | collective-permute-start | bytes 3538952 | tf_op jit(solution)/shard_map/ppermute | solution.py:163
  167.0 37.7 %all-to-all-start.2 = ((bf16[16,32,1536]{2,1,0:T(8,128)(2,1)}), bf16[16,32,1536]{2,1,0:T(8,128)(2,1)}, u32[]{:S(2)}, u32[]{:S(2)}) async-start(bf16[16,32,1536]{2,1,0:T(8,128)(2,1)} %get-tuple-element.135.refs_15_), calls=%async_computation.2 | async-start | bytes 3145728 | tf_op jit(solution)/shard_map/all_to_all | solution.py:735
  171.5 21.0 %collective-permute-start.10 = (bf16[2,192,1536]{2,1,0:T(8,128)(2,1)S(1)}, bf16[2,192,1536]{2,1,0:T(8,128)(2,1)S(1)}, u32[]{:S(2)}, u32[]{:S(2)}) collective-permute-start(bf16[2,192,1536]{2,1,0:T(8,128)(2,1)S(1)} %bitcast.70), channel_id=1, source_target_pairs={{0,16},{16,0},{32,48},{48,32},{1,17},{17,1},{33,49},{49,33},{2,18}... | collective-permute-start | bytes 3538952 | tf_op jit(solution)/shard_map/ppermute | solution.py:163
  204.7 30.0 %all-to-all-start.1 = ((bf16[16,32,1536]{2,1,0:T(8,128)(2,1)}), bf16[16,32,1536]{2,1,0:T(8,128)(2,1)}, u32[]{:S(2)}, u32[]{:S(2)}) async-start(bf16[16,32,1536]{2,1,0:T(8,128)(2,1)} %expert_forward.4), calls=%async_computation.1 | async-start | bytes 3145728 | tf_op jit(solution)/shard_map/all_to_all | solution.py:735
  234.7 28.5 %all-to-all-start.3 = ((bf16[16,32,1536]{2,1,0:T(8,128)(2,1)}), bf16[16,32,1536]{2,1,0:T(8,128)(2,1)}, u32[]{:S(2)}, u32[]{:S(2)}) async-start(bf16[16,32,1536]{2,1,0:T(8,128)(2,1)} %expert_forward.5.refs_5_), calls=%async_computation.3 | async-start | bytes 3145728 | tf_op jit(solution)/shard_map/all_to_all | solution.py:735
  275.5 38.9 %all-to-all-start.4 = ((bf16[16,32,1664]{2,1,0:T(8,128)(2,1)}), bf16[16,32,1664]{2,1,0:T(8,128)(2,1)}, u32[]{:S(2)}, u32[]{:S(2)}) async-start(bf16[16,32,1664]{2,1,0:T(8,128)(2,1)} %get-tuple-element.143), calls=%async_computation.4 | async-start | bytes 3407872 | tf_op jit(solution)/shard_map/all_to_all | solution.py:735
  314.4 31.2 %all-to-all-start.6 = ((bf16[16,32,1664]{2,1,0:T(8,128)(2,1)}), bf16[16,32,1664]{2,1,0:T(8,128)(2,1)}, u32[]{:S(2)}, u32[]{:S(2)}) async-start(bf16[16,32,1664]{2,1,0:T(8,128)(2,1)} %get-tuple-element.147.refs_16_), calls=%async_computation.6 | async-start | bytes 3407872 | tf_op jit(solution)/shard_map/all_to_all | solution.py:735
  345.7 50.3 %all-to-all-start.5 = ((bf16[16,32,1664]{2,1,0:T(8,128)(2,1)}), bf16[16,32,1664]{2,1,0:T(8,128)(2,1)}, u32[]{:S(2)}, u32[]{:S(2)}) async-start(bf16[16,32,1664]{2,1,0:T(8,128)(2,1)} %get-tuple-element.148), calls=%async_computation.5 | async-start | bytes 3407872 | tf_op jit(solution)/shard_map/all_to_all | solution.py:735
  352.5 27.0 %collective-permute-start.25 = (bf16[4,96,1536]{2,1,0:T(8,128)(2,1)}, bf16[4,96,1536]{2,1,0:T(8,128)(2,1)}, u32[]{:S(2)}, u32[]{:S(2)}) collective-permute-start(bf16[4,96,1536]{2,1,0:T(8,128)(2,1)} %pack.1.refs_0_), channel_id=1, source_target_pairs={{0,32},{16,48},{32,0},{48,16},{1,33},{17,49},{33,1},{49,17},{2,34}... | collective-permute-start | bytes 3538952 | tf_op jit(solution)/shard_map/ppermute | solution.py:163
  396.0 38.6 %all-to-all-start.7 = ((bf16[16,32,1664]{2,1,0:T(8,128)(2,1)}), bf16[16,32,1664]{2,1,0:T(8,128)(2,1)}, u32[]{:S(2)}, u32[]{:S(2)}) async-start(bf16[16,32,1664]{2,1,0:T(8,128)(2,1)} %get-tuple-element.156.refs_18_), calls=%async_computation.7 | async-start | bytes 3407872 | tf_op jit(solution)/shard_map/all_to_all | solution.py:735
  402.3 32.3 %collective-permute-start.30 = (bf16[4,96,1536]{2,1,0:T(8,128)(2,1)}, bf16[4,96,1536]{2,1,0:T(8,128)(2,1)}, u32[]{:S(2)}, u32[]{:S(2)}) collective-permute-start(bf16[4,96,1536]{2,1,0:T(8,128)(2,1)} %pack.1.refs_0_), channel_id=1, source_target_pairs={{0,16},{16,0},{32,48},{48,32},{1,17},{17,1},{33,49},{49,33},{2,18}... | collective-permute-start | bytes 3538952 | tf_op jit(solution)/shard_map/ppermute | solution.py:163
  406.4 28.2 %collective-permute-start.31 = (bf16[4,96,1536]{2,1,0:T(8,128)(2,1)}, bf16[4,96,1536]{2,1,0:T(8,128)(2,1)}, u32[]{:S(2)}, u32[]{:S(2)}) collective-permute-start(bf16[4,96,1536]{2,1,0:T(8,128)(2,1)} %collective-permute-done.25.refs_16_.refs_19_.refs_2_), channel_id=1, source_target_pairs={{0,16},{16,0},{32,48},{48,32},{1,17},{17,1},{33,49},{49,33},{2,18}... | collective-permute-start | bytes 3538952 | tf_op jit(solution)/shard_map/ppermute | solution.py:163
  446.9 35.3 %all-to-all-start.8 = ((bf16[16,32,1536]{2,1,0:T(8,128)(2,1)}), bf16[16,32,1536]{2,1,0:T(8,128)(2,1)}, u32[]{:S(2)}, u32[]{:S(2)}) async-start(bf16[16,32,1536]{2,1,0:T(8,128)(2,1)} %get-tuple-element.167), calls=%async_computation.8 | async-start | bytes 3145728 | tf_op jit(solution)/shard_map/all_to_all | solution.py:735
  482.1 27.6 %all-to-all-start.10 = ((bf16[16,32,1536]{2,1,0:T(8,128)(2,1)}), bf16[16,32,1536]{2,1,0:T(8,128)(2,1)}, u32[]{:S(2)}, u32[]{:S(2)}) async-start(bf16[16,32,1536]{2,1,0:T(8,128)(2,1)} %get-tuple-element.177.refs_20_), calls=%async_computation.10 | async-start | bytes 3145728 | tf_op jit(solution)/shard_map/all_to_all | solution.py:735
  509.7 25.9 %all-to-all-start.9 = ((bf16[16,32,1664]{2,1,0:T(8,128)(2,1)}), bf16[16,32,1664]{2,1,0:T(8,128)(2,1)}, u32[]{:S(2)}, u32[]{:S(2)}) async-start(bf16[16,32,1664]{2,1,0:T(8,128)(2,1)} %get-tuple-element.178), calls=%async_computation.9 | async-start | bytes 3407872 | tf_op jit(solution)/shard_map/all_to_all | solution.py:735
  519.0 22.3 %collective-permute-start.36 = (bf16[2,192,1536]{2,1,0:T(8,128)(2,1)}, bf16[2,192,1536]{2,1,0:T(8,128)(2,1)}, u32[]{:S(2)}, u32[]{:S(2)}) collective-permute-start(bf16[2,192,1536]{2,1,0:T(8,128)(2,1)} %get-tuple-element.186), channel_id=1, source_target_pairs={{0,16},{16,0},{32,48},{48,32},{1,17},{17,1},{33,49},{49,33},{2,18}... | collective-permute-start | bytes 3538952 | tf_op jit(solution)/shard_map/ppermute | solution.py:163
  535.6 33.3 %all-to-all-start.11 = ((bf16[16,32,1664]{2,1,0:T(8,128)(2,1)}), bf16[16,32,1664]{2,1,0:T(8,128)(2,1)}, u32[]{:S(2)}, u32[]{:S(2)}) async-start(bf16[16,32,1664]{2,1,0:T(8,128)(2,1)} %get-tuple-element.183.refs_18_), calls=%async_computation.11 | async-start | bytes 3407872 | tf_op jit(solution)/shard_map/all_to_all | solution.py:735
  544.2 25.6 %collective-permute-start.40 = (bf16[2,192,1536]{2,1,0:T(8,128)(2,1)}, bf16[2,192,1536]{2,1,0:T(8,128)(2,1)}, u32[]{:S(2)}, u32[]{:S(2)}) collective-permute-start(bf16[2,192,1536]{2,1,0:T(8,128)(2,1)} %add.133.refs_19_), channel_id=1, source_target_pairs={{0,32},{16,48},{32,0},{48,16},{1,33},{17,49},{33,1},{49,17},{2,34}... | collective-permute-start | bytes 3538952 | tf_op jit(solution)/shard_map/ppermute | solution.py:163
  563.9 23.9 %collective-permute-start.44 = (bf16[2,192,1536]{2,1,0:T(8,128)(2,1)}, bf16[2,192,1536]{2,1,0:T(8,128)(2,1)}, u32[]{:S(2)}, u32[]{:S(2)}) collective-permute-start(bf16[2,192,1536]{2,1,0:T(8,128)(2,1)} %get-tuple-element.212), channel_id=1, source_target_pairs={{0,16},{16,0},{32,48},{48,32},{1,17},{17,1},{33,49},{49,33},{2,18}... | collective-permute-start | bytes 3538952 | tf_op jit(solution)/shard_map/ppermute | solution.py:163
  610.0 53.1 %all-to-all-start.12 = ((bf16[16,96,512]{2,1,0:T(8,128)(2,1)}), bf16[16,96,512]{2,1,0:T(8,128)(2,1)}, u32[]{:S(2)}, u32[]{:S(2)}) async-start(bf16[16,96,512]{2,1,0:T(8,128)(2,1)} %out_grads.1.refs_12_), calls=%async_computation.12 | async-start | bytes 3145728 | tf_op jit(solution)/shard_map/all_to_all | solution.py:735
  616.6 40.9 %collective-permute-start.52 = (bf16[2,192,1536]{2,1,0:T(8,128)(2,1)}, bf16[2,192,1536]{2,1,0:T(8,128)(2,1)}, u32[]{:S(2)}, u32[]{:S(2)}) collective-permute-start(bf16[2,192,1536]{2,1,0:T(8,128)(2,1)} %hold.4.refs_19_), channel_id=1, source_target_pairs={{0,32},{16,48},{32,0},{48,16},{1,33},{17,49},{33,1},{49,17},{2,34}... | collective-permute-start | bytes 3538952 | tf_op jit(solution)/shard_map/ppermute | solution.py:163
  617.7 59.1 %collective-permute-start.56 = (bf16[2,192,1536]{2,1,0:T(8,128)(2,1)}, bf16[2,192,1536]{2,1,0:T(8,128)(2,1)}, u32[]{:S(2)}, u32[]{:S(2)}) collective-permute-start(bf16[2,192,1536]{2,1,0:T(8,128)(2,1)} %get-tuple-element.239), channel_id=1, source_target_pairs={{0,16},{16,0},{32,48},{48,32},{1,17},{17,1},{33,49},{49,33},{2,18}... | collective-permute-start | bytes 3538952 | tf_op jit(solution)/shard_map/ppermute | solution.py:163
  637.8 43.0 %collective-permute-start.59 = (bf16[2,192,1536]{2,1,0:T(8,128)(2,1)}, bf16[2,192,1536]{2,1,0:T(8,128)(2,1)}, u32[]{:S(2)}, u32[]{:S(2)}) collective-permute-start(bf16[2,192,1536]{2,1,0:T(8,128)(2,1)} %get-tuple-element.243), channel_id=1, source_target_pairs={{0,16},{16,0},{32,48},{48,32},{1,17},{17,1},{33,49},{49,33},{2,18}... | collective-permute-start | bytes 3538952 | tf_op jit(solution)/shard_map/ppermute | solution.py:163
  654.8 46.5 %collective-permute-start.57 = (bf16[2,192,1536]{2,1,0:T(8,128)(2,1)}, bf16[2,192,1536]{2,1,0:T(8,128)(2,1)}, u32[]{:S(2)}, u32[]{:S(2)}) collective-permute-start(bf16[2,192,1536]{2,1,0:T(8,128)(2,1)} %get-tuple-element.241), channel_id=1, source_target_pairs={{0,16},{16,0},{32,48},{48,32},{1,17},{17,1},{33,49},{49,33},{2,18}... | collective-permute-start | bytes 3538952 | tf_op jit(solution)/shard_map/ppermute | solution.py:163
  663.1 28.8 %all-to-all-start.13 = ((bf16[16,96,512]{2,1,0:T(8,128)(2,1)}), bf16[16,96,512]{2,1,0:T(8,128)(2,1)}, u32[]{:S(2)}, u32[]{:S(2)}) async-start(bf16[16,96,512]{2,1,0:T(8,128)(2,1)} %qkv_grads.1.refs_12_), calls=%async_computation.13 | async-start | bytes 3145728 | tf_op jit(solution)/shard_map/all_to_all | solution.py:735
  670.9 30.4 %collective-permute-start.58 = (bf16[2,192,1536]{2,1,0:T(8,128)(2,1)}, bf16[2,192,1536]{2,1,0:T(8,128)(2,1)}, u32[]{:S(2)}, u32[]{:S(2)}) collective-permute-start(bf16[2,192,1536]{2,1,0:T(8,128)(2,1)} %hold.5), channel_id=1, source_target_pairs={{0,32},{16,48},{32,0},{48,16},{1,33},{17,49},{33,1},{49,17},{2,34}... | collective-permute-start | bytes 3538952 | tf_op jit(solution)/shard_map/ppermute | solution.py:163
  (61 other events, 477.7 us)
Sparse Core Ops, SparseCore 0:
  11.7 105.9 all-gather.1
